TPU v7x, 32 devices: a whole 2x2x4 slice. The times are simulated.
32 devices in a mesh: dp: 16 (over z, y, x), tensor: 2 (over core).
Axes of the slice: x: 2, y: 2, z: 4, core: 2. Of those that a mesh axis runs over, the one named last changes fastest.
Arguments:
- layer_in: bfloat16 [2, 16, 1024, 1024], P(None, 'dp', 'tensor'), may hold values from -6 to 6
- segment_ids: int32 [2, 16, 1024], P(None, 'dp'), may hold values from 0 to 7, never falling along the last dimension, each value on 1 to 768 neighbouring positions
- w_mix_in: bfloat16 [1024, 1024], P('dp', 'tensor'), may hold values from -0.1875 to 0.1875
- w_query: bfloat16 [1024, 1024], P('dp', 'tensor'), may hold values from -0.1875 to 0.1875
- w_key: bfloat16 [1024, 1024], P('dp', 'tensor'), may hold values from -0.1875 to 0.1875
- w_value: bfloat16 [1024, 1024], P('dp', 'tensor'), may hold values from -0.1875 to 0.1875
- w_attn_out: bfloat16 [1024, 1024], P('tensor', 'dp'), may hold values from -0.5 to 0.5
- w_up: bfloat16 [1024, 4096], P('dp', 'tensor'), may hold values from -0.1875 to 0.1875
- w_down: bfloat16 [4096, 1024], P('tensor', 'dp'), may hold values from -0.09375 to 0.09375
- norm1_gain: bfloat16 [1024], P('dp'), may hold values from 0.5 to 1.5
- norm1_bias: bfloat16 [1024], P('dp'), may hold values from -1.75 to 1.75
- norm2_gain: bfloat16 [1024], P('dp'), may hold values from 0.5 to 1.5
- norm2_bias: bfloat16 [1024], P('dp'), may hold values from -1.75 to 1.75
- ssm_decay: float32 [16, 1024], P(None, 'tensor'), may hold values from 0.9 to 0.995
- ssm_inject: float32 [16, 1024], P(None, 'tensor'), may hold values from -0.875 to 0.875
- ssm_readout: float32 [16, 1024], P(None, 'tensor'), may hold values from -1.5 to 1.5
- out_grad: bfloat16 [2, 16, 1024, 1024], P(None, 'dp', 'tensor'), may hold values from -6 to 6
Outputs:
- layer_out: float32 [2, 16, 1024, 1024], P(None, 'dp', 'tensor')
- in_grad: float32 [2, 16, 1024, 1024], P(None, 'dp', 'tensor')
- grad_w_mix_in: float32 [1024, 1024], P('dp', 'tensor')
- grad_w_query: float32 [1024, 1024], P('dp', 'tensor')
- grad_w_key: float32 [1024, 1024], P('dp', 'tensor')
- grad_w_value: float32 [1024, 1024], P('dp', 'tensor')
- grad_w_attn_out: float32 [1024, 1024], P('tensor', 'dp')
- grad_w_up: float32 [1024, 4096], P('dp', 'tensor')
- grad_w_down: float32 [4096, 1024], P('tensor', 'dp')
- grad_norm1_gain: float32 [1024], P('dp')
- grad_norm1_bias: float32 [1024], P('dp')
- grad_norm2_gain: float32 [1024], P('dp')
- grad_norm2_bias: float32 [1024], P('dp')
- grad_decay: float32 [16, 1024], P(None, 'tensor')
- grad_inject: float32 [16, 1024], P(None, 'tensor')
- grad_readout: float32 [16, 1024], P(None, 'tensor')
Inputs may be any that keep to these rules, and one draw needn't show every extreme that they name: `segment_ids`: ids never decrease along a sequence; a document holds at most 768 tokens, and some document holds exactly 768.
All inputs are finite; a program needn't handle non-finite values.
Results may differ from a plain program's by a relative error of at most 0.015.
Values may be sent and summed in bfloat16 or wider, within the bound.
No kernel may reach another device: no remote copies, remote signals or barrier semaphores. Data moves between devices by JAX's collectives and lax.ppermute only.
A program may use at most 256 MiB of HBM per device.

v0:
```python
import jax
import jax.numpy as jnp
from jax import lax
from jax.sharding import PartitionSpec as P

HEAD_DIM = 128
BLOCK = 512
CTX = 128
SCAN_BLOCK = 64


norm_eps = 1e-05
masked_score = -1e30


def norm_forward(values, gain_vec, bias_vec):
    centred = values - jnp.mean(values, axis=-1, keepdims=True)
    inverse = lax.rsqrt(jnp.mean(centred * centred, axis=-1, keepdims=True) + norm_eps)
    return centred * inverse * gain_vec + bias_vec


def gelu_exact(values):
    return jax.nn.gelu(values, approximate=False)


def dot_plain(left_op, right_op):
    return jnp.dot(left_op, right_op, preferred_element_type=jnp.float32)


def dot_last(left_op, right_op):
    return lax.dot_general(
        left_op, right_op, (((1,), (1,)), ((), ())), preferred_element_type=jnp.float32
    )


def dot_first(left_op, right_op):
    return lax.dot_general(
        left_op, right_op, (((0,), (0,)), ((), ())), preferred_element_type=jnp.float32
    )


def state_blocks(driving, carry_keep, decay_rate, inject, readout):
    length, channels = driving.shape
    span = SCAN_BLOCK
    count_blocks = length // span
    states_count = decay_rate.shape[0]
    log_rate = jnp.log(decay_rate)
    offsets = jnp.arange(span, dtype=jnp.float32)
    power_up = jnp.exp(offsets[:, None, None] * log_rate[None])
    power_next = jnp.exp((offsets + 1.0)[:, None, None] * log_rate[None])
    power_down = jnp.exp(-offsets[:, None, None] * log_rate[None])
    position = jnp.arange(span, dtype=jnp.int32)
    ordered = position[:, None] >= position[None, :]

    def one_block(carry_state, parts):
        block_in, block_keep = parts
        breaks = jnp.cumsum(1.0 - block_keep)
        same_run = jnp.where(ordered & (breaks[:, None] == breaks[None, :]), 1.0, 0.0).astype(
            jnp.float32
        )
        alive = jnp.where(breaks == 0.0, 1.0, 0.0).astype(jnp.float32)
        scaled = power_down * inject[None] * block_in[:, None, :]
        summed = jnp.dot(
            same_run, scaled.reshape(span, states_count * channels), precision=lax.Precision.HIGHEST
        ).reshape(span, states_count, channels)
        states = power_up * summed + alive[:, None, None] * power_next * carry_state[None]
        return (states[span - 1], jnp.sum(states * readout[None], axis=1))

    blocks_in = driving.reshape(count_blocks, span, channels)
    blocks_keep = carry_keep.reshape(count_blocks, span)
    start_state = jnp.zeros(decay_rate.shape, jnp.float32)
    outputs = lax.scan(jax.checkpoint(one_block), start_state, (blocks_in, blocks_keep))[1]
    return outputs.reshape(length, channels)


def state_blocks_back(driving, carry_keep, decay_rate, inject, readout, upstream):

    def local_scan(d, a, b, c):
        return state_blocks(d, carry_keep, a, b, c)

    pullback = jax.vjp(local_scan, driving, decay_rate, inject, readout)[1]
    return pullback(upstream)


def split_heads(values):
    return values.reshape(values.shape[0], values.shape[1] // HEAD_DIM, HEAD_DIM)


def pad_front(values, fill_value):
    return jnp.concatenate(
        [jnp.full((CTX,) + values.shape[1:], fill_value, values.dtype), values], axis=0
    )


def block_mask(segment_pad, block_first):
    segment_query = segment_pad[block_first + CTX : block_first + CTX + BLOCK]
    segment_key = segment_pad[block_first : block_first + BLOCK + CTX]
    query_pos = jnp.arange(BLOCK, dtype=jnp.int32)[:, None] + CTX
    key_pos = jnp.arange(BLOCK + CTX, dtype=jnp.int32)[None, :]
    return (key_pos <= query_pos) & (segment_key[None, :] == segment_query[:, None])


def attention_forward(query_rows, key_all, value_all, segment_row):
    query_heads = split_heads(query_rows)
    key_pad = pad_front(split_heads(key_all), 0)
    value_pad = pad_front(split_heads(value_all), 0)
    segment_pad = pad_front(segment_row, -1)
    score_scale = HEAD_DIM ** (-0.5)
    outputs = []
    log_totals = []
    for block_index in range(query_rows.shape[0] // BLOCK):
        block_first = block_index * BLOCK
        allowed = block_mask(segment_pad, block_first)
        scores = (
            jnp.einsum(
                "ihd,jhd->hij",
                query_heads[block_first : block_first + BLOCK],
                key_pad[block_first : block_first + BLOCK + CTX],
                preferred_element_type=jnp.float32,
            )
            * score_scale
        )
        scores = jnp.where(allowed[None], scores, masked_score)
        top_score = jnp.max(scores, axis=-1, keepdims=True)
        raised = jnp.exp(scores - top_score)
        row_total = jnp.sum(raised, axis=-1, keepdims=True)
        attn_probs = (raised / row_total).astype(jnp.bfloat16)
        outputs.append(
            jnp.einsum(
                "hij,jhd->ihd",
                attn_probs,
                value_pad[block_first : block_first + BLOCK + CTX],
                preferred_element_type=jnp.float32,
            )
        )
        log_totals.append(top_score + jnp.log(row_total))
    attended = jnp.concatenate(outputs, axis=0).reshape(query_rows.shape).astype(jnp.bfloat16)
    return (attended, log_totals)


def attention_backward(query_rows, key_all, value_all, segment_row, log_totals, grad_attended):
    query_heads = split_heads(query_rows)
    key_pad = pad_front(split_heads(key_all), 0)
    value_pad = pad_front(split_heads(value_all), 0)
    segment_pad = pad_front(segment_row, -1)
    grad_heads = split_heads(grad_attended)
    score_scale = HEAD_DIM ** (-0.5)
    grad_key_pad = jnp.zeros(key_pad.shape, jnp.float32)
    grad_value_pad = jnp.zeros(value_pad.shape, jnp.float32)
    grad_query_blocks = []
    for block_index in range(query_rows.shape[0] // BLOCK):
        block_first = block_index * BLOCK
        allowed = block_mask(segment_pad, block_first)
        query_block = query_heads[block_first : block_first + BLOCK]
        key_block = key_pad[block_first : block_first + BLOCK + CTX]
        value_block = value_pad[block_first : block_first + BLOCK + CTX]
        grad_out_block = grad_heads[block_first : block_first + BLOCK]
        scores = (
            jnp.einsum("ihd,jhd->hij", query_block, key_block, preferred_element_type=jnp.float32)
            * score_scale
        )
        attn_probs = jnp.where(allowed[None], jnp.exp(scores - log_totals[block_index]), 0.0)
        grad_value_pad = grad_value_pad.at[block_first : block_first + BLOCK + CTX].add(
            jnp.einsum(
                "hij,ihd->jhd",
                attn_probs.astype(jnp.bfloat16),
                grad_out_block,
                preferred_element_type=jnp.float32,
            )
        )
        grad_probs = jnp.einsum(
            "ihd,jhd->hij", grad_out_block, value_block, preferred_element_type=jnp.float32
        )
        inner_sum = jnp.sum(attn_probs * grad_probs, axis=-1, keepdims=True)
        grad_scores = (attn_probs * (grad_probs - inner_sum)).astype(jnp.bfloat16)
        grad_query_blocks.append(
            jnp.einsum("hij,jhd->ihd", grad_scores, key_block, preferred_element_type=jnp.float32)
            * score_scale
        )
        grad_key_pad = grad_key_pad.at[block_first : block_first + BLOCK + CTX].add(
            jnp.einsum("hij,ihd->jhd", grad_scores, query_block, preferred_element_type=jnp.float32)
            * score_scale
        )
    grad_query = (
        jnp.concatenate(grad_query_blocks, axis=0).reshape(query_rows.shape).astype(jnp.bfloat16)
    )
    grad_key = grad_key_pad[CTX:].reshape(key_all.shape).astype(jnp.bfloat16)
    grad_value = grad_value_pad[CTX:].reshape(value_all.shape).astype(jnp.bfloat16)
    return (grad_query, grad_key, grad_value)


def gather_rows(values):
    return lax.all_gather(values, "tensor", axis=0, tiled=True)


def scatter_rows(term_fn, half_rows):
    return lax.psum_scatter(
        term_fn(jnp.int32(0), lax.axis_size("tensor") * half_rows).astype(jnp.bfloat16),
        "tensor",
        scatter_dimension=0,
        tiled=True,
    ).astype(jnp.float32)


def micro_step(weights, ssm_params, rows_bf, segment_row, cot_bf):
    (
        mix_full,
        query_full,
        key_full,
        value_full,
        attn_full,
        up_full,
        down_full,
        gain_one,
        bias_one,
        gain_two,
        bias_two,
    ) = weights
    decay_rate, inject, readout = ssm_params
    half_rows = rows_bf.shape[0]
    rows_now = rows_bf.astype(jnp.float32)
    normed = norm_forward(rows_now, gain_one, bias_one).astype(jnp.bfloat16)
    normed_all = gather_rows(normed)
    mixed_in = dot_plain(normed_all, mix_full)
    carry_keep = jnp.concatenate(
        [jnp.zeros((1,), jnp.float32), (segment_row[1:] == segment_row[:-1]).astype(jnp.float32)]
    )
    ssm_local = state_blocks(mixed_in, carry_keep, decay_rate, inject, readout).astype(jnp.bfloat16)
    ssm_all = lax.all_gather(ssm_local, "tensor", axis=1, tiled=True)
    query_rows = dot_plain(normed_all, query_full).astype(jnp.bfloat16)
    key_all = dot_plain(ssm_all, key_full).astype(jnp.bfloat16)
    value_all = dot_plain(ssm_all, value_full).astype(jnp.bfloat16)
    attended, log_totals = attention_forward(query_rows, key_all, value_all, segment_row)
    branch_one = scatter_rows(
        lambda row_first, row_count: dot_plain(attended, attn_full), half_rows
    )
    middle = rows_now + branch_one
    normed_two = norm_forward(middle, gain_two, bias_two).astype(jnp.bfloat16)
    normed_two_all = gather_rows(normed_two)
    hidden_pre = dot_plain(normed_two_all, up_full)
    hidden = gelu_exact(hidden_pre).astype(jnp.bfloat16)
    branch_two = scatter_rows(lambda row_first, row_count: dot_plain(hidden, down_full), half_rows)
    cot_all = gather_rows(cot_bf)
    grad_hidden = dot_last(cot_all, down_full)
    grad_down = dot_first(hidden, cot_all)
    grad_pre = jax.vjp(gelu_exact, hidden_pre)[1](grad_hidden)[0].astype(jnp.bfloat16)
    grad_up = dot_first(normed_two_all, grad_pre)
    grad_normed_two = scatter_rows(
        lambda row_first, row_count: dot_last(grad_pre, up_full), half_rows
    )
    layer_out = middle + branch_two
    norm_back_two = jax.vjp(norm_forward, middle, gain_two, bias_two)[1]
    grad_middle_norm, grad_gain_two, grad_bias_two = norm_back_two(grad_normed_two)
    grad_middle = cot_bf.astype(jnp.float32) + grad_middle_norm
    grad_branch_all = gather_rows(grad_middle.astype(jnp.bfloat16))
    grad_attended = dot_last(grad_branch_all, attn_full).astype(jnp.bfloat16)
    grad_attn = dot_first(attended, grad_branch_all)
    grad_query, grad_key, grad_value = attention_backward(
        query_rows, key_all, value_all, segment_row, log_totals, grad_attended
    )
    grad_query_w = dot_first(normed_all, grad_query)
    grad_key_w = dot_first(ssm_all, grad_key)
    grad_value_w = dot_first(ssm_all, grad_value)
    grad_ssm_part = dot_last(grad_key, key_full) + dot_last(grad_value, value_full)
    grad_ssm = lax.psum_scatter(
        grad_ssm_part.astype(jnp.bfloat16), "tensor", scatter_dimension=1, tiled=True
    ).astype(jnp.float32)
    grad_mixed, grad_decay, grad_inject, grad_readout = state_blocks_back(
        mixed_in, carry_keep, decay_rate, inject, readout, grad_ssm
    )
    grad_mixed = grad_mixed.astype(jnp.bfloat16)
    grad_mix_w = dot_first(normed_all, grad_mixed)

    def input_back(row_first, row_count):
        return dot_last(grad_query, query_full) + dot_last(grad_mixed, mix_full)

    grad_normed = scatter_rows(input_back, half_rows)
    norm_back_one = jax.vjp(norm_forward, rows_now, gain_one, bias_one)[1]
    grad_rows_norm, grad_gain_one, grad_bias_one = norm_back_one(grad_normed)
    grad_rows = grad_middle + grad_rows_norm
    local_grads = (
        grad_mix_w,
        grad_query_w,
        grad_key_w,
        grad_value_w,
        grad_attn,
        grad_up,
        grad_down,
        grad_gain_one,
        grad_bias_one,
        grad_gain_two,
        grad_bias_two,
        grad_decay,
        grad_inject,
        grad_readout,
    )
    return (layer_out, grad_rows, local_grads)


def finish_grads(local_grads):
    members = list(local_grads)
    shards = (
        lax.psum_scatter(members[0], "dp", scatter_dimension=0, tiled=True),
        lax.psum_scatter(members[1], "dp", scatter_dimension=0, tiled=True),
        lax.psum_scatter(members[2], "dp", scatter_dimension=0, tiled=True),
        lax.psum_scatter(members[3], "dp", scatter_dimension=0, tiled=True),
        lax.psum_scatter(members[4], "dp", scatter_dimension=1, tiled=True),
        lax.psum_scatter(members[5], "dp", scatter_dimension=0, tiled=True),
        lax.psum_scatter(members[6], "dp", scatter_dimension=1, tiled=True),
        lax.psum_scatter(members[7], "dp", scatter_dimension=0, tiled=True),
        lax.psum_scatter(members[8], "dp", scatter_dimension=0, tiled=True),
        lax.psum_scatter(members[9], "dp", scatter_dimension=0, tiled=True),
        lax.psum_scatter(members[10], "dp", scatter_dimension=0, tiled=True),
    )
    gain_sums = lax.psum((shards[7], shards[8], shards[9], shards[10]), "tensor")
    mixer_sums = lax.psum((members[11], members[12], members[13]), "dp")
    return tuple(shards[:7]) + tuple(gain_sums) + tuple(mixer_sums)


def per_device(
    layer_in,
    segment_ids,
    w_mix_in,
    w_query,
    w_key,
    w_value,
    w_attn_out,
    w_up,
    w_down,
    norm1_gain,
    norm1_bias,
    norm2_gain,
    norm2_bias,
    ssm_decay,
    ssm_inject,
    ssm_readout,
    out_grad,
):
    gathered = (
        lax.all_gather(w_mix_in, "dp", axis=0, tiled=True),
        lax.all_gather(w_query, "dp", axis=0, tiled=True),
        lax.all_gather(w_key, "dp", axis=0, tiled=True),
        lax.all_gather(w_value, "dp", axis=0, tiled=True),
        lax.all_gather(w_attn_out, "dp", axis=1, tiled=True),
        lax.all_gather(w_up, "dp", axis=0, tiled=True),
        lax.all_gather(w_down, "dp", axis=1, tiled=True),
        lax.all_gather(norm1_gain, "dp", axis=0, tiled=True),
        lax.all_gather(norm1_bias, "dp", axis=0, tiled=True),
        lax.all_gather(norm2_gain, "dp", axis=0, tiled=True),
        lax.all_gather(norm2_bias, "dp", axis=0, tiled=True),
    )
    mix_full, query_full, key_full, value_full, attn_full, up_full, down_full = gathered[:7]
    norm_params = tuple((member.astype(jnp.float32) for member in gathered[7:]))
    weights = (
        mix_full,
        query_full,
        key_full,
        value_full,
        attn_full,
        up_full,
        down_full,
    ) + norm_params
    ssm_params = (ssm_decay, ssm_inject, ssm_readout)
    start_like = weights + ssm_params
    running = tuple((jnp.zeros(member.shape, jnp.float32) for member in start_like))

    def run_micro(running_now, inputs_now):
        rows_bf, segment_row, cot_bf = inputs_now
        layer_out, grad_rows, local_grads = micro_step(
            weights, ssm_params, rows_bf, segment_row, cot_bf
        )
        running_now = tuple((a + b for a, b in zip(running_now, local_grads)))
        return (running_now, (layer_out, grad_rows))

    running, (outputs, grad_in) = lax.scan(
        run_micro, running, (layer_in[:, 0], segment_ids[:, 0], out_grad[:, 0])
    )
    results = finish_grads(running)
    return (outputs[:, None], grad_in[:, None]) + tuple(results)


def solution(mesh):
    return jax.shard_map(
        per_device,
        mesh=mesh,
        in_specs=(
            P(None, "dp", "tensor", None),
            P(None, "dp", None),
            P("dp", "tensor"),
            P("dp", "tensor"),
            P("dp", "tensor"),
            P("dp", "tensor"),
            P("tensor", "dp"),
            P("dp", "tensor"),
            P("tensor", "dp"),
            P("dp"),
            P("dp"),
            P("dp"),
            P("dp"),
            P(None, "tensor"),
            P(None, "tensor"),
            P(None, "tensor"),
            P(None, "dp", "tensor", None),
        ),
        out_specs=(
            P(None, "dp", "tensor", None),
            P(None, "dp", "tensor", None),
            P("dp", "tensor"),
            P("dp", "tensor"),
            P("dp", "tensor"),
            P("dp", "tensor"),
            P("tensor", "dp"),
            P("dp", "tensor"),
            P("tensor", "dp"),
            P("dp"),
            P("dp"),
            P("dp"),
            P("dp"),
            P(None, "tensor"),
            P(None, "tensor"),
            P(None, "tensor"),
        ),
        check_vma=False,
    )
```

profile of v0, /device:TPU:0, one launch (start us, length us, event | category | flops | bytes accessed | tf_op | source)
XLA Modules:
  0.0 3257.7 jit_solution(13383970954636432371)
XLA Ops:
  17.4 44.2 %all-reduce.16 = (bf16[1024]{0:T(1024)(128)(2,1)S(1)}, bf16[1024]{0:T(1024)(128)(2,1)S(1)}, bf16[1024]{0:T(1024)(128)(2,1)S(1)}, bf16[1024]{0:T(1024)(128)(2,1)S(1)}) all-reduce(bf16[1024]{0:T(1024)(128)(2,1)S(1)} %dynamic-update-slice.26, bf16[1024]{0:T(1024)(128)(2,1)S(1)} %dynamic-update-slice.27, ...), channel_id=1, replica_groups=mesh['dp'=16,'tensor'=2] {'dp'}, use_global_device_ids=true, to_apply=%add.6 | all-reduce | flops 4096 | bytes 16384
  71.2 75.4 %all-gather.29.cloned.1.call-done = bf16[2048,1024]{0,1:T(8,128)(2,1)} async-done(((bf16[2048,64]{0,1:T(8,128)(2,1)}), bf16[2048,1024]{0,1:T(8,128)(2,1)}) %all-gather.29.cloned.1.call-update) | async-done | bytes 4194320 | tf_op jit(solution)/shard_map/all_gather | solution.py:346
  153.0 50.3 %all-gather.17.cloned.1.call-done = bf16[1024,512]{1,0:T(8,128)(2,1)} async-done(((bf16[64,512]{1,0:T(8,128)(2,1)}), bf16[1024,512]{1,0:T(8,128)(2,1)}) %all-gather.17.cloned.1.call-update) | async-done | bytes 1048592 | tf_op jit(solution)/shard_map/all_gather | solution.py:341
  203.3 56.7 %all-gather.19.cloned.1.call-done = bf16[1024,512]{1,0:T(8,128)(2,1)} async-done(((bf16[64,512]{1,0:T(8,128)(2,1)}), bf16[1024,512]{1,0:T(8,128)(2,1)}) %all-gather.19.cloned.1.call-update) | async-done | bytes 1048592 | tf_op jit(solution)/shard_map/all_gather | solution.py:340
  260.0 56.7 %all-gather.21.cloned.1.call-done = bf16[1024,512]{1,0:T(8,128)(2,1)} async-done(((bf16[64,512]{1,0:T(8,128)(2,1)}), bf16[1024,512]{1,0:T(8,128)(2,1)}) %all-gather.21.cloned.1.call-update) | async-done | bytes 1048592 | tf_op jit(solution)/shard_map/all_gather | solution.py:342
  316.8 56.7 %all-gather.23.cloned.1.call-done = bf16[1024,512]{1,0:T(8,128)(2,1)} async-done(((bf16[64,512]{1,0:T(8,128)(2,1)}), bf16[1024,512]{1,0:T(8,128)(2,1)}) %all-gather.23.cloned.1.call-update) | async-done | bytes 1048592 | tf_op jit(solution)/shard_map/all_gather | solution.py:343
  373.5 77.7 %all-gather.27.cloned.1.call-done = bf16[1024,2048]{1,0:T(8,128)(2,1)} async-done(((bf16[64,2048]{1,0:T(8,128)(2,1)}), bf16[1024,2048]{1,0:T(8,128)(2,1)}) %all-gather.27.cloned.1.call-update) | async-done | bytes 4194320 | tf_op jit(solution)/shard_map/all_gather | solution.py:345
  451.2 1913.9 %while.181 = (s32[]{:T(128)}, f32[1024,512]{1,0:T(8,128)}, f32[1024,512]{1,0:T(8,128)}, f32[1024,512]{1,0:T(8,128)}, f32[1024,512]{1,0:T(8,128)}, /*index=5*/f32...) while((s32[]{:T(128)}, f32[1024,512]{1,0:T(8,128)}, ...), condition=%wide.region_41.42_spmd.clone, body=%wide.region_0.41_spmd.clone.sunk | while | flops 47861145600 | bytes 1027950208 | solution.py:375
  454.5 9.0 all-gather.31.cloned.1.call-done
  467.8 186.9 %while.183 = (s32[]{:T(128)}, f32[16,512]{1,0:T(8,128)S(1)}, bf16[16,64,512]{2,1,0:T(8,128)(2,1)S(1)}, f32[16,64]{1,0:T(8,128)S(1)}, f32[16,512]{1,0:T(8,128)}, ...) while((s32[]{:T(128)}, f32[16,512]{1,0:T(8,128)S(1)}, ...), condition=%wide.region_6.6_spmd.clone.clone, body=%wide.region_3.5_spmd.clone.clone.sunk | while | flops 408408192 | bytes 24022672 | solution.py:72
  693.4 10.9 reduce-scatter.27.cloned.1.call-done
  710.5 9.5 all-gather.35.cloned.1.call-done
  720.0 26.1 multiply_convert_fusion.6
  746.1 12.9 add_convert_fusion.12
  766.9 10.9 reduce-scatter.29.cloned.1.call-done
  784.4 11.8 all-gather.39.cloned.1.call-done
  823.7 162.4 %while.182 = (s32[]{:T(128)}, f32[16,512]{1,0:T(8,128)S(1)}, f32[16,16,512]{2,1,0:T(8,128)}, f32[16,64]{1,0:T(8,128)}, f32[16,64,512]{2,1,0:T(8,128)}, /*index=5...) while((s32[]{:T(128)}, f32[16,512]{1,0:T(8,128)S(1)}, ...), condition=%wide.region_22.22_spmd.clone.clone, body=%wide.region_20.21_spmd.clone.clone.sunk | while | flops 404312192 | bytes 7016093 | solution.py:72
  999.1 345.5 %while.184 = (s32[]{:T(128)}, f32[16,512]{1,0:T(8,128)S(1)}, f32[64,16,512]{2,0,1:T(8,128)}, f32[64,16,512]{2,0,1:T(8,128)}, f32[64,16,512]{2,0,1:T(8,128)}, /*i...) while((s32[]{:T(128)}, f32[16,512]{1,0:T(8,128)S(1)}, ...), condition=%wide.region_29.29_spmd.clone.clone.clone, body=%wide.region_23.28_spmd.clone.clone.clone.sunk | while | flops 822091904 | bytes 50252440 | solution.py:72
  1027.4 7.8 multiply_reduce_fusion.23
  1092.3 7.8 multiply_reduce_fusion.23
  1157.2 7.8 multiply_reduce_fusion.23
  1350.1 9.3 convolution_convert_fusion.20
  1361.2 9.2 select_add_fusion.37
  1406.7 11.6 all-gather.31.cloned.1.call-done
  1422.6 186.9 %while.183 = (s32[]{:T(128)}, f32[16,512]{1,0:T(8,128)S(1)}, bf16[16,64,512]{2,1,0:T(8,128)(2,1)S(1)}, f32[16,64]{1,0:T(8,128)S(1)}, f32[16,512]{1,0:T(8,128)}, ...) while((s32[]{:T(128)}, f32[16,512]{1,0:T(8,128)S(1)}, ...), condition=%wide.region_6.6_spmd.clone.clone, body=%wide.region_3.5_spmd.clone.clone.sunk | while | flops 408408192 | bytes 24022672 | solution.py:72
  1647.9 10.9 reduce-scatter.27.cloned.1.call-done
  1665.0 9.5 all-gather.35.cloned.1.call-done
  1674.5 26.1 multiply_convert_fusion.6
  1700.7 12.9 add_convert_fusion.12
  1721.4 10.9 reduce-scatter.29.cloned.1.call-done
  1739.0 11.8 all-gather.39.cloned.1.call-done
  1778.2 162.4 %while.182 = (s32[]{:T(128)}, f32[16,512]{1,0:T(8,128)S(1)}, f32[16,16,512]{2,1,0:T(8,128)}, f32[16,64]{1,0:T(8,128)}, f32[16,64,512]{2,1,0:T(8,128)}, /*index=5...) while((s32[]{:T(128)}, f32[16,512]{1,0:T(8,128)S(1)}, ...), condition=%wide.region_22.22_spmd.clone.clone, body=%wide.region_20.21_spmd.clone.clone.sunk | while | flops 404312192 | bytes 7016093 | solution.py:72
  1953.6 345.5 %while.184 = (s32[]{:T(128)}, f32[16,512]{1,0:T(8,128)S(1)}, f32[64,16,512]{2,0,1:T(8,128)}, f32[64,16,512]{2,0,1:T(8,128)}, f32[64,16,512]{2,0,1:T(8,128)}, /*i...) while((s32[]{:T(128)}, f32[16,512]{1,0:T(8,128)S(1)}, ...), condition=%wide.region_29.29_spmd.clone.clone.clone, body=%wide.region_23.28_spmd.clone.clone.clone.sunk | while | flops 822091904 | bytes 50252440 | solution.py:72
  1981.9 7.8 multiply_reduce_fusion.23
  2046.8 7.8 multiply_reduce_fusion.23
  2111.7 7.8 multiply_reduce_fusion.23
  2304.7 9.3 convolution_convert_fusion.20
  2315.7 10.5 select_add_fusion.37
  2326.3 9.9 select_add_fusion.38
  2371.5 9.2 copy.95
  2382.1 98.4 %all-reduce.19.cloned.1.call-done = (f32[1024]{0:T(1024)}, f32[1024]{0:T(1024)}, f32[1024]{0:T(1024)}, f32[1024]{0:T(1024)}, f32[16,512]{1,0:T(8,128)}, /*index=5*/f32[16,512]{1,0:T(8,128)}, f32[16,512]{1,0:T(8,128)}) async-done(((f32[1024]{0:T(1024)}, f32[1024]{0:T(1024)}, f32[1024]{0:T(1024)}, f32[1024]{0:T(1024)}, f32[16,512]{1,0:T(8,128)}, /*index=5*/f32[16,512]{1,0:T(8,128)}, f32[16,512]{1,0:T(8,128)}), ...) | async-done | bytes 114704
  2486.5 77.6 %reduce-scatter.21.cloned.1.call-done = f32[512,64]{0,1:T(8,128)} async-done(((f32[512,1024]{0,1:T(8,128)}), f32[512,64]{0,1:T(8,128)}) %reduce-scatter.21.cloned.1.call-update) | async-done | bytes 131088 | tf_op jit(solution)/shard_map/reduce_scatter | solution.py:307
  2564.1 80.3 %reduce-scatter.13.cloned.1.call-done = f32[64,512]{1,0:T(8,128)} async-done(((f32[1024,512]{1,0:T(8,128)}), f32[64,512]{1,0:T(8,128)}) %reduce-scatter.13.cloned.1.call-update) | async-done | bytes 131088 | tf_op jit(solution)/shard_map/reduce_scatter | solution.py:303
  2644.5 80.6 %reduce-scatter.15.cloned.1.call-done = f32[64,512]{1,0:T(8,128)} async-done(((f32[1024,512]{1,0:T(8,128)}), f32[64,512]{1,0:T(8,128)}) %reduce-scatter.15.cloned.1.call-update) | async-done | bytes 131088 | tf_op jit(solution)/shard_map/reduce_scatter | solution.py:304
  2725.1 80.4 %reduce-scatter.17.cloned.1.call-done = f32[64,512]{1,0:T(8,128)} async-done(((f32[1024,512]{1,0:T(8,128)}), f32[64,512]{1,0:T(8,128)}) %reduce-scatter.17.cloned.1.call-update) | async-done | bytes 131088 | tf_op jit(solution)/shard_map/reduce_scatter | solution.py:305
  2805.5 80.3 %reduce-scatter.19.cloned.1.call-done = f32[64,512]{1,0:T(8,128)} async-done(((f32[1024,512]{1,0:T(8,128)}), f32[64,512]{1,0:T(8,128)}) %reduce-scatter.19.cloned.1.call-update) | async-done | bytes 131088 | tf_op jit(solution)/shard_map/reduce_scatter | solution.py:306
  2885.8 177.9 %reduce-scatter.25.cloned.1.call-done = f32[2048,64]{0,1:T(8,128)} async-done(((f32[2048,1024]{0,1:T(8,128)}), f32[2048,64]{0,1:T(8,128)}) %reduce-scatter.25.cloned.1.call-update) | async-done | bytes 524304 | tf_op jit(solution)/shard_map/reduce_scatter | solution.py:309
  3063.7 183.2 %reduce-scatter.23.cloned.1.call-done = f32[64,2048]{1,0:T(8,128)} async-done(((f32[1024,2048]{1,0:T(8,128)}), f32[64,2048]{1,0:T(8,128)}) %reduce-scatter.23.cloned.1.call-update) | async-done | bytes 524304 | tf_op jit(solution)/shard_map/reduce_scatter | solution.py:308
  (2540 shorter events, 1664.6 us)
Async XLA Ops:
  7.2 61.8 %all-gather.25.cloned.1.call-start = ((), (), s32[]{:S(2)}) async-start(), calls=%async_computation.16 | async-start | bytes 1114112 | tf_op jit(solution)/shard_map/all_gather | solution.py:344
  7.9 138.7 %all-gather.29.cloned.1.call-start = ((), (), s32[]{:S(2)}) async-start(), calls=%async_computation.18 | async-start | bytes 4456448 | tf_op jit(solution)/shard_map/all_gather | solution.py:346
  8.7 194.6 %all-gather.17.cloned.1.call-start = ((), (), s32[]{:S(2)}) async-start(), calls=%async_computation.12 | async-start | bytes 1114112 | tf_op jit(solution)/shard_map/all_gather | solution.py:341
  9.4 250.6 %all-gather.19.cloned.1.call-start = ((), (), s32[]{:S(2)}) async-start(), calls=%async_computation.13 | async-start | bytes 1114112 | tf_op jit(solution)/shard_map/all_gather | solution.py:340
  10.0 306.8 %all-gather.21.cloned.1.call-start = ((), (), s32[]{:S(2)}) async-start(), calls=%async_computation.14 | async-start | bytes 1114112 | tf_op jit(solution)/shard_map/all_gather | solution.py:342
  10.6 362.9 %all-gather.23.cloned.1.call-start = ((), (), s32[]{:S(2)}) async-start(), calls=%async_computation.15 | async-start | bytes 1114112 | tf_op jit(solution)/shard_map/all_gather | solution.py:343
  11.1 440.0 %all-gather.27.cloned.1.call-start = ((), (), s32[]{:S(2)}) async-start(), calls=%async_computation.17 | async-start | bytes 4456448 | tf_op jit(solution)/shard_map/all_gather | solution.py:345
  71.2 379.9 %copy-start.7 = (bf16[2,1,512,1024]{3,2,1,0:T(8,128)(2,1)S(1)}, bf16[2,1,512,1024]{3,2,1,0:T(8,128)(2,1)}, u32[]{:S(2)}) copy-start(bf16[2,1,512,1024]{3,2,1,0:T(8,128)(2,1)} %param.33) | copy-start | bytes 6291460
  451.2 204.8 %copy-start.58 = (s32[2,1024]{1,0:T(2,128)}, s32[2,1024]{1,0:T(2,128)S(1)}, u32[]{:S(2)}) copy-start(s32[2,1024]{1,0:T(2,128)S(1)} %get-tuple-element.2980) | copy-start | bytes 24580 | tf_op jit(solution)/shard_map/while
  451.2 255.3 %copy-start.84 = (f32[1024]{0:T(1024)}, f32[1024]{0:T(1024)S(1)}, u32[]{:S(2)}) copy-start(f32[1024]{0:T(1024)S(1)} %get-tuple-element.2990) | copy-start | bytes 12292 | tf_op jit(solution)/shard_map/while
  451.2 329.5 %copy-start.67 = (f32[1024]{0:T(1024)}, f32[1024]{0:T(1024)S(1)}, u32[]{:S(2)}) copy-start(f32[1024]{0:T(1024)S(1)} %get-tuple-element.2989) | copy-start | bytes 12292 | tf_op jit(solution)/shard_map/while
  451.2 12.3 all-gather.31.cloned.1.call-start
  451.9 15.8 copy-start.73
  451.9 15.8 copy-start.71
  454.2 213.5 %all-gather.33.cloned.1.call-start = ((), (), s32[]{:S(2)}) async-start(), calls=%async_computation.28 | async-start | bytes 3145728 | tf_op jit(solution)/shard_map/while/body/eval_jaxpr/all_gather | solution.py:229
  655.8 48.5 %reduce-scatter.27.cloned.1.call-start = ((), (), s32[]{:S(2)}) async-start(), calls=%async_computation.29 | async-start | bytes 3145728 | tf_op jit(solution)/shard_map/while/body/eval_jaxpr/reduce_scatter | solution.py:197
  693.3 26.7 all-gather.35.cloned.1.call-start
  708.1 38.1 %all-gather.37.cloned.1.call-start = ((), (), s32[]{:S(2)}) async-start(), calls=%async_computation.31 | async-start | bytes 3145728 | tf_op jit(solution)/shard_map/while/body/eval_jaxpr/all_gather | solution.py:193
  710.4 67.3 %reduce-scatter.29.cloned.1.call-start = ((), (), s32[]{:S(2)}) async-start(), calls=%async_computation.32 | async-start | bytes 3145728 | tf_op jit(solution)/shard_map/while/body/eval_jaxpr/reduce_scatter | solution.py:197
  746.1 14.9 copy-start.94
  766.9 29.4 all-gather.39.cloned.1.call-start
  784.3 210.3 %reduce-scatter.31.cloned.1.call-start = ((), (), s32[]{:S(2)}) async-start(), calls=%async_computation.34 | async-start | bytes 3145728 | tf_op jit(solution)/shard_map/while/body/eval_jaxpr/reduce_scatter | solution.py:265
  823.0 571.8 %reduce-scatter.33.cloned.1.call-start = ((), (), s32[]{:S(2)}) async-start(), calls=%async_computation.35 | async-start | bytes 3145728 | tf_op jit(solution)/shard_map/while/body/eval_jaxpr/reduce_scatter | solution.py:197
  1350.1 48.5 %reduce-scatter.35.cloned.1.call-start = ((), (), s32[]{:S(2)}) async-start(), calls=%async_computation.36 | async-start | bytes 3145728 | tf_op jit(solution)/shard_map/while/body/eval_jaxpr/reduce_scatter | solution.py:197
  1403.3 207.3 %copy-start.58 = (s32[2,1024]{1,0:T(2,128)}, s32[2,1024]{1,0:T(2,128)S(1)}, u32[]{:S(2)}) copy-start(s32[2,1024]{1,0:T(2,128)S(1)} %get-tuple-element.2980) | copy-start | bytes 24580 | tf_op jit(solution)/shard_map/while
  1403.3 257.7 %copy-start.84 = (f32[1024]{0:T(1024)}, f32[1024]{0:T(1024)S(1)}, u32[]{:S(2)}) copy-start(f32[1024]{0:T(1024)S(1)} %get-tuple-element.2990) | copy-start | bytes 12292 | tf_op jit(solution)/shard_map/while
  1403.4 331.8 %copy-start.67 = (f32[1024]{0:T(1024)}, f32[1024]{0:T(1024)S(1)}, u32[]{:S(2)}) copy-start(f32[1024]{0:T(1024)S(1)} %get-tuple-element.2989) | copy-start | bytes 12292 | tf_op jit(solution)/shard_map/while
  1403.4 14.9 all-gather.31.cloned.1.call-start
  1404.1 18.4 copy-start.73
  1404.1 18.3 copy-start.71
  1406.3 216.0 %all-gather.33.cloned.1.call-start = ((), (), s32[]{:S(2)}) async-start(), calls=%async_computation.28 | async-start | bytes 3145728 | tf_op jit(solution)/shard_map/while/body/eval_jaxpr/all_gather | solution.py:229
  1610.5 48.3 %reduce-scatter.27.cloned.1.call-start = ((), (), s32[]{:S(2)}) async-start(), calls=%async_computation.29 | async-start | bytes 3145728 | tf_op jit(solution)/shard_map/while/body/eval_jaxpr/reduce_scatter | solution.py:197
  1647.9 26.6 all-gather.35.cloned.1.call-start
  1662.6 38.0 %all-gather.37.cloned.1.call-start = ((), (), s32[]{:S(2)}) async-start(), calls=%async_computation.31 | async-start | bytes 3145728 | tf_op jit(solution)/shard_map/while/body/eval_jaxpr/all_gather | solution.py:193
  1665.0 67.3 %reduce-scatter.29.cloned.1.call-start = ((), (), s32[]{:S(2)}) async-start(), calls=%async_computation.32 | async-start | bytes 3145728 | tf_op jit(solution)/shard_map/while/body/eval_jaxpr/reduce_scatter | solution.py:197
  1700.6 14.9 copy-start.94
  1721.4 29.4 all-gather.39.cloned.1.call-start
  1738.8 210.3 %reduce-scatter.31.cloned.1.call-start = ((), (), s32[]{:S(2)}) async-start(), calls=%async_computation.34 | async-start | bytes 3145728 | tf_op jit(solution)/shard_map/while/body/eval_jaxpr/reduce_scatter | solution.py:265
  1777.6 577.3 %reduce-scatter.33.cloned.1.call-start = ((), (), s32[]{:S(2)}) async-start(), calls=%async_computation.35 | async-start | bytes 3145728 | tf_op jit(solution)/shard_map/while/body/eval_jaxpr/reduce_scatter | solution.py:197
  2304.6 54.1 %reduce-scatter.35.cloned.1.call-start = ((), (), s32[]{:S(2)}) async-start(), calls=%async_computation.36 | async-start | bytes 3145728 | tf_op jit(solution)/shard_map/while/body/eval_jaxpr/reduce_scatter | solution.py:197
  2365.1 115.4 %all-reduce.19.cloned.1.call-start = ((), (), s32[]{:S(2)}) async-start(), calls=%async_computation.26 | async-start | bytes 229376
  2365.9 198.3 %reduce-scatter.21.cloned.1.call-start = ((), (), s32[]{:S(2)}) async-start(), calls=%async_computation.23 | async-start | bytes 2228224 | tf_op jit(solution)/shard_map/reduce_scatter | solution.py:307
  2368.8 275.6 %reduce-scatter.13.cloned.1.call-start = ((), (), s32[]{:S(2)}) async-start(), calls=%async_computation.19 | async-start | bytes 2228224 | tf_op jit(solution)/shard_map/reduce_scatter | solution.py:303
  2369.4 355.7 %reduce-scatter.15.cloned.1.call-start = ((), (), s32[]{:S(2)}) async-start(), calls=%async_computation.20 | async-start | bytes 2228224 | tf_op jit(solution)/shard_map/reduce_scatter | solution.py:304
  2370.2 435.3 %reduce-scatter.17.cloned.1.call-start = ((), (), s32[]{:S(2)}) async-start(), calls=%async_computation.21 | async-start | bytes 2228224 | tf_op jit(solution)/shard_map/reduce_scatter | solution.py:305
  2370.9 514.9 %reduce-scatter.19.cloned.1.call-start = ((), (), s32[]{:S(2)}) async-start(), calls=%async_computation.22 | async-start | bytes 2228224 | tf_op jit(solution)/shard_map/reduce_scatter | solution.py:306
  2371.5 692.2 %reduce-scatter.25.cloned.1.call-start = ((), (), s32[]{:S(2)}) async-start(), calls=%async_computation.25 | async-start | bytes 8912896 | tf_op jit(solution)/shard_map/reduce_scatter | solution.py:309
  2380.7 866.1 %reduce-scatter.23.cloned.1.call-start = ((), (), s32[]{:S(2)}) async-start(), calls=%async_computation.24 | async-start | bytes 8912896 | tf_op jit(solution)/shard_map/reduce_scatter | solution.py:308
  (382 other events, 1598.4 us)
Sparse Core Ops, SparseCore 0:
  10.8 58.1 all-gather.24
  71.7 74.8 all-gather.28
  149.4 53.8 all-gather.16
  205.9 54.0 all-gather.18
  262.6 54.0 all-gather.20
  319.4 54.0 all-gather.22
  376.2 74.8 all-gather.26
  454.3 9.1 all-gather.30
  655.9 11.7 all-gather.32
  693.4 10.7 reduce-scatter.26
  708.2 11.7 all-gather.34
  721.4 11.7 all-gather.36
  767.0 10.7 reduce-scatter.28
  784.4 11.7 all-gather.38
  823.1 10.7 reduce-scatter.30
  1350.2 10.7 reduce-scatter.32
  1363.1 10.7 reduce-scatter.34
  1406.5 11.7 all-gather.30
  1610.6 11.7 all-gather.32
  1648.0 10.7 reduce-scatter.26
  1662.7 11.7 all-gather.34
  1676.1 11.7 all-gather.36
  1721.5 10.7 reduce-scatter.28
  1738.9 11.7 all-gather.38
  1777.7 10.7 reduce-scatter.30
  2304.7 10.7 reduce-scatter.32
  2317.6 10.7 reduce-scatter.34
  2372.9 107.5 all-reduce.18
  2483.4 80.6 reduce-scatter.20
  2566.8 77.5 reduce-scatter.12
  2647.3 77.7 reduce-scatter.14
  2727.9 77.5 reduce-scatter.16
  2808.2 77.5 reduce-scatter.18
  2888.7 174.9 reduce-scatter.24
  3066.6 180.2 reduce-scatter.22
where the time goes:
time: 3290 us; the launch traced here: 3260 us
  waiting for transfers between devices  1360 us (41%)
  matrix products  880 us (27%)
  local copies, waits for them, and re-layouts  517 us (16%)
  other arithmetic  420 us (13%)
  blocking collectives  47.2 us (1%)
    dot_general x128, matrix products, one_block(): jnp.dot(same_run, scaled.reshape(span, states_count * channels), precisio...  607 us
    while x948, local copies, waits for them, and re-layouts  206 us
    reduce_scatter x1, waiting for transfers between devices, finish_grads(): lax.psum_scatter(members[5], 'dp', scatter_dimension=0, tiled=True)  183 us
    reduce_scatter x1, waiting for transfers between devices, finish_grads(): lax.psum_scatter(members[6], 'dp', scatter_dimension=1, tiled=True)  178 us
    exp x32, other arithmetic, state_blocks(): power_next = jnp.exp((offsets + 1.0)[:, None, None] * log_rate[None])  118 us
    unnamed x16, waiting for transfers between devices  107 us
    dot_general x14, matrix products, dot_plain(): return jnp.dot(left_op, right_op, preferred_element_type=jnp.float32)  104 us
    mul x64, other arithmetic, one_block(): scaled = power_down * inject[None] * block_in[:, None, :]  88.1 us
  transfers between devices with their start and end apart: 35, of which 27 were waited for; matrix products, arithmetic and copies ran while one was open for 16% of the time, Pallas kernels for 0%

commit v1 on v0

v1 whole, which is shorter than its diff:
```python
import functools
import math

import jax
import jax.numpy as jnp
from jax import lax
from jax.experimental import pallas as pl
from jax.experimental.pallas import tpu as pltpu
from jax.sharding import PartitionSpec as P

HEAD_DIM = 128
BLOCK = 512
CTX = 128
NDOCS = 8
LANES = 128
QTILE = 256

norm_eps = 1e-05
masked_score = -1e30
VMEM = 56 * 1024 * 1024
BF = jnp.bfloat16
F32 = jnp.float32


def dot_plain(left_op, right_op):
    return jnp.dot(left_op, right_op, preferred_element_type=F32)


def dot_last(left_op, right_op):
    return lax.dot_general(left_op, right_op, (((1,), (1,)), ((), ())), preferred_element_type=F32)


def dot_first(left_op, right_op):
    return lax.dot_general(left_op, right_op, (((0,), (0,)), ((), ())), preferred_element_type=F32)


def params(count=1):
    return pltpu.CompilerParams(
        dimension_semantics=("arbitrary",) * count, vmem_limit_bytes=VMEM
    )


def bits_of(count):
    out = []
    bit = 1
    while bit < count:
        out.append(bit)
        bit *= 2
    return out


def gather_order(count, flip):
    bits = bits_of(count)
    low = bits[:2]
    return bits[2:] + (low[::-1] if flip else low)


def swap(values, axis_name, count, bit):
    return lax.ppermute(values, axis_name, [(i, i ^ bit) for i in range(count)])


def after(values, earlier):
    return lax.optimization_barrier((values, earlier))[0]


def gather_rows(shard, count, index, flip):
    values = shard
    present = []
    half_way = None
    for bit in gather_order(count, flip):
        other = swap(values, "dp", count, bit)
        place = sum(1 for p in present if p > bit)
        upper = (index // bit) % 2 == 1
        first = jnp.where(upper, other, values)
        second = jnp.where(upper, values, other)
        values = jnp.stack([first, second], axis=place)
        present.append(bit)
        if len(present) == 2:
            half_way = values
    return values.reshape((count * shard.shape[0],) + shard.shape[1:]), half_way


def scatter_rows(full, count, index, flip):
    bits = bits_of(count)
    rows = full.shape[0] // count
    values = full.reshape((2,) * len(bits) + (rows,) + full.shape[1:])
    present = sorted(bits, reverse=True)
    for bit in gather_order(count, flip)[::-1]:
        place = present.index(bit)
        upper = (index // bit) % 2
        send = lax.dynamic_index_in_dim(values, 1 - upper, place, keepdims=False)
        keep = lax.dynamic_index_in_dim(values, upper, place, keepdims=False)
        got = swap(send, "dp", count, bit)
        present.remove(bit)
        values = keep.astype(F32) + got.astype(F32)
        if present:
            values = values.astype(BF)
    return values


def sum_all(values, count):
    for bit in bits_of(count):
        values = values + swap(values, "dp", count, bit)
    return values


def join_pair(own, other, side, axis):
    return jnp.where(
        side == 0,
        jnp.concatenate([own, other], axis=axis),
        jnp.concatenate([other, own], axis=axis),
    )


def pair(values):
    return lax.ppermute(values, "tensor", [(0, 1), (1, 0)])


def norm_of(values, gain_vec, bias_vec):
    centred = values - jnp.mean(values, axis=-1, keepdims=True)
    inverse = lax.rsqrt(jnp.mean(centred * centred, axis=-1, keepdims=True) + norm_eps)
    return centred * inverse * gain_vec + bias_vec


def to_steps(steps_ref, row_first, values, col_first):
    rows, cols = values.shape
    tiles = steps_ref.shape[1]
    for j in range(cols // LANES):
        steps_ref[pl.ds(row_first, rows), col_first // LANES + j, :] = values[
            :, j * LANES : (j + 1) * LANES
        ]


def run_docs(starts_ref, step, make_start, finish, backward, unroll=8):
    for doc in range(NDOCS):
        d = NDOCS - 1 - doc if backward else doc
        first = starts_ref[d]
        last = starts_ref[d + 1]
        length = last - first
        groups = length // unroll
        carry = make_start(doc)

        def group_body(g, carry):
            base = last - 1 - g * unroll if backward else first + g * unroll
            for i in range(unroll):
                carry = step(base - i if backward else base + i, carry)
            return carry

        carry = lax.fori_loop(0, groups, group_body, carry)
        done = groups * unroll

        def one_body(i, carry):
            return step(last - 1 - done - i if backward else first + done + i, carry)

        carry = lax.fori_loop(0, length - done, one_body, carry)
        finish(carry)


def ssm_forward_kernel(
    starts_ref, rows_ref, gain_ref, bias_ref, mix_ref, decay_ref, coef_ref,
    normed_ref, drive_ref, out_ref, y_ref,
):
    length, width = rows_ref.shape
    states = decay_ref.shape[0]
    chunk = 256

    def project(i, _):
        r = pl.multiple_of(i * chunk, chunk)
        normed = norm_of(
            rows_ref[pl.ds(r, chunk), :].astype(F32), gain_ref[...], bias_ref[...]
        ).astype(BF)
        normed_ref[pl.ds(r, chunk), :] = normed
        for c in range(0, width, 256):
            to_steps(drive_ref, r, dot_plain(normed, mix_ref[:, c : c + 256]), c)
        return 0

    lax.fori_loop(0, length // chunk, project, 0)

    def step(t, state):
        u = drive_ref[t]
        new = []
        parts = []
        for n in range(states):
            s = decay_ref[n] * state[n] + u
            new.append(s)
            parts.append(coef_ref[n] * s)
        while len(parts) > 1:
            parts = [parts[k] + parts[k + 1] for k in range(0, len(parts), 2)]
        y_ref[t] = parts[0]
        return tuple(new)

    zero = jnp.zeros(decay_ref.shape[1:], F32)
    run_docs(starts_ref, step, lambda doc: (zero,) * states, lambda carry: None, False)

    def write(i, _):
        r = pl.multiple_of(i * chunk, chunk)
        for j in range(width // LANES):
            out_ref[pl.ds(r, chunk), j * LANES : (j + 1) * LANES] = y_ref[
                pl.ds(r, chunk), j, :
            ].astype(BF)
        return 0

    lax.fori_loop(0, length // chunk, write, 0)


def ssm_forward(starts, rows, gain_vec, bias_vec, mix, decay, coef):
    length, width = rows.shape
    tiles = width // LANES
    vm = pl.BlockSpec(memory_space=pltpu.VMEM)
    return pl.pallas_call(
        ssm_forward_kernel,
        out_shape=(
            jax.ShapeDtypeStruct((length, width), BF),
            jax.ShapeDtypeStruct((length, tiles, LANES), F32),
            jax.ShapeDtypeStruct((length, width), BF),
        ),
        in_specs=[pl.BlockSpec(memory_space=pltpu.SMEM)] + [vm] * 6,
        out_specs=(vm,) * 3,
        scratch_shapes=[pltpu.VMEM((length, tiles, LANES), F32)],
        compiler_params=pltpu.CompilerParams(vmem_limit_bytes=VMEM),
        cost_estimate=pl.CostEstimate(
            flops=2 * length * width * width + 40 * 16 * length * width,
            bytes_accessed=16 * length * width,
            transcendentals=0,
        ),
        name="ssm_forward",
    )(starts, rows, gain_vec, bias_vec, mix, decay, coef)


def ssm_backward_kernel(
    starts_ref, gkey_ref, gvalue_ref, wkey_ref, wvalue_ref, drive_ref, decay_ref, coef_ref,
    gmixed_ref, sum_ref, dsum_ref, g_ref, gm_ref,
):
    length, width = gkey_ref.shape
    states = decay_ref.shape[0]
    chunk = 256

    def project(i, _):
        r = pl.multiple_of(i * chunk, chunk)
        gkey = gkey_ref[pl.ds(r, chunk), :]
        gvalue = gvalue_ref[pl.ds(r, chunk), :]
        for c in range(0, width, 256):
            to_steps(
                g_ref,
                r,
                dot_last(gkey, wkey_ref[c : c + 256, :])
                + dot_last(gvalue, wvalue_ref[c : c + 256, :]),
                c,
            )
        return 0

    lax.fori_loop(0, length // chunk, project, 0)

    zero = jnp.zeros(decay_ref.shape[1:], F32)
    part = states // 2
    for half in range(2):
        base = half * part

        def step(t, carry, half=half, base=base):
            mu, rho, total, dtotal = carry
            u = drive_ref[t]
            g = g_ref[t]
            new_mu, new_rho, new_total, new_dtotal, parts = [], [], [], [], []
            for n in range(part):
                a = decay_ref[base + n]
                r = a * rho[n] + mu[n]
                m = a * mu[n] + g
                new_mu.append(m)
                new_rho.append(r)
                new_total.append(total[n] + u * m)
                new_dtotal.append(dtotal[n] + u * r)
                parts.append(coef_ref[base + n] * m)
            while len(parts) > 1:
                parts = [parts[k] + parts[k + 1] for k in range(0, len(parts), 2)]
            if half == 0:
                gm_ref[t] = parts[0]
            else:
                gm_ref[t] = gm_ref[t] + parts[0]
            return tuple(new_mu), tuple(new_rho), tuple(new_total), tuple(new_dtotal)

        for n in range(part):
            sum_ref[base + n] = zero
            dsum_ref[base + n] = zero

        def make_start(doc):
            zeros = (zero,) * part
            return zeros, zeros, zeros, zeros

        def finish(carry, base=base):
            for n in range(part):
                sum_ref[base + n] = sum_ref[base + n] + carry[2][n]
                dsum_ref[base + n] = dsum_ref[base + n] + carry[3][n]

        run_docs(starts_ref, step, make_start, finish, True)

    def write(i, _):
        r = pl.multiple_of(i * chunk, chunk)
        for j in range(width // LANES):
            gmixed_ref[pl.ds(r, chunk), j * LANES : (j + 1) * LANES] = gm_ref[
                pl.ds(r, chunk), j, :
            ].astype(BF)
        return 0

    lax.fori_loop(0, length // chunk, write, 0)


def ssm_backward(starts, gkey, gvalue, wkey, wvalue, drive, decay, coef):
    length, width = gkey.shape
    tiles = width // LANES
    vm = pl.BlockSpec(memory_space=pltpu.VMEM)
    return pl.pallas_call(
        ssm_backward_kernel,
        out_shape=(
            jax.ShapeDtypeStruct((length, width), BF),
            jax.ShapeDtypeStruct(decay.shape, F32),
            jax.ShapeDtypeStruct(decay.shape, F32),
        ),
        in_specs=[pl.BlockSpec(memory_space=pltpu.SMEM)] + [vm] * 7,
        out_specs=(vm,) * 3,
        scratch_shapes=[
            pltpu.VMEM((length, tiles, LANES), F32),
            pltpu.VMEM((length, tiles, LANES), F32),
        ],
        compiler_params=pltpu.CompilerParams(vmem_limit_bytes=VMEM),
        cost_estimate=pl.CostEstimate(
            flops=4 * length * width * width + 100 * 16 * length * width,
            bytes_accessed=16 * length * width,
            transcendentals=0,
        ),
        name="ssm_backward",
    )(starts, gkey, gvalue, wkey, wvalue, drive, decay, coef)


def attention_tiles(length):
    tiles = []
    for first in range(0, length, QTILE):
        block_first = first // BLOCK * BLOCK
        key_first = max(0, block_first - CTX)
        tiles.append((first, key_first, first + QTILE - key_first))
    return tiles


def fill_bias(seg_col_ref, seg_row_ref, bias_ref, tiles):
    at = 0
    for first, key_first, count in tiles:
        same = seg_col_ref[first : first + QTILE, :] == seg_row_ref[:, key_first : key_first + count]
        query_pos = lax.broadcasted_iota(jnp.int32, (QTILE, count), 0) + first
        key_pos = lax.broadcasted_iota(jnp.int32, (QTILE, count), 1) + key_first
        bias_ref[:, at : at + count] = jnp.where(
            same & (key_pos <= query_pos), 0.0, masked_score
        ).astype(F32)
        at += count


EXP_SCALE = HEAD_DIM ** (-0.5) * math.log2(math.e)


def attention_forward_kernel(
    seg_col_ref, seg_row_ref, query_ref, key_ref, value_ref, out_ref, lse_ref, bias_ref
):
    tiles = attention_tiles(query_ref.shape[0])

    @pl.when(pl.program_id(0) == 0)
    def _():
        fill_bias(seg_col_ref, seg_row_ref, bias_ref, tiles)

    at = 0
    for first, key_first, count in tiles:
        keys = slice(key_first, key_first + count)
        scores = dot_last(query_ref[first : first + QTILE, :], key_ref[keys, :])
        scores = scores * EXP_SCALE + bias_ref[:, at : at + count]
        top = jnp.max(scores, axis=-1, keepdims=True)
        raised = jnp.exp2(scores - top)
        total = jnp.sum(raised, axis=-1, keepdims=True)
        probs = (raised * (1.0 / total)).astype(BF)
        out_ref[first : first + QTILE, :] = dot_plain(probs, value_ref[keys, :]).astype(BF)
        lse_ref[0, first : first + QTILE, :] = top + jnp.log2(total)
        at += count


def attention_forward(seg_col, seg_row, query, key, value):
    length, width = query.shape
    heads = width // HEAD_DIM
    tiles = attention_tiles(length)
    cols = sum(t[2] for t in tiles)
    head = pl.BlockSpec((length, HEAD_DIM), lambda h: (0, h))
    whole = lambda shape: pl.BlockSpec(shape, lambda h: (0, 0))
    return pl.pallas_call(
        attention_forward_kernel,
        grid=(heads,),
        out_shape=(
            jax.ShapeDtypeStruct((length, width), BF),
            jax.ShapeDtypeStruct((heads, length, 1), F32),
        ),
        in_specs=[whole((length, 1)), whole((1, length)), head, head, head],
        out_specs=(head, pl.BlockSpec((1, length, 1), lambda h: (h, 0, 0))),
        scratch_shapes=[pltpu.VMEM((QTILE, cols), F32)],
        compiler_params=params(),
        cost_estimate=pl.CostEstimate(
            flops=4 * QTILE * cols * width,
            bytes_accessed=8 * length * width,
            transcendentals=QTILE * cols * heads,
        ),
        name="attention_forward",
    )(seg_col, seg_row, query, key, value)


def attention_backward_kernel(
    seg_col_ref, seg_row_ref, query_ref, key_ref, value_ref, lse_ref, gout_ref,
    gquery_ref, gkey_ref, gvalue_ref, bias_ref, gk_ref, gv_ref,
):
    tiles = attention_tiles(query_ref.shape[0])
    scale = HEAD_DIM ** (-0.5)

    @pl.when(pl.program_id(0) == 0)
    def _():
        fill_bias(seg_col_ref, seg_row_ref, bias_ref, tiles)

    gk_ref[...] = jnp.zeros_like(gk_ref)
    gv_ref[...] = jnp.zeros_like(gv_ref)
    at = 0
    for first, key_first, count in tiles:
        keys = slice(key_first, key_first + count)
        query = query_ref[first : first + QTILE, :]
        gout = gout_ref[first : first + QTILE, :]
        scores = dot_last(query, key_ref[keys, :]) * EXP_SCALE + bias_ref[:, at : at + count]
        probs = jnp.exp2(scores - lse_ref[0, first : first + QTILE, :])
        gv_ref[keys, :] = gv_ref[keys, :] + dot_first(probs.astype(BF), gout)
        gprobs = dot_last(gout, value_ref[keys, :])
        inner = jnp.sum(probs * gprobs, axis=-1, keepdims=True)
        gscores = (probs * (gprobs - inner)).astype(BF)
        gquery_ref[first : first + QTILE, :] = (
            dot_plain(gscores, key_ref[keys, :]) * scale
        ).astype(BF)
        gk_ref[keys, :] = gk_ref[keys, :] + dot_first(gscores, query)
        at += count
    gkey_ref[...] = (gk_ref[...] * scale).astype(BF)
    gvalue_ref[...] = gv_ref[...].astype(BF)


def attention_backward(seg_col, seg_row, query, key, value, lse, gout):
    length, width = query.shape
    heads = width // HEAD_DIM
    tiles = attention_tiles(length)
    cols = sum(t[2] for t in tiles)
    head = pl.BlockSpec((length, HEAD_DIM), lambda h: (0, h))
    whole = lambda shape: pl.BlockSpec(shape, lambda h: (0, 0))
    return pl.pallas_call(
        attention_backward_kernel,
        grid=(heads,),
        out_shape=(jax.ShapeDtypeStruct((length, width), BF),) * 3,
        in_specs=[whole((length, 1)), whole((1, length)), head, head, head]
        + [pl.BlockSpec((1, length, 1), lambda h: (h, 0, 0)), head],
        out_specs=(head,) * 3,
        scratch_shapes=[
            pltpu.VMEM((QTILE, cols), F32),
            pltpu.VMEM((length, HEAD_DIM), F32),
            pltpu.VMEM((length, HEAD_DIM), F32),
        ],
        compiler_params=params(),
        cost_estimate=pl.CostEstimate(
            flops=10 * QTILE * cols * width,
            bytes_accessed=14 * length * width,
            transcendentals=QTILE * cols * heads,
        ),
        name="attention_backward",
    )(seg_col, seg_row, query, key, value, lse, gout)


def norm_backward(grad, values, gain_vec):
    centred = values - jnp.mean(values, axis=-1, keepdims=True)
    inverse = lax.rsqrt(jnp.mean(centred * centred, axis=-1, keepdims=True) + norm_eps)
    xhat = centred * inverse
    dxhat = grad * gain_vec
    back = (
        dxhat
        - jnp.mean(dxhat, axis=-1, keepdims=True)
        - xhat * jnp.mean(dxhat * xhat, axis=-1, keepdims=True)
    ) * inverse
    return back, jnp.sum(grad * xhat, axis=0), jnp.sum(grad, axis=0)


def gelu_parts(values):
    below = 0.5 * lax.erfc(values * (-(2.0**-0.5)))
    density = jnp.exp(-0.5 * values * values) * ((2.0 * math.pi) ** -0.5)
    return values * below, below + values * density


def per_device(
    count,
    layer_in,
    segment_ids,
    w_mix_in,
    w_query,
    w_key,
    w_value,
    w_attn_out,
    w_up,
    w_down,
    norm1_gain,
    norm1_bias,
    norm2_gain,
    norm2_bias,
    ssm_decay,
    ssm_inject,
    ssm_readout,
    out_grad,
):
    index = lax.axis_index("dp")
    side = lax.axis_index("tensor")
    half = layer_in.shape[2]
    width = layer_in.shape[3]
    length = 2 * half
    tiles = width // LANES
    states = ssm_decay.shape[0]

    def whole_sequence(halves):
        own = lax.dynamic_index_in_dim(halves, side, 0, keepdims=False)
        other = pair(lax.dynamic_index_in_dim(halves, 1 - side, 0, keepdims=False))
        return join_pair(own, other, side, 0)

    def both_halves(sequence):
        own = lax.dynamic_slice_in_dim(sequence, side * half, half, 0)
        other = pair(lax.dynamic_slice_in_dim(sequence, (1 - side) * half, half, 0))
        return jnp.where(side == 0, jnp.stack([own, other]), jnp.stack([other, own]))

    norms = jnp.stack([norm1_gain, norm1_bias, norm2_gain, norm2_bias])[None]
    norms_all, _ = gather_rows(norms, count, index, False)
    mix_half, mark = gather_rows(w_mix_in, count, index, False)
    attn_shard = jnp.concatenate([w_query, w_key, w_value, w_attn_out.T], axis=1)
    attn_half, mark = gather_rows(after(attn_shard, mark), count, index, True)
    up_half, mark = gather_rows(after(w_up, mark), count, index, False)
    down_half, mark = gather_rows(after(w_down.T, mark), count, index, True)
    norms_all = norms_all.astype(F32).transpose(1, 0, 2).reshape(4, width)
    gain_one, bias_one, gain_two, bias_two = (norms_all[i : i + 1] for i in range(4))
    mix_full = join_pair(mix_half, pair(mix_half), side, 1)
    attn_other = pair(attn_half)
    cols = w_query.shape[1]
    query_full, key_full, value_full, out_full = (
        join_pair(
            attn_half[:, i * cols : (i + 1) * cols],
            attn_other[:, i * cols : (i + 1) * cols],
            side,
            1,
        )
        for i in range(4)
    )

    coefs = jnp.stack([ssm_decay, ssm_inject, ssm_readout])
    coefs = join_pair(coefs, pair(coefs), side, 2)
    decay, inject, readout = coefs.reshape(3, states, tiles, LANES)
    coef = inject * readout

    rows = whole_sequence(layer_in[:, 0])
    cot = whole_sequence(out_grad[:, 0])
    cot_both = jnp.concatenate([cot, pair(cot)], axis=0)
    segments = lax.dynamic_index_in_dim(segment_ids[:, 0], side, 0, keepdims=False)
    starts = jnp.sum(
        (segments[None, :] < jnp.arange(16, dtype=jnp.int32)[:, None]).astype(jnp.int32), axis=1
    )
    seg_col, seg_row = segments[:, None], segments[None, :]

    normed, drive, ssm_out = ssm_forward(
        starts, rows, gain_one, bias_one, mix_full, decay, coef
    )
    query = dot_plain(normed, query_full).astype(BF)
    key = dot_plain(ssm_out, key_full).astype(BF)
    value = dot_plain(ssm_out, value_full).astype(BF)
    attended, lse = attention_forward(seg_col, seg_row, query, key, value)
    middle = rows.astype(F32) + dot_last(attended, out_full)
    normed_two = norm_of(middle, gain_two, bias_two).astype(BF)

    normed_both = jnp.concatenate([normed_two, pair(normed_two)], axis=0)
    hidden_pre = dot_plain(normed_both, up_half)
    hidden, slope = gelu_parts(hidden_pre)
    hidden = hidden.astype(BF)
    grad_pre = (dot_plain(cot_both, down_half) * slope).astype(BF)
    grad_two_part = dot_last(grad_pre, up_half)
    grad_two = grad_two_part[:length] + pair(grad_two_part[length:].astype(BF)).astype(F32)
    grad_up = dot_first(normed_both, grad_pre).astype(BF)
    grad_down = dot_first(cot_both, hidden).astype(BF)
    branch = dot_last(hidden, down_half)
    layer_out = middle + branch[:length] + pair(branch[length:].astype(BF)).astype(F32)
    layer_out = both_halves(layer_out)
    shard_up = scatter_rows(grad_up, count, index, False)
    shard_down = scatter_rows(grad_down, count, index, True)

    back_two, grad_gain_two, grad_bias_two = norm_backward(grad_two, middle, gain_two)
    grad_middle = cot.astype(F32) + back_two
    grad_branch = grad_middle.astype(BF)
    grad_attended = dot_plain(grad_branch, out_full).astype(BF)
    grad_query, grad_key, grad_value = attention_backward(
        seg_col, seg_row, query, key, value, lse, grad_attended
    )

    def pair_sum(grad):
        mine = lax.dynamic_slice_in_dim(grad, side * cols, cols, 1)
        theirs = lax.dynamic_slice_in_dim(grad, (1 - side) * cols, cols, 1)
        return (mine.astype(F32) + pair(theirs).astype(F32)).astype(BF)

    grad_attn = jnp.concatenate(
        [
            pair_sum(dot_first(normed, grad_query).astype(BF)),
            pair_sum(dot_first(ssm_out, grad_key).astype(BF)),
            pair_sum(dot_first(ssm_out, grad_value).astype(BF)),
            pair_sum(dot_first(grad_branch, attended).astype(BF)),
        ],
        axis=1,
    )
    shard_attn = scatter_rows(grad_attn, count, index, False)
    grad_mixed, state_sum, state_dsum = ssm_backward(
        starts, grad_key, grad_value, key_full, value_full, drive, decay, coef
    )
    grad_mix = pair_sum(dot_first(normed, grad_mixed).astype(BF))
    shard_mix = scatter_rows(grad_mix, count, index, True)
    grad_normed = dot_last(grad_query, query_full) + dot_last(grad_mixed, mix_full)
    back_one, grad_gain_one, grad_bias_one = norm_backward(
        grad_normed, rows.astype(F32), gain_one
    )
    in_grad = both_halves(grad_middle + back_one)

    norm_sums = jnp.stack([grad_gain_one, grad_bias_one, grad_gain_two, grad_bias_two])
    norm_sums = norm_sums + pair(norm_sums)
    state_sums = jnp.stack([state_sum, state_dsum]).reshape(2 * states, width)
    mine = lax.dynamic_slice_in_dim(state_sums, side * cols, cols, 1)
    theirs = lax.dynamic_slice_in_dim(state_sums, (1 - side) * cols, cols, 1)
    state_sums = mine + pair(theirs)
    small = jnp.concatenate([state_sums, norm_sums.reshape(-1, cols)], axis=0)
    small = sum_all(small, count)
    total, dtotal = small[:states], small[states : 2 * states]
    norm_sums = small[2 * states :].reshape(4, width)
    norm_sums = lax.dynamic_slice_in_dim(
        norm_sums, index * norm1_gain.shape[0], norm1_gain.shape[0], 1
    )
    return (
        layer_out[:, None],
        in_grad[:, None],
        shard_mix,
        shard_attn[:, :cols],
        shard_attn[:, cols : 2 * cols],
        shard_attn[:, 2 * cols : 3 * cols],
        shard_attn[:, 3 * cols :].T,
        shard_up,
        shard_down.T,
        norm_sums[0],
        norm_sums[1],
        norm_sums[2],
        norm_sums[3],
        ssm_inject * ssm_readout * dtotal,
        ssm_readout * total,
        ssm_inject * total,
    )


def solution(mesh):
    return jax.shard_map(
        functools.partial(per_device, mesh.shape["dp"]),
        mesh=mesh,
        in_specs=(
            P(None, "dp", "tensor", None),
            P(None, "dp", None),
            P("dp", "tensor"),
            P("dp", "tensor"),
            P("dp", "tensor"),
            P("dp", "tensor"),
            P("tensor", "dp"),
            P("dp", "tensor"),
            P("tensor", "dp"),
            P("dp"),
            P("dp"),
            P("dp"),
            P("dp"),
            P(None, "tensor"),
            P(None, "tensor"),
            P(None, "tensor"),
            P(None, "dp", "tensor", None),
        ),
        out_specs=(
            P(None, "dp", "tensor", None),
            P(None, "dp", "tensor", None),
            P("dp", "tensor"),
            P("dp", "tensor"),
            P("dp", "tensor"),
            P("dp", "tensor"),
            P("tensor", "dp"),
            P("dp", "tensor"),
            P("tensor", "dp"),
            P("dp"),
            P("dp"),
            P("dp"),
            P("dp"),
            P(None, "tensor"),
            P(None, "tensor"),
            P(None, "tensor"),
        ),
        check_vma=False,
    )
```

time: 3290 us -> 679 us (0.21)
  waiting for transfers between devices: 1360 us -> 216 us
  matrix products: 880 us -> 162 us
  local copies, waits for them, and re-layouts: 517 us -> 60.1 us
  other arithmetic: 420 us -> 78.1 us
  Pallas kernels: 0 us -> 110 us
  blocking collectives: 47.2 us -> 0 us
  starting transfers between devices: 1.47 us -> 41.5 us
    reduce_scatter x17 -> x0, waiting for transfers between devices: 804 us -> none  [the longest x1 183 us: finish_grads(): lax.psum_scatter(members[5], 'dp', scatter_dimension=0, tiled=True)]
    dot_general x166 -> x6, matrix products: 754 us -> 84.1 us  [dot_plain(): return jnp.dot(left_op, right_op, preferred_element_type=F32)]
    all_gather x17 -> x0, waiting for transfers between devices: 453 us -> none  [the longest x1 77.7 us: per_device(): lax.all_gather(w_up, 'dp', axis=0, tiled=True)]
    while x950 -> x0, local copies, waits for them, and re-layouts: 218 us -> none
    ppermute x0 -> x58, waiting for transfers between devices: none -> 216 us  [the longest x40 215 us: swap(): return lax.ppermute(values, axis_name, [(i, i ^ bit) for i in range(count)])]
    exp x64 -> x0, other arithmetic: 153 us -> none  [the longest x32 118 us: state_blocks(): power_next = jnp.exp((offsets + 1.0)[:, None, None] * log_rate[None])]
    pallas_call x0 -> x4, Pallas kernels: none -> 110 us  [the longest x1 42.3 us: ssm_backward(): pl.pallas_call(ssm_backward_kernel, out_shape=(jax.ShapeDtypeStruct((leng...]
    unnamed x16 -> x0, waiting for transfers between devices: 107 us -> none
  transfers between devices with their start and end apart: 35 -> 58, of which waited for: 27 -> 27; matrix products, arithmetic and copies ran while one was open for 16% -> 37% of each run, Pallas kernels for 0% -> 16%
where the time goes in v1:
time: 679 us; the launch traced here: 670 us
  waiting for transfers between devices  216 us (32%)
  matrix products  162 us (24%)
  Pallas kernels  110 us (16%)
  other arithmetic  78.1 us (12%)
  local copies, waits for them, and re-layouts  60.1 us (9%)
  starting transfers between devices  41.5 us (6%)
    ppermute x40, waiting for transfers between devices, swap(): return lax.ppermute(values, axis_name, [(i, i ^ bit) for i in range(count)])  215 us
    dot_general x6, matrix products, dot_plain(): return jnp.dot(left_op, right_op, preferred_element_type=F32)  84.1 us
    dot_general x7, matrix products, dot_first(): lax.dot_general(left_op, right_op, (((0,), (0,)), ((), ())), preferred_el...  42.9 us
    pallas_call x1, Pallas kernels, ssm_backward(): pl.pallas_call(ssm_backward_kernel, out_shape=(jax.ShapeDtypeStruct((leng...  42.3 us
    ppermute x40, starting transfers between devices, swap(): return lax.ppermute(values, axis_name, [(i, i ^ bit) for i in range(count)])  38.8 us
    dot_general x5, matrix products, dot_last(): lax.dot_general(left_op, right_op, (((1,), (1,)), ((), ())), preferred_el...  35 us
    pallas_call x1, Pallas kernels, ssm_forward(): pl.pallas_call(ssm_forward_kernel, out_shape=(jax.ShapeDtypeStruct((lengt...  25.1 us
    pallas_call x1, Pallas kernels, attention_backward(): pl.pallas_call(attention_backward_kernel, grid=(heads,), out_shape=(jax.S...  24.3 us
  transfers between devices with their start and end apart: 58, of which 27 were waited for; matrix products, arithmetic and copies ran while one was open for 37% of the time, Pallas kernels for 16%

profile of v1, /device:TPU:0, one launch (start us, length us, event | category | flops | bytes accessed | tf_op | source)
XLA Modules:
  0.0 670.1 jit_solution(9765701238512761300)
XLA Ops:
  5.3 3.1 collective-permute-start.1
  10.0 3.1 collective-permute-start.2
  19.3 5.4 collective-permute-done.6
  27.8 4.1 collective-permute-done.11
  32.7 3.4 collective-permute-start.12
  37.8 20.4 %collective-permute-done.12 = bf16[2,64,2048]{2,1,0:T(8,128)(2,1)} collective-permute-done((bf16[2,64,2048]{2,1,0:T(8,128)(2,1)S(1)}, bf16[2,64,2048]{2,1,0:T(8,128)(2,1)}, u32[]{:S(2)}, u32[]{:S(2)}) %collective-permute-start.12) | collective-permute-done | bytes 524320 | tf_op jit(solution)/shard_map/ppermute | solution.py:59
  67.2 4.3 collective-permute-done.7
  74.6 12.4 %collective-permute-done.13 = bf16[2,2,64,2048]{3,2,1,0:T(8,128)(2,1)} collective-permute-done((bf16[2,2,64,2048]{3,2,1,0:T(8,128)(2,1)}, bf16[2,2,64,2048]{3,2,1,0:T(8,128)(2,1)}, u32[]{:S(2)}, u32[]{:S(2)}) %collective-permute-start.13) | collective-permute-done | bytes 1048608 | tf_op jit(solution)/shard_map/ppermute | solution.py:59
  89.3 6.8 %collective-permute-done.8 = bf16[2,2,2,64,512]{4,3,1,0,2:T(8,128)(2,1)S(1)} collective-permute-done((bf16[2,2,2,64,512]{4,3,1,0,2:T(8,128)(2,1)S(1)}, bf16[2,2,2,64,512]{4,3,1,0,2:T(8,128)(2,1)S(1)}, u32[]{:S(2)}, u32[]{:S(2)}) %collective-permute-start.8) | collective-permute-done | bytes 524320 | tf_op jit(solution)/shard_map/ppermute | solution.py:59
  96.7 3.9 maximum_select_fusion.8
  103.2 17.3 %collective-permute-done.18 = bf16[2,64,2048]{2,1,0:T(8,128)(2,1)S(1)} collective-permute-done((bf16[2,64,2048]{2,1,0:T(8,128)(2,1)S(1)}, bf16[2,64,2048]{2,1,0:T(8,128)(2,1)S(1)}, u32[]{:S(2)}, u32[]{:S(2)}) %collective-permute-start.18) | collective-permute-done | bytes 524320 | tf_op jit(solution)/shard_map/ppermute | solution.py:59
  120.8 11.7 %collective-permute-done.14 = bf16[2,2,2,64,2048]{4,3,1,0,2:T(8,128)(2,1)S(1)} collective-permute-done((bf16[2,2,2,64,2048]{4,3,1,0,2:T(8,128)(2,1)S(1)}, bf16[2,2,2,64,2048]{4,3,1,0,2:T(8,128)(2,1)S(1)}, u32[]{:S(2)}, u32[]{:S(2)}) %collective-permute-start.14) | collective-permute-done | bytes 2097184 | tf_op jit(solution)/shard_map/ppermute | solution.py:59
  137.1 23.1 %collective-permute-done.22 = bf16[2,64,2048]{2,1,0:T(8,128)(2,1)S(1)} collective-permute-done((bf16[2,64,2048]{2,1,0:T(8,128)(2,1)S(1)}, bf16[2,64,2048]{2,1,0:T(8,128)(2,1)S(1)}, u32[]{:S(2)}, u32[]{:S(2)}) %collective-permute-start.22) | collective-permute-done | bytes 524320 | tf_op jit(solution)/shard_map/ppermute | solution.py:59
  163.6 25.1 %ssm_forward.1 = (bf16[1024,1024]{1,0:T(8,128)(2,1)}, f32[1024,8,128]{2,1,0:T(8,128)}, bf16[1024,1024]{1,0:T(8,128)(2,1)}) custom-call(s32[16]{0:T(128)} %convert_reduce_fusion.1.starts_ref, bf16[1024,1024]{1,0:T(8,128)(2,1)} %copy-done.4, f32[1,1024]{1,0:T(1,128)} %slice.95.gain_ref, f32[1,1024]{1,0:T(1,128)} %slice.97.bias_ref, ...), custom_call_target="tpu_custom_call" | custom-call | flops 2818572288 | bytes 16777216 | tf_op jit(solution)/shard_map/ssm_forward/pallas_call | solution.py:210
  203.5 3.7 convolution_convert_fusion.9.key_ref
  207.2 3.7 convolution_convert_fusion.8.value_ref
  210.9 3.7 convolution_convert_fusion.10.query_ref
  214.6 18.0 %attention_forward.1 = (bf16[1024,1024]{1,0:T(8,128)(2,1)}, f32[8,1024,1]{2,1,0:T(8,128)}) custom-call(s32[1024,1]{1,0:T(8,128)} %copy.99.seg_col_ref, s32[1,1024]{1,0:T(1,128)} %fusion.94.seg_row_ref, bf16[1024,1024]{1,0:T(8,128)(2,1)} %convolution_convert_fusion.10.query_ref, bf16[1024,1024]{1,0:T(8,128)(2,1)} %convolution_convert_fusion.9.key_ref, ...), custom_call_target="tpu_custom_call" | custom-call | flops 1879048192 | bytes 8388608 | tf_op jit(solution)/shard_map/attention_forward/pallas_call | solution.py:388
  232.7 4.1 fusion.64
  246.3 49.1 %multiply_convert_fusion = (bf16[2048,2048]{1,0:T(8,128)(2,1)}, f32[2048,2048]{1,0:T(8,128)}, f32[2048,2048]{1,0:T(8,128)}) fusion(bf16[1024,2048]{1,0:T(8,128)(2,1)S(1)} %bitcast.312, bf16[1024,1024]{1,0:T(8,128)(2,1)S(1)} %collective-permute-done.16, bf16[1024,1024]{1,0:T(8,128)(2,1)S(1)} %add_convert_fusion), kind=kOutput, calls=%fused_computation.10 | convolution fusion | flops 8866758656 | bytes 50331648 | tf_op jit(solution)/shard_map/dot_general | solution.py:26
  295.4 20.2 %fusion.7 = bf16[2048,2048]{1,0:T(8,128)(2,1)} fusion(f32[2048,2048]{1,0:T(8,128)} %get-tuple-element.55, f32[2048,2048]{1,0:T(8,128)} %get-tuple-element.133, bf16[1024,2048]{1,0:T(8,128)(2,1)S(1)} %bitcast.314, bf16[1024,1024]{1,0:T(8,128)(2,1)} %collective-permute-done.28, bf16[1024,1024]{1,0:T(8,128)(2,1)} %maximum_select_fusion.8), kind=kOutput, calls=%fused_computation.9 | convolution fusion | flops 8627683328 | bytes 50331648 | tf_op jit(solution)/shard_map/dot_general | solution.py:26
  315.6 11.3 %fusion.66 = f32[2048,1024]{1,0:T(8,128)S(1)} fusion(bf16[2048,2048]{1,0:T(8,128)(2,1)} %fusion.7, bf16[1024,2048]{1,0:T(8,128)(2,1)S(1)} %bitcast.313), kind=kOutput, calls=%fused_computation.265 | convolution fusion | flops 8589934592 | bytes 20971520 | tf_op jit(solution)/shard_map/dot_general | solution.py:30
  329.8 11.3 %fusion.65 = f32[2048,1024]{1,0:T(8,128)S(1)} fusion(bf16[2048,2048]{1,0:T(8,128)(2,1)} %get-tuple-element.54, bf16[1024,2048]{1,0:T(8,128)(2,1)S(1)} %bitcast.315), kind=kOutput, calls=%fused_computation.264 | convolution fusion | flops 8589934592 | bytes 20971520 | tf_op jit(solution)/shard_map/dot_general | solution.py:30
  344.3 12.6 %convolution_convert_fusion.1 = bf16[1024,2048]{1,0:T(8,128)(2,1)S(1)} fusion(bf16[2048,2048]{1,0:T(8,128)(2,1)} %fusion.7, bf16[1024,1024]{1,0:T(8,128)(2,1)} %copy-done.73, bf16[1024,1024]{1,0:T(8,128)(2,1)S(1)} %copy-done.26), kind=kOutput, calls=%fused_computation.64 | convolution fusion | flops 8600420352 | bytes 16777216 | tf_op jit(solution)/shard_map/dot_general | solution.py:34
  361.7 12.7 %convolution_convert_fusion = bf16[1024,2048]{1,0:T(8,128)(2,1)S(1)} fusion(bf16[2048,2048]{1,0:T(8,128)(2,1)} %get-tuple-element.54, bf16[1024,1024]{1,0:T(8,128)(2,1)} %collective-permute-done.28, bf16[1024,1024]{1,0:T(8,128)(2,1)} %maximum_select_fusion.8), kind=kOutput, calls=%fused_computation.63 | convolution fusion | flops 8600420352 | bytes 16777216 | tf_op jit(solution)/shard_map/dot_general | solution.py:34
  380.4 6.7 %multiply_add_fusion = (f32[1024,1024]{1,0:T(8,128)S(1)}, f32[1024,1024]{1,0:T(8,128)}) fusion(bf16[1024,1024]{1,0:T(8,128)(2,1)} %maximum_select_fusion.8, f32[1024,1024]{1,0:T(8,128)S(1)} %copy-done.3, f32[1024]{0:T(1024)S(1)} %broadcast_multiply_fusion.3, f32[1024]{0:T(1024)S(1)} %broadcast_multiply_fusion.4, f32[1024]{0:T(1024)S(1)} %copy-done.55, ...), kind=kLoop, calls=%fused_computation.58 | loop fusion | flops 14680064 | bytes 27283456 | tf_op jit(solution)/shard_map/add | solution.py:589
  387.2 3.7 convolution_convert_fusion.7.gout_ref
  390.9 24.3 %attention_backward.1 = (bf16[1024,1024]{1,0:T(8,128)(2,1)}, bf16[1024,1024]{1,0:T(8,128)(2,1)}, bf16[1024,1024]{1,0:T(8,128)(2,1)}) custom-call(s32[1024,1]{1,0:T(8,128)} %copy.99.seg_col_ref, s32[1,1024]{1,0:T(1,128)} %fusion.94.seg_row_ref, bf16[1024,1024]{1,0:T(8,128)(2,1)} %convolution_convert_fusion.10.query_ref, ...), custom_call_target="tpu_custom_call" | custom-call | flops 4697620480 | bytes 14680064 | tf_op jit(solution)/shard_map/attention_backward/pallas_call | solution.py:448
  415.1 42.3 %ssm_backward.1 = (bf16[1024,1024]{1,0:T(8,128)(2,1)}, f32[16,8,128]{2,1,0:T(8,128)}, f32[16,8,128]{2,1,0:T(8,128)}) custom-call(s32[16]{0:T(128)} %convert_reduce_fusion.1.starts_ref, bf16[1024,1024]{1,0:T(8,128)(2,1)} %get-tuple-element.38.gkey_ref, bf16[1024,1024]{1,0:T(8,128)(2,1)} %get-tuple-element.39.gvalue_ref, bf16[1024,1024]{1,0:T(8,128)(2,1)} %copy-done.34, ...), custom_call_target="tpu_custom_call" | custom-call | flops 5972688896 | bytes 16777216 | tf_op jit(solution)/shard_map/ssm_backward/pallas_call | solution.py:311
  457.4 4.7 fusion.67
  469.8 3.6 fusion.23
  479.1 3.8 convolution_convert_fusion.3
  486.6 3.8 convolution_convert_fusion.4
  490.4 3.8 convolution_convert_fusion.5
  494.2 3.8 convolution_convert_fusion.2
  515.1 3.3 collective-permute-done.56
  521.0 3.3 collective-permute-done.57
  539.6 6.4 copy.107
  547.9 8.6 %collective-permute-done.45 = bf16[2,2,64,2048]{3,2,1,0:T(8,128)(2,1)} collective-permute-done((bf16[2,2,64,2048]{3,2,1,0:T(8,128)(2,1)}, bf16[2,2,64,2048]{3,2,1,0:T(8,128)(2,1)}, u32[]{:S(2)}, u32[]{:S(2)}) %collective-permute-start.45) | collective-permute-done | bytes 1048608 | tf_op jit(solution)/shard_map/ppermute | solution.py:59
  560.4 6.7 %collective-permute-done.32 = bf16[2,2,2,64,512]{4,3,1,0,2:T(8,128)(2,1)S(1)} collective-permute-done((bf16[2,2,2,64,512]{4,3,1,0,2:T(8,128)(2,1)}, bf16[2,2,2,64,512]{4,3,1,0,2:T(8,128)(2,1)S(1)}, u32[]{:S(2)}, u32[]{:S(2)}) %collective-permute-start.32) | collective-permute-done | bytes 524320 | tf_op jit(solution)/shard_map/ppermute | solution.py:59
  567.3 26.8 %collective-permute-done.46 = bf16[2,64,2048]{2,1,0:T(8,128)(2,1)S(1)} collective-permute-done((bf16[2,64,2048]{2,1,0:T(8,128)(2,1)S(1)}, bf16[2,64,2048]{2,1,0:T(8,128)(2,1)S(1)}, u32[]{:S(2)}, u32[]{:S(2)}) %collective-permute-start.46) | collective-permute-done | bytes 524320 | tf_op jit(solution)/shard_map/ppermute | solution.py:59
  595.8 9.5 %collective-permute-done.50 = bf16[2,64,2048]{2,1,0:T(8,128)(2,1)S(1)} collective-permute-done((bf16[2,64,2048]{2,1,0:T(8,128)(2,1)S(1)}, bf16[2,64,2048]{2,1,0:T(8,128)(2,1)S(1)}, u32[]{:S(2)}, u32[]{:S(2)}) %collective-permute-start.50) | collective-permute-done | bytes 524320 | tf_op jit(solution)/shard_map/ppermute | solution.py:59
  610.0 4.5 collective-permute-done.47
  615.9 7.2 %collective-permute-done.34 = bf16[2,64,512]{2,1,0:T(8,128)(2,1)S(1)} collective-permute-done((bf16[2,64,512]{2,1,0:T(8,128)(2,1)S(1)}, bf16[2,64,512]{2,1,0:T(8,128)(2,1)S(1)}, u32[]{:S(2)}, u32[]{:S(2)}) %collective-permute-start.34) | collective-permute-done | bytes 131104 | tf_op jit(solution)/shard_map/ppermute | solution.py:59
  623.2 10.0 %collective-permute-done.41 = bf16[2,2,64,2048]{3,2,1,0:T(8,128)(2,1)S(1)} collective-permute-done((bf16[2,2,64,2048]{3,2,1,0:T(8,128)(2,1)S(1)}, bf16[2,2,64,2048]{3,2,1,0:T(8,128)(2,1)S(1)}, u32[]{:S(2)}, u32[]{:S(2)}) %collective-permute-start.41) | collective-permute-done | bytes 1048608 | tf_op jit(solution)/shard_map/ppermute | solution.py:59
  636.2 21.9 %collective-permute-done.42 = bf16[2,64,2048]{2,1,0:T(8,128)(2,1)S(1)} collective-permute-done((bf16[2,64,2048]{2,1,0:T(8,128)(2,1)S(1)}, bf16[2,64,2048]{2,1,0:T(8,128)(2,1)S(1)}, u32[]{:S(2)}, u32[]{:S(2)}) %collective-permute-start.42) | collective-permute-done | bytes 524320 | tf_op jit(solution)/shard_map/ppermute | solution.py:59
  658.4 5.3 maximum_select_fusion
  663.7 5.1 maximum_select_fusion.1
  (414 shorter events, 153.2 us)
Async XLA Ops:
  3.6 93.1 %collective-permute-start.27 = (bf16[512,1024]{1,0:T(8,128)(2,1)}, bf16[512,1024]{1,0:T(8,128)(2,1)}, u32[]{:S(2)}, u32[]{:S(2)}) collective-permute-start(bf16[512,1024]{1,0:T(8,128)(2,1)} %get-tuple-element.81), channel_id=1, source_target_pairs={{0,1},{1,0},{2,3},{3,2},{4,5},{5,4},{6,7},{7,6},{8,9},{9,8},{10,11... | collective-permute-start | bytes 3145736 | tf_op jit(solution)/shard_map/ppermute | solution.py:116
  5.2 95.9 %collective-permute-start = (bf16[512,1024]{1,0:T(8,128)(2,1)}, bf16[512,1024]{1,0:T(8,128)(2,1)}, u32[]{:S(2)}, u32[]{:S(2)}) collective-permute-start(bf16[512,1024]{1,0:T(8,128)(2,1)} %get-tuple-element.88), channel_id=1, source_target_pairs={{0,1},{1,0},{2,3},{3,2},{4,5},{5,4},{6,7},{7,6},{8,9},{9,8},{10,11... | collective-permute-start | bytes 3145736 | tf_op jit(solution)/shard_map/ppermute | solution.py:116
  8.4 8.2 %collective-permute-start.5 = (bf16[64,512]{1,0:T(8,128)(2,1)S(1)}, bf16[64,512]{1,0:T(8,128)(2,1)S(1)}, u32[]{:S(2)}, u32[]{:S(2)}) collective-permute-start(bf16[64,512]{1,0:T(8,128)(2,1)S(1)} %copy-done.58), channel_id=1, source_target_pairs={{0,8},{2,10},{4,12},{6,14},{8,0},{10,2},{12,4},{14,6},{16,24},{18,... | collective-permute-start | bytes 196616 | tf_op jit(solution)/shard_map/ppermute | solution.py:59
  9.2 55.7 %collective-permute-start.10 = (f32[3,16,512]{2,1,0:T(8,128)}, f32[3,16,512]{2,1,0:T(8,128)}, u32[]{:S(2)}, u32[]{:S(2)}) collective-permute-start(f32[3,16,512]{2,1,0:T(8,128)} %pad_maximum_fusion.25), channel_id=1, source_target_pairs={{0,1},{1,0},{2,3},{3,2},{4,5},{5,4},{6,7},{7,6},{8,9},{9,8},{10,11... | collective-permute-start | bytes 294920 | tf_op jit(solution)/shard_map/ppermute | solution.py:116
  16.6 8.1 %collective-permute-start.6 = (bf16[2,64,512]{2,1,0:T(8,128)(2,1)S(1)}, bf16[2,64,512]{2,1,0:T(8,128)(2,1)S(1)}, u32[]{:S(2)}, u32[]{:S(2)}) collective-permute-start(bf16[2,64,512]{2,1,0:T(8,128)(2,1)S(1)} %pad_maximum_fusion.23), channel_id=1, source_target_pairs={{0,16},{2,18},{4,20},{6,22},{8,24},{10,26},{12,28},{14,30},{16,0},... | collective-permute-start | bytes 393224 | tf_op jit(solution)/shard_map/ppermute | solution.py:59
  26.2 11.6 %collective-permute-start.4 = (bf16[2,2,2,1,4,64]{5,4,1,0,2,3:T(4,128)(2,1)S(1)}, bf16[2,2,2,1,4,64]{5,4,1,0,2,3:T(4,128)(2,1)S(1)}, u32[]{:S(2)}, u32[]{:S(2)}) collective-permute-start(bf16[2,2,2,1,4,64]{5,4,1,0,2,3:T(4,128)(2,1)S(1)} %fusion.45), channel_id=1, source_target_pairs={{0,4},{2,6},{4,0},{6,2},{8,12},{10,14},{12,8},{14,10},{16,20},{18,... | collective-permute-start | bytes 12296 | tf_op jit(solution)/shard_map/ppermute | solution.py:59
  32.7 25.5 %collective-permute-start.12 = (bf16[2,64,2048]{2,1,0:T(8,128)(2,1)S(1)}, bf16[2,64,2048]{2,1,0:T(8,128)(2,1)}, u32[]{:S(2)}, u32[]{:S(2)}) collective-permute-start(bf16[2,64,2048]{2,1,0:T(8,128)(2,1)S(1)} %pad_maximum_fusion.18), channel_id=1, source_target_pairs={{0,16},{2,18},{4,20},{6,22},{8,24},{10,26},{12,28},{14,30},{16,0},... | collective-permute-start | bytes 1572872 | tf_op jit(solution)/shard_map/ppermute | solution.py:59
  60.6 26.4 %collective-permute-start.13 = (bf16[2,2,64,2048]{3,2,1,0:T(8,128)(2,1)}, bf16[2,2,64,2048]{3,2,1,0:T(8,128)(2,1)}, u32[]{:S(2)}, u32[]{:S(2)}) collective-permute-start(bf16[2,2,64,2048]{3,2,1,0:T(8,128)(2,1)} %pad_maximum_fusion.14), channel_id=1, source_target_pairs={{0,4},{2,6},{4,0},{6,2},{8,12},{10,14},{12,8},{14,10},{16,20},{18,... | collective-permute-start | bytes 3145736 | tf_op jit(solution)/shard_map/ppermute | solution.py:59
  64.3 7.2 %collective-permute-start.7 = (bf16[2,2,64,512]{3,2,1,0:T(8,128)(2,1)}, bf16[2,2,64,512]{3,2,1,0:T(8,128)(2,1)S(1)}, u32[]{:S(2)}, u32[]{:S(2)}) collective-permute-start(bf16[2,2,64,512]{3,2,1,0:T(8,128)(2,1)} %pad_maximum_fusion.21), channel_id=1, source_target_pairs={{0,2},{2,0},{4,6},{6,4},{8,10},{10,8},{12,14},{14,12},{16,18},{18,... | collective-permute-start | bytes 786440 | tf_op jit(solution)/shard_map/ppermute | solution.py:59
  72.5 23.6 %collective-permute-start.8 = (bf16[2,2,2,64,512]{4,3,1,0,2:T(8,128)(2,1)S(1)}, bf16[2,2,2,64,512]{4,3,1,0,2:T(8,128)(2,1)S(1)}, u32[]{:S(2)}, u32[]{:S(2)}) collective-permute-start(bf16[2,2,2,64,512]{4,3,1,0,2:T(8,128)(2,1)S(1)} %pad_maximum_fusion.17), channel_id=1, source_target_pairs={{0,4},{2,6},{4,0},{6,2},{8,12},{10,14},{12,8},{14,10},{16,20},{18,... | collective-permute-start | bytes 1572872 | tf_op jit(solution)/shard_map/ppermute | solution.py:59
  73.1 23.2 %collective-permute-start.17 = (bf16[64,2048]{1,0:T(8,128)(2,1)}, bf16[64,2048]{1,0:T(8,128)(2,1)S(1)}, u32[]{:S(2)}, u32[]{:S(2)}) collective-permute-start(bf16[64,2048]{1,0:T(8,128)(2,1)} %param.24), channel_id=1, source_target_pairs={{0,8},{2,10},{4,12},{6,14},{8,0},{10,2},{12,4},{14,6},{16,24},{18,... | collective-permute-start | bytes 786440 | tf_op jit(solution)/shard_map/ppermute | solution.py:59
  88.7 43.8 %collective-permute-start.14 = (bf16[2,2,2,64,2048]{4,3,1,0,2:T(8,128)(2,1)S(1)}, bf16[2,2,2,64,2048]{4,3,1,0,2:T(8,128)(2,1)S(1)}, u32[]{:S(2)}, u32[]{:S(2)}) collective-permute-start(bf16[2,2,2,64,2048]{4,3,1,0,2:T(8,128)(2,1)S(1)} %pad_maximum_fusion.10), channel_id=1, source_target_pairs={{0,2},{2,0},{4,6},{6,4},{8,10},{10,8},{12,14},{14,12},{16,18},{18,... | collective-permute-start | bytes 6291464 | tf_op jit(solution)/shard_map/ppermute | solution.py:59
  96.4 24.2 %collective-permute-start.18 = (bf16[2,64,2048]{2,1,0:T(8,128)(2,1)S(1)}, bf16[2,64,2048]{2,1,0:T(8,128)(2,1)S(1)}, u32[]{:S(2)}, u32[]{:S(2)}) collective-permute-start(bf16[2,64,2048]{2,1,0:T(8,128)(2,1)S(1)} %pad_maximum_fusion.19), channel_id=1, source_target_pairs={{0,16},{2,18},{4,20},{6,22},{8,24},{10,26},{12,28},{14,30},{16,0},... | collective-permute-start | bytes 1572872 | tf_op jit(solution)/shard_map/ppermute | solution.py:59
  96.6 38.4 %collective-permute-start.9 = (bf16[1024,512]{1,0:T(8,128)(2,1)S(1)}, bf16[1024,512]{1,0:T(8,128)(2,1)S(1)}, u32[]{:S(2)}, u32[]{:S(2)}) collective-permute-start(bf16[1024,512]{1,0:T(8,128)(2,1)S(1)} %bitcast.310), channel_id=1, source_target_pairs={{0,1},{1,0},{2,3},{3,2},{4,5},{5,4},{6,7},{7,6},{8,9},{9,8},{10,11... | collective-permute-start | bytes 3145736 | tf_op jit(solution)/shard_map/ppermute | solution.py:116
  100.6 194.8 %collective-permute-start.28 = (bf16[1024,1024]{1,0:T(8,128)(2,1)}, bf16[1024,1024]{1,0:T(8,128)(2,1)}, u32[]{:S(2)}, u32[]{:S(2)}) collective-permute-start(bf16[1024,1024]{1,0:T(8,128)(2,1)} %maximum_select_fusion.8), channel_id=1, source_target_pairs={{0,1},{1,0},{2,3},{3,2},{4,5},{5,4},{6,7},{7,6},{8,9},{9,8},{10,11... | collective-permute-start | bytes 6291464 | tf_op jit(solution)/shard_map/ppermute | solution.py:116
  120.7 12.8 %collective-permute-start.21 = (bf16[64,2048]{1,0:T(8,128)(2,1)S(1)}, bf16[64,2048]{1,0:T(8,128)(2,1)S(1)}, u32[]{:S(2)}, u32[]{:S(2)}) collective-permute-start(bf16[64,2048]{1,0:T(8,128)(2,1)S(1)} %bitcast.326), channel_id=1, source_target_pairs={{0,8},{2,10},{4,12},{6,14},{8,0},{10,2},{12,4},{14,6},{16,24},{18,... | collective-permute-start | bytes 786440 | tf_op jit(solution)/shard_map/ppermute | solution.py:59
  133.5 64.8 %collective-permute-start.15 = (bf16[1024,2048]{1,0:T(8,128)(2,1)S(1)}, bf16[1024,2048]{1,0:T(8,128)(2,1)}, u32[]{:S(2)}, u32[]{:S(2)}) collective-permute-start(bf16[1024,2048]{1,0:T(8,128)(2,1)S(1)} %bitcast.308), channel_id=1, source_target_pairs={{0,1},{1,0},{2,3},{3,2},{4,5},{5,4},{6,7},{7,6},{8,9},{9,8},{10,11... | collective-permute-start | bytes 12582920 | tf_op jit(solution)/shard_map/ppermute | solution.py:116
  133.7 26.5 %collective-permute-start.22 = (bf16[2,64,2048]{2,1,0:T(8,128)(2,1)S(1)}, bf16[2,64,2048]{2,1,0:T(8,128)(2,1)S(1)}, u32[]{:S(2)}, u32[]{:S(2)}) collective-permute-start(bf16[2,64,2048]{2,1,0:T(8,128)(2,1)S(1)} %pad_maximum_fusion.20), channel_id=1, source_target_pairs={{0,16},{2,18},{4,20},{6,22},{8,24},{10,26},{12,28},{14,30},{16,0},... | collective-permute-start | bytes 1572872 | tf_op jit(solution)/shard_map/ppermute | solution.py:59
  134.5 54.3 %collective-permute-start.19 = (bf16[2,2,64,2048]{3,2,1,0:T(8,128)(2,1)S(1)}, bf16[2,2,64,2048]{3,2,1,0:T(8,128)(2,1)}, u32[]{:S(2)}, u32[]{:S(2)}) collective-permute-start(bf16[2,2,64,2048]{3,2,1,0:T(8,128)(2,1)S(1)} %pad_maximum_fusion.15), channel_id=1, source_target_pairs={{0,2},{2,0},{4,6},{6,4},{8,10},{10,8},{12,14},{14,12},{16,18},{18,... | collective-permute-start | bytes 3145736 | tf_op jit(solution)/shard_map/ppermute | solution.py:59
  162.1 30.3 %collective-permute-start.23 = (bf16[2,2,64,2048]{3,2,1,0:T(8,128)(2,1)}, bf16[2,2,64,2048]{3,2,1,0:T(8,128)(2,1)}, u32[]{:S(2)}, u32[]{:S(2)}) collective-permute-start(bf16[2,2,64,2048]{3,2,1,0:T(8,128)(2,1)} %pad_maximum_fusion.16), channel_id=1, source_target_pairs={{0,4},{2,6},{4,0},{6,2},{8,12},{10,14},{12,8},{14,10},{16,20},{18,... | collective-permute-start | bytes 3145736 | tf_op jit(solution)/shard_map/ppermute | solution.py:59
  191.9 47.5 %collective-permute-start.20 = (bf16[2,2,2,64,2048]{4,3,2,1,0:T(8,128)(2,1)}, bf16[2,2,2,64,2048]{4,3,2,1,0:T(8,128)(2,1)}, u32[]{:S(2)}, u32[]{:S(2)}) collective-permute-start(bf16[2,2,2,64,2048]{4,3,2,1,0:T(8,128)(2,1)} %pad_maximum_fusion.11), channel_id=1, source_target_pairs={{0,4},{2,6},{4,0},{6,2},{8,12},{10,14},{12,8},{14,10},{16,20},{18,... | collective-permute-start | bytes 6291464 | tf_op jit(solution)/shard_map/ppermute | solution.py:59
  196.4 46.9 %collective-permute-start.24 = (bf16[2,2,2,64,2048]{4,3,1,0,2:T(8,128)(2,1)}, bf16[2,2,2,64,2048]{4,3,1,0,2:T(8,128)(2,1)}, u32[]{:S(2)}, u32[]{:S(2)}) collective-permute-start(bf16[2,2,2,64,2048]{4,3,1,0,2:T(8,128)(2,1)} %pad_maximum_fusion.12), channel_id=1, source_target_pairs={{0,2},{2,0},{4,6},{6,4},{8,10},{10,8},{12,14},{14,12},{16,18},{18,... | collective-permute-start | bytes 6291464 | tf_op jit(solution)/shard_map/ppermute | solution.py:59
  238.8 7.5 %collective-permute-start.16 = (bf16[1024,1024]{1,0:T(8,128)(2,1)S(1)}, bf16[1024,1024]{1,0:T(8,128)(2,1)S(1)}, u32[]{:S(2)}, u32[]{:S(2)}) collective-permute-start(bf16[1024,1024]{1,0:T(8,128)(2,1)S(1)} %add_convert_fusion), channel_id=1, source_target_pairs={{0,1},{1,0},{2,3},{3,2},{4,5},{5,4},{6,7},{7,6},{8,9},{9,8},{10,11... | collective-permute-start | bytes 6291464 | tf_op jit(solution)/shard_map/ppermute | solution.py:116
  328.6 48.9 %collective-permute-start.29 = (bf16[1024,1024]{1,0:T(8,128)(2,1)}, bf16[1024,1024]{1,0:T(8,128)(2,1)S(1)}, u32[]{:S(2)}, u32[]{:S(2)}) collective-permute-start(bf16[1024,1024]{1,0:T(8,128)(2,1)} %slice.170), channel_id=1, source_target_pairs={{0,1},{1,0},{2,3},{3,2},{4,5},{5,4},{6,7},{7,6},{8,9},{9,8},{10,11... | collective-permute-start | bytes 6291464 | tf_op jit(solution)/shard_map/ppermute | solution.py:116
  341.5 38.9 %collective-permute-start.25 = (bf16[1024,1024]{1,0:T(8,128)(2,1)S(1)}, bf16[1024,1024]{1,0:T(8,128)(2,1)}, u32[]{:S(2)}, u32[]{:S(2)}) collective-permute-start(bf16[1024,1024]{1,0:T(8,128)(2,1)S(1)} %slice.171), channel_id=1, source_target_pairs={{0,1},{1,0},{2,3},{3,2},{4,5},{5,4},{6,7},{7,6},{8,9},{9,8},{10,11... | collective-permute-start | bytes 6291464 | tf_op jit(solution)/shard_map/ppermute | solution.py:116
  360.2 122.6 %collective-permute-start.44 = (bf16[2,2,2,64,2048]{4,3,1,0,2:T(8,128)(2,1)}, bf16[2,2,2,64,2048]{4,3,1,0,2:T(8,128)(2,1)}, u32[]{:S(2)}, u32[]{:S(2)}) collective-permute-start(bf16[2,2,2,64,2048]{4,3,1,0,2:T(8,128)(2,1)} %bitcast.303), channel_id=1, source_target_pairs={{0,4},{2,6},{4,0},{6,2},{8,12},{10,14},{12,8},{14,10},{16,20},{18,... | collective-permute-start | bytes 6291464 | tf_op jit(solution)/shard_map/ppermute | solution.py:59
  376.4 121.6 %collective-permute-start.48 = (bf16[2,2,2,64,2048]{4,3,1,0,2:T(8,128)(2,1)}, bf16[2,2,2,64,2048]{4,3,1,0,2:T(8,128)(2,1)}, u32[]{:S(2)}, u32[]{:S(2)}) collective-permute-start(bf16[2,2,2,64,2048]{4,3,1,0,2:T(8,128)(2,1)} %bitcast.302), channel_id=1, source_target_pairs={{0,2},{2,0},{4,6},{6,4},{8,10},{10,8},{12,14},{14,12},{16,18},{18,... | collective-permute-start | bytes 6291464 | tf_op jit(solution)/shard_map/ppermute | solution.py:59
  467.2 191.2 %collective-permute-start.26 = (f32[512,1024]{1,0:T(8,128)}, f32[512,1024]{1,0:T(8,128)}, u32[]{:S(2)}, u32[]{:S(2)}) collective-permute-start(f32[512,1024]{1,0:T(8,128)} %get-tuple-element.65), channel_id=1, source_target_pairs={{0,1},{1,0},{2,3},{3,2},{4,5},{5,4},{6,7},{7,6},{8,9},{9,8},{10,11... | collective-permute-start | bytes 6291464 | tf_op jit(solution)/shard_map/ppermute | solution.py:116
  467.9 57.6 %collective-permute-start.31 = (bf16[1024,512]{1,0:T(8,128)(2,1)S(1)}, bf16[1024,512]{1,0:T(8,128)(2,1)}, u32[]{:S(2)}, u32[]{:S(2)}) collective-permute-start(bf16[1024,512]{1,0:T(8,128)(2,1)S(1)} %constant_dynamic-slice_fusion.12), channel_id=1, source_target_pairs={{0,1},{1,0},{2,3},{3,2},{4,5},{5,4},{6,7},{7,6},{8,9},{9,8},{10,11... | collective-permute-start | bytes 3145736 | tf_op jit(solution)/shard_map/ppermute | solution.py:116
  507.9 20.1 %collective-permute-start.39 = (bf16[1024,512]{0,1:T(8,128)(2,1)}, bf16[1024,512]{0,1:T(8,128)(2,1)}, u32[]{:S(2)}, u32[]{:S(2)}) collective-permute-start(bf16[1024,512]{0,1:T(8,128)(2,1)} %constant_dynamic-slice_fusion.6), channel_id=1, source_target_pairs={{0,1},{1,0},{2,3},{3,2},{4,5},{5,4},{6,7},{7,6},{8,9},{9,8},{10,11... | collective-permute-start | bytes 3145736 | tf_op jit(solution)/shard_map/ppermute | solution.py:116
  510.9 19.3 %collective-permute-start.38 = (bf16[1024,512]{0,1:T(8,128)(2,1)}, bf16[1024,512]{0,1:T(8,128)(2,1)}, u32[]{:S(2)}, u32[]{:S(2)}) collective-permute-start(bf16[1024,512]{0,1:T(8,128)(2,1)} %constant_dynamic-slice_fusion.7), channel_id=1, source_target_pairs={{0,1},{1,0},{2,3},{3,2},{4,5},{5,4},{6,7},{7,6},{8,9},{9,8},{10,11... | collective-permute-start | bytes 3145736 | tf_op jit(solution)/shard_map/ppermute | solution.py:116
  524.2 8.6 %collective-permute-start.37 = (bf16[1024,512]{0,1:T(8,128)(2,1)}, bf16[1024,512]{0,1:T(8,128)(2,1)}, u32[]{:S(2)}, u32[]{:S(2)}) collective-permute-start(bf16[1024,512]{0,1:T(8,128)(2,1)} %constant_dynamic-slice_fusion.8), channel_id=1, source_target_pairs={{0,1},{1,0},{2,3},{3,2},{4,5},{5,4},{6,7},{7,6},{8,9},{9,8},{10,11... | collective-permute-start | bytes 3145736 | tf_op jit(solution)/shard_map/ppermute | solution.py:116
  525.6 10.4 %collective-permute-start.36 = (bf16[1024,512]{0,1:T(8,128)(2,1)}, bf16[1024,512]{0,1:T(8,128)(2,1)S(1)}, u32[]{:S(2)}, u32[]{:S(2)}) collective-permute-start(bf16[1024,512]{0,1:T(8,128)(2,1)} %constant_dynamic-slice_fusion.9), channel_id=1, source_target_pairs={{0,1},{1,0},{2,3},{3,2},{4,5},{5,4},{6,7},{7,6},{8,9},{9,8},{10,11... | collective-permute-start | bytes 3145736 | tf_op jit(solution)/shard_map/ppermute | solution.py:116
  528.0 135.7 %collective-permute-start.30 = (f32[512,1024]{1,0:T(8,128)S(1)}, f32[512,1024]{1,0:T(8,128)}, u32[]{:S(2)}, u32[]{:S(2)}) collective-permute-start(f32[512,1024]{1,0:T(8,128)S(1)} %copy-done.24), channel_id=1, source_target_pairs={{0,1},{1,0},{2,3},{3,2},{4,5},{5,4},{6,7},{7,6},{8,9},{9,8},{10,11... | collective-permute-start | bytes 6291464 | tf_op jit(solution)/shard_map/ppermute | solution.py:116
  530.2 26.3 %collective-permute-start.45 = (bf16[2,2,64,2048]{3,2,1,0:T(8,128)(2,1)}, bf16[2,2,64,2048]{3,2,1,0:T(8,128)(2,1)}, u32[]{:S(2)}, u32[]{:S(2)}) collective-permute-start(bf16[2,2,64,2048]{3,2,1,0:T(8,128)(2,1)} %dynamic-slice_bitcast_fusion.4), channel_id=1, source_target_pairs={{0,2},{2,0},{4,6},{6,4},{8,10},{10,8},{12,14},{14,12},{16,18},{18,... | collective-permute-start | bytes 3145736 | tf_op jit(solution)/shard_map/ppermute | solution.py:59
  532.8 25.9 %collective-permute-start.49 = (bf16[2,2,64,2048]{3,2,1,0:T(8,128)(2,1)}, bf16[2,2,64,2048]{3,2,1,0:T(8,128)(2,1)}, u32[]{:S(2)}, u32[]{:S(2)}) collective-permute-start(bf16[2,2,64,2048]{3,2,1,0:T(8,128)(2,1)} %dynamic-slice_bitcast_fusion.3), channel_id=1, source_target_pairs={{0,4},{2,6},{4,0},{6,2},{8,12},{10,14},{12,8},{14,10},{16,20},{18,... | collective-permute-start | bytes 3145736 | tf_op jit(solution)/shard_map/ppermute | solution.py:59
  535.9 31.2 %collective-permute-start.32 = (bf16[2,2,2,64,512]{4,3,1,0,2:T(8,128)(2,1)}, bf16[2,2,2,64,512]{4,3,1,0,2:T(8,128)(2,1)S(1)}, u32[]{:S(2)}, u32[]{:S(2)}) collective-permute-start(bf16[2,2,2,64,512]{4,3,1,0,2:T(8,128)(2,1)} %bitcast.304), channel_id=1, source_target_pairs={{0,2},{2,0},{4,6},{6,4},{8,10},{10,8},{12,14},{14,12},{16,18},{18,... | collective-permute-start | bytes 1572872 | tf_op jit(solution)/shard_map/ppermute | solution.py:59
  556.5 49.0 %collective-permute-start.40 = (bf16[2,2,2,64,2048]{4,3,2,1,0:T(8,128)(2,1)S(1)}, bf16[2,2,2,64,2048]{4,3,2,1,0:T(8,128)(2,1)S(1)}, u32[]{:S(2)}, u32[]{:S(2)}) collective-permute-start(bf16[2,2,2,64,2048]{4,3,2,1,0:T(8,128)(2,1)S(1)} %dynamic-slice_bitcast_fusion), channel_id=1, source_target_pairs={{0,4},{2,6},{4,0},{6,2},{8,12},{10,14},{12,8},{14,10},{16,20},{18,... | collective-permute-start | bytes 6291464 | tf_op jit(solution)/shard_map/ppermute | solution.py:59
  558.7 35.5 %collective-permute-start.46 = (bf16[2,64,2048]{2,1,0:T(8,128)(2,1)S(1)}, bf16[2,64,2048]{2,1,0:T(8,128)(2,1)S(1)}, u32[]{:S(2)}, u32[]{:S(2)}) collective-permute-start(bf16[2,64,2048]{2,1,0:T(8,128)(2,1)S(1)} %dynamic-slice_bitcast_fusion.11), channel_id=1, source_target_pairs={{0,16},{2,18},{4,20},{6,22},{8,24},{10,26},{12,28},{14,30},{16,0},... | collective-permute-start | bytes 1572872 | tf_op jit(solution)/shard_map/ppermute | solution.py:59
  567.2 38.2 %collective-permute-start.50 = (bf16[2,64,2048]{2,1,0:T(8,128)(2,1)S(1)}, bf16[2,64,2048]{2,1,0:T(8,128)(2,1)S(1)}, u32[]{:S(2)}, u32[]{:S(2)}) collective-permute-start(bf16[2,64,2048]{2,1,0:T(8,128)(2,1)S(1)} %dynamic-slice_bitcast_fusion.10), channel_id=1, source_target_pairs={{0,16},{2,18},{4,20},{6,22},{8,24},{10,26},{12,28},{14,30},{16,0},... | collective-permute-start | bytes 1572872 | tf_op jit(solution)/shard_map/ppermute | solution.py:59
  594.2 14.7 %collective-permute-start.33 = (bf16[2,2,64,512]{3,2,1,0:T(8,128)(2,1)S(1)}, bf16[2,2,64,512]{3,2,1,0:T(8,128)(2,1)S(1)}, u32[]{:S(2)}, u32[]{:S(2)}) collective-permute-start(bf16[2,2,64,512]{3,2,1,0:T(8,128)(2,1)S(1)} %dynamic-slice_bitcast_fusion.16), channel_id=1, source_target_pairs={{0,4},{2,6},{4,0},{6,2},{8,12},{10,14},{12,8},{14,10},{16,20},{18,... | collective-permute-start | bytes 786440 | tf_op jit(solution)/shard_map/ppermute | solution.py:59
  605.3 9.2 %collective-permute-start.47 = (bf16[64,2048]{1,0:T(8,128)(2,1)S(1)}, bf16[64,2048]{1,0:T(8,128)(2,1)S(1)}, u32[]{:S(2)}, u32[]{:S(2)}) collective-permute-start(bf16[64,2048]{1,0:T(8,128)(2,1)S(1)} %dynamic-slice_bitcast_fusion.14), channel_id=1, source_target_pairs={{0,8},{2,10},{4,12},{6,14},{8,0},{10,2},{12,4},{14,6},{16,24},{18,... | collective-permute-start | bytes 786440 | tf_op jit(solution)/shard_map/ppermute | solution.py:59
  605.5 29.1 %collective-permute-start.51 = (bf16[64,2048]{1,0:T(8,128)(2,1)S(1)}, bf16[64,2048]{1,0:T(8,128)(2,1)S(1)}, u32[]{:S(2)}, u32[]{:S(2)}) collective-permute-start(bf16[64,2048]{1,0:T(8,128)(2,1)S(1)} %dynamic-slice_bitcast_fusion.13), channel_id=1, source_target_pairs={{0,8},{2,10},{4,12},{6,14},{8,0},{10,2},{12,4},{14,6},{16,24},{18,... | collective-permute-start | bytes 786440 | tf_op jit(solution)/shard_map/ppermute | solution.py:59
  608.9 24.4 %collective-permute-start.41 = (bf16[2,2,64,2048]{3,2,1,0:T(8,128)(2,1)S(1)}, bf16[2,2,64,2048]{3,2,1,0:T(8,128)(2,1)S(1)}, u32[]{:S(2)}, u32[]{:S(2)}) collective-permute-start(bf16[2,2,64,2048]{3,2,1,0:T(8,128)(2,1)S(1)} %dynamic-slice_bitcast_fusion.5), channel_id=1, source_target_pairs={{0,2},{2,0},{4,6},{6,4},{8,10},{10,8},{12,14},{14,12},{16,18},{18,... | collective-permute-start | bytes 3145736 | tf_op jit(solution)/shard_map/ppermute | solution.py:59
  614.5 8.6 %collective-permute-start.34 = (bf16[2,64,512]{2,1,0:T(8,128)(2,1)S(1)}, bf16[2,64,512]{2,1,0:T(8,128)(2,1)S(1)}, u32[]{:S(2)}, u32[]{:S(2)}) collective-permute-start(bf16[2,64,512]{2,1,0:T(8,128)(2,1)S(1)} %dynamic-slice_bitcast_fusion.17), channel_id=1, source_target_pairs={{0,16},{2,18},{4,20},{6,22},{8,24},{10,26},{12,28},{14,30},{16,0},... | collective-permute-start | bytes 393224 | tf_op jit(solution)/shard_map/ppermute | solution.py:59
  623.2 12.3 %collective-permute-start.35 = (bf16[64,512]{1,0:T(8,128)(2,1)S(1)}, bf16[64,512]{1,0:T(8,128)(2,1)S(1)}, u32[]{:S(2)}, u32[]{:S(2)}) collective-permute-start(bf16[64,512]{1,0:T(8,128)(2,1)S(1)} %dynamic-slice_bitcast_fusion.18), channel_id=1, source_target_pairs={{0,8},{2,10},{4,12},{6,14},{8,0},{10,2},{12,4},{14,6},{16,24},{18,... | collective-permute-start | bytes 196616 | tf_op jit(solution)/shard_map/ppermute | solution.py:59
  633.7 24.4 %collective-permute-start.42 = (bf16[2,64,2048]{2,1,0:T(8,128)(2,1)S(1)}, bf16[2,64,2048]{2,1,0:T(8,128)(2,1)S(1)}, u32[]{:S(2)}, u32[]{:S(2)}) collective-permute-start(bf16[2,64,2048]{2,1,0:T(8,128)(2,1)S(1)} %dynamic-slice_bitcast_fusion.12), channel_id=1, source_target_pairs={{0,16},{2,18},{4,20},{6,22},{8,24},{10,26},{12,28},{14,30},{16,0},... | collective-permute-start | bytes 1572872 | tf_op jit(solution)/shard_map/ppermute | solution.py:59
  658.3 10.6 %collective-permute-start.43 = (bf16[64,2048]{1,0:T(8,128)(2,1)S(1)}, bf16[64,2048]{1,0:T(8,128)(2,1)S(1)}, u32[]{:S(2)}, u32[]{:S(2)}) collective-permute-start(bf16[64,2048]{1,0:T(8,128)(2,1)S(1)} %dynamic-slice_bitcast_fusion.15), channel_id=1, source_target_pairs={{0,8},{2,10},{4,12},{6,14},{8,0},{10,2},{12,4},{14,6},{16,24},{18,... | collective-permute-start | bytes 786440 | tf_op jit(solution)/shard_map/ppermute | solution.py:59
  (93 other events, 966.6 us)

commit v2 on v1

v2 whole, which is shorter than its diff:
```python
import functools
import math

import jax
import jax.numpy as jnp
from jax import lax
from jax.experimental import pallas as pl
from jax.experimental.pallas import tpu as pltpu
from jax.sharding import PartitionSpec as P

HEAD_DIM = 128
BLOCK = 512
CTX = 128
NDOCS = 8
LANES = 128
QTILE = 256

norm_eps = 1e-05
masked_score = -1e30
VMEM = 56 * 1024 * 1024
BF = jnp.bfloat16
F32 = jnp.float32


def dot_plain(left_op, right_op):
    return jnp.dot(left_op, right_op, preferred_element_type=F32)


def dot_last(left_op, right_op):
    return lax.dot_general(left_op, right_op, (((1,), (1,)), ((), ())), preferred_element_type=F32)


def dot_first(left_op, right_op):
    return lax.dot_general(left_op, right_op, (((0,), (0,)), ((), ())), preferred_element_type=F32)


def params(count=1):
    return pltpu.CompilerParams(
        dimension_semantics=("arbitrary",) * count, vmem_limit_bytes=VMEM
    )


def bits_of(count):
    out = []
    bit = 1
    while bit < count:
        out.append(bit)
        bit *= 2
    return out


def gather_order(count, flip):
    bits = bits_of(count)
    low = bits[:2]
    return bits[2:] + (low[::-1] if flip else low)


def swap(values, axis_name, count, bit):
    return lax.ppermute(values, axis_name, [(i, i ^ bit) for i in range(count)])


def tie(*trees):
    return lax.optimization_barrier(trees)


class Gather:
    def __init__(self, shard, count, index, flip):
        self.values, self.count, self.index = shard, count, index
        self.shape = (count * shard.shape[0],) + shard.shape[1:]
        self.left = gather_order(count, flip)
        self.present = []

    def send(self):
        self.got = swap(self.values, "dp", self.count, self.left[0])

    def merge(self):
        bit = self.left.pop(0)
        place = sum(1 for p in self.present if p > bit)
        self.present.append(bit)
        upper = (self.index // bit) % 2 == 1
        self.values = jnp.where(
            upper,
            jnp.stack([self.got, self.values], axis=place),
            jnp.stack([self.values, self.got], axis=place),
        )

    def result(self):
        return self.values.reshape(self.shape)


class Scatter:
    def __init__(self, full, count, index, flip):
        bits = bits_of(count)
        self.values = full.reshape((2,) * len(bits) + (full.shape[0] // count,) + full.shape[1:])
        self.count, self.index = count, index
        self.present = sorted(bits, reverse=True)
        self.left = gather_order(count, flip)[::-1]

    def send(self):
        bit = self.left[0]
        place = self.present.index(bit)
        upper = (self.index // bit) % 2
        send = lax.dynamic_index_in_dim(self.values, 1 - upper, place, keepdims=False)
        self.got = swap(send, "dp", self.count, bit)

    def merge(self):
        bit = self.left.pop(0)
        place = self.present.index(bit)
        upper = (self.index // bit) % 2
        keep = lax.dynamic_index_in_dim(self.values, upper, place, keepdims=False)
        self.present.remove(bit)
        self.values = keep.astype(F32) + self.got.astype(F32)
        if self.present:
            self.values = self.values.astype(BF)

    def result(self):
        return self.values


class Total:
    def __init__(self, values, count):
        self.values, self.count, self.left = values, count, bits_of(count)

    def send(self):
        self.got = swap(self.values, "dp", self.count, self.left[0])

    def merge(self):
        self.left.pop(0)
        self.values = self.values + self.got


def send(chains, *gates):
    chains = [c for c in chains if c.left]
    held = tie([c.values for c in chains], gates)[0]
    for c, v in zip(chains, held):
        c.values = v
    for c in chains:
        c.send()


def fence(chains, *values):
    chains = [c for c in chains if c.left]
    held, values = tie([(c.values, c.got) for c in chains], values)
    for c, (v, g) in zip(chains, held):
        c.values, c.got = v, g
        c.merge()
    held, values = tie(marks(chains), values)
    for c, v in zip(chains, held):
        c.values = v
    return values if len(values) != 1 else values[0]


def step(chains, *gates):
    send(chains, *gates)
    fence(chains)


def complete(chains):
    while any(c.left for c in chains):
        step(chains)


def join_chains(chains):
    chains[0].values = jnp.concatenate([c.values for c in chains], axis=-1)
    del chains[1:]


def marks(chains):
    return [c.values for c in chains]


def join_pair(own, other, side, axis):
    return jnp.where(
        side == 0,
        jnp.concatenate([own, other], axis=axis),
        jnp.concatenate([other, own], axis=axis),
    )


def pair(values):
    return lax.ppermute(values, "tensor", [(0, 1), (1, 0)])


def norm_of(values, gain_vec, bias_vec):
    centred = values - jnp.mean(values, axis=-1, keepdims=True)
    inverse = lax.rsqrt(jnp.mean(centred * centred, axis=-1, keepdims=True) + norm_eps)
    return centred * inverse * gain_vec + bias_vec


def to_steps(steps_ref, row_first, values, col_first):
    rows, cols = values.shape
    tiles = steps_ref.shape[1]
    for j in range(cols // LANES):
        steps_ref[pl.ds(row_first, rows), col_first // LANES + j, :] = values[
            :, j * LANES : (j + 1) * LANES
        ]


def run_docs(starts_ref, low, high, one_step, make_start, finish, backward, unroll=8):
    for doc in range(NDOCS):
        d = NDOCS - 1 - doc if backward else doc
        first = jnp.minimum(jnp.maximum(starts_ref[d], low), high)
        last = jnp.minimum(jnp.maximum(starts_ref[d + 1], low), high)
        length = last - first
        groups = length // unroll
        carry = make_start(d)

        def group_body(g, carry):
            base = last - 1 - g * unroll if backward else first + g * unroll
            for i in range(unroll):
                carry = one_step(base - i if backward else base + i, carry)
            return carry

        carry = lax.fori_loop(0, groups, group_body, carry)
        done = groups * unroll

        def one_body(i, carry):
            return one_step(last - 1 - done - i if backward else first + done + i, carry)

        carry = lax.fori_loop(0, length - done, one_body, carry)
        finish(d, length, carry)


def add_up(parts):
    while len(parts) > 1:
        parts = [parts[k] + parts[k + 1] for k in range(0, len(parts), 2)]
    return parts[0]


def scan_states(starts_ref, low, high, drive_ref, decay_ref, coef_ref, y_ref, start_ref, end_ref):
    states = decay_ref.shape[0]
    zero = jnp.zeros(decay_ref.shape[1:], F32)

    def one_step(t, state):
        u = drive_ref[t]
        new = [decay_ref[n] * state[n] + u for n in range(states)]
        y_ref[t - low] = add_up([coef_ref[n] * new[n] for n in range(states)])
        return tuple(new)

    def make_start(d):
        if start_ref is None:
            return (zero,) * states
        going = starts_ref[d] < low
        return tuple(jnp.where(going, start_ref[n], zero) for n in range(states))

    def finish(d, length, carry):
        if end_ref is not None:

            @pl.when(length > 0)
            def _():
                for n in range(states):
                    end_ref[n] = carry[n]

    run_docs(starts_ref, low, high, one_step, make_start, finish, False)


def from_steps(steps_ref, out_ref):
    length, tiles, _ = steps_ref.shape
    chunk = 256

    def write(i, _):
        r = pl.multiple_of(i * chunk, chunk)
        for j in range(tiles):
            out_ref[pl.ds(r, chunk), j * LANES : (j + 1) * LANES] = steps_ref[
                pl.ds(r, chunk), j, :
            ].astype(BF)
        return 0

    lax.fori_loop(0, length // chunk, write, 0)


def ssm_forward_kernel(
    starts_ref, rows_ref, gain_ref, bias_ref, mix_ref, decay_ref, coef_ref,
    normed_ref, drive_ref, out_ref, end_ref, y_ref,
):
    length, width = rows_ref.shape
    chunk = 256

    def project(i, _):
        r = pl.multiple_of(i * chunk, chunk)
        normed = norm_of(
            rows_ref[pl.ds(r, chunk), :].astype(F32), gain_ref[...], bias_ref[...]
        ).astype(BF)
        normed_ref[pl.ds(r, chunk), :] = normed
        for c in range(0, width, 256):
            to_steps(drive_ref, r, dot_plain(normed, mix_ref[:, c : c + 256]), c)
        return 0

    lax.fori_loop(0, length // chunk, project, 0)
    scan_states(
        starts_ref, 0, length // 2, drive_ref, decay_ref, coef_ref, y_ref, None, end_ref
    )
    from_steps(y_ref, out_ref)


def ssm_rest_kernel(
    starts_ref, drive_ref, decay_ref, coef_ref, start_ref, first_ref, out_ref, y_ref
):
    length = drive_ref.shape[0]
    half = length // 2
    scan_states(
        starts_ref, half, length, drive_ref, decay_ref, coef_ref, y_ref, start_ref, None
    )
    out_ref[:half, :] = first_ref[...]
    from_steps(y_ref, out_ref.at[half:])


def ssm_forward(starts, rows, gain_vec, bias_vec, mix, decay, coef):
    length, width = rows.shape
    tiles = width // LANES
    vm = pl.BlockSpec(memory_space=pltpu.VMEM)
    return pl.pallas_call(
        ssm_forward_kernel,
        out_shape=(
            jax.ShapeDtypeStruct((length, width), BF),
            jax.ShapeDtypeStruct((length, tiles, LANES), F32),
            jax.ShapeDtypeStruct((length // 2, width), BF),
            jax.ShapeDtypeStruct(decay.shape, F32),
        ),
        in_specs=[pl.BlockSpec(memory_space=pltpu.SMEM)] + [vm] * 6,
        out_specs=(vm,) * 4,
        scratch_shapes=[pltpu.VMEM((length // 2, tiles, LANES), F32)],
        compiler_params=pltpu.CompilerParams(vmem_limit_bytes=VMEM),
        cost_estimate=pl.CostEstimate(
            flops=12 * length * width * width,
            bytes_accessed=16 * length * width,
            transcendentals=0,
        ),
        name="ssm_forward",
    )(starts, rows, gain_vec, bias_vec, mix, decay, coef)


def ssm_rest(starts, drive, decay, coef, start, first):
    length, tiles, _ = drive.shape
    width = tiles * LANES
    vm = pl.BlockSpec(memory_space=pltpu.VMEM)
    return pl.pallas_call(
        ssm_rest_kernel,
        out_shape=jax.ShapeDtypeStruct((length, width), BF),
        in_specs=[pl.BlockSpec(memory_space=pltpu.SMEM)] + [vm] * 5,
        out_specs=vm,
        scratch_shapes=[pltpu.VMEM((length // 2, tiles, LANES), F32)],
        compiler_params=pltpu.CompilerParams(vmem_limit_bytes=VMEM),
        cost_estimate=pl.CostEstimate(
            flops=10 * length * width * width,
            bytes_accessed=16 * length * width,
            transcendentals=0,
        ),
        name="ssm_rest",
    )(starts, drive, decay, coef, start, first)


def adjoint_states(starts_ref, low, drive_ref, g_ref, decay_ref, coef_ref, gm_ref, sum_ref, dsum_ref, given_ref):
    length = g_ref.shape[0]
    part = sum_ref.shape[0]
    zero = jnp.zeros(decay_ref.shape[1:], F32)

    def one_step(t, carry):
        mu, rho, total, dtotal = carry
        u = drive_ref[t]
        g = g_ref[t]
        new_mu, new_rho, new_total, new_dtotal, parts = [], [], [], [], []
        for n in range(part):
            a = decay_ref[low + n]
            r = a * rho[n] + mu[n]
            m = a * mu[n] + g
            new_mu.append(m)
            new_rho.append(r)
            new_total.append(total[n] + u * m)
            new_dtotal.append(dtotal[n] + u * r)
            parts.append(coef_ref[low + n] * m)
        gm = add_up(parts)
        gm_ref[t] = gm if given_ref is None else gm + given_ref[t]
        return tuple(new_mu), tuple(new_rho), tuple(new_total), tuple(new_dtotal)

    for n in range(part):
        sum_ref[n] = zero
        dsum_ref[n] = zero

    def make_start(d):
        zeros = (zero,) * part
        return zeros, zeros, zeros, zeros

    def finish(d, count, carry):
        for n in range(part):
            sum_ref[n] = sum_ref[n] + carry[2][n]
            dsum_ref[n] = dsum_ref[n] + carry[3][n]

    run_docs(starts_ref, 0, length, one_step, make_start, finish, True)


def ssm_backward_kernel(
    starts_ref, gkey_ref, gvalue_ref, wkey_ref, wvalue_ref, drive_ref, decay_ref, coef_ref,
    g_ref, gm_ref, sum_ref, dsum_ref,
):
    length, width = gkey_ref.shape
    chunk = 256

    def project(i, _):
        r = pl.multiple_of(i * chunk, chunk)
        gkey = gkey_ref[pl.ds(r, chunk), :]
        gvalue = gvalue_ref[pl.ds(r, chunk), :]
        for c in range(0, width, 256):
            to_steps(
                g_ref,
                r,
                dot_last(gkey, wkey_ref[c : c + 256, :])
                + dot_last(gvalue, wvalue_ref[c : c + 256, :]),
                c,
            )
        return 0

    lax.fori_loop(0, length // chunk, project, 0)
    adjoint_states(
        starts_ref, 0, drive_ref, g_ref, decay_ref, coef_ref, gm_ref, sum_ref, dsum_ref, None
    )


def ssm_backward_rest_kernel(
    starts_ref, g_ref, given_ref, drive_ref, decay_ref, coef_ref,
    gmixed_ref, sum_ref, dsum_ref, gm_ref,
):
    adjoint_states(
        starts_ref, decay_ref.shape[0] // 2, drive_ref, g_ref, decay_ref, coef_ref, gm_ref,
        sum_ref, dsum_ref, given_ref,
    )
    from_steps(gm_ref, gmixed_ref)


def ssm_backward(starts, gkey, gvalue, wkey, wvalue, drive, decay, coef):
    length, width = gkey.shape
    tiles = width // LANES
    vm = pl.BlockSpec(memory_space=pltpu.VMEM)
    half = (decay.shape[0] // 2,) + decay.shape[1:]
    return pl.pallas_call(
        ssm_backward_kernel,
        out_shape=(
            jax.ShapeDtypeStruct((length, tiles, LANES), F32),
            jax.ShapeDtypeStruct((length, tiles, LANES), F32),
            jax.ShapeDtypeStruct(half, F32),
            jax.ShapeDtypeStruct(half, F32),
        ),
        in_specs=[pl.BlockSpec(memory_space=pltpu.SMEM)] + [vm] * 7,
        out_specs=(vm,) * 4,
        compiler_params=pltpu.CompilerParams(vmem_limit_bytes=VMEM),
        cost_estimate=pl.CostEstimate(
            flops=20 * length * width * width,
            bytes_accessed=20 * length * width,
            transcendentals=0,
        ),
        name="ssm_backward",
    )(starts, gkey, gvalue, wkey, wvalue, drive, decay, coef)


def ssm_backward_rest(starts, g, given, drive, decay, coef):
    length, tiles, _ = drive.shape
    width = tiles * LANES
    vm = pl.BlockSpec(memory_space=pltpu.VMEM)
    half = (decay.shape[0] // 2,) + decay.shape[1:]
    return pl.pallas_call(
        ssm_backward_rest_kernel,
        out_shape=(
            jax.ShapeDtypeStruct((length, width), BF),
            jax.ShapeDtypeStruct(half, F32),
            jax.ShapeDtypeStruct(half, F32),
        ),
        in_specs=[pl.BlockSpec(memory_space=pltpu.SMEM)] + [vm] * 5,
        out_specs=(vm,) * 3,
        scratch_shapes=[pltpu.VMEM((length, tiles, LANES), F32)],
        compiler_params=pltpu.CompilerParams(vmem_limit_bytes=VMEM),
        cost_estimate=pl.CostEstimate(
            flops=20 * length * width * width,
            bytes_accessed=20 * length * width,
            transcendentals=0,
        ),
        name="ssm_backward_rest",
    )(starts, g, given, drive, decay, coef)


def attention_tiles(length):
    tiles = []
    for first in range(0, length, QTILE):
        block_first = first // BLOCK * BLOCK
        key_first = max(0, block_first - CTX)
        tiles.append((first, key_first, first + QTILE - key_first))
    return tiles


def fill_bias(seg_col_ref, seg_row_ref, bias_ref, tiles):
    at = 0
    for first, key_first, count in tiles:
        same = seg_col_ref[first : first + QTILE, :] == seg_row_ref[:, key_first : key_first + count]
        query_pos = lax.broadcasted_iota(jnp.int32, (QTILE, count), 0) + first
        key_pos = lax.broadcasted_iota(jnp.int32, (QTILE, count), 1) + key_first
        bias_ref[:, at : at + count] = jnp.where(
            same & (key_pos <= query_pos), 0.0, masked_score
        ).astype(F32)
        at += count


EXP_SCALE = HEAD_DIM ** (-0.5) * math.log2(math.e)


def attention_forward_kernel(
    seg_col_ref, seg_row_ref, query_ref, key_ref, value_ref, out_ref, lse_ref, bias_ref
):
    tiles = attention_tiles(query_ref.shape[0])

    @pl.when(pl.program_id(0) == 0)
    def _():
        fill_bias(seg_col_ref, seg_row_ref, bias_ref, tiles)

    at = 0
    for first, key_first, count in tiles:
        keys = slice(key_first, key_first + count)
        scores = dot_last(query_ref[first : first + QTILE, :], key_ref[keys, :])
        scores = scores * EXP_SCALE + bias_ref[:, at : at + count]
        top = jnp.max(scores, axis=-1, keepdims=True)
        raised = jnp.exp2(scores - top)
        total = jnp.sum(raised, axis=-1, keepdims=True)
        probs = (raised * (1.0 / total)).astype(BF)
        out_ref[first : first + QTILE, :] = dot_plain(probs, value_ref[keys, :]).astype(BF)
        lse_ref[0, first : first + QTILE, :] = top + jnp.log2(total)
        at += count


def attention_forward(seg_col, seg_row, query, key, value):
    length, width = query.shape
    heads = width // HEAD_DIM
    tiles = attention_tiles(length)
    cols = sum(t[2] for t in tiles)
    head = pl.BlockSpec((length, HEAD_DIM), lambda h: (0, h))
    whole = lambda shape: pl.BlockSpec(shape, lambda h: (0, 0))
    return pl.pallas_call(
        attention_forward_kernel,
        grid=(heads,),
        out_shape=(
            jax.ShapeDtypeStruct((length, width), BF),
            jax.ShapeDtypeStruct((heads, length, 1), F32),
        ),
        in_specs=[whole((length, 1)), whole((1, length)), head, head, head],
        out_specs=(head, pl.BlockSpec((1, length, 1), lambda h: (h, 0, 0))),
        scratch_shapes=[pltpu.VMEM((QTILE, cols), F32)],
        compiler_params=params(),
        cost_estimate=pl.CostEstimate(
            flops=4 * QTILE * cols * width,
            bytes_accessed=8 * length * width,
            transcendentals=QTILE * cols * heads,
        ),
        name="attention_forward",
    )(seg_col, seg_row, query, key, value)


def attention_backward_kernel(
    seg_col_ref, seg_row_ref, query_ref, key_ref, value_ref, lse_ref, gout_ref,
    gquery_ref, gkey_ref, gvalue_ref, bias_ref, gk_ref, gv_ref,
):
    tiles = attention_tiles(query_ref.shape[0])
    scale = HEAD_DIM ** (-0.5)

    @pl.when(pl.program_id(0) == 0)
    def _():
        fill_bias(seg_col_ref, seg_row_ref, bias_ref, tiles)

    gk_ref[...] = jnp.zeros_like(gk_ref)
    gv_ref[...] = jnp.zeros_like(gv_ref)
    at = 0
    for first, key_first, count in tiles:
        keys = slice(key_first, key_first + count)
        query = query_ref[first : first + QTILE, :]
        gout = gout_ref[first : first + QTILE, :]
        scores = dot_last(query, key_ref[keys, :]) * EXP_SCALE + bias_ref[:, at : at + count]
        probs = jnp.exp2(scores - lse_ref[0, first : first + QTILE, :])
        gv_ref[keys, :] = gv_ref[keys, :] + dot_first(probs.astype(BF), gout)
        gprobs = dot_last(gout, value_ref[keys, :])
        inner = jnp.sum(probs * gprobs, axis=-1, keepdims=True)
        gscores = (probs * (gprobs - inner)).astype(BF)
        gquery_ref[first : first + QTILE, :] = (
            dot_plain(gscores, key_ref[keys, :]) * scale
        ).astype(BF)
        gk_ref[keys, :] = gk_ref[keys, :] + dot_first(gscores, query)
        at += count
    gkey_ref[...] = (gk_ref[...] * scale).astype(BF)
    gvalue_ref[...] = gv_ref[...].astype(BF)


def attention_backward(seg_col, seg_row, query, key, value, lse, gout):
    length, width = query.shape
    heads = width // HEAD_DIM
    tiles = attention_tiles(length)
    cols = sum(t[2] for t in tiles)
    head = pl.BlockSpec((length, HEAD_DIM), lambda h: (0, h))
    whole = lambda shape: pl.BlockSpec(shape, lambda h: (0, 0))
    return pl.pallas_call(
        attention_backward_kernel,
        grid=(heads,),
        out_shape=(jax.ShapeDtypeStruct((length, width), BF),) * 3,
        in_specs=[whole((length, 1)), whole((1, length)), head, head, head]
        + [pl.BlockSpec((1, length, 1), lambda h: (h, 0, 0)), head],
        out_specs=(head,) * 3,
        scratch_shapes=[
            pltpu.VMEM((QTILE, cols), F32),
            pltpu.VMEM((length, HEAD_DIM), F32),
            pltpu.VMEM((length, HEAD_DIM), F32),
        ],
        compiler_params=params(),
        cost_estimate=pl.CostEstimate(
            flops=10 * QTILE * cols * width,
            bytes_accessed=14 * length * width,
            transcendentals=QTILE * cols * heads,
        ),
        name="attention_backward",
    )(seg_col, seg_row, query, key, value, lse, gout)


def norm_backward(grad, values, gain_vec):
    centred = values - jnp.mean(values, axis=-1, keepdims=True)
    inverse = lax.rsqrt(jnp.mean(centred * centred, axis=-1, keepdims=True) + norm_eps)
    xhat = centred * inverse
    dxhat = grad * gain_vec
    back = (
        dxhat
        - jnp.mean(dxhat, axis=-1, keepdims=True)
        - xhat * jnp.mean(dxhat * xhat, axis=-1, keepdims=True)
    ) * inverse
    return back, jnp.sum(grad * xhat, axis=0, keepdims=True), jnp.sum(grad, axis=0, keepdims=True)


ERF_RATE = 0.3275911 * 2.0**-0.5
ERF_TERMS = (0.254829592, -0.284496736, 1.421413741, -1.453152027, 1.061405429)


def gelu_parts(values):
    near = 1.0 / (1.0 + ERF_RATE * jnp.abs(values))
    bell = jnp.exp2((-0.5 * math.log2(math.e)) * (values * values))
    poly = 0.5 * ERF_TERMS[4]
    for term in ERF_TERMS[3::-1]:
        poly = 0.5 * term + near * poly
    tail = near * poly * bell
    below = jnp.where(values < 0, tail, 1.0 - tail)
    return values * below, below + values * bell * ((2.0 * math.pi) ** -0.5)


def feed_forward_kernel(part, *refs):
    ins, refs = refs[: 6 + 6 * (part > 0)], refs[6 + 6 * (part > 0) :]
    own_ref, other_ref, cot_own_ref, cot_other_ref, up_ref, down_ref = ins[:6]
    earlier = ins[6:10]
    outs, (gup_ref, gdown_ref) = refs[:4], refs[4:6]
    hidden_ref, gpre_ref, up_sum_ref, down_sum_ref, sems = refs[6:]
    length, width = own_ref.shape
    units = up_ref.shape[1]
    tile = 512

    for s, (normed_ref, cot_ref) in enumerate(
        ((own_ref, cot_own_ref), (other_ref, cot_other_ref))
    ):

        def one(i, _, s=s, normed_ref=normed_ref, cot_ref=cot_ref):
            rows = pl.ds(pl.multiple_of(i * tile, tile), tile)
            held = pl.ds(pl.multiple_of(s * length + i * tile, tile), tile)
            for n in range(0, units, tile):
                pre = dot_plain(normed_ref[rows, :], up_ref[:, n : n + tile])
                ghidden = dot_plain(cot_ref[rows, :], down_ref[:, n : n + tile])
                hidden, slope = gelu_parts(pre)
                hidden_ref[held, n : n + tile] = hidden.astype(BF)
                gpre_ref[held, n : n + tile] = (ghidden * slope).astype(BF)
            return 0

        lax.fori_loop(0, length // tile, one, 0)

    copies = []
    for k, (first_ref, second_ref, held_ref, sum_ref, out_ref) in enumerate(
        (
            (own_ref, other_ref, gpre_ref, up_sum_ref, gup_ref),
            (cot_own_ref, cot_other_ref, hidden_ref, down_sum_ref, gdown_ref),
        )
    ):

        def three(i, _, first_ref=first_ref, second_ref=second_ref, held_ref=held_ref, sum_ref=sum_ref):
            cols = pl.ds(pl.multiple_of(i * tile, tile), tile)
            total = dot_first(first_ref[:, cols], held_ref[:length, :])
            total = total + dot_first(second_ref[:, cols], held_ref[length:, :])
            sum_ref[cols, :] = total.astype(BF)
            return 0

        lax.fori_loop(0, width // tile, three, 0)
        copy = pltpu.make_async_copy(
            sum_ref, out_ref.at[:, pl.ds(part * units, units)], sems.at[k]
        )
        copy.start()
        copies.append(copy)

    for s in range(2):

        def two(i, _, s=s):
            rows = pl.ds(pl.multiple_of(i * tile, tile), tile)
            held = pl.ds(pl.multiple_of(s * length + i * tile, tile), tile)
            for k, (held_ref, weight_ref) in enumerate(
                ((hidden_ref, down_ref), (gpre_ref, up_ref))
            ):
                total = dot_last(held_ref[held, :], weight_ref[...])
                if earlier:
                    total = total + earlier[2 * k + s][rows, :].astype(F32)
                outs[2 * k + s][rows, :] = total.astype(BF)
            return 0

        lax.fori_loop(0, length // tile, two, 0)

    for copy in copies:
        copy.wait()


def feed_forward(part, parts, own, other, cot_own, cot_other, up, down, earlier):
    length, width = own.shape
    units = up.shape[1]
    vm = pl.BlockSpec(memory_space=pltpu.VMEM)
    anywhere = pl.BlockSpec(memory_space=pl.ANY)
    return pl.pallas_call(
        functools.partial(feed_forward_kernel, part),
        out_shape=(jax.ShapeDtypeStruct((length, width), BF),) * 4
        + (jax.ShapeDtypeStruct((width, parts * units), BF),) * 2,
        in_specs=[vm] * 6 + ([vm] * 4 + [anywhere] * 2 if part else []),
        out_specs=(vm,) * 4 + (anywhere,) * 2,
        scratch_shapes=[pltpu.VMEM((2 * length, units), BF)] * 2
        + [pltpu.VMEM((width, units), BF)] * 2
        + [pltpu.SemaphoreType.DMA((2,))],
        input_output_aliases={10: 4, 11: 5} if part else {},
        compiler_params=pltpu.CompilerParams(vmem_limit_bytes=VMEM),
        cost_estimate=pl.CostEstimate(
            flops=28 * length * width * units,
            bytes_accessed=48 * length * width,
            transcendentals=4 * length * units,
        ),
        name="feed_forward",
    )(own, other, cot_own, cot_other, up, down, *earlier)


def middle_kernel(attended_ref, out_ref, rows_ref, gain_ref, bias_ref, middle_ref, normed_ref):
    middle = rows_ref[...].astype(F32) + dot_last(attended_ref[...], out_ref[...])
    middle_ref[...] = middle
    normed_ref[...] = norm_of(middle, gain_ref[...], bias_ref[...]).astype(BF)


def row_spec(width, tile=256):
    return pl.BlockSpec((tile, width), lambda i: (i, 0))


def fixed(*shape):
    return pl.BlockSpec(shape, lambda i: (0,) * len(shape))


def middle_of(attended, out_full, rows, gain_vec, bias_vec):
    length, width = rows.shape
    row = row_spec(width)
    return pl.pallas_call(
        middle_kernel,
        grid=(length // 256,),
        out_shape=(
            jax.ShapeDtypeStruct((length, width), F32),
            jax.ShapeDtypeStruct((length, width), BF),
        ),
        in_specs=[row, fixed(width, width), row, fixed(1, width), fixed(1, width)],
        out_specs=(row, row),
        compiler_params=params(),
        cost_estimate=pl.CostEstimate(
            flops=2 * length * width * width, bytes_accessed=12 * length * width, transcendentals=0
        ),
        name="middle",
    )(attended, out_full, rows, gain_vec, bias_vec)


def norm_two_kernel(
    mine_ref, theirs_ref, middle_ref, cot_ref, gain_ref, out_ref,
    gmiddle_ref, gbranch_ref, gattended_ref, sums_ref,
):
    grad = mine_ref[...].astype(F32) + theirs_ref[...].astype(F32)
    back, gain_sum, bias_sum = norm_backward(grad, middle_ref[...], gain_ref[...])
    gmiddle = cot_ref[...].astype(F32) + back
    gmiddle_ref[...] = gmiddle
    gbranch = gmiddle.astype(BF)
    gbranch_ref[...] = gbranch
    gattended_ref[...] = dot_plain(gbranch, out_ref[...]).astype(BF)
    add_sums(sums_ref, gain_sum, bias_sum)


def add_sums(sums_ref, gain_sum, bias_sum):
    @pl.when(pl.program_id(0) == 0)
    def _():
        sums_ref[...] = jnp.zeros_like(sums_ref)

    sums_ref[0:1, :] = sums_ref[0:1, :] + gain_sum
    sums_ref[1:2, :] = sums_ref[1:2, :] + bias_sum


def norm_two_back(mine, theirs, middle, cot, gain_vec, out_full):
    length, width = middle.shape
    row = row_spec(width)
    return pl.pallas_call(
        norm_two_kernel,
        grid=(length // 256,),
        out_shape=(
            jax.ShapeDtypeStruct((length, width), F32),
            jax.ShapeDtypeStruct((length, width), BF),
            jax.ShapeDtypeStruct((length, width), BF),
            jax.ShapeDtypeStruct((2, width), F32),
        ),
        in_specs=[row] * 4 + [fixed(1, width), fixed(width, width)],
        out_specs=(row, row, row, fixed(2, width)),
        compiler_params=params(),
        cost_estimate=pl.CostEstimate(
            flops=2 * length * width * width, bytes_accessed=24 * length * width, transcendentals=0
        ),
        name="norm_two_back",
    )(mine, theirs, middle, cot, gain_vec, out_full)


def norm_one_kernel(
    gquery_ref, gmixed_ref, query_ref, mix_ref, rows_ref, gmiddle_ref, gain_ref, grad_ref, sums_ref
):
    grad = dot_last(gquery_ref[...], query_ref[...]) + dot_last(gmixed_ref[...], mix_ref[...])
    back, gain_sum, bias_sum = norm_backward(grad, rows_ref[...].astype(F32), gain_ref[...])
    grad_ref[...] = gmiddle_ref[...] + back
    add_sums(sums_ref, gain_sum, bias_sum)


def norm_one_back(gquery, gmixed, query_full, mix_full, rows, gmiddle, gain_vec):
    length, width = rows.shape
    row = row_spec(width)
    return pl.pallas_call(
        norm_one_kernel,
        grid=(length // 256,),
        out_shape=(
            jax.ShapeDtypeStruct((length, width), F32),
            jax.ShapeDtypeStruct((2, width), F32),
        ),
        in_specs=[row, row, fixed(width, width), fixed(width, width), row, row, fixed(1, width)],
        out_specs=(row, fixed(2, width)),
        compiler_params=params(),
        cost_estimate=pl.CostEstimate(
            flops=4 * length * width * width, bytes_accessed=20 * length * width, transcendentals=0
        ),
        name="norm_one_back",
    )(gquery, gmixed, query_full, mix_full, rows, gmiddle, gain_vec)


def weight_grads_kernel(count, side_ref, *refs):
    lefts, rights = refs[:count], refs[count : 2 * count]
    mine_ref, theirs_ref = refs[2 * count :]
    cols = mine_ref.shape[1] // count
    side = side_ref[0]
    for ref, at in ((theirs_ref, 1 - side), (mine_ref, side)):
        for k in range(count):
            part = rights[k][:, pl.ds(pl.multiple_of(at * cols, cols), cols)]
            ref[:, k * cols : (k + 1) * cols] = dot_first(lefts[k][...], part).astype(BF)


def weight_grads(side, lefts, rights):
    count = len(lefts)
    length, width = lefts[0].shape
    vm = pl.BlockSpec(memory_space=pltpu.VMEM)
    return pl.pallas_call(
        functools.partial(weight_grads_kernel, count),
        out_shape=(jax.ShapeDtypeStruct((width, count * width // 2), BF),) * 2,
        in_specs=[pl.BlockSpec(memory_space=pltpu.SMEM)] + [vm] * (2 * count),
        out_specs=(vm, vm),
        compiler_params=pltpu.CompilerParams(vmem_limit_bytes=VMEM),
        cost_estimate=pl.CostEstimate(
            flops=2 * count * length * width * width,
            bytes_accessed=6 * count * length * width,
            transcendentals=0,
        ),
        name="weight_grads",
    )(jnp.reshape(side, (1,)), *lefts, *rights)


def per_device(
    count,
    layer_in,
    segment_ids,
    w_mix_in,
    w_query,
    w_key,
    w_value,
    w_attn_out,
    w_up,
    w_down,
    norm1_gain,
    norm1_bias,
    norm2_gain,
    norm2_bias,
    ssm_decay,
    ssm_inject,
    ssm_readout,
    out_grad,
):
    index = lax.axis_index("dp")
    side = lax.axis_index("tensor")
    half = layer_in.shape[2]
    width = layer_in.shape[3]
    length = 2 * half
    tiles = width // LANES
    states = ssm_decay.shape[0]

    def whole_sequence(halves):
        own = lax.dynamic_index_in_dim(halves, side, 0, keepdims=False)
        other = pair(lax.dynamic_index_in_dim(halves, 1 - side, 0, keepdims=False))
        return join_pair(own, other, side, 0)

    def both_halves(sequence):
        own = lax.dynamic_slice_in_dim(sequence, side * half, half, 0)
        other = pair(lax.dynamic_slice_in_dim(sequence, (1 - side) * half, half, 0))
        return jnp.where(side == 0, jnp.stack([own, other]), jnp.stack([other, own]))

    cols = w_query.shape[1]

    rows = whole_sequence(layer_in[:, 0])
    coefs = jnp.stack([ssm_decay, ssm_inject, ssm_readout])
    coefs = join_pair(coefs, pair(coefs), side, 2)
    decay, inject, readout = coefs.reshape(3, states, tiles, LANES)
    coef = inject * readout
    segments = lax.dynamic_index_in_dim(segment_ids[:, 0], side, 0, keepdims=False)
    starts = jnp.sum(
        (segments[None, :] < jnp.arange(16, dtype=jnp.int32)[:, None]).astype(jnp.int32), axis=1
    )
    seg_col, seg_row = segments[:, None], segments[None, :]

    def pieces(kind, left, right):
        return [kind(left, count, index, False), kind(right, count, index, True)]

    parts = 2
    units = w_up.shape[1] // parts
    turned_out, turned_down = w_attn_out.T, w_down.T
    shard_rows = w_mix_in.shape[0]
    norms = jnp.concatenate([norm1_gain, norm1_bias, norm2_gain, norm2_bias])
    norms = jnp.pad(norms[None], ((0, 7), (0, cols - norms.shape[0])))
    mix = [Gather(jnp.concatenate([w_mix_in, norms], axis=0), count, index, False)]
    attn = pieces(
        Gather,
        jnp.concatenate([w_query, w_key], axis=1),
        jnp.concatenate([w_value, turned_out], axis=1),
    )
    ffn = [
        pieces(
            Gather,
            w_up[:, i * units : (i + 1) * units],
            turned_down[:, i * units : (i + 1) * units],
        )
        for i in range(parts)
    ]
    step(mix + attn)
    step(mix)
    step(mix + attn[:1])
    step(mix + attn[1:])
    complete(mix)
    send(attn + ffn[0], marks(mix))
    mix_all = mix[0].result().reshape(count, shard_rows + 8, cols)
    mix_half = mix_all[:, :shard_rows].reshape(width, cols)
    norms_all = mix_all[:, shard_rows, : 4 * shard_rows].reshape(count, 4, shard_rows)
    norms_all = norms_all.astype(F32).transpose(1, 0, 2).reshape(4, width)
    gain_one, bias_one, gain_two, bias_two = (norms_all[i : i + 1] for i in range(4))
    mix_full = join_pair(mix_half, pair(mix_half), side, 1)
    rows, coef, mix_full = fence(attn + ffn[0], rows, coef, mix_full)
    send(attn + ffn[0])

    normed, drive, ssm_first, state_mid = ssm_forward(
        starts, rows, gain_one, bias_one, mix_full, decay, coef
    )
    state_mid = fence(attn + ffn[0], state_mid)
    complete(attn)
    send(ffn[0] + ffn[1], marks(attn))
    ssm_out = ssm_rest(starts, drive, decay, coef, state_mid, ssm_first)
    cot = whole_sequence(tie(out_grad, state_mid)[0][:, 0])
    halves = [m.result() for m in attn]
    others = [pair(h) for h in halves]
    query_full, key_full, value_full, out_full = (
        join_pair(h[:, i * cols : (i + 1) * cols], o[:, i * cols : (i + 1) * cols], side, 1)
        for h, o in zip(halves, others)
        for i in range(2)
    )
    ssm_out, cot, query_full, key_full, value_full, out_full = fence(
        ffn[0] + ffn[1], ssm_out, cot, query_full, key_full, value_full, out_full
    )
    send(ffn[0] + ffn[1])
    cot_other = pair(cot)
    query = dot_plain(normed, query_full).astype(BF)
    key = dot_plain(ssm_out, key_full).astype(BF)
    value = dot_plain(ssm_out, value_full).astype(BF)
    attended, lse = attention_forward(seg_col, seg_row, query, key, value)
    attended, cot_other = fence(ffn[0] + ffn[1], attended, cot_other)
    complete(ffn[0])
    send(ffn[1])
    middle, normed_two = middle_of(attended, out_full, rows, gain_two, bias_two)

    normed_other = pair(normed_two)
    normed_two, normed_other = fence(ffn[1], normed_two, normed_other)
    send(ffn[1])
    both = feed_forward(
        0, parts, normed_two, normed_other, cot, cot_other, *(m.result() for m in ffn[0]), ()
    )
    both = fence(ffn[1], both)
    complete(ffn[1])
    own, other, gown, gother, grad_up, grad_down = feed_forward(
        1, parts, normed_two, normed_other, cot, cot_other, *(m.result() for m in ffn[1]), both
    )
    sums_ffn = pieces(Scatter, grad_up, grad_down)
    send(sums_ffn)

    def pair_sum(mine, theirs):
        return mine.astype(F32) + pair(theirs).astype(F32)

    grad_middle, grad_branch, grad_attended, norm_two_sums = norm_two_back(
        gown, pair(gother), middle, cot, gain_two, out_full
    )
    grads_out = weight_grads(side, (grad_branch,), (attended,))
    grads_out, grad_attended = tie(grads_out, grad_attended)
    sum_out = pair_sum(*grads_out).astype(BF)
    grad_query, grad_key, grad_value = attention_backward(
        seg_col, seg_row, query, key, value, lse, grad_attended
    )
    sum_out, grad_query, grad_key, grad_value = fence(
        sums_ffn, sum_out, grad_query, grad_key, grad_value
    )
    send(sums_ffn)
    grads_qkv = weight_grads(side, (normed, ssm_out, ssm_out), (grad_query, grad_key, grad_value))
    grads_qkv, own, other = tie(grads_qkv, own, other)
    sum_qkv = pair_sum(*grads_qkv).astype(BF)
    layer_out = both_halves(middle + pair_sum(own, other))
    sum_qkv, sum_out, layer_out, grad_key, grad_value = fence(
        sums_ffn, sum_qkv, sum_out, layer_out, grad_key, grad_value
    )
    sums_attn = pieces(
        Scatter,
        sum_qkv[:, : 2 * cols],
        jnp.concatenate([sum_qkv[:, 2 * cols :], sum_out], axis=1),
    )
    join_chains(sums_ffn)
    send(sums_attn + sums_ffn)
    g_steps, gm_steps, sum_one, dsum_one = ssm_backward(
        starts, grad_key, grad_value, key_full, value_full, drive, decay, coef
    )
    g_steps, gm_steps = fence(sums_attn, g_steps, gm_steps)
    send(sums_attn)
    grad_mixed, sum_two, dsum_two = ssm_backward_rest(
        starts, g_steps, gm_steps, drive, decay, coef
    )
    grad_mixed = fence(sums_attn + sums_ffn, grad_mixed)
    join_chains(sums_attn)
    send(sums_attn + sums_ffn)
    grad_mix = pair_sum(*weight_grads(side, (normed,), (grad_mixed,))).astype(BF)
    grad_mixed, grad_mix = tie(grad_mixed, grad_mix)
    sums_mix = [Scatter(grad_mix, count, index, False)]
    send(sums_mix)
    grad_rows, norm_one_sums = norm_one_back(
        grad_query, grad_mixed, query_full, mix_full, rows, grad_middle, gain_one
    )
    grad_rows, norm_one_sums = fence(
        sums_mix + sums_attn + sums_ffn, grad_rows, norm_one_sums
    )
    in_grad = both_halves(grad_rows)

    state_sums = jnp.concatenate([sum_one, sum_two, dsum_one, dsum_two]).reshape(
        2 * states, width
    )
    sums = jnp.concatenate(
        [
            lax.dynamic_slice_in_dim(state_sums, (1 - side) * cols, cols, 1),
            norm_one_sums.reshape(-1, cols),
            norm_two_sums.reshape(-1, cols),
        ]
    )
    mine = lax.dynamic_slice_in_dim(state_sums, side * cols, cols, 1)
    small = [Total(jnp.concatenate([mine, sums[2 * states :]]) + pair(sums), count)]
    complete(sums_mix + small + sums_attn + sums_ffn)
    small = small[0].values
    total, dtotal = small[:states], small[states : 2 * states]
    norm_sums = lax.dynamic_slice_in_dim(
        small[2 * states :].reshape(4, width), index * shard_rows, shard_rows, 1
    )
    shard_attn = sums_attn[0].result()
    shard_ffn = sums_ffn[0].result()
    return (
        layer_out[:, None],
        in_grad[:, None],
        sums_mix[0].result(),
        shard_attn[:, :cols],
        shard_attn[:, cols : 2 * cols],
        shard_attn[:, 2 * cols : 3 * cols],
        shard_attn[:, 3 * cols :].T,
        shard_ffn[:, : parts * units],
        shard_ffn[:, parts * units :].T,
        norm_sums[0],
        norm_sums[1],
        norm_sums[2],
        norm_sums[3],
        ssm_inject * ssm_readout * dtotal,
        ssm_readout * total,
        ssm_inject * total,
    )


def solution(mesh):
    return jax.shard_map(
        functools.partial(per_device, mesh.shape["dp"]),
        mesh=mesh,
        in_specs=(
            P(None, "dp", "tensor", None),
            P(None, "dp", None),
            P("dp", "tensor"),
            P("dp", "tensor"),
            P("dp", "tensor"),
            P("dp", "tensor"),
            P("tensor", "dp"),
            P("dp", "tensor"),
            P("tensor", "dp"),
            P("dp"),
            P("dp"),
            P("dp"),
            P("dp"),
            P(None, "tensor"),
            P(None, "tensor"),
            P(None, "tensor"),
            P(None, "dp", "tensor", None),
        ),
        out_specs=(
            P(None, "dp", "tensor", None),
            P(None, "dp", "tensor", None),
            P("dp", "tensor"),
            P("dp", "tensor"),
            P("dp", "tensor"),
            P("dp", "tensor"),
            P("tensor", "dp"),
            P("dp", "tensor"),
            P("tensor", "dp"),
            P("dp"),
            P("dp"),
            P("dp"),
            P("dp"),
            P(None, "tensor"),
            P(None, "tensor"),
            P(None, "tensor"),
        ),
        check_vma=False,
    )
```

time: 679 us -> 570 us (0.84)
  matrix products: 162 us -> 13.2 us
  Pallas kernels: 110 us -> 258 us
  waiting for transfers between devices: 216 us -> 97.2 us
  starting transfers between devices: 41.5 us -> 57.7 us
  local copies, waits for them, and re-layouts: 60.1 us -> 49.3 us
    pallas_call x0 -> x10, Pallas kernels: none -> 171 us  [the longest x2 81.9 us: feed_forward(): pl.pallas_call(functools.partial(feed_forward_kernel, part), out_shape=(j...]
    ppermute x40 -> x48, waiting for transfers between devices: 215 us -> 91.9 us  [swap(): return lax.ppermute(values, axis_name, [(i, i ^ bit) for i in range(count)])]
    dot_general x12 -> x0, matrix products: 77.9 us -> none  [the longest x7 42.9 us: dot_first(): lax.dot_general(left_op, right_op, (((0,), (0,)), ((), ())), preferred_el...]
    dot_general x6 -> x3, matrix products: 84.1 us -> 13.2 us  [dot_plain(): return jnp.dot(left_op, right_op, preferred_element_type=F32)]
    another operation x44 -> x0, other arithmetic: 19.3 us -> none  [the longest x42 19.3 us: gather_rows(): values = jnp.stack([first, second], axis=place)]
    select_n x0 -> x28, other arithmetic: none -> 16.7 us  [merge(): jnp.where(upper, jnp.stack([self.got, self.values], axis=place), jnp.stac...]
    ppermute x40 -> x48, starting transfers between devices: 38.8 us -> 54.9 us  [swap(): return lax.ppermute(values, axis_name, [(i, i ^ bit) for i in range(count)])]
    pallas_call x1, Pallas kernels: 42.3 us -> 27.4 us  [ssm_backward(): pl.pallas_call(ssm_backward_kernel, out_shape=(jax.ShapeDtypeStruct((leng...]
  transfers between devices with their start and end apart: 58 -> 64, of which waited for: 27 -> 24; matrix products, arithmetic and copies ran while one was open for 37% -> 18% of each run, Pallas kernels for 16% -> 34%
where the time goes in v2:
time: 570 us; the launch traced here: 560 us
  Pallas kernels  258 us (45%)
  waiting for transfers between devices  97.2 us (17%)
  other arithmetic  82.5 us (14%)
  starting transfers between devices  57.7 us (10%)
  local copies, waits for them, and re-layouts  49.3 us (9%)
  matrix products  13.2 us (2%)
    ppermute x48, waiting for transfers between devices, swap(): return lax.ppermute(values, axis_name, [(i, i ^ bit) for i in range(count)])  91.9 us
    pallas_call x2, Pallas kernels, feed_forward(): pl.pallas_call(functools.partial(feed_forward_kernel, part), out_shape=(j...  81.9 us
    ppermute x48, starting transfers between devices, swap(): return lax.ppermute(values, axis_name, [(i, i ^ bit) for i in range(count)])  54.9 us
    pallas_call x1, Pallas kernels, ssm_backward(): pl.pallas_call(ssm_backward_kernel, out_shape=(jax.ShapeDtypeStruct((leng...  27.4 us
    pallas_call x1, Pallas kernels, attention_backward(): pl.pallas_call(attention_backward_kernel, grid=(heads,), out_shape=(jax.S...  24.6 us
    pallas_call x3, Pallas kernels, weight_grads(): pl.pallas_call(functools.partial(weight_grads_kernel, count), out_shape=(...  24.2 us
    pallas_call x1, Pallas kernels, ssm_backward_rest(): pl.pallas_call(ssm_backward_rest_kernel, out_shape=(jax.ShapeDtypeStruct(...  22.8 us
    select_n x8, other arithmetic, join_pair(): jnp.where(side == 0, jnp.concatenate([own, other], axis=axis), jnp.concat...  19 us
  transfers between devices with their start and end apart: 64, of which 24 were waited for; matrix products, arithmetic and copies ran while one was open for 18% of the time, Pallas kernels for 34%

profile of v2, /device:TPU:0, one launch (start us, length us, event | category | flops | bytes accessed | tf_op | source)
XLA Modules:
  0.0 560.2 jit_solution(16479341648996960557)
XLA Ops:
  3.3 3.1 collective-permute-start.1
  8.4 5.9 %collective-permute-done = bf16[72,512]{1,0:T(8,128)(2,1)S(1)} collective-permute-done((bf16[72,512]{1,0:T(8,128)(2,1)S(1)}, bf16[72,512]{1,0:T(8,128)(2,1)S(1)}, u32[]{:S(2)}, u32[]{:S(2)}) %collective-permute-start) | collective-permute-done | bytes 73760 | tf_op jit(solution)/shard_map/ppermute | solution.py:59
  14.3 2.8 collective-permute-start.3
  17.2 6.3 %collective-permute-done.3 = bf16[2,72,512]{2,1,0:T(8,128)(2,1)S(1)} collective-permute-done((bf16[2,72,512]{2,1,0:T(8,128)(2,1)S(1)}, bf16[2,72,512]{2,1,0:T(8,128)(2,1)S(1)}, u32[]{:S(2)}, u32[]{:S(2)}) %collective-permute-start.3) | collective-permute-done | bytes 147488 | tf_op jit(solution)/shard_map/ppermute | solution.py:59
  24.9 13.4 %collective-permute-done.5 = bf16[2,64,1024]{2,1,0:T(8,128)(2,1)S(1)} collective-permute-done((bf16[2,64,1024]{2,1,0:T(8,128)(2,1)S(1)}, bf16[2,64,1024]{2,1,0:T(8,128)(2,1)S(1)}, u32[]{:S(2)}, u32[]{:S(2)}) %collective-permute-start.5) | collective-permute-done | bytes 262176 | tf_op jit(solution)/shard_map/ppermute | solution.py:59
  40.8 2.7 dynamic-slice_bitcast_fusion.8
  44.7 9.0 %collective-permute-done.7 = bf16[2,64,1024]{2,1,0:T(8,128)(2,1)S(1)} collective-permute-done((bf16[2,64,1024]{2,1,0:T(8,128)(2,1)S(1)}, bf16[2,64,1024]{2,1,0:T(8,128)(2,1)S(1)}, u32[]{:S(2)}, u32[]{:S(2)}) %collective-permute-start.7) | collective-permute-done | bytes 262176 | tf_op jit(solution)/shard_map/ppermute | solution.py:59
  60.8 3.8 maximum_select_fusion.2.rows_ref
  68.8 3.6 maximum_select_fusion.3.mix_ref
  80.6 2.9 collective-permute-start.18
  83.5 17.4 %ssm_forward.1 = (bf16[1024,1024]{1,0:T(8,128)(2,1)}, f32[1024,8,128]{2,1,0:T(8,128)}, bf16[512,1024]{1,0:T(8,128)(2,1)}, f32[16,8,128]{2,1,0:T(8,128)}) custom-call(s32[16]{0:T(128)} %convert_reduce_fusion.starts_ref, bf16[1024,1024]{1,0:T(8,128)(2,1)} %maximum_select_fusion.2.rows_ref, f32[1,1024]{1,0:T(1,128)} %slice.121.gain_ref, ...), custom_call_target="tpu_custom_call" | custom-call | flops 12884901888 | bytes 16777216 | tf_op jit(solution)/shard_map/ssm_forward/pallas_call | solution.py:312
  101.0 3.6 collective-permute-done.18
  113.9 11.3 %ssm_rest.1.refs_1_.refs_2_ = bf16[1024,1024]{1,0:T(8,128)(2,1)} custom-call(s32[16]{0:T(128)} %convert_reduce_fusion.starts_ref, f32[1024,8,128]{2,1,0:T(8,128)} %get-tuple-element.395.drive_ref, f32[16,8,128]{2,1,0:T(8,128)} %bitcast.295, f32[16,8,128]{2,1,0:T(8,128)} %bitcast.291, f32[16,8,128]{2,1,0:T(8,128)} %get-tuple-element.396.start_ref, ...), custom_call_target="tpu_custom_call" | custom-call | flops 10737418240 | bytes 16777216 | tf_op jit(solution)/shard_map/ssm_rest/pallas_call | solution.py:337
  126.2 2.6 maximum_select_fusion.6.refs_2_.cot_ref
  143.7 2.7 maximum_select_fusion.18
  154.8 5.9 %convolution_convert_fusion.value_ref = bf16[1024,1024]{1,0:T(8,128)(2,1)} fusion(bf16[1024,1024]{1,0:T(8,128)(2,1)} %ssm_rest.1.refs_1_.refs_2_, bf16[1024,1024]{1,0:T(8,128)(2,1)} %maximum_select_fusion.9.wvalue_ref), kind=kOutput, calls=%fused_computation.39 | convolution fusion | flops 2148532224 | bytes 6291456 | tf_op jit(solution)/shard_map/dot_general | solution.py:26
  160.8 3.6 convolution_convert_fusion.1.key_ref
  164.4 3.7 convolution_convert_fusion.2.query_ref
  168.1 17.9 %attention_forward.1 = (bf16[1024,1024]{1,0:T(8,128)(2,1)}, f32[8,1024,1]{2,1,0:T(8,128)}) custom-call(s32[1024,1]{1,0:T(8,128)} %copy.73.seg_col_ref, s32[1,1024]{1,0:T(1,128)} %fusion.30.seg_row_ref, bf16[1024,1024]{1,0:T(8,128)(2,1)} %convolution_convert_fusion.2.query_ref, bf16[1024,1024]{1,0:T(8,128)(2,1)} %convolution_convert_fusion.1.key_ref, ...), custom_call_target="tpu_custom_call" | custom-call | flops 1879048192 | bytes 8388608 | tf_op jit(solution)/shard_map/attention_forward/pallas_call | solution.py:534
  189.6 7.6 %middle.1 = (f32[1024,1024]{1,0:T(8,128)}, bf16[1024,1024]{1,0:T(8,128)(2,1)}) custom-call(bf16[1024,1024]{1,0:T(8,128)(2,1)} %get-tuple-element.442.attended_ref.refs_1_, bf16[1024,1024]{1,0:T(8,128)(2,1)} %maximum_select_fusion.10.out_ref, bf16[1024,1024]{1,0:T(8,128)(2,1)} %maximum_select_fusion.2.rows_ref, f32[1,1024]{1,0:T(1,128)} %slice.135.gain_ref, ...), custom_call_target="tpu_custom_call" | custom-call | flops 2147483648 | bytes 12582912 | tf_op jit(solution)/shard_map/middle/pallas_call | solution.py:755
  201.8 9.7 %collective-permute-done.31 = bf16[2,2,64,1024]{3,2,1,0:T(8,128)(2,1)S(1)} collective-permute-done((bf16[2,2,64,1024]{3,2,1,0:T(8,128)(2,1)S(1)}, bf16[2,2,64,1024]{3,2,1,0:T(8,128)(2,1)S(1)}, u32[]{:S(2)}, u32[]{:S(2)}) %collective-permute-start.31) | collective-permute-done | bytes 524320 | tf_op jit(solution)/shard_map/ppermute | solution.py:59
  215.2 39.7 %feed_forward.2 = (bf16[1024,1024]{1,0:T(8,128)(2,1)}, bf16[1024,1024]{1,0:T(8,128)(2,1)}, bf16[1024,1024]{1,0:T(8,128)(2,1)}, bf16[1024,1024]{1,0:T(8,128)(2,1)...) custom-call(bf16[1024,1024]{1,0:T(8,128)(2,1)} %get-tuple-element.451.refs_0_, bf16[1024,1024]{1,0:T(8,128)(2,1)} %copy-done.44, ...), custom_call_target="tpu_custom_call" | custom-call | flops 30064771072 | bytes 50331648 | tf_op jit(solution)/shard_map/feed_forward/pallas_call | solution.py:718
  258.8 42.3 %feed_forward.3 = (bf16[1024,1024]{1,0:T(8,128)(2,1)}, bf16[1024,1024]{1,0:T(8,128)(2,1)}, bf16[1024,1024]{1,0:T(8,128)(2,1)}, bf16[1024,1024]{1,0:T(8,128)(2,1)...) custom-call(bf16[1024,1024]{1,0:T(8,128)(2,1)} %get-tuple-element.451.re, ...), custom_call_target="tpu_custom_call", output_to_operand_aliasing={{4}: (10, {}), {5}: (11, {})} | custom-call | flops 30064771072 | bytes 50331648 | tf_op jit(solution)/shard_map/feed_forward/pallas_call | solution.py:718
  301.1 3.3 copy_bitcast_fusion
  308.0 11.3 %norm_two_back.1 = (f32[1024,1024]{1,0:T(8,128)}, bf16[1024,1024]{1,0:T(8,128)(2,1)}, bf16[1024,1024]{1,0:T(8,128)(2,1)}, f32[2,1024]{1,0:T(2,128)}) custom-call(bf16[1024,1024]{1,0:T(8,128)(2,1)} %get-tuple-element.488.mine_ref, bf16[1024,1024]{1,0:T(8,128)(2,1)} %collective-permute-done.38.theirs_ref, f32[1024,1024]{1,0:T(8,128)} %get-tuple-element.490.middle_ref, ...), custom_call_target="tpu_custom_call" | custom-call | flops 2147483648 | bytes 25165824 | tf_op jit(solution)/shard_map/norm_two_back/pallas_call | solution.py:798
  319.3 5.6 weight_grads.3
  324.9 24.6 %attention_backward.1 = (bf16[1024,1024]{1,0:T(8,128)(2,1)}, bf16[1024,1024]{1,0:T(8,128)(2,1)}, bf16[1024,1024]{1,0:T(8,128)(2,1)}) custom-call(s32[1024,1]{1,0:T(8,128)} %copy.73.seg_col_ref, s32[1,1024]{1,0:T(1,128)} %fusion.30.seg_row_ref, bf16[1024,1024]{1,0:T(8,128)(2,1)} %convolution_convert_fusion.2.query_ref, ...), custom_call_target="tpu_custom_call" | custom-call | flops 4697620480 | bytes 14680064 | tf_op jit(solution)/shard_map/attention_backward/pallas_call | solution.py:594
  354.7 2.5 fusion
  357.5 3.7 fusion.1
  361.2 13.0 %weight_grads.4 = (bf16[1024,1536]{1,0:T(8,128)(2,1)}, bf16[1024,1536]{1,0:T(8,128)(2,1)}) custom-call(s32[1]{0:T(128)} %bitcast.81.side_ref, bf16[1024,1024]{1,0:T(8,128)(2,1)} %get-tuple-element.421.refs_0_, bf16[1024,1024]{1,0:T(8,128)(2,1)} %ssm_rest.1.refs_1_.refs_2_, bf16[1024,1024]{1,0:T(8,128)(2,1)} %ssm_rest.1.refs_1_.refs_2_, ...), custom_call_target="tpu_custom_call" | custom-call | flops 6442450944 | bytes 18874368 | tf_op jit(solution)/shard_map/weight_grads/pallas_call | solution.py:861
  374.8 4.0 collective-permute-done.43
  378.8 4.5 add_add_fusion
  383.3 2.3 dynamic-slice_bitcast_fusion.1
  390.4 3.8 add_convert_fusion
  394.3 6.2 %maximum_select_fusion = f32[2,512,1024]{2,1,0:T(8,128)} fusion(f32[1,512,1024]{2,1,0:T(8,128)} %bitcast.87, f32[1,512,1024]{2,1,0:T(8,128)S(1)} %copy-done.5, pred[]{:T(512)S(6)} %eq.113), kind=kLoop, calls=%fused_computation.1 | loop fusion | flops 3145728 | bytes 8388609 | tf_op jit(solution)/shard_map/jit(_where)/select_n | solution.py:912
  400.5 12.0 %collective-permute-done.41 = bf16[2,2,64,2048]{3,2,1,0:T(8,128)(2,1)} collective-permute-done((bf16[2,2,64,2048]{3,2,1,0:T(8,128)(2,1)}, bf16[2,2,64,2048]{3,2,1,0:T(8,128)(2,1)}, u32[]{:S(2)}, u32[]{:S(2)}) %collective-permute-start.41) | collective-permute-done | bytes 1048608 | tf_op jit(solution)/shard_map/ppermute | solution.py:59
  425.8 27.4 %ssm_backward.1 = (f32[1024,8,128]{2,1,0:T(8,128)}, f32[1024,8,128]{2,1,0:T(8,128)}, f32[8,8,128]{2,1,0:T(8,128)}, f32[8,8,128]{2,1,0:T(8,128)}) custom-call(s32[16]{0:T(128)} %convert_reduce_fusion.starts_ref, bf16[1024,1024]{1,0:T(8,128)(2,1)} %get-tuple-element.542.refs_4_.gkey_ref, bf16[1024,1024]{1,0:T(8,128)(2,1)} %get-tuple-element.543.refs_5_.gvalue_ref, ...), custom_call_target="tpu_custom_call" | custom-call | flops 21474836480 | bytes 20971520 | tf_op jit(solution)/shard_map/ssm_backward/pallas_call | solution.py:435
  458.4 22.8 %ssm_backward_rest.1 = (bf16[1024,1024]{1,0:T(8,128)(2,1)}, f32[8,8,128]{2,1,0:T(8,128)}, f32[8,8,128]{2,1,0:T(8,128)}) custom-call(s32[16]{0:T(128)} %convert_reduce_fusion.starts_ref, f32[1024,8,128]{2,1,0:T(8,128)} %get-tuple-element.557.g_ref, f32[1024,8,128]{2,1,0:T(8,128)} %get-tuple-element.558.given_ref, ...), custom_call_target="tpu_custom_call" | custom-call | flops 21474836480 | bytes 20971520 | tf_op jit(solution)/shard_map/ssm_backward_rest/pallas_call | solution.py:460
  483.1 5.6 weight_grads.5
  494.5 11.7 %norm_one_back.1 = (f32[1024,1024]{1,0:T(8,128)}, f32[2,1024]{1,0:T(2,128)}) custom-call(bf16[1024,1024]{1,0:T(8,128)(2,1)} %get-tuple-element.514.refs_3_.gquery_ref, bf16[1024,1024]{1,0:T(8,128)(2,1)} %get-tuple-element.576.refs_1_.gmixed_ref, bf16[1024,1024]{1,0:T(8,128)(2,1)} %maximum_select_fusion.7.query_ref, ...), custom_call_target="tpu_custom_call" | custom-call | flops 4294967296 | bytes 20971520 | tf_op jit(solution)/shard_map/norm_one_back/pallas_call | solution.py:829
  506.3 7.8 %collective-permute-done.53 = bf16[64,4096]{1,0:T(8,128)(2,1)S(1)} collective-permute-done((bf16[64,4096]{1,0:T(8,128)(2,1)S(1)}, bf16[64,4096]{1,0:T(8,128)(2,1)S(1)}, u32[]{:S(2)}, u32[]{:S(2)}) %collective-permute-start.53) | collective-permute-done | bytes 524320 | tf_op jit(solution)/shard_map/ppermute | solution.py:59
  514.0 2.3 collective-permute-done.52
  520.9 4.0 dynamic-slice_bitcast_fusion
  524.9 4.0 collective-permute-done.57
  530.6 2.5 collective-permute-start.59
  533.9 3.7 collective-permute-done.60
  550.0 3.3 collective-permute-done.63
  554.7 5.1 maximum_select_fusion.1
  (325 shorter events, 139.6 us)
Async XLA Ops:
  3.3 11.0 %collective-permute-start.1 = (bf16[64,1024]{1,0:T(8,128)(2,1)S(1)}, bf16[64,1024]{1,0:T(8,128)(2,1)S(1)}, u32[]{:S(2)}, u32[]{:S(2)}) collective-permute-start(bf16[64,1024]{1,0:T(8,128)(2,1)S(1)} %get-tuple-element.327), channel_id=1, source_target_pairs={{0,8},{2,10},{4,12},{6,14},{8,0},{10,2},{12,4},{14,6},{16,24},{18,... | collective-permute-start | bytes 393224 | tf_op jit(solution)/shard_map/ppermute | solution.py:59
  23.5 14.8 %collective-permute-start.4 = (bf16[2,2,72,512]{3,2,1,0:T(8,128)(2,1)S(1)}, bf16[2,2,72,512]{3,2,1,0:T(8,128)(2,1)S(1)}, u32[]{:S(2)}, u32[]{:S(2)}) collective-permute-start(bf16[2,2,72,512]{3,2,1,0:T(8,128)(2,1)S(1)} %maximum_select_fusion.29), channel_id=1, source_target_pairs={{0,2},{2,0},{4,6},{6,4},{8,10},{10,8},{12,14},{14,12},{16,18},{18,... | collective-permute-start | bytes 884744 | tf_op jit(solution)/shard_map/ppermute | solution.py:59
  24.9 13.4 %collective-permute-start.5 = (bf16[2,64,1024]{2,1,0:T(8,128)(2,1)S(1)}, bf16[2,64,1024]{2,1,0:T(8,128)(2,1)S(1)}, u32[]{:S(2)}, u32[]{:S(2)}) collective-permute-start(bf16[2,64,1024]{2,1,0:T(8,128)(2,1)S(1)} %maximum_select_fusion.30), channel_id=1, source_target_pairs={{0,16},{2,18},{4,20},{6,22},{8,24},{10,26},{12,28},{14,30},{16,0},... | collective-permute-start | bytes 786440 | tf_op jit(solution)/shard_map/ppermute | solution.py:59
  39.2 14.5 %collective-permute-start.6 = (bf16[2,2,2,72,512]{4,3,2,1,0:T(8,128)(2,1)S(1)}, bf16[2,2,2,72,512]{4,3,2,1,0:T(8,128)(2,1)S(1)}, u32[]{:S(2)}, u32[]{:S(2)}) collective-permute-start(bf16[2,2,2,72,512]{4,3,2,1,0:T(8,128)(2,1)S(1)} %maximum_select_fusion.22), channel_id=1, source_target_pairs={{0,4},{2,6},{4,0},{6,2},{8,12},{10,14},{12,8},{14,10},{16,20},{18,... | collective-permute-start | bytes 1769480 | tf_op jit(solution)/shard_map/ppermute | solution.py:59
  40.8 12.9 %collective-permute-start.7 = (bf16[2,64,1024]{2,1,0:T(8,128)(2,1)S(1)}, bf16[2,64,1024]{2,1,0:T(8,128)(2,1)S(1)}, u32[]{:S(2)}, u32[]{:S(2)}) collective-permute-start(bf16[2,64,1024]{2,1,0:T(8,128)(2,1)S(1)} %maximum_select_fusion.31), channel_id=1, source_target_pairs={{0,16},{2,18},{4,20},{6,22},{8,24},{10,26},{12,28},{14,30},{16,0},... | collective-permute-start | bytes 786440 | tf_op jit(solution)/shard_map/ppermute | solution.py:59
  43.6 17.2 %collective-permute-start.12 = (bf16[512,1024]{1,0:T(8,128)(2,1)}, bf16[512,1024]{1,0:T(8,128)(2,1)}, u32[]{:S(2)}, u32[]{:S(2)}) collective-permute-start(bf16[512,1024]{1,0:T(8,128)(2,1)} %get-tuple-element.693), channel_id=1, source_target_pairs={{0,1},{1,0},{2,3},{3,2},{4,5},{5,4},{6,7},{7,6},{8,9},{9,8},{10,11... | collective-permute-start | bytes 3145736 | tf_op jit(solution)/shard_map/ppermute | solution.py:181
  44.2 12.7 %collective-permute-start.13 = (f32[3,16,512]{2,1,0:T(8,128)}, f32[3,16,512]{2,1,0:T(8,128)}, u32[]{:S(2)}, u32[]{:S(2)}) collective-permute-start(f32[3,16,512]{2,1,0:T(8,128)} %pad_maximum_fusion.10), channel_id=1, source_target_pairs={{0,1},{1,0},{2,3},{3,2},{4,5},{5,4},{6,7},{7,6},{8,9},{9,8},{10,11... | collective-permute-start | bytes 294920 | tf_op jit(solution)/shard_map/ppermute | solution.py:181
  54.8 14.0 %collective-permute-start.14 = (bf16[1024,512]{1,0:T(8,128)(2,1)S(1)}, bf16[1024,512]{1,0:T(8,128)(2,1)}, u32[]{:S(2)}, u32[]{:S(2)}) collective-permute-start(bf16[1024,512]{1,0:T(8,128)(2,1)S(1)} %bitcast.228), channel_id=1, source_target_pairs={{0,1},{1,0},{2,3},{3,2},{4,5},{5,4},{6,7},{7,6},{8,9},{9,8},{10,11... | collective-permute-start | bytes 3145736 | tf_op jit(solution)/shard_map/ppermute | solution.py:181
  59.3 14.0 %collective-permute-start.8 = (bf16[2,2,64,1024]{3,2,1,0:T(8,128)(2,1)}, bf16[2,2,64,1024]{3,2,1,0:T(8,128)(2,1)}, u32[]{:S(2)}, u32[]{:S(2)}) collective-permute-start(bf16[2,2,64,1024]{3,2,1,0:T(8,128)(2,1)} %maximum_select_fusion.23), channel_id=1, source_target_pairs={{0,2},{2,0},{4,6},{6,4},{8,10},{10,8},{12,14},{14,12},{16,18},{18,... | collective-permute-start | bytes 1572872 | tf_op jit(solution)/shard_map/ppermute | solution.py:59
  59.8 13.7 %collective-permute-start.9 = (bf16[2,2,64,1024]{3,2,1,0:T(8,128)(2,1)}, bf16[2,2,64,1024]{3,2,1,0:T(8,128)(2,1)}, u32[]{:S(2)}, u32[]{:S(2)}) collective-permute-start(bf16[2,2,64,1024]{3,2,1,0:T(8,128)(2,1)} %maximum_select_fusion.24), channel_id=1, source_target_pairs={{0,4},{2,6},{4,0},{6,2},{8,12},{10,14},{12,8},{14,10},{16,20},{18,... | collective-permute-start | bytes 1572872 | tf_op jit(solution)/shard_map/ppermute | solution.py:59
  78.4 26.2 %collective-permute-start.15 = (bf16[2,2,2,64,1024]{4,3,1,0,2:T(8,128)(2,1)S(1)}, bf16[2,2,2,64,1024]{4,3,1,0,2:T(8,128)(2,1)S(1)}, u32[]{:S(2)}, u32[]{:S(2)}) collective-permute-start(bf16[2,2,2,64,1024]{4,3,1,0,2:T(8,128)(2,1)S(1)} %maximum_select_fusion.16), channel_id=1, source_target_pairs={{0,4},{2,6},{4,0},{6,2},{8,12},{10,14},{12,8},{14,10},{16,20},{18,... | collective-permute-start | bytes 3145736 | tf_op jit(solution)/shard_map/ppermute | solution.py:59
  79.5 25.1 %collective-permute-start.16 = (bf16[2,2,2,64,1024]{4,3,1,0,2:T(8,128)(2,1)S(1)}, bf16[2,2,2,64,1024]{4,3,1,0,2:T(8,128)(2,1)S(1)}, u32[]{:S(2)}, u32[]{:S(2)}) collective-permute-start(bf16[2,2,2,64,1024]{4,3,1,0,2:T(8,128)(2,1)S(1)} %maximum_select_fusion.17), channel_id=1, source_target_pairs={{0,2},{2,0},{4,6},{6,4},{8,10},{10,8},{12,14},{14,12},{16,18},{18,... | collective-permute-start | bytes 3145736 | tf_op jit(solution)/shard_map/ppermute | solution.py:59
  80.6 20.4 %collective-permute-start.17 = (bf16[2,64,1024]{2,1,0:T(8,128)(2,1)S(1)}, bf16[2,64,1024]{2,1,0:T(8,128)(2,1)S(1)}, u32[]{:S(2)}, u32[]{:S(2)}) collective-permute-start(bf16[2,64,1024]{2,1,0:T(8,128)(2,1)S(1)} %maximum_select_fusion.32), channel_id=1, source_target_pairs={{0,16},{2,18},{4,20},{6,22},{8,24},{10,26},{12,28},{14,30},{16,0},... | collective-permute-start | bytes 786440 | tf_op jit(solution)/shard_map/ppermute | solution.py:59
  80.6 23.9 %collective-permute-start.18 = (bf16[2,64,1024]{2,1,0:T(8,128)(2,1)S(1)}, bf16[2,64,1024]{2,1,0:T(8,128)(2,1)S(1)}, u32[]{:S(2)}, u32[]{:S(2)}) collective-permute-start(bf16[2,64,1024]{2,1,0:T(8,128)(2,1)S(1)} %maximum_select_fusion.33), channel_id=1, source_target_pairs={{0,16},{2,18},{4,20},{6,22},{8,24},{10,26},{12,28},{14,30},{16,0},... | collective-permute-start | bytes 786440 | tf_op jit(solution)/shard_map/ppermute | solution.py:59
  106.5 22.3 %collective-permute-start.25 = (bf16[1024,1024]{1,0:T(8,128)(2,1)S(1)}, bf16[1024,1024]{1,0:T(8,128)(2,1)}, u32[]{:S(2)}, u32[]{:S(2)}) collective-permute-start(bf16[1024,1024]{1,0:T(8,128)(2,1)S(1)} %bitcast.210), channel_id=1, source_target_pairs={{0,1},{1,0},{2,3},{3,2},{4,5},{5,4},{6,7},{7,6},{8,9},{9,8},{10,11... | collective-permute-start | bytes 6291464 | tf_op jit(solution)/shard_map/ppermute | solution.py:181
  106.9 26.8 %collective-permute-start.24 = (bf16[1024,1024]{1,0:T(8,128)(2,1)S(1)}, bf16[1024,1024]{1,0:T(8,128)(2,1)}, u32[]{:S(2)}, u32[]{:S(2)}) collective-permute-start(bf16[1024,1024]{1,0:T(8,128)(2,1)S(1)} %bitcast.208), channel_id=1, source_target_pairs={{0,1},{1,0},{2,3},{3,2},{4,5},{5,4},{6,7},{7,6},{8,9},{9,8},{10,11... | collective-permute-start | bytes 6291464 | tf_op jit(solution)/shard_map/ppermute | solution.py:181
  110.0 15.2 %collective-permute-start.23 = (bf16[512,1024]{1,0:T(8,128)(2,1)}, bf16[512,1024]{1,0:T(8,128)(2,1)S(1)}, u32[]{:S(2)}, u32[]{:S(2)}) collective-permute-start(bf16[512,1024]{1,0:T(8,128)(2,1)} %get-tuple-element.691), channel_id=1, source_target_pairs={{0,1},{1,0},{2,3},{3,2},{4,5},{5,4},{6,7},{7,6},{8,9},{9,8},{10,11... | collective-permute-start | bytes 3145736 | tf_op jit(solution)/shard_map/ppermute | solution.py:181
  112.4 29.1 %collective-permute-start.19 = (bf16[2,2,64,1024]{3,2,1,0:T(8,128)(2,1)}, bf16[2,2,64,1024]{3,2,1,0:T(8,128)(2,1)}, u32[]{:S(2)}, u32[]{:S(2)}) collective-permute-start(bf16[2,2,64,1024]{3,2,1,0:T(8,128)(2,1)} %maximum_select_fusion.25), channel_id=1, source_target_pairs={{0,2},{2,0},{4,6},{6,4},{8,10},{10,8},{12,14},{14,12},{16,18},{18,... | collective-permute-start | bytes 1572872 | tf_op jit(solution)/shard_map/ppermute | solution.py:59
  113.1 28.4 %collective-permute-start.20 = (bf16[2,2,64,1024]{3,2,1,0:T(8,128)(2,1)S(1)}, bf16[2,2,64,1024]{3,2,1,0:T(8,128)(2,1)}, u32[]{:S(2)}, u32[]{:S(2)}) collective-permute-start(bf16[2,2,64,1024]{3,2,1,0:T(8,128)(2,1)S(1)} %maximum_select_fusion.26), channel_id=1, source_target_pairs={{0,4},{2,6},{4,0},{6,2},{8,12},{10,14},{12,8},{14,10},{16,20},{18,... | collective-permute-start | bytes 1572872 | tf_op jit(solution)/shard_map/ppermute | solution.py:59
  125.2 16.3 %collective-permute-start.21 = (bf16[64,1024]{1,0:T(8,128)(2,1)S(1)}, bf16[64,1024]{1,0:T(8,128)(2,1)S(1)}, u32[]{:S(2)}, u32[]{:S(2)}) collective-permute-start(bf16[64,1024]{1,0:T(8,128)(2,1)S(1)} %get-tuple-element.404), channel_id=1, source_target_pairs={{0,8},{2,10},{4,12},{6,14},{8,0},{10,2},{12,4},{14,6},{16,24},{18,... | collective-permute-start | bytes 393224 | tf_op jit(solution)/shard_map/ppermute | solution.py:59
  128.8 12.6 %collective-permute-start.22 = (bf16[64,1024]{1,0:T(8,128)(2,1)S(1)}, bf16[64,1024]{1,0:T(8,128)(2,1)S(1)}, u32[]{:S(2)}, u32[]{:S(2)}) collective-permute-start(bf16[64,1024]{1,0:T(8,128)(2,1)S(1)} %get-tuple-element.406), channel_id=1, source_target_pairs={{0,8},{2,10},{4,12},{6,14},{8,0},{10,2},{12,4},{14,6},{16,24},{18,... | collective-permute-start | bytes 393224 | tf_op jit(solution)/shard_map/ppermute | solution.py:59
  146.3 39.7 %collective-permute-start.30 = (bf16[1024,1024]{1,0:T(8,128)(2,1)S(1)}, bf16[1024,1024]{1,0:T(8,128)(2,1)}, u32[]{:S(2)}, u32[]{:S(2)}) collective-permute-start(bf16[1024,1024]{1,0:T(8,128)(2,1)S(1)} %maximum_select_fusion.6.refs_2_.cot_ref), channel_id=1, source_target_pairs={{0,1},{1,0},{2,3},{3,2},{4,5},{5,4},{6,7},{7,6},{8,9},{9,8},{10,11... | collective-permute-start | bytes 6291464 | tf_op jit(solution)/shard_map/ppermute | solution.py:181
  149.3 36.7 %collective-permute-start.26 = (bf16[2,2,2,64,1024]{4,3,1,0,2:T(8,128)(2,1)}, bf16[2,2,2,64,1024]{4,3,1,0,2:T(8,128)(2,1)S(1)}, u32[]{:S(2)}, u32[]{:S(2)}) collective-permute-start(bf16[2,2,2,64,1024]{4,3,1,0,2:T(8,128)(2,1)} %maximum_select_fusion.18), channel_id=1, source_target_pairs={{0,4},{2,6},{4,0},{6,2},{8,12},{10,14},{12,8},{14,10},{16,20},{18,... | collective-permute-start | bytes 3145736 | tf_op jit(solution)/shard_map/ppermute | solution.py:59
  150.7 35.4 %collective-permute-start.27 = (bf16[2,2,2,64,1024]{4,3,1,0,2:T(8,128)(2,1)S(1)}, bf16[2,2,2,64,1024]{4,3,1,0,2:T(8,128)(2,1)S(1)}, u32[]{:S(2)}, u32[]{:S(2)}) collective-permute-start(bf16[2,2,2,64,1024]{4,3,1,0,2:T(8,128)(2,1)S(1)} %maximum_select_fusion.19), channel_id=1, source_target_pairs={{0,2},{2,0},{4,6},{6,4},{8,10},{10,8},{12,14},{14,12},{16,18},{18,... | collective-permute-start | bytes 3145736 | tf_op jit(solution)/shard_map/ppermute | solution.py:59
  151.9 34.1 %collective-permute-start.28 = (bf16[2,64,1024]{2,1,0:T(8,128)(2,1)S(1)}, bf16[2,64,1024]{2,1,0:T(8,128)(2,1)S(1)}, u32[]{:S(2)}, u32[]{:S(2)}) collective-permute-start(bf16[2,64,1024]{2,1,0:T(8,128)(2,1)S(1)} %maximum_select_fusion.34), channel_id=1, source_target_pairs={{0,16},{2,18},{4,20},{6,22},{8,24},{10,26},{12,28},{14,30},{16,0},... | collective-permute-start | bytes 786440 | tf_op jit(solution)/shard_map/ppermute | solution.py:59
  152.7 33.4 %collective-permute-start.29 = (bf16[2,64,1024]{2,1,0:T(8,128)(2,1)}, bf16[2,64,1024]{2,1,0:T(8,128)(2,1)S(1)}, u32[]{:S(2)}, u32[]{:S(2)}) collective-permute-start(bf16[2,64,1024]{2,1,0:T(8,128)(2,1)} %maximum_select_fusion.35), channel_id=1, source_target_pairs={{0,16},{2,18},{4,20},{6,22},{8,24},{10,26},{12,28},{14,30},{16,0},... | collective-permute-start | bytes 786440 | tf_op jit(solution)/shard_map/ppermute | solution.py:59
  197.1 14.8 %collective-permute-start.33 = (bf16[1024,1024]{1,0:T(8,128)(2,1)}, bf16[1024,1024]{1,0:T(8,128)(2,1)S(1)}, u32[]{:S(2)}, u32[]{:S(2)}) collective-permute-start(bf16[1024,1024]{1,0:T(8,128)(2,1)} %get-tuple-element.451.refs_0_), channel_id=1, source_target_pairs={{0,1},{1,0},{2,3},{3,2},{4,5},{5,4},{6,7},{7,6},{8,9},{9,8},{10,11... | collective-permute-start | bytes 6291464 | tf_op jit(solution)/shard_map/ppermute | solution.py:181
  197.1 14.3 %collective-permute-start.31 = (bf16[2,2,64,1024]{3,2,1,0:T(8,128)(2,1)S(1)}, bf16[2,2,64,1024]{3,2,1,0:T(8,128)(2,1)S(1)}, u32[]{:S(2)}, u32[]{:S(2)}) collective-permute-start(bf16[2,2,64,1024]{3,2,1,0:T(8,128)(2,1)S(1)} %maximum_select_fusion.27), channel_id=1, source_target_pairs={{0,2},{2,0},{4,6},{6,4},{8,10},{10,8},{12,14},{14,12},{16,18},{18,... | collective-permute-start | bytes 1572872 | tf_op jit(solution)/shard_map/ppermute | solution.py:59
  198.0 14.0 %collective-permute-start.32 = (bf16[2,2,64,1024]{3,2,1,0:T(8,128)(2,1)S(1)}, bf16[2,2,64,1024]{3,2,1,0:T(8,128)(2,1)S(1)}, u32[]{:S(2)}, u32[]{:S(2)}) collective-permute-start(bf16[2,2,64,1024]{3,2,1,0:T(8,128)(2,1)S(1)} %maximum_select_fusion.28), channel_id=1, source_target_pairs={{0,4},{2,6},{4,0},{6,2},{8,12},{10,14},{12,8},{14,10},{16,20},{18,... | collective-permute-start | bytes 1572872 | tf_op jit(solution)/shard_map/ppermute | solution.py:59
  213.3 41.6 %collective-permute-start.34 = (bf16[2,2,2,64,1024]{4,3,1,0,2:T(8,128)(2,1)S(1)}, bf16[2,2,2,64,1024]{4,3,1,0,2:T(8,128)(2,1)S(1)}, u32[]{:S(2)}, u32[]{:S(2)}) collective-permute-start(bf16[2,2,2,64,1024]{4,3,1,0,2:T(8,128)(2,1)S(1)} %maximum_select_fusion.20), channel_id=1, source_target_pairs={{0,4},{2,6},{4,0},{6,2},{8,12},{10,14},{12,8},{14,10},{16,20},{18,... | collective-permute-start | bytes 3145736 | tf_op jit(solution)/shard_map/ppermute | solution.py:59
  213.9 40.9 %collective-permute-start.35 = (bf16[2,2,2,64,1024]{4,3,1,0,2:T(8,128)(2,1)S(1)}, bf16[2,2,2,64,1024]{4,3,1,0,2:T(8,128)(2,1)S(1)}, u32[]{:S(2)}, u32[]{:S(2)}) collective-permute-start(bf16[2,2,2,64,1024]{4,3,1,0,2:T(8,128)(2,1)S(1)} %maximum_select_fusion.21), channel_id=1, source_target_pairs={{0,2},{2,0},{4,6},{6,4},{8,10},{10,8},{12,14},{14,12},{16,18},{18,... | collective-permute-start | bytes 3145736 | tf_op jit(solution)/shard_map/ppermute | solution.py:59
  304.4 48.2 %collective-permute-start.37 = (bf16[2,2,2,64,2048]{4,3,1,0,2:T(8,128)(2,1)}, bf16[2,2,2,64,2048]{4,3,1,0,2:T(8,128)(2,1)S(1)}, u32[]{:S(2)}, u32[]{:S(2)}) collective-permute-start(bf16[2,2,2,64,2048]{4,3,1,0,2:T(8,128)(2,1)} %copy_bitcast_fusion), channel_id=1, source_target_pairs={{0,2},{2,0},{4,6},{6,4},{8,10},{10,8},{12,14},{14,12},{16,18},{18,... | collective-permute-start | bytes 6291464 | tf_op jit(solution)/shard_map/ppermute | solution.py:59
  306.7 48.0 %collective-permute-start.36 = (bf16[2,2,2,64,2048]{4,3,1,0,2:T(8,128)(2,1)}, bf16[2,2,2,64,2048]{4,3,1,0,2:T(8,128)(2,1)}, u32[]{:S(2)}, u32[]{:S(2)}) collective-permute-start(bf16[2,2,2,64,2048]{4,3,1,0,2:T(8,128)(2,1)} %copy_bitcast_fusion.1), channel_id=1, source_target_pairs={{0,4},{2,6},{4,0},{6,2},{8,12},{10,14},{12,8},{14,10},{16,20},{18,... | collective-permute-start | bytes 6291464 | tf_op jit(solution)/shard_map/ppermute | solution.py:59
  324.9 24.6 %collective-permute-start.39 = (bf16[1024,512]{1,0:T(8,128)(2,1)}, bf16[1024,512]{1,0:T(8,128)(2,1)}, u32[]{:S(2)}, u32[]{:S(2)}) collective-permute-start(bf16[1024,512]{1,0:T(8,128)(2,1)} %get-tuple-element.496), channel_id=1, source_target_pairs={{0,1},{1,0},{2,3},{3,2},{4,5},{5,4},{6,7},{7,6},{8,9},{9,8},{10,11... | collective-permute-start | bytes 3145736 | tf_op jit(solution)/shard_map/ppermute | solution.py:181
  374.3 16.2 %collective-permute-start.42 = (bf16[1024,1536]{1,0:T(8,128)(2,1)}, bf16[1024,1536]{1,0:T(8,128)(2,1)}, u32[]{:S(2)}, u32[]{:S(2)}) collective-permute-start(bf16[1024,1536]{1,0:T(8,128)(2,1)} %get-tuple-element.522), channel_id=1, source_target_pairs={{0,1},{1,0},{2,3},{3,2},{4,5},{5,4},{6,7},{7,6},{8,9},{9,8},{10,11... | collective-permute-start | bytes 9437192 | tf_op jit(solution)/shard_map/ppermute | solution.py:181
  386.8 25.8 %collective-permute-start.41 = (bf16[2,2,64,2048]{3,2,1,0:T(8,128)(2,1)}, bf16[2,2,64,2048]{3,2,1,0:T(8,128)(2,1)}, u32[]{:S(2)}, u32[]{:S(2)}) collective-permute-start(bf16[2,2,64,2048]{3,2,1,0:T(8,128)(2,1)} %dynamic-slice_bitcast_fusion.3), channel_id=1, source_target_pairs={{0,4},{2,6},{4,0},{6,2},{8,12},{10,14},{12,8},{14,10},{16,20},{18,... | collective-permute-start | bytes 3145736 | tf_op jit(solution)/shard_map/ppermute | solution.py:59
  389.2 25.5 %collective-permute-start.40 = (bf16[2,2,64,2048]{3,2,1,0:T(8,128)(2,1)}, bf16[2,2,64,2048]{3,2,1,0:T(8,128)(2,1)}, u32[]{:S(2)}, u32[]{:S(2)}) collective-permute-start(bf16[2,2,64,2048]{3,2,1,0:T(8,128)(2,1)} %dynamic-slice_bitcast_fusion.4), channel_id=1, source_target_pairs={{0,2},{2,0},{4,6},{6,4},{8,10},{10,8},{12,14},{14,12},{16,18},{18,... | collective-permute-start | bytes 3145736 | tf_op jit(solution)/shard_map/ppermute | solution.py:59
  420.0 33.2 %collective-permute-start.46 = (bf16[2,2,2,64,1024]{4,3,1,0,2:T(8,128)(2,1)S(1)}, bf16[2,2,2,64,1024]{4,3,1,0,2:T(8,128)(2,1)}, u32[]{:S(2)}, u32[]{:S(2)}) collective-permute-start(bf16[2,2,2,64,1024]{4,3,1,0,2:T(8,128)(2,1)S(1)} %copy_bitcast_fusion.2), channel_id=1, source_target_pairs={{0,2},{2,0},{4,6},{6,4},{8,10},{10,8},{12,14},{14,12},{16,18},{18,... | collective-permute-start | bytes 3145736 | tf_op jit(solution)/shard_map/ppermute | solution.py:59
  422.4 30.8 %collective-permute-start.45 = (bf16[2,2,2,64,1024]{4,3,1,0,2:T(8,128)(2,1)}, bf16[2,2,2,64,1024]{4,3,1,0,2:T(8,128)(2,1)}, u32[]{:S(2)}, u32[]{:S(2)}) collective-permute-start(bf16[2,2,2,64,1024]{4,3,1,0,2:T(8,128)(2,1)} %copy_bitcast_fusion.3), channel_id=1, source_target_pairs={{0,4},{2,6},{4,0},{6,2},{8,12},{10,14},{12,8},{14,10},{16,20},{18,... | collective-permute-start | bytes 3145736 | tf_op jit(solution)/shard_map/ppermute | solution.py:59
  424.3 56.9 %collective-permute-start.49 = (bf16[2,64,4096]{2,1,0:T(8,128)(2,1)}, bf16[2,64,4096]{2,1,0:T(8,128)(2,1)}, u32[]{:S(2)}, u32[]{:S(2)}) collective-permute-start(bf16[2,64,4096]{2,1,0:T(8,128)(2,1)} %dynamic-slice_bitcast_fusion.2), channel_id=1, source_target_pairs={{0,16},{2,18},{4,20},{6,22},{8,24},{10,26},{12,28},{14,30},{16,0},... | collective-permute-start | bytes 3145736 | tf_op jit(solution)/shard_map/ppermute | solution.py:59
  456.6 24.6 %collective-permute-start.48 = (bf16[2,2,64,1024]{3,2,1,0:T(8,128)(2,1)S(1)}, bf16[2,2,64,1024]{3,2,1,0:T(8,128)(2,1)S(1)}, u32[]{:S(2)}, u32[]{:S(2)}) collective-permute-start(bf16[2,2,64,1024]{3,2,1,0:T(8,128)(2,1)S(1)} %dynamic-slice_bitcast_fusion.11), channel_id=1, source_target_pairs={{0,4},{2,6},{4,0},{6,2},{8,12},{10,14},{12,8},{14,10},{16,20},{18,... | collective-permute-start | bytes 1572872 | tf_op jit(solution)/shard_map/ppermute | solution.py:59
  457.5 23.7 %collective-permute-start.47 = (bf16[2,2,64,1024]{3,2,1,0:T(8,128)(2,1)S(1)}, bf16[2,2,64,1024]{3,2,1,0:T(8,128)(2,1)S(1)}, u32[]{:S(2)}, u32[]{:S(2)}) collective-permute-start(bf16[2,2,64,1024]{3,2,1,0:T(8,128)(2,1)S(1)} %dynamic-slice_bitcast_fusion.12), channel_id=1, source_target_pairs={{0,2},{2,0},{4,6},{6,4},{8,10},{10,8},{12,14},{14,12},{16,18},{18,... | collective-permute-start | bytes 1572872 | tf_op jit(solution)/shard_map/ppermute | solution.py:59
  488.9 25.1 %collective-permute-start.53 = (bf16[64,4096]{1,0:T(8,128)(2,1)S(1)}, bf16[64,4096]{1,0:T(8,128)(2,1)S(1)}, u32[]{:S(2)}, u32[]{:S(2)}) collective-permute-start(bf16[64,4096]{1,0:T(8,128)(2,1)S(1)} %dynamic-slice_bitcast_fusion.9), channel_id=1, source_target_pairs={{0,8},{2,10},{4,12},{6,14},{8,0},{10,2},{12,4},{14,6},{16,24},{18,... | collective-permute-start | bytes 1572872 | tf_op jit(solution)/shard_map/ppermute | solution.py:59
  490.0 26.3 %collective-permute-start.52 = (bf16[2,64,2048]{2,1,0:T(8,128)(2,1)S(1)}, bf16[2,64,2048]{2,1,0:T(8,128)(2,1)S(1)}, u32[]{:S(2)}, u32[]{:S(2)}) collective-permute-start(bf16[2,64,2048]{2,1,0:T(8,128)(2,1)S(1)} %dynamic-slice_bitcast_fusion.10), channel_id=1, source_target_pairs={{0,16},{2,18},{4,20},{6,22},{8,24},{10,26},{12,28},{14,30},{16,0},... | collective-permute-start | bytes 1572872 | tf_op jit(solution)/shard_map/ppermute | solution.py:59
  493.5 22.9 %collective-permute-start.51 = (bf16[2,2,2,64,512]{4,3,1,0,2:T(8,128)(2,1)S(1)}, bf16[2,2,2,64,512]{4,3,1,0,2:T(8,128)(2,1)S(1)}, u32[]{:S(2)}, u32[]{:S(2)}) collective-permute-start(bf16[2,2,2,64,512]{4,3,1,0,2:T(8,128)(2,1)S(1)} %copy_bitcast_fusion.4), channel_id=1, source_target_pairs={{0,4},{2,6},{4,0},{6,2},{8,12},{10,14},{12,8},{14,10},{16,20},{18,... | collective-permute-start | bytes 1572872 | tf_op jit(solution)/shard_map/ppermute | solution.py:59
  518.7 10.3 %collective-permute-start.58 = (bf16[64,2048]{1,0:T(8,128)(2,1)S(1)}, bf16[64,2048]{1,0:T(8,128)(2,1)S(1)}, u32[]{:S(2)}, u32[]{:S(2)}) collective-permute-start(bf16[64,2048]{1,0:T(8,128)(2,1)S(1)} %dynamic-slice_bitcast_fusion.13), channel_id=1, source_target_pairs={{0,8},{2,10},{4,12},{6,14},{8,0},{10,2},{12,4},{14,6},{16,24},{18,... | collective-permute-start | bytes 786440 | tf_op jit(solution)/shard_map/ppermute | solution.py:59
  518.8 10.2 %collective-permute-start.56 = (bf16[2,2,64,512]{3,2,1,0:T(8,128)(2,1)S(1)}, bf16[2,2,64,512]{3,2,1,0:T(8,128)(2,1)S(1)}, u32[]{:S(2)}, u32[]{:S(2)}) collective-permute-start(bf16[2,2,64,512]{3,2,1,0:T(8,128)(2,1)S(1)} %dynamic-slice_bitcast_fusion.14), channel_id=1, source_target_pairs={{0,2},{2,0},{4,6},{6,4},{8,10},{10,8},{12,14},{14,12},{16,18},{18,... | collective-permute-start | bytes 786440 | tf_op jit(solution)/shard_map/ppermute | solution.py:59
  524.9 29.7 %collective-permute-start.54 = (f32[512,1024]{1,0:T(8,128)}, f32[512,1024]{1,0:T(8,128)}, u32[]{:S(2)}, u32[]{:S(2)}) collective-permute-start(f32[512,1024]{1,0:T(8,128)} %get-tuple-element.679), channel_id=1, source_target_pairs={{0,1},{1,0},{2,3},{3,2},{4,5},{5,4},{6,7},{7,6},{8,9},{9,8},{10,11... | collective-permute-start | bytes 6291464 | tf_op jit(solution)/shard_map/ppermute | solution.py:181
  (64 other events, 443.5 us)

commit v3 on v2

v3 whole, which is shorter than its diff:
```python
import functools
import math

import jax
import jax.numpy as jnp
from jax import lax
from jax.experimental import pallas as pl
from jax.experimental.pallas import tpu as pltpu
from jax.sharding import PartitionSpec as P

HEAD_DIM = 128
BLOCK = 512
CTX = 128
NDOCS = 8
LANES = 128
QTILE = 256
HEADS_EACH = 2

norm_eps = 1e-05
masked_score = -1e30
VMEM = 56 * 1024 * 1024
BF = jnp.bfloat16
F32 = jnp.float32


def dot_plain(left_op, right_op):
    return jnp.dot(left_op, right_op, preferred_element_type=F32)


def dot_last(left_op, right_op):
    return lax.dot_general(left_op, right_op, (((1,), (1,)), ((), ())), preferred_element_type=F32)


def dot_first(left_op, right_op):
    return lax.dot_general(left_op, right_op, (((0,), (0,)), ((), ())), preferred_element_type=F32)


def params(count=1):
    return pltpu.CompilerParams(
        dimension_semantics=("arbitrary",) * count, vmem_limit_bytes=VMEM
    )


def bits_of(count):
    out = []
    bit = 1
    while bit < count:
        out.append(bit)
        bit *= 2
    return out


def groups_of(count, low_groups):
    high = bits_of(count)[2:]
    return [tuple(high[k : k + 2]) for k in range(0, len(high), 2)] + [
        tuple(b for b in g if b < count) for g in low_groups
    ]


X_FIRST = ((1,), (2,))
Y_FIRST = ((2,), (1,))
DIRECT = ((1, 2),)


def swap(values, count, mask):
    return lax.ppermute(values, "dp", [(i, i ^ mask) for i in range(count)])


def tie(*trees):
    return lax.optimization_barrier(trees)


def in_order(upper, own, got, axis):
    return jnp.where(
        upper, jnp.stack([got, own], axis=axis), jnp.stack([own, got], axis=axis)
    )


class Gather:
    def __init__(self, shard, count, index, low):
        self.values, self.count, self.index = shard, count, index
        self.shape = (count * shard.shape[0],) + shard.shape[1:]
        self.left = groups_of(count, low)
        self.present = []

    def send(self):
        self.got = [swap(self.values, self.count, m) for m in masks_of(self.left[0])]

    def merge(self):
        pieces = [self.values] + list(self.got)
        for bit in self.left.pop(0):
            place = sum(1 for p in self.present if p > bit)
            self.present.append(bit)
            upper = (self.index // bit) % 2 == 1
            pieces = [
                in_order(upper, pieces[k], pieces[k + 1], place)
                for k in range(0, len(pieces), 2)
            ]
        self.values = pieces[0]

    def split(self, lows):
        cols = self.values.shape[-1] // 2
        out = []
        for k, low in enumerate(lows):
            part = Gather.__new__(Gather)
            part.count, part.index, part.present = self.count, self.index, list(self.present)
            part.values = self.values[..., k * cols : (k + 1) * cols]
            part.shape = self.shape[:-1] + (cols,)
            part.left = self.left[: -len(lows)] + list(low)
            out.append(part)
        return out

    def result(self):
        return self.values.reshape(self.shape)


def masks_of(group):
    return [group[0]] if len(group) == 1 else [group[0], group[1], group[0] | group[1]]


class Scatter:
    def __init__(self, full, count, index, low):
        bits = bits_of(count)
        self.values = full.reshape((2,) * len(bits) + (full.shape[0] // count,) + full.shape[1:])
        self.count, self.index = count, index
        self.present = sorted(bits, reverse=True)
        self.left = groups_of(count, low)[::-1]

    def block(self, group, mask):
        values, present = self.values, list(self.present)
        for bit in group:
            place = present.index(bit)
            digit = ((self.index ^ mask) // bit) % 2
            values = lax.dynamic_index_in_dim(values, digit, place, keepdims=False)
            present.remove(bit)
        return values

    def send(self):
        group = self.left[0]
        self.got = [swap(self.block(group, m), self.count, m) for m in masks_of(group)]

    def merge(self):
        group = self.left.pop(0)
        total = self.block(group, 0).astype(F32)
        for got in self.got:
            total = total + got.astype(F32)
        for bit in group:
            self.present.remove(bit)
        self.values = total.astype(BF) if self.present else total

    def result(self):
        return self.values


class Total:
    def __init__(self, values, count):
        self.values, self.count = values, count
        self.left = groups_of(count, DIRECT)[::-1]

    def send(self):
        self.got = [swap(self.values, self.count, m) for m in masks_of(self.left[0])]

    def merge(self):
        self.left.pop(0)
        total = self.values + self.got[0]
        if len(self.got) > 1:
            total = total + (self.got[1] + self.got[2])
        self.values = total


def send(chains, *gates):
    chains = [c for c in chains if c.left]
    held = tie([c.values for c in chains], gates)[0]
    for c, v in zip(chains, held):
        c.values = v
    for c in chains:
        c.send()


def fence(chains, *values):
    chains = [c for c in chains if c.left]
    held, values = tie([(c.values, c.got) for c in chains], values)
    for c, (v, g) in zip(chains, held):
        c.values, c.got = v, g
        c.merge()
    held, values = tie(marks(chains), values)
    for c, v in zip(chains, held):
        c.values = v
    return values if len(values) != 1 else values[0]


def step(chains, *gates):
    send(chains, *gates)
    fence(chains)


def complete(chains):
    while any(c.left for c in chains):
        step(chains)


def join_chains(chains):
    chains[0].values = jnp.concatenate([c.values for c in chains], axis=-1)
    del chains[1:]


def marks(chains):
    return [c.values for c in chains]


def pair(values):
    return lax.ppermute(values, "tensor", [(0, 1), (1, 0)])


def norm_of(values, gain_vec, bias_vec):
    centred = values - jnp.mean(values, axis=-1, keepdims=True)
    inverse = lax.rsqrt(jnp.mean(centred * centred, axis=-1, keepdims=True) + norm_eps)
    return centred * inverse * gain_vec + bias_vec


def to_steps(steps_ref, row_first, values, col_first):
    rows, cols = values.shape
    tiles = steps_ref.shape[1]
    for j in range(cols // LANES):
        steps_ref[pl.ds(row_first, rows), col_first // LANES + j, :] = values[
            :, j * LANES : (j + 1) * LANES
        ]


def run_docs(starts_ref, low, high, one_step, make_start, finish, backward, unroll=8):
    for doc in range(NDOCS):
        d = NDOCS - 1 - doc if backward else doc
        first = jnp.minimum(jnp.maximum(starts_ref[d], low), high)
        last = jnp.minimum(jnp.maximum(starts_ref[d + 1], low), high)
        length = last - first
        groups = length // unroll
        carry = make_start(d)

        def group_body(g, carry):
            base = last - 1 - g * unroll if backward else first + g * unroll
            for i in range(unroll):
                carry = one_step(base - i if backward else base + i, carry)
            return carry

        carry = lax.fori_loop(0, groups, group_body, carry)
        done = groups * unroll

        def one_body(i, carry):
            return one_step(last - 1 - done - i if backward else first + done + i, carry)

        carry = lax.fori_loop(0, length - done, one_body, carry)
        finish(d, length, carry)


def add_up(parts):
    while len(parts) > 1:
        parts = [parts[k] + parts[k + 1] for k in range(0, len(parts), 2)]
    return parts[0]


def scan_states(starts_ref, low, high, drive_ref, decay_ref, coef_ref, y_ref, start_ref, end_ref):
    states = decay_ref.shape[0]
    zero = jnp.zeros(decay_ref.shape[1:], F32)

    def one_step(t, state):
        u = drive_ref[t]
        new = [decay_ref[n] * state[n] + u for n in range(states)]
        y_ref[t - low] = add_up([coef_ref[n] * new[n] for n in range(states)])
        return tuple(new)

    def make_start(d):
        if start_ref is None:
            return (zero,) * states
        going = starts_ref[d] < low
        return tuple(jnp.where(going, start_ref[n], zero) for n in range(states))

    def finish(d, length, carry):
        if end_ref is not None:

            @pl.when(length > 0)
            def _():
                for n in range(states):
                    end_ref[n] = carry[n]

    run_docs(starts_ref, low, high, one_step, make_start, finish, False)


def from_steps(steps_ref, out_ref):
    length, tiles, _ = steps_ref.shape
    chunk = 256

    def write(i, _):
        r = pl.multiple_of(i * chunk, chunk)
        for j in range(tiles):
            out_ref[pl.ds(r, chunk), j * LANES : (j + 1) * LANES] = steps_ref[
                pl.ds(r, chunk), j, :
            ].astype(BF)
        return 0

    lax.fori_loop(0, length // chunk, write, 0)


def both_parts(own, other, joined, at, sems):
    copies = [
        pltpu.make_async_copy(own, joined.at[at(0)], sems.at[0]),
        pltpu.make_async_copy(other, joined.at[at(1)], sems.at[1]),
    ]
    for copy in copies:
        copy.start()
    return copies


def cols_at(side, cols):
    return lambda k: (
        slice(None),
        pl.ds(pl.multiple_of((side if k == 0 else 1 - side) * cols, cols), cols),
    )


def rows_at(side, rows, *lead):
    return lambda k: lead + (
        pl.ds(pl.multiple_of((side if k == 0 else 1 - side) * rows, rows), rows),
    )


def wait_all(copies):
    for copy in copies:
        copy.wait()


def ssm_forward_kernel(
    starts_ref, side_ref, mine_ref, got_ref, mix_own_ref, mix_other_ref, gain_ref, bias_ref, decay_ref, coef_ref,
    rows_ref, normed_ref, drive_ref, out_ref, end_ref, y_ref, mix_ref, sems,
):
    length, width = rows_ref.shape
    side = side_ref[0]
    copies = both_parts(
        mine_ref.at[side], got_ref.at[side], rows_ref, rows_at(side, length // 2), sems.at[0]
    ) + both_parts(
        mix_own_ref, mix_other_ref, mix_ref, cols_at(side, width // 2), sems.at[1]
    )
    wait_all(copies)
    chunk = 256

    def project(i, _):
        r = pl.multiple_of(i * chunk, chunk)
        normed = norm_of(
            rows_ref[pl.ds(r, chunk), :].astype(F32), gain_ref[...], bias_ref[...]
        ).astype(BF)
        normed_ref[pl.ds(r, chunk), :] = normed
        for c in range(0, width, 256):
            to_steps(drive_ref, r, dot_plain(normed, mix_ref[:, c : c + 256]), c)
        return 0

    lax.fori_loop(0, length // chunk, project, 0)
    scan_states(
        starts_ref, 0, length // 2, drive_ref, decay_ref, coef_ref, y_ref, None, end_ref
    )
    from_steps(y_ref, out_ref)


def ssm_rest_kernel(
    starts_ref, side_ref, mine_ref, got_ref, drive_ref, decay_ref, coef_ref, start_ref, first_ref,
    out_ref, cot_ref, y_ref, sems,
):
    length = drive_ref.shape[0]
    half = length // 2
    side = side_ref[0]
    copies = both_parts(
        mine_ref.at[side], got_ref.at[side], cot_ref, rows_at(side, half, 0), sems.at[0]
    ) + both_parts(
        mine_ref.at[1 - side], got_ref.at[1 - side], cot_ref, rows_at(side, half, 1), sems.at[1]
    )
    scan_states(
        starts_ref, half, length, drive_ref, decay_ref, coef_ref, y_ref, start_ref, None
    )
    out_ref[:half, :] = first_ref[...]
    from_steps(y_ref, out_ref.at[half:])
    wait_all(copies)


SMALL = pl.BlockSpec(memory_space=pltpu.SMEM)
WHOLE = pl.BlockSpec(memory_space=pltpu.VMEM)
ANYWHERE = pl.BlockSpec(memory_space=pl.ANY)
COPIES = pltpu.SemaphoreType.DMA((2, 2))


def ssm_forward(starts, side, mine, got, mix_own, mix_other, gain_vec, bias_vec, decay, coef):
    length, width = 2 * mine.shape[1], mine.shape[2]
    tiles = width // LANES
    return pl.pallas_call(
        ssm_forward_kernel,
        out_shape=(
            jax.ShapeDtypeStruct((length, width), BF),
            jax.ShapeDtypeStruct((length, width), BF),
            jax.ShapeDtypeStruct((length, tiles, LANES), F32),
            jax.ShapeDtypeStruct((length // 2, width), BF),
            jax.ShapeDtypeStruct(decay.shape, F32),
        ),
        in_specs=[SMALL] * 2 + [ANYWHERE] * 4 + [WHOLE] * 4,
        out_specs=(WHOLE,) * 5,
        scratch_shapes=[
            pltpu.VMEM((length // 2, tiles, LANES), F32),
            pltpu.VMEM((width, width), BF),
            COPIES,
        ],
        compiler_params=pltpu.CompilerParams(vmem_limit_bytes=VMEM),
        cost_estimate=pl.CostEstimate(
            flops=12 * length * width * width,
            bytes_accessed=16 * length * width,
            transcendentals=0,
        ),
        name="ssm_forward",
    )(starts, side, mine, got, mix_own, mix_other, gain_vec, bias_vec, decay, coef)


def ssm_rest(starts, side, mine, got, drive, decay, coef, start, first):
    length, tiles, _ = drive.shape
    width = tiles * LANES
    return pl.pallas_call(
        ssm_rest_kernel,
        out_shape=(
            jax.ShapeDtypeStruct((length, width), BF),
            jax.ShapeDtypeStruct((2, length, width), BF),
        ),
        in_specs=[SMALL] * 2 + [ANYWHERE] * 2 + [WHOLE] * 5,
        out_specs=(WHOLE, WHOLE),
        scratch_shapes=[pltpu.VMEM((length // 2, tiles, LANES), F32), COPIES],
        compiler_params=pltpu.CompilerParams(vmem_limit_bytes=VMEM),
        cost_estimate=pl.CostEstimate(
            flops=10 * length * width * width,
            bytes_accessed=16 * length * width,
            transcendentals=0,
        ),
        name="ssm_rest",
    )(starts, side, mine, got, drive, decay, coef, start, first)


def project_kernel(
    side_ref, normed_ref, ssm_ref, left_own_ref, left_other_ref, right_own_ref, right_other_ref,
    query_ref, key_ref, value_ref, weights_ref, sems,
):
    width = normed_ref.shape[1]
    cols = width // 2
    at = cols_at(side_ref[0], cols)
    sources = (
        (left_own_ref, left_other_ref, 0),
        (left_own_ref, left_other_ref, cols),
        (right_own_ref, right_other_ref, 0),
    )
    copies = [
        both_parts(
            own.at[:, c : c + cols], other.at[:, c : c + cols], weights_ref.at[k], at, sems.at[k]
        )
        for k, (own, other, c) in enumerate(sources)
    ]
    for k, (rows_ref, out_ref) in enumerate(
        ((normed_ref, query_ref), (ssm_ref, key_ref), (ssm_ref, value_ref))
    ):
        wait_all(copies[k])
        for c in range(0, width, cols):
            out_ref[:, c : c + cols] = dot_plain(
                rows_ref[...], weights_ref[k, :, c : c + cols]
            ).astype(BF)


def project(side, normed, ssm_out, left, right):
    length, width = normed.shape
    return pl.pallas_call(
        project_kernel,
        out_shape=(jax.ShapeDtypeStruct((length, width), BF),) * 3,
        in_specs=[SMALL] + [WHOLE] * 2 + [ANYWHERE] * 4,
        out_specs=(WHOLE,) * 3,
        scratch_shapes=[pltpu.VMEM((3, width, width), BF), pltpu.SemaphoreType.DMA((3, 2))],
        compiler_params=pltpu.CompilerParams(vmem_limit_bytes=VMEM),
        cost_estimate=pl.CostEstimate(
            flops=6 * length * width * width, bytes_accessed=16 * length * width, transcendentals=0
        ),
        name="project",
    )(side, normed, ssm_out, *left, *right)


def adjoint_states(starts_ref, low, drive_ref, g_ref, decay_ref, coef_ref, gm_ref, sum_ref, dsum_ref, given_ref):
    length = g_ref.shape[0]
    part = sum_ref.shape[0]
    zero = jnp.zeros(decay_ref.shape[1:], F32)

    def one_step(t, carry):
        mu, rho, total, dtotal = carry
        u = drive_ref[t]
        g = g_ref[t]
        new_mu, new_rho, new_total, new_dtotal, parts = [], [], [], [], []
        for n in range(part):
            a = decay_ref[low + n]
            r = a * rho[n] + mu[n]
            m = a * mu[n] + g
            new_mu.append(m)
            new_rho.append(r)
            new_total.append(total[n] + u * m)
            new_dtotal.append(dtotal[n] + u * r)
            parts.append(coef_ref[low + n] * m)
        gm = add_up(parts)
        gm_ref[t] = gm if given_ref is None else gm + given_ref[t]
        return tuple(new_mu), tuple(new_rho), tuple(new_total), tuple(new_dtotal)

    for n in range(part):
        sum_ref[n] = zero
        dsum_ref[n] = zero

    def make_start(d):
        zeros = (zero,) * part
        return zeros, zeros, zeros, zeros

    def finish(d, count, carry):
        for n in range(part):
            sum_ref[n] = sum_ref[n] + carry[2][n]
            dsum_ref[n] = dsum_ref[n] + carry[3][n]

    run_docs(starts_ref, 0, length, one_step, make_start, finish, True)


def ssm_backward_kernel(
    starts_ref, side_ref, gkey_ref, gvalue_ref, left_own_ref, left_other_ref, right_own_ref, right_other_ref,
    drive_ref, decay_ref, coef_ref, g_ref, gm_ref, sum_ref, dsum_ref, wkey_ref, wvalue_ref, sems,
):
    length, width = gkey_ref.shape
    cols = width // 2
    at = cols_at(side_ref[0], cols)
    copies = both_parts(
        left_own_ref.at[:, cols:], left_other_ref.at[:, cols:], wkey_ref, at, sems.at[0]
    ) + both_parts(
        right_own_ref.at[:, :cols], right_other_ref.at[:, :cols], wvalue_ref, at, sems.at[1]
    )
    wait_all(copies)
    chunk = 256

    def project(i, _):
        r = pl.multiple_of(i * chunk, chunk)
        gkey = gkey_ref[pl.ds(r, chunk), :]
        gvalue = gvalue_ref[pl.ds(r, chunk), :]
        for c in range(0, width, 256):
            to_steps(
                g_ref,
                r,
                dot_last(gkey, wkey_ref[c : c + 256, :])
                + dot_last(gvalue, wvalue_ref[c : c + 256, :]),
                c,
            )
        return 0

    lax.fori_loop(0, length // chunk, project, 0)
    adjoint_states(
        starts_ref, 0, drive_ref, g_ref, decay_ref, coef_ref, gm_ref, sum_ref, dsum_ref, None
    )


def ssm_backward_rest_kernel(
    starts_ref, g_ref, given_ref, drive_ref, decay_ref, coef_ref,
    gmixed_ref, sum_ref, dsum_ref, gm_ref,
):
    adjoint_states(
        starts_ref, decay_ref.shape[0] // 2, drive_ref, g_ref, decay_ref, coef_ref, gm_ref,
        sum_ref, dsum_ref, given_ref,
    )
    from_steps(gm_ref, gmixed_ref)


def ssm_backward(starts, side, gkey, gvalue, left, right, drive, decay, coef):
    length, width = gkey.shape
    tiles = width // LANES
    vm = pl.BlockSpec(memory_space=pltpu.VMEM)
    half = (decay.shape[0] // 2,) + decay.shape[1:]
    return pl.pallas_call(
        ssm_backward_kernel,
        out_shape=(
            jax.ShapeDtypeStruct((length, tiles, LANES), F32),
            jax.ShapeDtypeStruct((length, tiles, LANES), F32),
            jax.ShapeDtypeStruct(half, F32),
            jax.ShapeDtypeStruct(half, F32),
        ),
        in_specs=[SMALL] * 2 + [vm] * 2 + [ANYWHERE] * 4 + [vm] * 3,
        out_specs=(vm,) * 4,
        scratch_shapes=[pltpu.VMEM((width, width), BF)] * 2 + [COPIES],
        compiler_params=pltpu.CompilerParams(vmem_limit_bytes=VMEM),
        cost_estimate=pl.CostEstimate(
            flops=20 * length * width * width,
            bytes_accessed=20 * length * width,
            transcendentals=0,
        ),
        name="ssm_backward",
    )(starts, side, gkey, gvalue, *left, *right, drive, decay, coef)


def ssm_backward_rest(starts, g, given, drive, decay, coef):
    length, tiles, _ = drive.shape
    width = tiles * LANES
    vm = pl.BlockSpec(memory_space=pltpu.VMEM)
    half = (decay.shape[0] // 2,) + decay.shape[1:]
    return pl.pallas_call(
        ssm_backward_rest_kernel,
        out_shape=(
            jax.ShapeDtypeStruct((length, width), BF),
            jax.ShapeDtypeStruct(half, F32),
            jax.ShapeDtypeStruct(half, F32),
        ),
        in_specs=[pl.BlockSpec(memory_space=pltpu.SMEM)] + [vm] * 5,
        out_specs=(vm,) * 3,
        scratch_shapes=[pltpu.VMEM((length, tiles, LANES), F32)],
        compiler_params=pltpu.CompilerParams(vmem_limit_bytes=VMEM),
        cost_estimate=pl.CostEstimate(
            flops=20 * length * width * width,
            bytes_accessed=20 * length * width,
            transcendentals=0,
        ),
        name="ssm_backward_rest",
    )(starts, g, given, drive, decay, coef)


def attention_tiles(length):
    tiles = []
    for first in range(0, length, QTILE):
        block_first = first // BLOCK * BLOCK
        key_first = max(0, block_first - CTX)
        tiles.append((first, key_first, first + QTILE - key_first))
    return tiles


def fill_bias(seg_col_ref, seg_row_ref, bias_ref, tiles):
    at = 0
    for first, key_first, count in tiles:
        same = seg_col_ref[first : first + QTILE, :] == seg_row_ref[:, key_first : key_first + count]
        query_pos = lax.broadcasted_iota(jnp.int32, (QTILE, count), 0) + first
        key_pos = lax.broadcasted_iota(jnp.int32, (QTILE, count), 1) + key_first
        bias_ref[:, at : at + count] = jnp.where(
            same & (key_pos <= query_pos), 0.0, masked_score
        ).astype(F32)
        at += count


EXP_SCALE = HEAD_DIM ** (-0.5) * math.log2(math.e)


def attention_jobs(length):
    jobs = []
    for h in range(HEADS_EACH):
        at = 0
        for first, key_first, count in attention_tiles(length):
            jobs.append(
                (
                    h,
                    slice(h * HEAD_DIM, (h + 1) * HEAD_DIM),
                    slice(first, first + QTILE),
                    slice(key_first, key_first + count),
                    slice(at, at + count),
                )
            )
            at += count
    return jobs


def attention_forward_kernel(
    seg_col_ref, seg_row_ref, query_ref, key_ref, value_ref, out_ref, lse_ref, bias_ref, value_one_ref
):
    length = query_ref.shape[0]

    @pl.when(pl.program_id(0) == 0)
    def _():
        fill_bias(seg_col_ref, seg_row_ref, bias_ref, attention_tiles(length))
        for h in range(HEADS_EACH):
            value_one_ref[h, :, HEAD_DIM:] = jnp.ones((length, HEAD_DIM), BF)

    for h in range(HEADS_EACH):
        value_one_ref[h, :, :HEAD_DIM] = value_ref[:, h * HEAD_DIM : (h + 1) * HEAD_DIM]
    jobs = attention_jobs(length)

    def scores_of(job):
        _, lanes, rows, keys, _ = job
        return dot_last(query_ref[rows, lanes], key_ref[keys, lanes])

    ahead = scores_of(jobs[0])
    for k, (h, lanes, rows, keys, mask) in enumerate(jobs):
        scores = ahead
        if k + 1 < len(jobs):
            ahead = scores_of(jobs[k + 1])
        scores = scores * EXP_SCALE + bias_ref[:, mask]
        top = jnp.max(scores, axis=-1, keepdims=True)
        raised = jnp.exp2(scores - top).astype(BF)
        both = dot_plain(raised, value_one_ref[h, keys, :])
        total = both[:, HEAD_DIM:]
        out_ref[rows, lanes] = (both[:, :HEAD_DIM] / total).astype(BF)
        lse_ref[h, rows, :] = top + jnp.log2(total[:, :1])


def attention_forward(seg_col, seg_row, query, key, value):
    length, width = query.shape
    heads = width // HEAD_DIM
    tiles = attention_tiles(length)
    cols = sum(t[2] for t in tiles)
    head = pl.BlockSpec((length, HEADS_EACH * HEAD_DIM), lambda h: (0, h))
    whole = lambda shape: pl.BlockSpec(shape, lambda h: (0, 0))
    return pl.pallas_call(
        attention_forward_kernel,
        grid=(heads // HEADS_EACH,),
        out_shape=(
            jax.ShapeDtypeStruct((length, width), BF),
            jax.ShapeDtypeStruct((heads, length, 1), F32),
        ),
        in_specs=[whole((length, 1)), whole((1, length)), head, head, head],
        out_specs=(head, pl.BlockSpec((HEADS_EACH, length, 1), lambda h: (h, 0, 0))),
        scratch_shapes=[
            pltpu.VMEM((QTILE, cols), F32),
            pltpu.VMEM((HEADS_EACH, length, 2 * HEAD_DIM), BF),
        ],
        compiler_params=params(),
        cost_estimate=pl.CostEstimate(
            flops=4 * QTILE * cols * width,
            bytes_accessed=8 * length * width,
            transcendentals=QTILE * cols * heads,
        ),
        name="attention_forward",
    )(seg_col, seg_row, query, key, value)


def attention_backward_kernel(
    seg_col_ref, seg_row_ref, query_ref, key_ref, value_ref, lse_ref, gout_ref,
    gquery_ref, gkey_ref, gvalue_ref, bias_ref, gk_ref, gv_ref,
):
    length = query_ref.shape[0]
    scale = HEAD_DIM ** (-0.5)

    @pl.when(pl.program_id(0) == 0)
    def _():
        fill_bias(seg_col_ref, seg_row_ref, bias_ref, attention_tiles(length))

    gk_ref[...] = jnp.zeros_like(gk_ref)
    gv_ref[...] = jnp.zeros_like(gv_ref)
    jobs = attention_jobs(length)

    def scores_of(job):
        _, lanes, rows, keys, _ = job
        return (
            dot_last(query_ref[rows, lanes], key_ref[keys, lanes]),
            dot_last(gout_ref[rows, lanes], value_ref[keys, lanes]),
        )

    ahead = scores_of(jobs[0])
    for k, (h, lanes, rows, keys, mask) in enumerate(jobs):
        scores, gprobs = ahead
        if k + 1 < len(jobs):
            ahead = scores_of(jobs[k + 1])
        gout = gout_ref[rows, lanes]
        probs = jnp.exp2(scores * EXP_SCALE + bias_ref[:, mask] - lse_ref[h, rows, :])
        gv_ref[keys, lanes] = gv_ref[keys, lanes] + dot_first(probs.astype(BF), gout)
        inner = jnp.sum(probs * gprobs, axis=-1, keepdims=True)
        gscores = (probs * (gprobs - inner)).astype(BF)
        gquery_ref[rows, lanes] = (dot_plain(gscores, key_ref[keys, lanes]) * scale).astype(BF)
        gk_ref[keys, lanes] = gk_ref[keys, lanes] + dot_first(gscores, query_ref[rows, lanes])
    gkey_ref[...] = (gk_ref[...] * scale).astype(BF)
    gvalue_ref[...] = gv_ref[...].astype(BF)


def attention_backward(seg_col, seg_row, query, key, value, lse, gout):
    length, width = query.shape
    heads = width // HEAD_DIM
    tiles = attention_tiles(length)
    cols = sum(t[2] for t in tiles)
    head = pl.BlockSpec((length, HEADS_EACH * HEAD_DIM), lambda h: (0, h))
    whole = lambda shape: pl.BlockSpec(shape, lambda h: (0, 0))
    return pl.pallas_call(
        attention_backward_kernel,
        grid=(heads // HEADS_EACH,),
        out_shape=(jax.ShapeDtypeStruct((length, width), BF),) * 3,
        in_specs=[whole((length, 1)), whole((1, length)), head, head, head]
        + [pl.BlockSpec((HEADS_EACH, length, 1), lambda h: (h, 0, 0)), head],
        out_specs=(head,) * 3,
        scratch_shapes=[
            pltpu.VMEM((QTILE, cols), F32),
            pltpu.VMEM((length, HEADS_EACH * HEAD_DIM), F32),
            pltpu.VMEM((length, HEADS_EACH * HEAD_DIM), F32),
        ],
        compiler_params=params(),
        cost_estimate=pl.CostEstimate(
            flops=10 * QTILE * cols * width,
            bytes_accessed=14 * length * width,
            transcendentals=QTILE * cols * heads,
        ),
        name="attention_backward",
    )(seg_col, seg_row, query, key, value, lse, gout)


def norm_backward(grad, values, gain_vec):
    centred = values - jnp.mean(values, axis=-1, keepdims=True)
    inverse = lax.rsqrt(jnp.mean(centred * centred, axis=-1, keepdims=True) + norm_eps)
    xhat = centred * inverse
    dxhat = grad * gain_vec
    back = (
        dxhat
        - jnp.mean(dxhat, axis=-1, keepdims=True)
        - xhat * jnp.mean(dxhat * xhat, axis=-1, keepdims=True)
    ) * inverse
    return back, jnp.sum(grad * xhat, axis=0, keepdims=True), jnp.sum(grad, axis=0, keepdims=True)


def gelu_parts(values):
    below = 0.5 + 0.5 * lax.erf(values * (2.0**-0.5))
    bell = jnp.exp2((-0.5 * math.log2(math.e)) * (values * values))
    return values * below, below + values * (bell * ((2.0 * math.pi) ** -0.5))


FTILE = 512


def feed_forward_kernel(part, *refs):
    ins, refs = refs[: 5 + 4 * (part > 0)], refs[5 + 4 * (part > 0) :]
    own_ref, other_ref, cot_ref, up_in_ref, down_in_ref = ins[:5]
    outs, grads, refs = refs[:4], refs[4:6], refs[6:]
    normed_ref, cots_ref, up_ref, down_ref, hidden_ref, gpre_ref, sums_ref, total_ref = refs[:8]
    row_sems, weight_sems, out_sems, grad_sems = refs[8:12]
    length, width = own_ref.shape
    units = up_ref.shape[1]
    tile = FTILE
    per = length // tile
    count = 2 * per

    def tile_of(i):
        return pl.ds(pl.multiple_of(i * tile, tile), tile)

    weights = [
        pltpu.make_async_copy(up_in_ref, up_ref, weight_sems.at[0]),
        pltpu.make_async_copy(down_in_ref, down_ref, weight_sems.at[1]),
    ]
    for copy in weights:
        copy.start()
    for i in range(count):
        rows = tile_of(i % per)
        source = (own_ref, other_ref)[i // per]
        pltpu.make_async_copy(source.at[rows], normed_ref.at[tile_of(i)], row_sems.at[0, i]).start()
        pltpu.make_async_copy(
            cot_ref.at[i // per, rows], cots_ref.at[tile_of(i)], row_sems.at[1, i]
        ).start()
    if part:
        earlier = [
            pltpu.make_async_copy(ins[5 + k], total_ref.at[k], out_sems.at[k, count])
            for k in range(4)
        ]
        for copy in earlier:
            copy.start()
    wait_all(weights)

    def one(i, _):
        rows = tile_of(i)
        for k, ref in enumerate((normed_ref, cots_ref)):
            pltpu.make_async_copy(ref.at[rows], ref.at[rows], row_sems.at[k, i]).wait()
        for n in range(0, units, tile):
            pre = dot_plain(normed_ref[rows, :], up_ref[:, n : n + tile])
            ghidden = dot_plain(cots_ref[rows, :], down_ref[:, n : n + tile])
            hidden, slope = gelu_parts(pre)
            hidden_ref[rows, n : n + tile] = hidden.astype(BF)
            gpre_ref[rows, n : n + tile] = (ghidden * slope).astype(BF)
        return 0

    lax.fori_loop(0, count, one, 0)

    grad_copies = []
    for k, (first_ref, held_ref) in enumerate(((normed_ref, gpre_ref), (cots_ref, hidden_ref))):

        def three(i, _, k=k, first_ref=first_ref, held_ref=held_ref):
            cols = tile_of(i)
            sums_ref[k, cols, :] = dot_first(first_ref[:, cols], held_ref[...]).astype(BF)
            return 0

        lax.fori_loop(0, width // tile, three, 0)
        copy = pltpu.make_async_copy(
            sums_ref.at[k], grads[k], grad_sems.at[k]
        )
        copy.start()
        grad_copies.append(copy)

    if part:
        wait_all(earlier)
    out_copies = []
    for i in range(count):
        s, rows = i // per, slice(i % per * tile, (i % per + 1) * tile)
        held = slice(i * tile, (i + 1) * tile)
        for k, (held_ref, weight_ref) in enumerate(((hidden_ref, down_ref), (gpre_ref, up_ref))):
            total = dot_last(held_ref[held, :], weight_ref[...])
            if part:
                total = total + total_ref[2 * k + s, rows, :].astype(F32)
            total_ref[2 * k + s, rows, :] = total.astype(BF)
            copy = pltpu.make_async_copy(
                total_ref.at[2 * k + s, rows], outs[2 * k + s].at[rows], out_sems.at[k, i]
            )
            copy.start()
            out_copies.append(copy)
    wait_all(grad_copies + out_copies)


def feed_forward(part, own, other, cot, up, down, earlier):
    length, width = own.shape
    units = up.shape[1]
    count = 2 * length // FTILE
    dma = pltpu.SemaphoreType.DMA
    return pl.pallas_call(
        functools.partial(feed_forward_kernel, part),
        out_shape=(jax.ShapeDtypeStruct((length, width), BF),) * 4
        + (jax.ShapeDtypeStruct((width, units), BF),) * 2,
        in_specs=[ANYWHERE] * (9 if part else 5),
        out_specs=(ANYWHERE,) * 6,
        scratch_shapes=[pltpu.VMEM((2 * length, width), BF)] * 2
        + [pltpu.VMEM((width, units), BF)] * 2
        + [pltpu.VMEM((2 * length, units), BF)] * 2
        + [pltpu.VMEM((2, width, units), BF), pltpu.VMEM((4, length, width), BF)]
        + [dma((2, count)), dma((2,)), dma((4, count + 1)), dma((2,))],
        compiler_params=pltpu.CompilerParams(vmem_limit_bytes=VMEM),
        cost_estimate=pl.CostEstimate(
            flops=28 * length * width * units,
            bytes_accessed=48 * length * width,
            transcendentals=4 * length * units,
        ),
        name="feed_forward",
    )(own, other, cot, up, down, *earlier)


def at_first(joins, sems, side):
    @pl.when(pl.program_id(0) == 0)
    def _():
        copies = []
        for k, (own, other, joined) in enumerate(joins):
            copies += both_parts(own, other, joined, cols_at(side, joined.shape[1] // 2), sems.at[k])
        wait_all(copies)


ROWS = 256


def row_spec(width, lead=None):
    if lead is None:
        return pl.BlockSpec((ROWS, width), lambda i: (i, 0))
    return pl.BlockSpec((None, ROWS, width), lambda i: (lead, i, 0))


def fixed(*shape):
    return pl.BlockSpec(shape, lambda i: (0,) * len(shape))


def middle_kernel(
    side_ref, attended_ref, own_ref, other_ref, rows_ref, gain_ref, bias_ref, middle_ref, normed_ref, out_ref, sems
):
    cols = out_ref.shape[1] // 2
    at_first([(own_ref.at[:, cols:], other_ref.at[:, cols:], out_ref)], sems, side_ref[0])
    middle = rows_ref[...].astype(F32) + dot_last(attended_ref[...], out_ref[...])
    middle_ref[...] = middle
    normed_ref[...] = norm_of(middle, gain_ref[...], bias_ref[...]).astype(BF)


def middle_of(side, attended, right, rows, gain_vec, bias_vec):
    length, width = rows.shape
    row = row_spec(width)
    return pl.pallas_call(
        middle_kernel,
        grid=(length // ROWS,),
        out_shape=(
            jax.ShapeDtypeStruct((length, width), F32),
            jax.ShapeDtypeStruct((length, width), BF),
        ),
        in_specs=[SMALL, row, ANYWHERE, ANYWHERE, row, fixed(1, width), fixed(1, width)],
        out_specs=(row, row),
        scratch_shapes=[pltpu.VMEM((width, width), BF), COPIES],
        compiler_params=params(),
        cost_estimate=pl.CostEstimate(
            flops=2 * length * width * width, bytes_accessed=12 * length * width, transcendentals=0
        ),
        name="middle",
    )(side, attended, *right, rows, gain_vec, bias_vec)


def norm_two_kernel(
    side_ref, mine_ref, theirs_ref, middle_ref, cot_ref, gain_ref, own_ref, other_ref,
    gmiddle_ref, gbranch_ref, gattended_ref, sums_ref, out_ref, sems,
):
    cols = out_ref.shape[1] // 2
    at_first([(own_ref.at[:, cols:], other_ref.at[:, cols:], out_ref)], sems, side_ref[0])
    grad = mine_ref[...].astype(F32) + theirs_ref[...].astype(F32)
    back, gain_sum, bias_sum = norm_backward(grad, middle_ref[...], gain_ref[...])
    gmiddle = cot_ref[...].astype(F32) + back
    gmiddle_ref[...] = gmiddle
    gbranch = gmiddle.astype(BF)
    gbranch_ref[...] = gbranch
    gattended_ref[...] = dot_plain(gbranch, out_ref[...]).astype(BF)
    add_sums(sums_ref, gain_sum, bias_sum)


def add_sums(sums_ref, gain_sum, bias_sum):
    @pl.when(pl.program_id(0) == 0)
    def _():
        sums_ref[...] = jnp.zeros_like(sums_ref)

    sums_ref[0:1, :] = sums_ref[0:1, :] + gain_sum
    sums_ref[1:2, :] = sums_ref[1:2, :] + bias_sum


def norm_two_back(side, mine, theirs, middle, cot, gain_vec, right):
    length, width = middle.shape
    row = row_spec(width)
    return pl.pallas_call(
        norm_two_kernel,
        grid=(length // ROWS,),
        out_shape=(
            jax.ShapeDtypeStruct((length, width), F32),
            jax.ShapeDtypeStruct((length, width), BF),
            jax.ShapeDtypeStruct((length, width), BF),
            jax.ShapeDtypeStruct((2, width), F32),
        ),
        in_specs=[SMALL, row, row, row, row_spec(width, 0), fixed(1, width), ANYWHERE, ANYWHERE],
        out_specs=(row, row, row, fixed(2, width)),
        scratch_shapes=[pltpu.VMEM((width, width), BF), COPIES],
        compiler_params=params(),
        cost_estimate=pl.CostEstimate(
            flops=2 * length * width * width, bytes_accessed=24 * length * width, transcendentals=0
        ),
        name="norm_two_back",
    )(side, mine, theirs, middle, cot, gain_vec, *right)


def norm_one_kernel(
    side_ref, gquery_ref, gmixed_ref, rows_ref, gmiddle_ref, gain_ref,
    left_own_ref, left_other_ref, mix_own_ref, mix_other_ref, grad_ref, sums_ref, query_ref, mix_ref, sems,
):
    cols = query_ref.shape[1] // 2
    at_first(
        [
            (left_own_ref.at[:, :cols], left_other_ref.at[:, :cols], query_ref),
            (mix_own_ref, mix_other_ref, mix_ref),
        ],
        sems,
        side_ref[0],
    )
    grad = dot_last(gquery_ref[...], query_ref[...]) + dot_last(gmixed_ref[...], mix_ref[...])
    back, gain_sum, bias_sum = norm_backward(grad, rows_ref[...].astype(F32), gain_ref[...])
    grad_ref[...] = gmiddle_ref[...] + back
    add_sums(sums_ref, gain_sum, bias_sum)


def norm_one_back(side, gquery, gmixed, rows, gmiddle, gain_vec, left, mix, for_partner):
    length, width = rows.shape
    half = length // 2
    steps = half // ROWS

    def place(side):
        return 1 - side[0] if for_partner else side[0]

    row = pl.BlockSpec((ROWS, width), lambda i, side: (place(side) * steps + i, 0))
    whole = lambda *shape: pl.BlockSpec(shape, lambda i, side: (0,) * len(shape))
    if for_partner:
        out = jax.ShapeDtypeStruct((half, width), F32)
        out_spec = pl.BlockSpec((ROWS, width), lambda i, side: (i, 0))
    else:
        out = jax.ShapeDtypeStruct((2, half, width), F32)
        out_spec = pl.BlockSpec((None, ROWS, width), lambda i, side: (side[0], i, 0))
    return pl.pallas_call(
        norm_one_kernel,
        grid_spec=pltpu.PrefetchScalarGridSpec(
            num_scalar_prefetch=1,
            grid=(steps,),
            in_specs=[row] * 4 + [whole(1, width)] + [ANYWHERE] * 4,
            out_specs=(out_spec, whole(2, width)),
            scratch_shapes=[pltpu.VMEM((width, width), BF)] * 2 + [COPIES],
        ),
        out_shape=(out, jax.ShapeDtypeStruct((2, width), F32)),
        compiler_params=params(),
        cost_estimate=pl.CostEstimate(
            flops=4 * half * width * width, bytes_accessed=20 * half * width, transcendentals=0
        ),
        name="norm_one_back",
    )(side, gquery, gmixed, rows, gmiddle, gain_vec, *left, *mix)


def put_kernel(side_ref, got_ref, given_ref, out_ref):
    out_ref[...] = got_ref[...]


def put(side, got, given):
    half, width = got.shape
    return pl.pallas_call(
        put_kernel,
        grid_spec=pltpu.PrefetchScalarGridSpec(
            num_scalar_prefetch=1,
            grid=(half // ROWS,),
            in_specs=[pl.BlockSpec((ROWS, width), lambda i, side: (i, 0)), ANYWHERE],
            out_specs=pl.BlockSpec((None, ROWS, width), lambda i, side: (1 - side[0], i, 0)),
        ),
        out_shape=jax.ShapeDtypeStruct(given.shape, given.dtype),
        input_output_aliases={2: 0},
        compiler_params=params(),
        name="put",
    )(side, got, given)


def layer_out_kernel(side_ref, middle_ref, own_ref, other_ref, sum_ref, theirs_ref, out_ref):
    side = side_ref[0]
    out_ref[side] = (
        middle_ref[...] + own_ref[...].astype(F32) + theirs_ref[...].astype(F32)
    )
    out_ref[1 - side] = sum_ref[...] + other_ref[...].astype(F32)


def layer_out_of(side, middle, own, other, partner_sum, partner_other):
    length, width = middle.shape
    half = length // 2
    steps = half // ROWS
    mine = pl.BlockSpec((ROWS, width), lambda i, side: (side[0] * steps + i, 0))
    row = pl.BlockSpec((ROWS, width), lambda i, side: (i, 0))
    return pl.pallas_call(
        layer_out_kernel,
        grid_spec=pltpu.PrefetchScalarGridSpec(
            num_scalar_prefetch=1,
            grid=(steps,),
            in_specs=[mine] * 3 + [row] * 2,
            out_specs=pl.BlockSpec((2, ROWS, width), lambda i, side: (0, i, 0)),
        ),
        out_shape=jax.ShapeDtypeStruct((2, half, width), F32),
        compiler_params=params(),
        cost_estimate=pl.CostEstimate(
            flops=4 * half * width, bytes_accessed=24 * half * width, transcendentals=0
        ),
        name="layer_out",
    )(side, middle, own, other, partner_sum, partner_other)


def weight_grads_kernel(count, side_ref, *refs):
    lefts, rights = refs[: len(refs) - 2 - count], refs[len(refs) - 2 - count : -2]
    theirs_ref, mine_ref = refs[-2:]
    cols = rights[0].shape[1] // 2
    side = side_ref[0]
    for k in range(count):
        for ref, at in ((theirs_ref, 1 - side), (mine_ref, side)):
            part = rights[k][:, pl.ds(pl.multiple_of(at * cols, cols), cols)]
            ref[:, k * cols : (k + 1) * cols] = dot_first(
                lefts[k % len(lefts)][...], part
            ).astype(BF)


def weight_grads(side, lefts, rights):
    count = len(rights)
    length, width = lefts[0].shape
    cols = width // 2
    vm = pl.BlockSpec(memory_space=pltpu.VMEM)
    return pl.pallas_call(
        functools.partial(weight_grads_kernel, count),
        out_shape=(jax.ShapeDtypeStruct((width, count * cols), BF),) * 2,
        in_specs=[SMALL] + [vm] * (len(lefts) + count),
        out_specs=(vm,) * 2,
        compiler_params=pltpu.CompilerParams(vmem_limit_bytes=VMEM),
        cost_estimate=pl.CostEstimate(
            flops=2 * count * length * width * width,
            bytes_accessed=6 * count * length * width,
            transcendentals=0,
        ),
        name="weight_grads",
    )(side, *lefts, *rights)


def per_device(
    count,
    layer_in,
    segment_ids,
    w_mix_in,
    w_query,
    w_key,
    w_value,
    w_attn_out,
    w_up,
    w_down,
    norm1_gain,
    norm1_bias,
    norm2_gain,
    norm2_bias,
    ssm_decay,
    ssm_inject,
    ssm_readout,
    out_grad,
):
    index = lax.axis_index("dp")
    side = lax.axis_index("tensor")
    at_side = jnp.reshape(side, (1,))
    half = layer_in.shape[2]
    width = layer_in.shape[3]
    tiles = width // LANES
    states = ssm_decay.shape[0]
    cols = w_query.shape[1]
    parts = 2
    units = w_up.shape[1] // parts
    shard_rows = w_mix_in.shape[0]

    norms = jnp.concatenate([norm1_gain, norm1_bias, norm2_gain, norm2_bias])
    norms = jnp.pad(norms[None], ((0, 7), (0, cols - norms.shape[0])))
    mix = [Gather(jnp.concatenate([w_mix_in, norms], axis=0), count, index, DIRECT)]
    send(mix)
    mine_in, got_in = layer_in[:, 0], pair(layer_in[:, 0])
    coefs = jnp.stack([ssm_decay, ssm_inject, ssm_readout])
    coefs_got = pair(coefs)
    fence(mix)
    attn = [
        Gather(
            jnp.concatenate([w_query, w_key, w_value, w_attn_out.T], axis=1), count, index, X_FIRST
        )
    ]
    turned_down = w_down.T
    ffn = [
        [
            Gather(
                jnp.concatenate(
                    [
                        w_up[:, i * units : (i + 1) * units],
                        turned_down[:, i * units : (i + 1) * units],
                    ],
                    axis=1,
                ),
                count,
                index,
                X_FIRST,
            )
        ]
        for i in range(parts)
    ]
    both_ways = (X_FIRST, Y_FIRST)
    while len(mix[0].left) > 1:
        step(mix)
    send(mix + attn)
    fence(mix + attn)
    mix_all = mix[0].result().reshape(count, shard_rows + 8, cols)
    mix_half = mix_all[:, :shard_rows].reshape(width, cols)
    mix_both = (mix_half, pair(mix_half))
    norms_all = mix_all[:, shard_rows, : 4 * shard_rows].reshape(count, 4, shard_rows)
    norms_all = norms_all.astype(F32).transpose(1, 0, 2).reshape(4, width)
    gain_one, bias_one, gain_two, bias_two = (norms_all[i : i + 1] for i in range(4))
    coefs = jnp.where(
        side == 0,
        jnp.concatenate([coefs, coefs_got], axis=2),
        jnp.concatenate([coefs_got, coefs], axis=2),
    )
    decay, inject, readout = coefs.reshape(3, states, tiles, LANES)
    coef = inject * readout
    segments = lax.dynamic_index_in_dim(segment_ids[:, 0], side, 0, keepdims=False)
    starts = jnp.sum(
        (segments[None, :] < jnp.arange(16, dtype=jnp.int32)[:, None]).astype(jnp.int32), axis=1
    )
    seg_col, seg_row = segments[:, None], segments[None, :]
    while len(attn[0].left) > 2:
        step(attn)
    attn = attn[0].split(both_ways)
    send(attn)

    rows, normed, drive, ssm_first, state_mid = ssm_forward(
        starts, at_side, mine_in, got_in, *mix_both, gain_one, bias_one, decay, coef
    )
    state_mid = fence(attn, state_mid)
    send(attn + ffn[0])
    mine_cot, got_cot = out_grad[:, 0], pair(tie(out_grad, state_mid)[0][:, 0])
    ssm_out, cot = ssm_rest(
        starts, at_side, mine_cot, got_cot, drive, decay, coef, state_mid, ssm_first
    )
    ssm_out = fence(attn + ffn[0], ssm_out)
    left, right = ((h, pair(h)) for h in (m.result() for m in attn))
    while len(ffn[0][0].left) > 2:
        step(ffn[0])
    ffn[0] = ffn[0][0].split(both_ways)
    send(ffn[0] + ffn[1])
    query, key, value = project(at_side, normed, ssm_out, left, right)
    query = fence(ffn[0], query)
    send(ffn[0])
    attended, lse = attention_forward(seg_col, seg_row, query, key, value)
    attended = fence(ffn[0] + ffn[1], attended)
    while len(ffn[1][0].left) > 2:
        step(ffn[1])
    ffn[1] = ffn[1][0].split(both_ways)
    send(ffn[1])
    middle, normed_two = middle_of(at_side, attended, right, rows, gain_two, bias_two)

    middle, normed_two = fence(ffn[1], middle, normed_two)
    send(ffn[1])

    def scatters(left, right):
        return [Scatter(left, count, index, X_FIRST), Scatter(right, count, index, Y_FIRST)]

    normed_other = pair(normed_two)
    *both, grad_up, grad_down = feed_forward(
        0, normed_two, normed_other, cot, *(m.result() for m in ffn[0]), ()
    )
    both, grad_up, grad_down = fence(ffn[1], both, grad_up, grad_down)
    sums_one = scatters(grad_up, grad_down)
    send(sums_one)
    own, other, gown, gother, grad_up, grad_down = feed_forward(
        1, normed_two, normed_other, cot, *(m.result() for m in ffn[1]), both
    )
    own, other, gown, gother, grad_up, grad_down = fence(
        sums_one, own, other, gown, gother, grad_up, grad_down
    )
    send(sums_one)
    sums_two = scatters(grad_up, grad_down)

    grad_middle, grad_branch, grad_attended, norm_two_sums = norm_two_back(
        at_side, gown, pair(gother), middle, cot, gain_two, right
    )
    grad_attended = fence(sums_one, grad_attended)
    send(sums_two)
    grad_query, grad_key, grad_value = attention_backward(
        seg_col, seg_row, query, key, value, lse, grad_attended
    )
    grad_query, grad_key, grad_value = fence(sums_two, grad_query, grad_key, grad_value)
    send(sums_two)

    def pair_sum(theirs, mine):
        return (mine.astype(F32) + pair(theirs).astype(F32)).astype(BF)

    grads_left = weight_grads(at_side, (normed, grad_branch), (grad_query, attended))
    grads_left, ssm_out = tie(grads_left, ssm_out)
    grads_right = weight_grads(at_side, (ssm_out,), (grad_key, grad_value))
    sums_left = pair_sum(*grads_left)
    grads_right = fence(sums_two, grads_right)
    sums_attn = scatters(sums_left, pair_sum(*grads_right))
    sums_ffn = sums_one + sums_two
    join_chains(sums_ffn)
    send(sums_attn + sums_ffn)
    g_steps, gm_steps, sum_one, dsum_one = ssm_backward(
        starts, at_side, grad_key, grad_value, left, right, drive, decay, coef
    )
    g_steps, gm_steps = fence(sums_attn, g_steps, gm_steps)
    send(sums_attn)
    grad_mixed, sum_two, dsum_two = ssm_backward_rest(
        starts, g_steps, gm_steps, drive, decay, coef
    )
    grad_mixed = fence(sums_attn + sums_ffn, grad_mixed)
    join_chains(sums_attn)
    send(sums_attn)
    grads_mix = weight_grads(at_side, (normed,), (grad_mixed,))
    grads_mix, grad_mixed = tie(grads_mix, grad_mixed)
    sums_mix = [Scatter(pair_sum(*grads_mix), count, index, DIRECT)]
    for_partner, norm_one_first = norm_one_back(
        at_side, grad_query, grad_mixed, rows, grad_middle, gain_one, left, mix_both, True
    )
    for_partner, grad_mixed, sums_mix[0].values = fence(
        sums_attn, for_partner, grad_mixed, sums_mix[0].values
    )
    send(sums_mix)
    got_grad = pair(for_partner)
    in_grad, norm_one_second = norm_one_back(
        at_side, grad_query, grad_mixed, rows, grad_middle, gain_one, left, mix_both, False
    )
    in_grad, norm_one_second, middle, own, other = fence(
        sums_mix, in_grad, norm_one_second, middle, own, other
    )

    state_sums = jnp.concatenate([sum_one, sum_two, dsum_one, dsum_two]).reshape(
        2 * states, width
    )
    sums = jnp.concatenate(
        [
            lax.dynamic_slice_in_dim(state_sums, (1 - side) * cols, cols, 1),
            (norm_one_first + norm_one_second).reshape(-1, cols),
            norm_two_sums.reshape(-1, cols),
        ]
    )
    mine = lax.dynamic_slice_in_dim(state_sums, side * cols, cols, 1)
    small = [Total(jnp.concatenate([mine, sums[2 * states :]]) + pair(sums), count)]
    send(sums_mix + small)
    in_half = (1 - side) * half
    partner_sum = pair(
        lax.dynamic_slice_in_dim(middle, in_half, half, 0)
        + lax.dynamic_slice_in_dim(own, in_half, half, 0).astype(F32)
    )
    partner_other = pair(lax.dynamic_slice_in_dim(other, in_half, half, 0))
    in_grad = put(at_side, got_grad, in_grad)
    in_grad, middle = fence(sums_mix + small, in_grad, middle)
    send(small)
    layer_out = layer_out_of(at_side, middle, own, other, partner_sum, partner_other)
    layer_out = fence(small, layer_out)
    complete(sums_mix + small + sums_attn + sums_ffn)
    small = small[0].values
    total, dtotal = small[:states], small[states : 2 * states]
    norm_sums = lax.dynamic_slice_in_dim(
        small[2 * states :].reshape(4, width), index * shard_rows, shard_rows, 1
    )
    shard_attn = sums_attn[0].result()
    ups, downs = (
        [sums_ffn[0].result()[:, k * units : (k + 1) * units] for k in at] for at in ((0, 2), (1, 3))
    )
    return (
        layer_out[:, None],
        in_grad[:, None],
        sums_mix[0].result(),
        shard_attn[:, :cols],
        shard_attn[:, 2 * cols : 3 * cols],
        shard_attn[:, 3 * cols :],
        shard_attn[:, cols : 2 * cols].T,
        jnp.concatenate(ups, axis=1),
        jnp.concatenate(downs, axis=1).T,
        norm_sums[0],
        norm_sums[1],
        norm_sums[2],
        norm_sums[3],
        ssm_inject * ssm_readout * dtotal,
        ssm_readout * total,
        ssm_inject * total,
    )


def solution(mesh):
    return jax.shard_map(
        functools.partial(per_device, mesh.shape["dp"]),
        mesh=mesh,
        in_specs=(
            P(None, "dp", "tensor", None),
            P(None, "dp", None),
            P("dp", "tensor"),
            P("dp", "tensor"),
            P("dp", "tensor"),
            P("dp", "tensor"),
            P("tensor", "dp"),
            P("dp", "tensor"),
            P("tensor", "dp"),
            P("dp"),
            P("dp"),
            P("dp"),
            P("dp"),
            P(None, "tensor"),
            P(None, "tensor"),
            P(None, "tensor"),
            P(None, "dp", "tensor", None),
        ),
        out_specs=(
            P(None, "dp", "tensor", None),
            P(None, "dp", "tensor", None),
            P("dp", "tensor"),
            P("dp", "tensor"),
            P("dp", "tensor"),
            P("dp", "tensor"),
            P("tensor", "dp"),
            P("dp", "tensor"),
            P("tensor", "dp"),
            P("dp"),
            P("dp"),
            P("dp"),
            P("dp"),
            P(None, "tensor"),
            P(None, "tensor"),
            P(None, "tensor"),
        ),
        check_vma=False,
    )
```

time: 570 us -> 514 us (0.902)
  starting transfers between devices: 57.7 us -> 99.1 us
  waiting for transfers between devices: 97.2 us -> 61.7 us
  other arithmetic: 82.5 us -> 48.2 us
  local copies, waits for them, and re-layouts: 49.3 us -> 31.6 us
  matrix products: 13.2 us -> 0 us
  Pallas kernels: 258 us -> 265 us
    ppermute x48 -> x57, starting transfers between devices: 54.9 us -> 97 us  [swap(): return lax.ppermute(values, 'dp', [(i, i ^ mask) for i in range(count)])]
    ppermute x48 -> x57, waiting for transfers between devices: 91.9 us -> 57.6 us  [swap(): return lax.ppermute(values, 'dp', [(i, i ^ mask) for i in range(count)])]
    select_n x38 -> x26, other arithmetic: 47.1 us -> 15.3 us  [the longest x25 15.3 us: in_order(): jnp.where(upper, jnp.stack([got, own], axis=axis), jnp.stack([own, got],...]
    pallas_call x6 -> x10, Pallas kernels: 84.5 us -> 99.4 us  [the longest x2 18.4 us: norm_one_back(): pl.pallas_call(norm_one_kernel, grid_spec=pltpu.PrefetchScalarGridSpec(nu...]
    dot_general x3 -> x0, matrix products: 13.2 us -> none  [dot_plain(): return jnp.dot(left_op, right_op, preferred_element_type=F32)]
    pallas_call x2, Pallas kernels: 81.9 us -> 71 us  [feed_forward(): pl.pallas_call(functools.partial(feed_forward_kernel, part), out_shape=(j...]
    squeeze x18 -> x16, local copies, waits for them, and re-layouts: 14.1 us -> 6.54 us  [block(): values = lax.dynamic_index_in_dim(values, digit, place, keepdims=False)]
    slice x7 -> x5, local copies, waits for them, and re-layouts: 7.77 us -> 1.23 us  [the longest x3 1.14 us: split(): part.values = self.values[..., k * cols:(k + 1) * cols]]
  transfers between devices with their start and end apart: 64 -> 72, of which waited for: 24 -> 19; matrix products, arithmetic and copies ran while one was open for 18% -> 8% of each run, Pallas kernels for 34% -> 51%
where the time goes in v3:
time: 514 us; the launch traced here: 507 us
  Pallas kernels  265 us (52%)
  starting transfers between devices  99.1 us (19%)
  waiting for transfers between devices  61.7 us (12%)
  other arithmetic  48.2 us (9%)
  local copies, waits for them, and re-layouts  31.6 us (6%)
    ppermute x57, starting transfers between devices, swap(): return lax.ppermute(values, 'dp', [(i, i ^ mask) for i in range(count)])  97 us
    pallas_call x2, Pallas kernels, feed_forward(): pl.pallas_call(functools.partial(feed_forward_kernel, part), out_shape=(j...  71 us
    ppermute x57, waiting for transfers between devices, swap(): return lax.ppermute(values, 'dp', [(i, i ^ mask) for i in range(count)])  57.6 us
    pallas_call x1, Pallas kernels, ssm_backward(): pl.pallas_call(ssm_backward_kernel, out_shape=(jax.ShapeDtypeStruct((leng...  28.5 us
    pallas_call x3, Pallas kernels, weight_grads(): pl.pallas_call(functools.partial(weight_grads_kernel, count), out_shape=(...  23.7 us
    pallas_call x1, Pallas kernels, ssm_backward_rest(): pl.pallas_call(ssm_backward_rest_kernel, out_shape=(jax.ShapeDtypeStruct(...  23.1 us
    pallas_call x1, Pallas kernels, ssm_forward(): pl.pallas_call(ssm_forward_kernel, out_shape=(jax.ShapeDtypeStruct((lengt...  18.9 us
    pallas_call x2, Pallas kernels, norm_one_back(): pl.pallas_call(norm_one_kernel, grid_spec=pltpu.PrefetchScalarGridSpec(nu...  18.4 us
  transfers between devices with their start and end apart: 72, of which 19 were waited for; matrix products, arithmetic and copies ran while one was open for 8% of the time, Pallas kernels for 51%

profile of v3, /device:TPU:0, one launch (start us, length us, event | category | flops | bytes accessed | tf_op | source)
XLA Modules:
  0.0 507.3 jit_solution(18221488533242756582)
XLA Ops:
  2.3 3.0 collective-permute-start.1
  5.3 2.6 collective-permute-start.2
  8.9 4.2 collective-permute-done.2
  20.6 2.3 collective-permute-done.7
  25.4 13.3 %collective-permute-done.8 = bf16[64,2048]{1,0:T(8,128)(2,1)S(1)} collective-permute-done((bf16[64,2048]{1,0:T(8,128)(2,1)S(1)}, bf16[64,2048]{1,0:T(8,128)(2,1)S(1)}, u32[]{:S(2)}, u32[]{:S(2)}) %collective-permute-start.8) | collective-permute-done | bytes 262176 | tf_op jit(solution)/shard_map/ppermute | solution.py:66
  48.0 18.9 %ssm_forward.1 = (bf16[1024,1024]{1,0:T(8,128)(2,1)}, bf16[1024,1024]{1,0:T(8,128)(2,1)}, f32[1024,8,128]{2,1,0:T(8,128)}, bf16[512,1024]{1,0:T(8,128)(2,1)}, f32[16,8,128]{2,1,0:T(8,128)}) custom-call(s32[16]{0:T(128)} %convert_reduce_fusion.starts_ref, s32[1]{0:T(128)} %bitcast.side_ref, bf16[2,512,1024]{2,1,0:T(8,128)(2,1)} %bitcast.296, ...), custom_call_target="tpu_custom_call" | custom-call | flops 12884901888 | bytes 16777216 | tf_op jit(solution)/shard_map/ssm_forward/pallas_call | solution.py:391
  71.3 3.5 collective-permute-start.16
  77.8 13.1 %ssm_rest.1 = (bf16[1024,1024]{1,0:T(8,128)(2,1)}, bf16[2,1024,1024]{2,1,0:T(8,128)(2,1)}) custom-call(s32[16]{0:T(128)} %convert_reduce_fusion.starts_ref, s32[1]{0:T(128)} %bitcast.side_ref, bf16[2,512,1024]{2,1,0:T(8,128)(2,1)} %bitcast.297, bf16[2,512,1024]{2,1,0:T(8,128)(2,1)} %copy-done.48, f32[1024,8,128]{2,1,0:T(8,128)} %get-tuple-element.338.drive_ref, ...), custom_call_target="tpu_custom_call" | custom-call | flops 10737418240 | bytes 16777216 | tf_op jit(solution)/shard_map/ssm_rest/pallas_call | solution.py:420
  90.9 5.2 %collective-permute-done.17 = bf16[64,2048]{1,0:T(8,128)(2,1)S(1)} collective-permute-done((bf16[64,2048]{1,0:T(8,128)(2,1)S(1)}, bf16[64,2048]{1,0:T(8,128)(2,1)S(1)}, u32[]{:S(2)}, u32[]{:S(2)}) %collective-permute-start.17) | collective-permute-done | bytes 262176 | tf_op jit(solution)/shard_map/ppermute | solution.py:66
  102.6 2.0 collective-permute-done.23.right_other_ref.other_ref
  106.0 12.2 %project.1 = (bf16[1024,1024]{1,0:T(8,128)(2,1)}, bf16[1024,1024]{1,0:T(8,128)(2,1)}, bf16[1024,1024]{1,0:T(8,128)(2,1)}) custom-call(s32[1]{0:T(128)} %bitcast.side_ref, bf16[1024,1024]{1,0:T(8,128)(2,1)} %get-tuple-element.321.normed_ref.refs_0_, bf16[1024,1024]{1,0:T(8,128)(2,1)} %get-tuple-element.482.ssm_ref.refs_0_, bf16[1024,1024]{1,0:T(8,128)(2,1)} %bitcast.208, ...), custom_call_target="tpu_custom_call" | custom-call | flops 6442450944 | bytes 16777216 | tf_op jit(solution)/shard_map/project/pallas_call | solution.py:469
  119.0 1.8 maximum_select_fusion.12
  125.0 4.8 collective-permute-start.26
  133.4 10.7 %attention_forward.1 = (bf16[1024,1024]{1,0:T(8,128)(2,1)}, f32[8,1024,1]{2,1,0:T(8,128)}) custom-call(s32[1024,1]{1,0:T(8,128)} %copy.87.seg_col_ref, s32[1,1024]{1,0:T(1,128)} %fusion.33.seg_row_ref, bf16[1024,1024]{1,0:T(8,128)(2,1)} %get-tuple-element.367.query_ref, bf16[1024,1024]{1,0:T(8,128)(2,1)} %get-tuple-element.368.key_ref, ...), custom_call_target="tpu_custom_call" | custom-call | flops 1879048192 | bytes 8388608 | tf_op jit(solution)/shard_map/attention_forward/pallas_call | solution.py:701
  144.1 7.1 %collective-permute-done.27 = bf16[64,2048]{1,0:T(8,128)(2,1)S(1)} collective-permute-done((bf16[64,2048]{1,0:T(8,128)(2,1)S(1)}, bf16[64,2048]{1,0:T(8,128)(2,1)S(1)}, u32[]{:S(2)}, u32[]{:S(2)}) %collective-permute-start.27) | collective-permute-done | bytes 262176 | tf_op jit(solution)/shard_map/ppermute | solution.py:66
  152.2 2.1 maximum_select_fusion.3
  158.7 8.6 %middle.1 = (f32[1024,1024]{1,0:T(8,128)}, bf16[1024,1024]{1,0:T(8,128)(2,1)}) custom-call(s32[1]{0:T(128)} %bitcast.side_ref, bf16[1024,1024]{1,0:T(8,128)(2,1)} %get-tuple-element.383.attended_ref.refs_3_, bf16[1024,1024]{1,0:T(8,128)(2,1)} %bitcast.204, bf16[1024,1024]{1,0:T(8,128)(2,1)} %copy-done.6, bf16[1024,1024]{1,0:T(8,128)(2,1)} %get-tuple-element.384.rows_ref, ...), custom_call_target="tpu_custom_call" | custom-call | flops 2147483648 | bytes 12582912 | tf_op jit(solution)/shard_map/middle/pallas_call | solution.py:959
  167.7 2.4 maximum_select_fusion.15
  171.8 3.1 copy.88
  179.2 34.4 %feed_forward.2 = (bf16[1024,1024]{1,0:T(8,128)(2,1)}, bf16[1024,1024]{1,0:T(8,128)(2,1)}, bf16[1024,1024]{1,0:T(8,128)(2,1)}, bf16[1024,1024]{1,0:T(8,128)(2,1)...) custom-call(bf16[1024,1024]{1,0:T(8,128)(2,1)} %get-tuple-element.397.refs_0_, ...), custom_call_target="tpu_custom_call" | custom-call | flops 30064771072 | bytes 50331648 | tf_op jit(solution)/shard_map/feed_forward/pallas_call | solution.py:903
  220.3 36.5 %feed_forward.3 = (bf16[1024,1024]{1,0:T(8,128)(2,1)}, bf16[1024,1024]{1,0:T(8,128)(2,1)}, bf16[1024,1024]{1,0:T(8,128)(2,1)}, bf16[1024,1024]{1,0:T(8,128)(2,1)...) custom-call(bf16[1024,1024]{1,0:T(8,128)(2,1)} %get-tuple-element.397.refs_0_, ...), custom_call_target="tpu_custom_call" | custom-call | flops 30064771072 | bytes 50331648 | tf_op jit(solution)/shard_map/feed_forward/pallas_call | solution.py:903
  257.3 1.9 fusion.5
  266.4 12.0 %norm_two_back.1 = (f32[1024,1024]{1,0:T(8,128)}, bf16[1024,1024]{1,0:T(8,128)(2,1)}, bf16[1024,1024]{1,0:T(8,128)(2,1)}, f32[2,1024]{1,0:T(2,128)}) custom-call(s32[1]{0:T(128)} %bitcast.side_ref, bf16[1024,1024]{1,0:T(8,128)(2,1)} %get-tuple-element.443.mine_ref, bf16[1024,1024]{1,0:T(8,128)(2,1)} %collective-permute-done.36.theirs_ref, ...), custom_call_target="tpu_custom_call" | custom-call | flops 2147483648 | bytes 25165824 | tf_op jit(solution)/shard_map/norm_two_back/pallas_call | solution.py:1005
  278.9 17.1 %attention_backward.1 = (bf16[1024,1024]{1,0:T(8,128)(2,1)}, bf16[1024,1024]{1,0:T(8,128)(2,1)}, bf16[1024,1024]{1,0:T(8,128)(2,1)}) custom-call(s32[1024,1]{1,0:T(8,128)} %copy.87.seg_col_ref, s32[1,1024]{1,0:T(1,128)} %fusion.33.seg_row_ref, bf16[1024,1024]{1,0:T(8,128)(2,1)} %get-tuple-element.367.query_ref, ...), custom_call_target="tpu_custom_call" | custom-call | flops 4697620480 | bytes 14680064 | tf_op jit(solution)/shard_map/attention_backward/pallas_call | solution.py:769
  295.9 2.3 collective-permute-done.38
  303.8 9.4 %weight_grads.3 = (bf16[1024,1024]{1,0:T(8,128)(2,1)}, bf16[1024,1024]{1,0:T(8,128)(2,1)}) custom-call(s32[1]{0:T(128)} %bitcast.side_ref, bf16[1024,1024]{1,0:T(8,128)(2,1)} %get-tuple-element.321.normed_ref.refs_0_, bf16[1024,1024]{1,0:T(8,128)(2,1)} %get-tuple-element.446.refs_1_, bf16[1024,1024]{1,0:T(8,128)(2,1)} %get-tuple-element.473.refs_2_.gquery_ref, ...), custom_call_target="tpu_custom_call" | custom-call | flops 4294967296 | bytes 12582912 | tf_op jit(solution)/shard_map/weight_grads/pallas_call | solution.py:1148
  313.2 8.7 %weight_grads.4 = (bf16[1024,1024]{1,0:T(8,128)(2,1)}, bf16[1024,1024]{1,0:T(8,128)(2,1)}) custom-call(s32[1]{0:T(128)} %bitcast.side_ref, bf16[1024,1024]{1,0:T(8,128)(2,1)} %get-tuple-element.482.ssm_ref.refs_0_, bf16[1024,1024]{1,0:T(8,128)(2,1)} %get-tuple-element.483.refs_1_.gkey_ref, bf16[1024,1024]{1,0:T(8,128)(2,1)} %get-tuple-element.484.refs_2_.gvalue_ref), custom_call_target="tpu_custom_call" | custom-call | flops 4294967296 | bytes 12582912 | tf_op jit(solution)/shard_map/weight_grads/pallas_call | solution.py:1148
  325.4 2.7 add_convert_fusion.1
  328.2 2.6 add_convert_fusion
  334.0 28.5 %ssm_backward.1 = (f32[1024,8,128]{2,1,0:T(8,128)}, f32[1024,8,128]{2,1,0:T(8,128)}, f32[8,8,128]{2,1,0:T(8,128)}, f32[8,8,128]{2,1,0:T(8,128)}) custom-call(s32[16]{0:T(128)} %convert_reduce_fusion.starts_ref, s32[1]{0:T(128)} %bitcast.side_ref, bf16[1024,1024]{1,0:T(8,128)(2,1)} %get-tuple-element.483.refs_1_.gkey_ref, ...), custom_call_target="tpu_custom_call" | custom-call | flops 21474836480 | bytes 20971520 | tf_op jit(solution)/shard_map/ssm_backward/pallas_call | solution.py:573
  363.7 5.1 %collective-permute-start.49 = (bf16[64,4096]{1,0:T(8,128)(2,1)}, bf16[64,4096]{1,0:T(8,128)(2,1)}, u32[]{:S(2)}, u32[]{:S(2)}) collective-permute-start(bf16[64,4096]{1,0:T(8,128)(2,1)} %get-tuple-element.646), channel_id=1, source_target_pairs={{0,8},{2,10},{4,12},{6,14},{8,0},{10,2},{12,4},{14,6},{16,24},{18,... | collective-permute-start | bytes 1572872 | tf_op jit(solution)/shard_map/ppermute | solution.py:66
  377.8 23.1 %ssm_backward_rest.1 = (bf16[1024,1024]{1,0:T(8,128)(2,1)}, f32[8,8,128]{2,1,0:T(8,128)}, f32[8,8,128]{2,1,0:T(8,128)}) custom-call(s32[16]{0:T(128)} %convert_reduce_fusion.starts_ref, f32[1024,8,128]{2,1,0:T(8,128)} %get-tuple-element.514.g_ref, f32[1024,8,128]{2,1,0:T(8,128)} %get-tuple-element.515.given_ref, ...), custom_call_target="tpu_custom_call" | custom-call | flops 21474836480 | bytes 20971520 | tf_op jit(solution)/shard_map/ssm_backward_rest/pallas_call | solution.py:599
  400.9 6.5 %collective-permute-done.50 = bf16[64,4096]{1,0:T(8,128)(2,1)} collective-permute-done((bf16[64,4096]{1,0:T(8,128)(2,1)}, bf16[64,4096]{1,0:T(8,128)(2,1)}, u32[]{:S(2)}, u32[]{:S(2)}) %collective-permute-start.50) | collective-permute-done | bytes 524320 | tf_op jit(solution)/shard_map/ppermute | solution.py:66
  407.8 2.6 fusion.7
  410.5 5.6 %weight_grads.5 = (bf16[1024,512]{1,0:T(8,128)(2,1)}, bf16[1024,512]{1,0:T(8,128)(2,1)}) custom-call(s32[1]{0:T(128)} %bitcast.side_ref, bf16[1024,1024]{1,0:T(8,128)(2,1)} %get-tuple-element.321.normed_ref.refs_0_, bf16[1024,1024]{1,0:T(8,128)(2,1)} %get-tuple-element.544.refs_1_.gmixed_ref), custom_call_target="tpu_custom_call" | custom-call | flops 2147483648 | bytes 6291456 | tf_op jit(solution)/shard_map/weight_grads/pallas_call | solution.py:1148
  416.2 10.0 %collective-permute-start.52 = (bf16[64,2048]{1,0:T(8,128)(2,1)S(1)}, bf16[64,2048]{1,0:T(8,128)(2,1)S(1)}, u32[]{:S(2)}, u32[]{:S(2)}) collective-permute-start(bf16[64,2048]{1,0:T(8,128)(2,1)S(1)} %get-tuple-element.656), channel_id=1, source_target_pairs={{0,8},{2,10},{4,12},{6,14},{8,0},{10,2},{12,4},{14,6},{16,24},{18,... | collective-permute-start | bytes 786440 | tf_op jit(solution)/shard_map/ppermute | solution.py:66
  429.1 8.7 %norm_one_back.2 = (f32[512,1024]{1,0:T(8,128)}, f32[2,1024]{1,0:T(2,128)}) custom-call(s32[1]{0:T(128)} %bitcast.side_ref, bf16[1024,1024]{1,0:T(8,128)(2,1)} %get-tuple-element.473.refs_2_.gquery_ref, bf16[1024,1024]{1,0:T(8,128)(2,1)} %get-tuple-element.544.refs_1_.gmixed_ref, bf16[1024,1024]{1,0:T(8,128)(2,1)} %get-tuple-element.384.rows_ref, ...), custom_call_target="tpu_custom_call" | custom-call | flops 2147483648 | bytes 10485760 | tf_op jit(solution)/shard_map/norm_one_back/pallas_call | solution.py:1060
  438.6 8.9 %collective-permute-done.53 = bf16[64,2048]{1,0:T(8,128)(2,1)S(1)} collective-permute-done((bf16[64,2048]{1,0:T(8,128)(2,1)S(1)}, bf16[64,2048]{1,0:T(8,128)(2,1)S(1)}, u32[]{:S(2)}, u32[]{:S(2)}) %collective-permute-start.53) | collective-permute-done | bytes 262176 | tf_op jit(solution)/shard_map/ppermute | solution.py:66
  452.9 9.7 %norm_one_back.3 = (f32[2,512,1024]{2,1,0:T(8,128)}, f32[2,1024]{1,0:T(2,128)}) custom-call(s32[1]{0:T(128)} %bitcast.side_ref, bf16[1024,1024]{1,0:T(8,128)(2,1)} %get-tuple-element.473.refs_2_.gquery_ref, bf16[1024,1024]{1,0:T(8,128)(2,1)} %get-tuple-element.544.refs_1_.gmixed_ref, bf16[1024,1024]{1,0:T(8,128)(2,1)} %get-tuple-element.384.rows_ref, ...), custom_call_target="tpu_custom_call" | custom-call | flops 2147483648 | bytes 10485760 | tf_op jit(solution)/shard_map/norm_one_back/pallas_call | solution.py:1060
  466.1 1.8 convert_add_fusion.6
  470.1 2.1 collective-permute-done.59
  472.2 5.5 %collective-permute-start.60 = (bf16[64,512]{1,0:T(8,128)(2,1)S(1)}, bf16[64,512]{1,0:T(8,128)(2,1)S(1)}, u32[]{:S(2)}, u32[]{:S(2)}) collective-permute-start(bf16[64,512]{1,0:T(8,128)(2,1)S(1)} %get-tuple-element.671), channel_id=1, source_target_pairs={{0,8},{2,10},{4,12},{6,14},{8,0},{10,2},{12,4},{14,6},{16,24},{18,... | collective-permute-start | bytes 196616 | tf_op jit(solution)/shard_map/ppermute | solution.py:66
  480.2 3.1 collective-permute-start.62
  484.1 2.4 collective-permute-done.61
  490.8 2.7 put.1
  495.7 1.8 collective-permute-start.68
  497.5 1.8 collective-permute-start.69
  501.1 4.6 layer_out.1
  (331 shorter events, 121.8 us)
Async XLA Ops:
  15.4 23.9 %collective-permute-start.4 = (bf16[2,2,72,512]{3,2,1,0:T(8,128)(2,1)S(1)}, bf16[2,2,72,512]{3,2,1,0:T(8,128)(2,1)S(1)}, u32[]{:S(2)}, u32[]{:S(2)}) collective-permute-start(bf16[2,2,72,512]{3,2,1,0:T(8,128)(2,1)S(1)} %maximum_select_fusion.23), channel_id=1, source_target_pairs={{0,2},{2,0},{4,6},{6,4},{8,10},{10,8},{12,14},{14,12},{16,18},{18,... | collective-permute-start | bytes 884744 | tf_op jit(solution)/shard_map/ppermute | solution.py:66
  16.9 22.4 %collective-permute-start.5 = (bf16[2,2,72,512]{3,2,1,0:T(8,128)(2,1)S(1)}, bf16[2,2,72,512]{3,2,1,0:T(8,128)(2,1)S(1)}, u32[]{:S(2)}, u32[]{:S(2)}) collective-permute-start(bf16[2,2,72,512]{3,2,1,0:T(8,128)(2,1)S(1)} %maximum_select_fusion.23), channel_id=1, source_target_pairs={{0,4},{2,6},{4,0},{6,2},{8,12},{10,14},{12,8},{14,10},{16,20},{18,... | collective-permute-start | bytes 884744 | tf_op jit(solution)/shard_map/ppermute | solution.py:66
  18.4 20.9 %collective-permute-start.6 = (bf16[2,2,72,512]{3,2,1,0:T(8,128)(2,1)S(1)}, bf16[2,2,72,512]{3,2,1,0:T(8,128)(2,1)S(1)}, u32[]{:S(2)}, u32[]{:S(2)}) collective-permute-start(bf16[2,2,72,512]{3,2,1,0:T(8,128)(2,1)S(1)} %maximum_select_fusion.23), channel_id=1, source_target_pairs={{0,6},{2,4},{4,2},{6,0},{8,14},{10,12},{12,10},{14,8},{16,22},{18,... | collective-permute-start | bytes 884744 | tf_op jit(solution)/shard_map/ppermute | solution.py:66
  18.9 19.9 %collective-permute-start.8 = (bf16[64,2048]{1,0:T(8,128)(2,1)S(1)}, bf16[64,2048]{1,0:T(8,128)(2,1)S(1)}, u32[]{:S(2)}, u32[]{:S(2)}) collective-permute-start(bf16[64,2048]{1,0:T(8,128)(2,1)S(1)} %pad_maximum_fusion.5), channel_id=1, source_target_pairs={{0,16},{2,18},{4,20},{6,22},{8,24},{10,26},{12,28},{14,30},{16,0},... | collective-permute-start | bytes 786440 | tf_op jit(solution)/shard_map/ppermute | solution.py:66
  22.9 15.9 %collective-permute-start.9 = (bf16[64,2048]{1,0:T(8,128)(2,1)S(1)}, bf16[64,2048]{1,0:T(8,128)(2,1)S(1)}, u32[]{:S(2)}, u32[]{:S(2)}) collective-permute-start(bf16[64,2048]{1,0:T(8,128)(2,1)S(1)} %pad_maximum_fusion.5), channel_id=1, source_target_pairs={{0,24},{2,26},{4,28},{6,30},{8,16},{10,18},{12,20},{14,22},{16,8},... | collective-permute-start | bytes 786440 | tf_op jit(solution)/shard_map/ppermute | solution.py:66
  42.4 24.4 %collective-permute-start.12 = (bf16[2,2,64,1024]{3,2,1,0:T(8,128)(2,1)S(1)}, bf16[2,2,64,1024]{3,2,1,0:T(8,128)(2,1)}, u32[]{:S(2)}, u32[]{:S(2)}) collective-permute-start(bf16[2,2,64,1024]{3,2,1,0:T(8,128)(2,1)S(1)} %get-tuple-element.327), channel_id=1, source_target_pairs={{0,2},{2,0},{4,6},{6,4},{8,10},{10,8},{12,14},{14,12},{16,18},{18,... | collective-permute-start | bytes 1572872 | tf_op jit(solution)/shard_map/ppermute | solution.py:66
  44.0 22.9 %collective-permute-start.13 = (bf16[2,2,64,1024]{3,2,1,0:T(8,128)(2,1)S(1)}, bf16[2,2,64,1024]{3,2,1,0:T(8,128)(2,1)}, u32[]{:S(2)}, u32[]{:S(2)}) collective-permute-start(bf16[2,2,64,1024]{3,2,1,0:T(8,128)(2,1)S(1)} %get-tuple-element.329), channel_id=1, source_target_pairs={{0,4},{2,6},{4,0},{6,2},{8,12},{10,14},{12,8},{14,10},{16,20},{18,... | collective-permute-start | bytes 1572872 | tf_op jit(solution)/shard_map/ppermute | solution.py:66
  70.1 26.0 %collective-permute-start.14 = (bf16[2,2,2,64,1024]{4,3,1,0,2:T(8,128)(2,1)S(1)}, bf16[2,2,2,64,1024]{4,3,1,0,2:T(8,128)(2,1)S(1)}, u32[]{:S(2)}, u32[]{:S(2)}) collective-permute-start(bf16[2,2,2,64,1024]{4,3,1,0,2:T(8,128)(2,1)S(1)} %maximum_select_fusion.8), channel_id=1, source_target_pairs={{0,4},{2,6},{4,0},{6,2},{8,12},{10,14},{12,8},{14,10},{16,20},{18,... | collective-permute-start | bytes 3145736 | tf_op jit(solution)/shard_map/ppermute | solution.py:66
  70.6 25.5 %collective-permute-start.15 = (bf16[2,2,2,64,1024]{4,3,1,0,2:T(8,128)(2,1)S(1)}, bf16[2,2,2,64,1024]{4,3,1,0,2:T(8,128)(2,1)S(1)}, u32[]{:S(2)}, u32[]{:S(2)}) collective-permute-start(bf16[2,2,2,64,1024]{4,3,1,0,2:T(8,128)(2,1)S(1)} %maximum_select_fusion.9), channel_id=1, source_target_pairs={{0,2},{2,0},{4,6},{6,4},{8,10},{10,8},{12,14},{14,12},{16,18},{18,... | collective-permute-start | bytes 3145736 | tf_op jit(solution)/shard_map/ppermute | solution.py:66
  71.3 19.7 %collective-permute-start.16 = (bf16[64,2048]{1,0:T(8,128)(2,1)S(1)}, bf16[64,2048]{1,0:T(8,128)(2,1)S(1)}, u32[]{:S(2)}, u32[]{:S(2)}) collective-permute-start(bf16[64,2048]{1,0:T(8,128)(2,1)S(1)} %get-tuple-element.348), channel_id=1, source_target_pairs={{0,8},{2,10},{4,12},{6,14},{8,0},{10,2},{12,4},{14,6},{16,24},{18,... | collective-permute-start | bytes 786440 | tf_op jit(solution)/shard_map/ppermute | solution.py:66
  74.8 21.4 %collective-permute-start.17 = (bf16[64,2048]{1,0:T(8,128)(2,1)S(1)}, bf16[64,2048]{1,0:T(8,128)(2,1)S(1)}, u32[]{:S(2)}, u32[]{:S(2)}) collective-permute-start(bf16[64,2048]{1,0:T(8,128)(2,1)S(1)} %get-tuple-element.348), channel_id=1, source_target_pairs={{0,16},{2,18},{4,20},{6,22},{8,24},{10,26},{12,28},{14,30},{16,0},... | collective-permute-start | bytes 786440 | tf_op jit(solution)/shard_map/ppermute | solution.py:66
  76.3 19.9 %collective-permute-start.18 = (bf16[64,2048]{1,0:T(8,128)(2,1)S(1)}, bf16[64,2048]{1,0:T(8,128)(2,1)S(1)}, u32[]{:S(2)}, u32[]{:S(2)}) collective-permute-start(bf16[64,2048]{1,0:T(8,128)(2,1)S(1)} %get-tuple-element.348), channel_id=1, source_target_pairs={{0,24},{2,26},{4,28},{6,30},{8,16},{10,18},{12,20},{14,22},{16,8},... | collective-permute-start | bytes 786440 | tf_op jit(solution)/shard_map/ppermute | solution.py:66
  99.7 18.5 %collective-permute-start.20 = (bf16[2,2,64,1024]{3,2,1,0:T(8,128)(2,1)S(1)}, bf16[2,2,64,1024]{3,2,1,0:T(8,128)(2,1)S(1)}, u32[]{:S(2)}, u32[]{:S(2)}) collective-permute-start(bf16[2,2,64,1024]{3,2,1,0:T(8,128)(2,1)S(1)} %get-tuple-element.358), channel_id=1, source_target_pairs={{0,2},{2,0},{4,6},{6,4},{8,10},{10,8},{12,14},{14,12},{16,18},{18,... | collective-permute-start | bytes 1572872 | tf_op jit(solution)/shard_map/ppermute | solution.py:66
  101.2 17.1 %collective-permute-start.21 = (bf16[2,2,64,1024]{3,2,1,0:T(8,128)(2,1)}, bf16[2,2,64,1024]{3,2,1,0:T(8,128)(2,1)}, u32[]{:S(2)}, u32[]{:S(2)}) collective-permute-start(bf16[2,2,64,1024]{3,2,1,0:T(8,128)(2,1)} %get-tuple-element.360), channel_id=1, source_target_pairs={{0,4},{2,6},{4,0},{6,2},{8,12},{10,14},{12,8},{14,10},{16,20},{18,... | collective-permute-start | bytes 1572872 | tf_op jit(solution)/shard_map/ppermute | solution.py:66
  121.0 30.2 %collective-permute-start.24 = (bf16[2,2,2,64,1024]{4,3,1,0,2:T(8,128)(2,1)S(1)}, bf16[2,2,2,64,1024]{4,3,1,0,2:T(8,128)(2,1)S(1)}, u32[]{:S(2)}, u32[]{:S(2)}) collective-permute-start(bf16[2,2,2,64,1024]{4,3,1,0,2:T(8,128)(2,1)S(1)} %maximum_select_fusion.11), channel_id=1, source_target_pairs={{0,4},{2,6},{4,0},{6,2},{8,12},{10,14},{12,8},{14,10},{16,20},{18,... | collective-permute-start | bytes 3145736 | tf_op jit(solution)/shard_map/ppermute | solution.py:66
  122.5 28.8 %collective-permute-start.25 = (bf16[2,2,2,64,1024]{4,3,1,0,2:T(8,128)(2,1)S(1)}, bf16[2,2,2,64,1024]{4,3,1,0,2:T(8,128)(2,1)}, u32[]{:S(2)}, u32[]{:S(2)}) collective-permute-start(bf16[2,2,2,64,1024]{4,3,1,0,2:T(8,128)(2,1)S(1)} %maximum_select_fusion.12), channel_id=1, source_target_pairs={{0,2},{2,0},{4,6},{6,4},{8,10},{10,8},{12,14},{14,12},{16,18},{18,... | collective-permute-start | bytes 3145736 | tf_op jit(solution)/shard_map/ppermute | solution.py:66
  125.0 19.1 %collective-permute-start.26 = (bf16[64,2048]{1,0:T(8,128)(2,1)S(1)}, bf16[64,2048]{1,0:T(8,128)(2,1)S(1)}, u32[]{:S(2)}, u32[]{:S(2)}) collective-permute-start(bf16[64,2048]{1,0:T(8,128)(2,1)S(1)} %get-tuple-element.378), channel_id=1, source_target_pairs={{0,8},{2,10},{4,12},{6,14},{8,0},{10,2},{12,4},{14,6},{16,24},{18,... | collective-permute-start | bytes 786440 | tf_op jit(solution)/shard_map/ppermute | solution.py:66
  129.8 21.4 %collective-permute-start.27 = (bf16[64,2048]{1,0:T(8,128)(2,1)S(1)}, bf16[64,2048]{1,0:T(8,128)(2,1)S(1)}, u32[]{:S(2)}, u32[]{:S(2)}) collective-permute-start(bf16[64,2048]{1,0:T(8,128)(2,1)S(1)} %get-tuple-element.378), channel_id=1, source_target_pairs={{0,16},{2,18},{4,20},{6,22},{8,24},{10,26},{12,28},{14,30},{16,0},... | collective-permute-start | bytes 786440 | tf_op jit(solution)/shard_map/ppermute | solution.py:66
  131.3 19.9 %collective-permute-start.28 = (bf16[64,2048]{1,0:T(8,128)(2,1)S(1)}, bf16[64,2048]{1,0:T(8,128)(2,1)S(1)}, u32[]{:S(2)}, u32[]{:S(2)}) collective-permute-start(bf16[64,2048]{1,0:T(8,128)(2,1)S(1)} %get-tuple-element.378), channel_id=1, source_target_pairs={{0,24},{2,26},{4,28},{6,30},{8,16},{10,18},{12,20},{14,22},{16,8},... | collective-permute-start | bytes 786440 | tf_op jit(solution)/shard_map/ppermute | solution.py:66
  156.1 11.3 %collective-permute-start.29 = (bf16[2,2,64,1024]{3,2,1,0:T(8,128)(2,1)S(1)}, bf16[2,2,64,1024]{3,2,1,0:T(8,128)(2,1)}, u32[]{:S(2)}, u32[]{:S(2)}) collective-permute-start(bf16[2,2,64,1024]{3,2,1,0:T(8,128)(2,1)S(1)} %get-tuple-element.388), channel_id=1, source_target_pairs={{0,2},{2,0},{4,6},{6,4},{8,10},{10,8},{12,14},{14,12},{16,18},{18,... | collective-permute-start | bytes 1572872 | tf_op jit(solution)/shard_map/ppermute | solution.py:66
  176.6 37.0 %collective-permute-start.31 = (bf16[2,2,2,64,1024]{4,3,1,0,2:T(8,128)(2,1)S(1)}, bf16[2,2,2,64,1024]{4,3,1,0,2:T(8,128)(2,1)S(1)}, u32[]{:S(2)}, u32[]{:S(2)}) collective-permute-start(bf16[2,2,2,64,1024]{4,3,1,0,2:T(8,128)(2,1)S(1)} %maximum_select_fusion.14), channel_id=1, source_target_pairs={{0,4},{2,6},{4,0},{6,2},{8,12},{10,14},{12,8},{14,10},{16,20},{18,... | collective-permute-start | bytes 3145736 | tf_op jit(solution)/shard_map/ppermute | solution.py:66
  177.7 35.9 %collective-permute-start.32 = (bf16[2,2,2,64,1024]{4,3,1,0,2:T(8,128)(2,1)S(1)}, bf16[2,2,2,64,1024]{4,3,1,0,2:T(8,128)(2,1)S(1)}, u32[]{:S(2)}, u32[]{:S(2)}) collective-permute-start(bf16[2,2,2,64,1024]{4,3,1,0,2:T(8,128)(2,1)S(1)} %copy-done.11), channel_id=1, source_target_pairs={{0,2},{2,0},{4,6},{6,4},{8,10},{10,8},{12,14},{14,12},{16,18},{18,... | collective-permute-start | bytes 3145736 | tf_op jit(solution)/shard_map/ppermute | solution.py:66
  218.3 38.5 %collective-permute-start.35 = (bf16[2,2,2,64,1024]{4,3,1,0,2:T(8,128)(2,1)S(1)}, bf16[2,2,2,64,1024]{4,3,1,0,2:T(8,128)(2,1)S(1)}, u32[]{:S(2)}, u32[]{:S(2)}) collective-permute-start(bf16[2,2,2,64,1024]{4,3,1,0,2:T(8,128)(2,1)S(1)} %copy_bitcast_fusion.4), channel_id=1, source_target_pairs={{0,2},{2,0},{4,6},{6,4},{8,10},{10,8},{12,14},{14,12},{16,18},{18,... | collective-permute-start | bytes 3145736 | tf_op jit(solution)/shard_map/ppermute | solution.py:66
  219.4 37.5 %collective-permute-start.34 = (bf16[2,2,2,64,1024]{4,3,1,0,2:T(8,128)(2,1)S(1)}, bf16[2,2,2,64,1024]{4,3,1,0,2:T(8,128)(2,1)}, u32[]{:S(2)}, u32[]{:S(2)}) collective-permute-start(bf16[2,2,2,64,1024]{4,3,1,0,2:T(8,128)(2,1)S(1)} %copy_bitcast_fusion.5), channel_id=1, source_target_pairs={{0,4},{2,6},{4,0},{6,2},{8,12},{10,14},{12,8},{14,10},{16,20},{18,... | collective-permute-start | bytes 3145736 | tf_op jit(solution)/shard_map/ppermute | solution.py:66
  259.3 19.1 %collective-permute-start.40 = (bf16[2,2,64,1024]{3,2,1,0:T(8,128)(2,1)S(1)}, bf16[2,2,64,1024]{3,2,1,0:T(8,128)(2,1)S(1)}, u32[]{:S(2)}, u32[]{:S(2)}) collective-permute-start(bf16[2,2,64,1024]{3,2,1,0:T(8,128)(2,1)S(1)} %dynamic-slice_bitcast_fusion.7), channel_id=1, source_target_pairs={{0,4},{2,6},{4,0},{6,2},{8,12},{10,14},{12,8},{14,10},{16,20},{18,... | collective-permute-start | bytes 1572872 | tf_op jit(solution)/shard_map/ppermute | solution.py:66
  261.4 17.0 %collective-permute-start.39 = (bf16[2,2,64,1024]{3,2,1,0:T(8,128)(2,1)}, bf16[2,2,64,1024]{3,2,1,0:T(8,128)(2,1)S(1)}, u32[]{:S(2)}, u32[]{:S(2)}) collective-permute-start(bf16[2,2,64,1024]{3,2,1,0:T(8,128)(2,1)} %dynamic-slice_bitcast_fusion.8), channel_id=1, source_target_pairs={{0,2},{2,0},{4,6},{6,4},{8,10},{10,8},{12,14},{14,12},{16,18},{18,... | collective-permute-start | bytes 1572872 | tf_op jit(solution)/shard_map/ppermute | solution.py:66
  263.6 34.7 %collective-permute-start.38 = (bf16[2,2,2,64,1024]{4,3,1,0,2:T(8,128)(2,1)}, bf16[2,2,2,64,1024]{4,3,1,0,2:T(8,128)(2,1)}, u32[]{:S(2)}, u32[]{:S(2)}) collective-permute-start(bf16[2,2,2,64,1024]{4,3,1,0,2:T(8,128)(2,1)} %copy_bitcast_fusion.2), channel_id=1, source_target_pairs={{0,2},{2,0},{4,6},{6,4},{8,10},{10,8},{12,14},{14,12},{16,18},{18,... | collective-permute-start | bytes 3145736 | tf_op jit(solution)/shard_map/ppermute | solution.py:66
  265.6 32.7 %collective-permute-start.37 = (bf16[2,2,2,64,1024]{4,3,1,0,2:T(8,128)(2,1)}, bf16[2,2,2,64,1024]{4,3,1,0,2:T(8,128)(2,1)}, u32[]{:S(2)}, u32[]{:S(2)}) collective-permute-start(bf16[2,2,2,64,1024]{4,3,1,0,2:T(8,128)(2,1)} %copy_bitcast_fusion.3), channel_id=1, source_target_pairs={{0,4},{2,6},{4,0},{6,2},{8,12},{10,14},{12,8},{14,10},{16,20},{18,... | collective-permute-start | bytes 3145736 | tf_op jit(solution)/shard_map/ppermute | solution.py:66
  301.6 20.3 %collective-permute-start.43 = (bf16[2,2,64,1024]{3,2,1,0:T(8,128)(2,1)S(1)}, bf16[2,2,64,1024]{3,2,1,0:T(8,128)(2,1)S(1)}, u32[]{:S(2)}, u32[]{:S(2)}) collective-permute-start(bf16[2,2,64,1024]{3,2,1,0:T(8,128)(2,1)S(1)} %dynamic-slice_bitcast_fusion.5), channel_id=1, source_target_pairs={{0,4},{2,6},{4,0},{6,2},{8,12},{10,14},{12,8},{14,10},{16,20},{18,... | collective-permute-start | bytes 1572872 | tf_op jit(solution)/shard_map/ppermute | solution.py:66
  302.6 19.3 %collective-permute-start.42 = (bf16[2,2,64,1024]{3,2,1,0:T(8,128)(2,1)S(1)}, bf16[2,2,64,1024]{3,2,1,0:T(8,128)(2,1)S(1)}, u32[]{:S(2)}, u32[]{:S(2)}) collective-permute-start(bf16[2,2,64,1024]{3,2,1,0:T(8,128)(2,1)S(1)} %dynamic-slice_bitcast_fusion.6), channel_id=1, source_target_pairs={{0,2},{2,0},{4,6},{6,4},{8,10},{10,8},{12,14},{14,12},{16,18},{18,... | collective-permute-start | bytes 1572872 | tf_op jit(solution)/shard_map/ppermute | solution.py:66
  313.2 11.8 %collective-permute-start.41 = (bf16[1024,1024]{1,0:T(8,128)(2,1)}, bf16[1024,1024]{1,0:T(8,128)(2,1)}, u32[]{:S(2)}, u32[]{:S(2)}) collective-permute-start(bf16[1024,1024]{1,0:T(8,128)(2,1)} %get-tuple-element.477), channel_id=1, source_target_pairs={{0,1},{1,0},{2,3},{3,2},{4,5},{5,4},{6,7},{7,6},{8,9},{9,8},{10,11... | collective-permute-start | bytes 6291464 | tf_op jit(solution)/shard_map/ppermute | solution.py:212
  330.8 41.0 %collective-permute-start.46 = (bf16[2,2,2,64,1024]{4,3,1,0,2:T(8,128)(2,1)S(1)}, bf16[2,2,2,64,1024]{4,3,1,0,2:T(8,128)(2,1)}, u32[]{:S(2)}, u32[]{:S(2)}) collective-permute-start(bf16[2,2,2,64,1024]{4,3,1,0,2:T(8,128)(2,1)S(1)} %copy_bitcast_fusion), channel_id=1, source_target_pairs={{0,2},{2,0},{4,6},{6,4},{8,10},{10,8},{12,14},{14,12},{16,18},{18,... | collective-permute-start | bytes 3145736 | tf_op jit(solution)/shard_map/ppermute | solution.py:66
  332.8 38.9 %collective-permute-start.45 = (bf16[2,2,2,64,1024]{4,3,1,0,2:T(8,128)(2,1)}, bf16[2,2,2,64,1024]{4,3,1,0,2:T(8,128)(2,1)}, u32[]{:S(2)}, u32[]{:S(2)}) collective-permute-start(bf16[2,2,2,64,1024]{4,3,1,0,2:T(8,128)(2,1)} %copy_bitcast_fusion.1), channel_id=1, source_target_pairs={{0,4},{2,6},{4,0},{6,2},{8,12},{10,14},{12,8},{14,10},{16,20},{18,... | collective-permute-start | bytes 3145736 | tf_op jit(solution)/shard_map/ppermute | solution.py:66
  363.7 37.2 %collective-permute-start.49 = (bf16[64,4096]{1,0:T(8,128)(2,1)}, bf16[64,4096]{1,0:T(8,128)(2,1)}, u32[]{:S(2)}, u32[]{:S(2)}) collective-permute-start(bf16[64,4096]{1,0:T(8,128)(2,1)} %get-tuple-element.646), channel_id=1, source_target_pairs={{0,8},{2,10},{4,12},{6,14},{8,0},{10,2},{12,4},{14,6},{16,24},{18,... | collective-permute-start | bytes 1572872 | tf_op jit(solution)/shard_map/ppermute | solution.py:66
  368.8 38.5 %collective-permute-start.50 = (bf16[64,4096]{1,0:T(8,128)(2,1)}, bf16[64,4096]{1,0:T(8,128)(2,1)}, u32[]{:S(2)}, u32[]{:S(2)}) collective-permute-start(bf16[64,4096]{1,0:T(8,128)(2,1)} %get-tuple-element.645), channel_id=1, source_target_pairs={{0,16},{2,18},{4,20},{6,22},{8,24},{10,26},{12,28},{14,30},{16,0},... | collective-permute-start | bytes 1572872 | tf_op jit(solution)/shard_map/ppermute | solution.py:66
  370.3 37.1 %collective-permute-start.51 = (bf16[64,4096]{1,0:T(8,128)(2,1)S(1)}, bf16[64,4096]{1,0:T(8,128)(2,1)}, u32[]{:S(2)}, u32[]{:S(2)}) collective-permute-start(bf16[64,4096]{1,0:T(8,128)(2,1)S(1)} %get-tuple-element.644), channel_id=1, source_target_pairs={{0,24},{2,26},{4,28},{6,30},{8,16},{10,18},{12,20},{14,22},{16,8},... | collective-permute-start | bytes 1572872 | tf_op jit(solution)/shard_map/ppermute | solution.py:66
  375.2 32.2 %collective-permute-start.48 = (bf16[2,2,64,1024]{3,2,1,0:T(8,128)(2,1)S(1)}, bf16[2,2,64,1024]{3,2,1,0:T(8,128)(2,1)S(1)}, u32[]{:S(2)}, u32[]{:S(2)}) collective-permute-start(bf16[2,2,64,1024]{3,2,1,0:T(8,128)(2,1)S(1)} %dynamic-slice_bitcast_fusion.3), channel_id=1, source_target_pairs={{0,4},{2,6},{4,0},{6,2},{8,12},{10,14},{12,8},{14,10},{16,20},{18,... | collective-permute-start | bytes 1572872 | tf_op jit(solution)/shard_map/ppermute | solution.py:66
  376.7 30.6 %collective-permute-start.47 = (bf16[2,2,64,1024]{3,2,1,0:T(8,128)(2,1)S(1)}, bf16[2,2,64,1024]{3,2,1,0:T(8,128)(2,1)S(1)}, u32[]{:S(2)}, u32[]{:S(2)}) collective-permute-start(bf16[2,2,64,1024]{3,2,1,0:T(8,128)(2,1)S(1)} %dynamic-slice_bitcast_fusion.4), channel_id=1, source_target_pairs={{0,2},{2,0},{4,6},{6,4},{8,10},{10,8},{12,14},{14,12},{16,18},{18,... | collective-permute-start | bytes 1572872 | tf_op jit(solution)/shard_map/ppermute | solution.py:66
  416.0 21.9 %collective-permute-start.55 = (bf16[1024,512]{1,0:T(8,128)(2,1)}, bf16[1024,512]{1,0:T(8,128)(2,1)S(1)}, u32[]{:S(2)}, u32[]{:S(2)}) collective-permute-start(bf16[1024,512]{1,0:T(8,128)(2,1)} %get-tuple-element.535), channel_id=1, source_target_pairs={{0,1},{1,0},{2,3},{3,2},{4,5},{5,4},{6,7},{7,6},{8,9},{9,8},{10,11... | collective-permute-start | bytes 3145736 | tf_op jit(solution)/shard_map/ppermute | solution.py:212
  416.2 22.4 %collective-permute-start.52 = (bf16[64,2048]{1,0:T(8,128)(2,1)S(1)}, bf16[64,2048]{1,0:T(8,128)(2,1)S(1)}, u32[]{:S(2)}, u32[]{:S(2)}) collective-permute-start(bf16[64,2048]{1,0:T(8,128)(2,1)S(1)} %get-tuple-element.656), channel_id=1, source_target_pairs={{0,8},{2,10},{4,12},{6,14},{8,0},{10,2},{12,4},{14,6},{16,24},{18,... | collective-permute-start | bytes 786440 | tf_op jit(solution)/shard_map/ppermute | solution.py:66
  426.2 21.3 %collective-permute-start.53 = (bf16[64,2048]{1,0:T(8,128)(2,1)S(1)}, bf16[64,2048]{1,0:T(8,128)(2,1)S(1)}, u32[]{:S(2)}, u32[]{:S(2)}) collective-permute-start(bf16[64,2048]{1,0:T(8,128)(2,1)S(1)} %get-tuple-element.655), channel_id=1, source_target_pairs={{0,16},{2,18},{4,20},{6,22},{8,24},{10,26},{12,28},{14,30},{16,0},... | collective-permute-start | bytes 786440 | tf_op jit(solution)/shard_map/ppermute | solution.py:66
  427.7 19.8 %collective-permute-start.54 = (bf16[64,2048]{1,0:T(8,128)(2,1)S(1)}, bf16[64,2048]{1,0:T(8,128)(2,1)S(1)}, u32[]{:S(2)}, u32[]{:S(2)}) collective-permute-start(bf16[64,2048]{1,0:T(8,128)(2,1)S(1)} %get-tuple-element.654), channel_id=1, source_target_pairs={{0,24},{2,26},{4,28},{6,30},{8,16},{10,18},{12,20},{14,22},{16,8},... | collective-permute-start | bytes 786440 | tf_op jit(solution)/shard_map/ppermute | solution.py:66
  448.4 40.4 %collective-permute-start.66 = (f32[512,1024]{1,0:T(8,128)}, f32[512,1024]{1,0:T(8,128)}, u32[]{:S(2)}, u32[]{:S(2)}) collective-permute-start(f32[512,1024]{1,0:T(8,128)} %get-tuple-element.568), channel_id=1, source_target_pairs={{0,1},{1,0},{2,3},{3,2},{4,5},{5,4},{6,7},{7,6},{8,9},{9,8},{10,11... | collective-permute-start | bytes 6291464 | tf_op jit(solution)/shard_map/ppermute | solution.py:212
  449.3 13.2 %collective-permute-start.56 = (bf16[2,2,64,512]{3,2,1,0:T(8,128)(2,1)}, bf16[2,2,64,512]{3,2,1,0:T(8,128)(2,1)S(1)}, u32[]{:S(2)}, u32[]{:S(2)}) collective-permute-start(bf16[2,2,64,512]{3,2,1,0:T(8,128)(2,1)} %get-tuple-element.653), channel_id=1, source_target_pairs={{0,2},{2,0},{4,6},{6,4},{8,10},{10,8},{12,14},{14,12},{16,18},{18,... | collective-permute-start | bytes 786440 | tf_op jit(solution)/shard_map/ppermute | solution.py:66
  450.4 13.3 %collective-permute-start.57 = (bf16[2,2,64,512]{3,2,1,0:T(8,128)(2,1)}, bf16[2,2,64,512]{3,2,1,0:T(8,128)(2,1)}, u32[]{:S(2)}, u32[]{:S(2)}) collective-permute-start(bf16[2,2,64,512]{3,2,1,0:T(8,128)(2,1)} %get-tuple-element.652), channel_id=1, source_target_pairs={{0,4},{2,6},{4,0},{6,2},{8,12},{10,14},{12,8},{14,10},{16,20},{18,... | collective-permute-start | bytes 786440 | tf_op jit(solution)/shard_map/ppermute | solution.py:66
  451.9 13.0 %collective-permute-start.58 = (bf16[2,2,64,512]{3,2,1,0:T(8,128)(2,1)S(1)}, bf16[2,2,64,512]{3,2,1,0:T(8,128)(2,1)}, u32[]{:S(2)}, u32[]{:S(2)}) collective-permute-start(bf16[2,2,64,512]{3,2,1,0:T(8,128)(2,1)S(1)} %get-tuple-element.651), channel_id=1, source_target_pairs={{0,6},{2,4},{4,2},{6,0},{8,14},{10,12},{12,10},{14,8},{16,22},{18,... | collective-permute-start | bytes 786440 | tf_op jit(solution)/shard_map/ppermute | solution.py:66
  467.9 32.2 %collective-permute-start.70 = (f32[512,1024]{1,0:T(8,128)}, f32[512,1024]{1,0:T(8,128)}, u32[]{:S(2)}, u32[]{:S(2)}) collective-permute-start(f32[512,1024]{1,0:T(8,128)} %convert_add_fusion.6), channel_id=1, source_target_pairs={{0,1},{1,0},{2,3},{3,2},{4,5},{5,4},{6,7},{7,6},{8,9},{9,8},{10,11... | collective-permute-start | bytes 6291464 | tf_op jit(solution)/shard_map/ppermute | solution.py:212
  477.9 22.3 %collective-permute-start.71 = (bf16[512,1024]{1,0:T(8,128)(2,1)S(1)}, bf16[512,1024]{1,0:T(8,128)(2,1)S(1)}, u32[]{:S(2)}, u32[]{:S(2)}) collective-permute-start(bf16[512,1024]{1,0:T(8,128)(2,1)S(1)} %constant_dynamic-slice_fusion), channel_id=1, source_target_pairs={{0,1},{1,0},{2,3},{3,2},{4,5},{5,4},{6,7},{7,6},{8,9},{9,8},{10,11... | collective-permute-start | bytes 3145736 | tf_op jit(solution)/shard_map/ppermute | solution.py:212
  (73 other events, 450.9 us)

commit v4 on v3

--- a/solution.py
+++ b/solution.py
@@ -15,6 +15,7 @@
 LANES = 128
 QTILE = 256
 HEADS_EACH = 2
+CUT = 4
 
 norm_eps = 1e-05
 masked_score = -1e30
@@ -82,12 +83,18 @@
         self.shape = (count * shard.shape[0],) + shard.shape[1:]
         self.left = groups_of(count, low)
         self.present = []
+        self.loose = False
+        self.last = None
 
     def send(self):
         self.got = [swap(self.values, self.count, m) for m in masks_of(self.left[0])]
 
     def merge(self):
         pieces = [self.values] + list(self.got)
+        if self.loose and len(self.left) == 1:
+            self.last = self.left.pop()[0]
+            self.values = pieces
+            return
         for bit in self.left.pop(0):
             place = sum(1 for p in self.present if p > bit)
             self.present.append(bit)
@@ -98,7 +105,12 @@
             ]
         self.values = pieces[0]
 
-    def split(self, lows):
+    def blocks(self, low):
+        after = low[-1][0]
+        rows = after * self.shape[0] // self.count
+        return self.shape[0] // (2 * rows), rows
+
+    def split(self, lows, loose=False):
         cols = self.values.shape[-1] // 2
         out = []
         for k, low in enumerate(lows):
@@ -107,11 +119,23 @@
             part.values = self.values[..., k * cols : (k + 1) * cols]
             part.shape = self.shape[:-1] + (cols,)
             part.left = self.left[: -len(lows)] + list(low)
+            part.last = None
+            part.loose = loose and self.blocks(low)[1] % 16 == 0
             out.append(part)
         return out
 
     def result(self):
         return self.values.reshape(self.shape)
+
+    def parts(self):
+        if self.last is None:
+            return [self.result()], (1, self.shape[0]), jnp.int32(0)
+        half = (self.shape[0] // 2,) + self.shape[1:]
+        return (
+            [v.reshape(half) for v in self.values],
+            self.blocks(((self.last,),)),
+            (self.index // self.last) % 2,
+        )
 
 
 def masks_of(group):
@@ -354,7 +378,7 @@
 
     lax.fori_loop(0, length // chunk, project, 0)
     scan_states(
-        starts_ref, 0, length // 2, drive_ref, decay_ref, coef_ref, y_ref, None, end_ref
+        starts_ref, 0, length // CUT, drive_ref, decay_ref, coef_ref, y_ref, None, end_ref
     )
     from_steps(y_ref, out_ref)
 
@@ -365,6 +389,7 @@
 ):
     length = drive_ref.shape[0]
     half = length // 2
+    cut = length // CUT
     side = side_ref[0]
     copies = both_parts(
         mine_ref.at[side], got_ref.at[side], cot_ref, rows_at(side, half, 0), sems.at[0]
@@ -372,10 +397,10 @@
         mine_ref.at[1 - side], got_ref.at[1 - side], cot_ref, rows_at(side, half, 1), sems.at[1]
     )
     scan_states(
-        starts_ref, half, length, drive_ref, decay_ref, coef_ref, y_ref, start_ref, None
-    )
-    out_ref[:half, :] = first_ref[...]
-    from_steps(y_ref, out_ref.at[half:])
+        starts_ref, cut, length, drive_ref, decay_ref, coef_ref, y_ref, start_ref, None
+    )
+    out_ref[:cut, :] = first_ref[...]
+    from_steps(y_ref, out_ref.at[cut:])
     wait_all(copies)
 
 
@@ -394,13 +419,13 @@
             jax.ShapeDtypeStruct((length, width), BF),
             jax.ShapeDtypeStruct((length, width), BF),
             jax.ShapeDtypeStruct((length, tiles, LANES), F32),
-            jax.ShapeDtypeStruct((length // 2, width), BF),
+            jax.ShapeDtypeStruct((length // CUT, width), BF),
             jax.ShapeDtypeStruct(decay.shape, F32),
         ),
         in_specs=[SMALL] * 2 + [ANYWHERE] * 4 + [WHOLE] * 4,
         out_specs=(WHOLE,) * 5,
         scratch_shapes=[
-            pltpu.VMEM((length // 2, tiles, LANES), F32),
+            pltpu.VMEM((length // CUT, tiles, LANES), F32),
             pltpu.VMEM((width, width), BF),
             COPIES,
         ],
@@ -425,7 +450,7 @@
         ),
         in_specs=[SMALL] * 2 + [ANYWHERE] * 2 + [WHOLE] * 5,
         out_specs=(WHOLE, WHOLE),
-        scratch_shapes=[pltpu.VMEM((length // 2, tiles, LANES), F32), COPIES],
+        scratch_shapes=[pltpu.VMEM((length - length // CUT, tiles, LANES), F32), COPIES],
         compiler_params=pltpu.CompilerParams(vmem_limit_bytes=VMEM),
         cost_estimate=pl.CostEstimate(
             flops=10 * length * width * width,
@@ -810,9 +835,9 @@
 FTILE = 512
 
 
-def feed_forward_kernel(part, *refs):
-    ins, refs = refs[: 5 + 4 * (part > 0)], refs[5 + 4 * (part > 0) :]
-    own_ref, other_ref, cot_ref, up_in_ref, down_in_ref = ins[:5]
+def feed_forward_kernel(part, blocks, place_ref, own_ref, other_ref, cot_ref, *refs):
+    pieces, refs = refs[: sum(b[0] for b in blocks)], refs[sum(b[0] for b in blocks) :]
+    ins, refs = refs[: 4 * part], refs[4 * part :]
     outs, grads, refs = refs[:4], refs[4:6], refs[6:]
     normed_ref, cots_ref, up_ref, down_ref, hidden_ref, gpre_ref, sums_ref, total_ref = refs[:8]
     row_sems, weight_sems, out_sems, grad_sems = refs[8:12]
@@ -825,12 +850,19 @@
     def tile_of(i):
         return pl.ds(pl.multiple_of(i * tile, tile), tile)
 
-    weights = [
-        pltpu.make_async_copy(up_in_ref, up_ref, weight_sems.at[0]),
-        pltpu.make_async_copy(down_in_ref, down_ref, weight_sems.at[1]),
-    ]
-    for copy in weights:
-        copy.start()
+    weights = []
+    for k, (ref, (number, (many, rows))) in enumerate(zip((up_ref, down_ref), blocks)):
+        for p in range(number):
+            source = pieces[k * blocks[0][0] + p]
+            place = place_ref[k] if p == 0 else 1 - place_ref[k]
+            for h in range(many):
+                at = (2 * h + place) * rows if number == 2 else 0
+                pltpu.make_async_copy(
+                    source.at[pl.ds(h * rows, rows)],
+                    ref.at[pl.ds(pl.multiple_of(at, 16), rows)],
+                    weight_sems.at[k],
+                ).start()
+        weights.append(pltpu.make_async_copy(ref, ref, weight_sems.at[k]))
     for i in range(count):
         rows = tile_of(i % per)
         source = (own_ref, other_ref)[i // per]
@@ -840,7 +872,7 @@
         ).start()
     if part:
         earlier = [
-            pltpu.make_async_copy(ins[5 + k], total_ref.at[k], out_sems.at[k, count])
+            pltpu.make_async_copy(ins[k], total_ref.at[k], out_sems.at[k, count])
             for k in range(4)
         ]
         for copy in earlier:
@@ -897,14 +929,17 @@
 
 def feed_forward(part, own, other, cot, up, down, earlier):
     length, width = own.shape
-    units = up.shape[1]
+    pieces, blocks, places = zip(*(chain.parts() for chain in (up, down)))
+    blocks = tuple((len(p), b) for p, b in zip(pieces, blocks))
+    pieces = [p for each in pieces for p in each]
+    units = pieces[0].shape[1]
     count = 2 * length // FTILE
     dma = pltpu.SemaphoreType.DMA
     return pl.pallas_call(
-        functools.partial(feed_forward_kernel, part),
+        functools.partial(feed_forward_kernel, part, blocks),
         out_shape=(jax.ShapeDtypeStruct((length, width), BF),) * 4
         + (jax.ShapeDtypeStruct((width, units), BF),) * 2,
-        in_specs=[ANYWHERE] * (9 if part else 5),
+        in_specs=[SMALL] + [ANYWHERE] * (3 + len(pieces) + 4 * part),
         out_specs=(ANYWHERE,) * 6,
         scratch_shapes=[pltpu.VMEM((2 * length, width), BF)] * 2
         + [pltpu.VMEM((width, units), BF)] * 2
@@ -918,7 +953,7 @@
             transcendentals=4 * length * units,
         ),
         name="feed_forward",
-    )(own, other, cot, up, down, *earlier)
+    )(jnp.stack(places), own, other, cot, *pieces, *earlier)
 
 
 def at_first(joins, sems, side):
@@ -1128,28 +1163,55 @@
 
 
 def weight_grads_kernel(count, side_ref, *refs):
-    lefts, rights = refs[: len(refs) - 2 - count], refs[len(refs) - 2 - count : -2]
-    theirs_ref, mine_ref = refs[-2:]
-    cols = rights[0].shape[1] // 2
+    ins, outs, refs = refs[:-6], refs[-6:-4], refs[-4:]
+    held_ref, sums_ref, in_sems, out_sems = refs
+    lefts = len(ins) - count
+    width = held_ref.shape[2]
+    cols = width // 2
     side = side_ref[0]
+    order = []
     for k in range(count):
-        for ref, at in ((theirs_ref, 1 - side), (mine_ref, side)):
-            part = rights[k][:, pl.ds(pl.multiple_of(at * cols, cols), cols)]
-            ref[:, k * cols : (k + 1) * cols] = dot_first(
-                lefts[k % len(lefts)][...], part
-            ).astype(BF)
+        order += [k % lefts, lefts + k]
+    order = list(dict.fromkeys(order))
+    loads = {
+        j: pltpu.make_async_copy(ins[j], held_ref.at[j], in_sems.at[j]) for j in order
+    }
+    for j in order:
+        loads[j].start()
+    stores = []
+    for k in range(count):
+        for j in (k % lefts, lefts + k):
+            if j in loads:
+                loads.pop(j).wait()
+        for which, at in enumerate((1 - side, side)):
+            part = held_ref[lefts + k, :, pl.ds(pl.multiple_of(at * cols, cols), cols)]
+            sums_ref[which, k] = dot_first(held_ref[k % lefts], part).astype(BF)
+            copy = pltpu.make_async_copy(
+                sums_ref.at[which, k],
+                outs[which].at[:, k * cols : (k + 1) * cols],
+                out_sems.at[which, k],
+            )
+            copy.start()
+            stores.append(copy)
+    wait_all(stores)
 
 
 def weight_grads(side, lefts, rights):
     count = len(rights)
     length, width = lefts[0].shape
     cols = width // 2
-    vm = pl.BlockSpec(memory_space=pltpu.VMEM)
+    many = len(lefts) + count
     return pl.pallas_call(
         functools.partial(weight_grads_kernel, count),
         out_shape=(jax.ShapeDtypeStruct((width, count * cols), BF),) * 2,
-        in_specs=[SMALL] + [vm] * (len(lefts) + count),
-        out_specs=(vm,) * 2,
+        in_specs=[SMALL] + [ANYWHERE] * many,
+        out_specs=(ANYWHERE,) * 2,
+        scratch_shapes=[
+            pltpu.VMEM((many, length, width), BF),
+            pltpu.VMEM((2, count, width, cols), BF),
+            pltpu.SemaphoreType.DMA((many,)),
+            pltpu.SemaphoreType.DMA((2, count)),
+        ],
         compiler_params=pltpu.CompilerParams(vmem_limit_bytes=VMEM),
         cost_estimate=pl.CostEstimate(
             flops=2 * count * length * width * width,
@@ -1264,7 +1326,7 @@
     left, right = ((h, pair(h)) for h in (m.result() for m in attn))
     while len(ffn[0][0].left) > 2:
         step(ffn[0])
-    ffn[0] = ffn[0][0].split(both_ways)
+    ffn[0] = ffn[0][0].split(both_ways, True)
     send(ffn[0] + ffn[1])
     query, key, value = project(at_side, normed, ssm_out, left, right)
     query = fence(ffn[0], query)
@@ -1273,7 +1335,7 @@
     attended = fence(ffn[0] + ffn[1], attended)
     while len(ffn[1][0].left) > 2:
         step(ffn[1])
-    ffn[1] = ffn[1][0].split(both_ways)
+    ffn[1] = ffn[1][0].split(both_ways, True)
     send(ffn[1])
     middle, normed_two = middle_of(at_side, attended, right, rows, gain_two, bias_two)
 
@@ -1285,13 +1347,13 @@
 
     normed_other = pair(normed_two)
     *both, grad_up, grad_down = feed_forward(
-        0, normed_two, normed_other, cot, *(m.result() for m in ffn[0]), ()
+        0, normed_two, normed_other, cot, *ffn[0], ()
     )
     both, grad_up, grad_down = fence(ffn[1], both, grad_up, grad_down)
     sums_one = scatters(grad_up, grad_down)
     send(sums_one)
     own, other, gown, gother, grad_up, grad_down = feed_forward(
-        1, normed_two, normed_other, cot, *(m.result() for m in ffn[1]), both
+        1, normed_two, normed_other, cot, *ffn[1], both
     )
     own, other, gown, gother, grad_up, grad_down = fence(
         sums_one, own, other, gown, gother, grad_up, grad_down
@@ -1303,11 +1365,14 @@
         at_side, gown, pair(gother), middle, cot, gain_two, right
     )
     grad_attended = fence(sums_one, grad_attended)
-    send(sums_two)
+    join_chains(sums_one)
+    send(sums_one + sums_two)
     grad_query, grad_key, grad_value = attention_backward(
         seg_col, seg_row, query, key, value, lse, grad_attended
     )
-    grad_query, grad_key, grad_value = fence(sums_two, grad_query, grad_key, grad_value)
+    grad_query, grad_key, grad_value = fence(
+        sums_one + sums_two, grad_query, grad_key, grad_value
+    )
     send(sums_two)
 
     def pair_sum(theirs, mine):
@@ -1319,28 +1384,29 @@
     sums_left = pair_sum(*grads_left)
     grads_right = fence(sums_two, grads_right)
     sums_attn = scatters(sums_left, pair_sum(*grads_right))
-    sums_ffn = sums_one + sums_two
-    join_chains(sums_ffn)
-    send(sums_attn + sums_ffn)
+    join_chains(sums_two)
+    send(sums_attn + sums_two)
     g_steps, gm_steps, sum_one, dsum_one = ssm_backward(
         starts, at_side, grad_key, grad_value, left, right, drive, decay, coef
     )
-    g_steps, gm_steps = fence(sums_attn, g_steps, gm_steps)
+    g_steps, gm_steps = fence(sums_attn + sums_two, g_steps, gm_steps)
     send(sums_attn)
     grad_mixed, sum_two, dsum_two = ssm_backward_rest(
         starts, g_steps, gm_steps, drive, decay, coef
     )
-    grad_mixed = fence(sums_attn + sums_ffn, grad_mixed)
+    grad_mixed = fence(sums_attn, grad_mixed)
     join_chains(sums_attn)
     send(sums_attn)
     grads_mix = weight_grads(at_side, (normed,), (grad_mixed,))
     grads_mix, grad_mixed = tie(grads_mix, grad_mixed)
     sums_mix = [Scatter(pair_sum(*grads_mix), count, index, DIRECT)]
+    sums_mix[0].values, grad_mixed = tie(sums_mix[0].values, grad_mixed)
+    send(sums_mix)
     for_partner, norm_one_first = norm_one_back(
         at_side, grad_query, grad_mixed, rows, grad_middle, gain_one, left, mix_both, True
     )
-    for_partner, grad_mixed, sums_mix[0].values = fence(
-        sums_attn, for_partner, grad_mixed, sums_mix[0].values
+    for_partner, norm_one_first, grad_mixed = fence(
+        sums_mix + sums_attn, for_partner, norm_one_first, grad_mixed
     )
     send(sums_mix)
     got_grad = pair(for_partner)
@@ -1363,7 +1429,7 @@
     )
     mine = lax.dynamic_slice_in_dim(state_sums, side * cols, cols, 1)
     small = [Total(jnp.concatenate([mine, sums[2 * states :]]) + pair(sums), count)]
-    send(sums_mix + small)
+    send(small)
     in_half = (1 - side) * half
     partner_sum = pair(
         lax.dynamic_slice_in_dim(middle, in_half, half, 0)
@@ -1371,20 +1437,18 @@
     )
     partner_other = pair(lax.dynamic_slice_in_dim(other, in_half, half, 0))
     in_grad = put(at_side, got_grad, in_grad)
-    in_grad, middle = fence(sums_mix + small, in_grad, middle)
+    in_grad, middle = fence(small, in_grad, middle)
     send(small)
     layer_out = layer_out_of(at_side, middle, own, other, partner_sum, partner_other)
     layer_out = fence(small, layer_out)
-    complete(sums_mix + small + sums_attn + sums_ffn)
+    complete(sums_mix + small + sums_attn + sums_one + sums_two)
     small = small[0].values
     total, dtotal = small[:states], small[states : 2 * states]
     norm_sums = lax.dynamic_slice_in_dim(
         small[2 * states :].reshape(4, width), index * shard_rows, shard_rows, 1
     )
     shard_attn = sums_attn[0].result()
-    ups, downs = (
-        [sums_ffn[0].result()[:, k * units : (k + 1) * units] for k in at] for at in ((0, 2), (1, 3))
-    )
+    shards = [sums_one[0].result(), sums_two[0].result()]
     return (
         layer_out[:, None],
         in_grad[:, None],
@@ -1393,8 +1457,8 @@
         shard_attn[:, 2 * cols : 3 * cols],
         shard_attn[:, 3 * cols :],
         shard_attn[:, cols : 2 * cols].T,
-        jnp.concatenate(ups, axis=1),
-        jnp.concatenate(downs, axis=1).T,
+        jnp.concatenate([v[:, :units] for v in shards], axis=1),
+        jnp.concatenate([v[:, units:] for v in shards], axis=1).T,
         norm_sums[0],
         norm_sums[1],
         norm_sums[2],

time: 514 us -> 482 us (0.938)
  waiting for transfers between devices: 61.7 us -> 43.4 us
  other arithmetic: 48.2 us -> 34.7 us
  local copies, waits for them, and re-layouts: 31.6 us -> 37.3 us
    ppermute x57 -> x60, waiting for transfers between devices: 57.6 us -> 36.1 us  [swap(): return lax.ppermute(values, 'dp', [(i, i ^ mask) for i in range(count)])]
    select_n x25 -> x21, other arithmetic: 15.3 us -> 6.83 us  [in_order(): jnp.where(upper, jnp.stack([got, own], axis=axis), jnp.stack([own, got],...]
    ppermute x57 -> x60, starting transfers between devices: 97 us -> 92.5 us  [swap(): return lax.ppermute(values, 'dp', [(i, i ^ mask) for i in range(count)])]
    optimization_barrier x6 -> x10, local copies, waits for them, and re-layouts: 8.47 us -> 10.3 us  [tie(): return lax.optimization_barrier(trees)]
  transfers between devices with their start and end apart: 72 -> 75, of which waited for: 19 -> 14; matrix products, arithmetic and copies ran while one was open for 8% -> 6% of each run, Pallas kernels for 51% -> 54%
where the time goes in v4:
time: 482 us; the launch traced here: 475 us
  Pallas kernels  263 us (55%)
  starting transfers between devices  94.6 us (20%)
  waiting for transfers between devices  43.4 us (9%)
  local copies, waits for them, and re-layouts  37.3 us (8%)
  other arithmetic  34.7 us (7%)
    ppermute x60, starting transfers between devices, swap(): return lax.ppermute(values, 'dp', [(i, i ^ mask) for i in range(count)])  92.5 us
    pallas_call x2, Pallas kernels, feed_forward(): pl.pallas_call(functools.partial(feed_forward_kernel, part, blocks), out_...  71.9 us
    ppermute x60, waiting for transfers between devices, swap(): return lax.ppermute(values, 'dp', [(i, i ^ mask) for i in range(count)])  36.1 us
    pallas_call x1, Pallas kernels, ssm_backward(): pl.pallas_call(ssm_backward_kernel, out_shape=(jax.ShapeDtypeStruct((leng...  28.7 us
    pallas_call x1, Pallas kernels, ssm_backward_rest(): pl.pallas_call(ssm_backward_rest_kernel, out_shape=(jax.ShapeDtypeStruct(...  22.8 us
    pallas_call x3, Pallas kernels, weight_grads(): pl.pallas_call(functools.partial(weight_grads_kernel, count), out_shape=(...  21.8 us
    pallas_call x2, Pallas kernels, norm_one_back(): pl.pallas_call(norm_one_kernel, grid_spec=pltpu.PrefetchScalarGridSpec(nu...  17.8 us
    pallas_call x1, Pallas kernels, attention_backward(): pl.pallas_call(attention_backward_kernel, grid=(heads // HEADS_EACH,), ou...  17.2 us
  transfers between devices with their start and end apart: 75, of which 14 were waited for; matrix products, arithmetic and copies ran while one was open for 6% of the time, Pallas kernels for 54%

profile of v4, /device:TPU:0, one launch (start us, length us, event | category | flops | bytes accessed | tf_op | source)
XLA Modules:
  0.0 474.9 jit_solution(11056878735930951544)
XLA Ops:
  2.3 3.0 collective-permute-start
  5.3 2.6 collective-permute-start.1
  8.9 4.2 collective-permute-done.1
  18.9 1.7 collective-permute-start.7
  20.6 2.3 collective-permute-done.6
  22.9 1.7 collective-permute-start.8
  25.4 13.3 %collective-permute-done.7 = bf16[64,2048]{1,0:T(8,128)(2,1)S(1)} collective-permute-done((bf16[64,2048]{1,0:T(8,128)(2,1)S(1)}, bf16[64,2048]{1,0:T(8,128)(2,1)S(1)}, u32[]{:S(2)}, u32[]{:S(2)}) %collective-permute-start.7) | collective-permute-done | bytes 262176 | tf_op jit(solution)/shard_map/ppermute | solution.py:67
  48.0 15.1 %ssm_forward.1 = (bf16[1024,1024]{1,0:T(8,128)(2,1)}, bf16[1024,1024]{1,0:T(8,128)(2,1)}, f32[1024,8,128]{2,1,0:T(8,128)}, bf16[256,1024]{1,0:T(8,128)(2,1)}, f32[16,8,128]{2,1,0:T(8,128)}) custom-call(s32[16]{0:T(128)} %convert_reduce_fusion.starts_ref, s32[1]{0:T(128)} %bitcast.1.side_ref, bf16[2,512,1024]{2,1,0:T(8,128)(2,1)} %bitcast.304, ...), custom_call_target="tpu_custom_call" | custom-call | flops 12884901888 | bytes 16777216 | tf_op jit(solution)/shard_map/ssm_forward/pallas_call | solution.py:416
  66.1 3.6 collective-permute-start.16
  73.8 16.4 %ssm_rest.1 = (bf16[1024,1024]{1,0:T(8,128)(2,1)}, bf16[2,1024,1024]{2,1,0:T(8,128)(2,1)}) custom-call(s32[16]{0:T(128)} %convert_reduce_fusion.starts_ref, s32[1]{0:T(128)} %bitcast.1.side_ref, bf16[2,512,1024]{2,1,0:T(8,128)(2,1)} %bitcast.305, bf16[2,512,1024]{2,1,0:T(8,128)(2,1)} %copy-done.47, f32[1024,8,128]{2,1,0:T(8,128)} %get-tuple-element.337.drive_ref, ...), custom_call_target="tpu_custom_call" | custom-call | flops 10737418240 | bytes 16777216 | tf_op jit(solution)/shard_map/ssm_rest/pallas_call | solution.py:445
  96.7 2.8 collective-permute-done.23.right_other_ref.other_ref
  100.9 12.2 %project.1 = (bf16[1024,1024]{1,0:T(8,128)(2,1)}, bf16[1024,1024]{1,0:T(8,128)(2,1)}, bf16[1024,1024]{1,0:T(8,128)(2,1)}) custom-call(s32[1]{0:T(128)} %bitcast.1.side_ref, bf16[1024,1024]{1,0:T(8,128)(2,1)} %get-tuple-element.352.normed_ref.refs_0_, bf16[1024,1024]{1,0:T(8,128)(2,1)} %get-tuple-element.486.ssm_ref.refs_0_, bf16[1024,1024]{1,0:T(8,128)(2,1)} %bitcast.215, ...), custom_call_target="tpu_custom_call" | custom-call | flops 6442450944 | bytes 16777216 | tf_op jit(solution)/shard_map/project/pallas_call | solution.py:494
  117.5 4.8 %collective-permute-start.26 = (bf16[64,2048]{1,0:T(8,128)(2,1)S(1)}, bf16[64,2048]{1,0:T(8,128)(2,1)S(1)}, u32[]{:S(2)}, u32[]{:S(2)}) collective-permute-start(bf16[64,2048]{1,0:T(8,128)(2,1)S(1)} %get-tuple-element.378), channel_id=1, source_target_pairs={{0,8},{2,10},{4,12},{6,14},{8,0},{10,2},{12,4},{14,6},{16,24},{18,... | collective-permute-start | bytes 786440 | tf_op jit(solution)/shard_map/ppermute | solution.py:67
  125.9 10.7 %attention_forward.1 = (bf16[1024,1024]{1,0:T(8,128)(2,1)}, f32[8,1024,1]{2,1,0:T(8,128)}) custom-call(s32[1024,1]{1,0:T(8,128)} %copy.95.seg_col_ref, s32[1,1024]{1,0:T(1,128)} %fusion.36.seg_row_ref, bf16[1024,1024]{1,0:T(8,128)(2,1)} %get-tuple-element.367.query_ref, bf16[1024,1024]{1,0:T(8,128)(2,1)} %get-tuple-element.368.key_ref, ...), custom_call_target="tpu_custom_call" | custom-call | flops 1879048192 | bytes 8388608 | tf_op jit(solution)/shard_map/attention_forward/pallas_call | solution.py:726
  136.6 7.1 %collective-permute-done.27 = bf16[64,2048]{1,0:T(8,128)(2,1)S(1)} collective-permute-done((bf16[64,2048]{1,0:T(8,128)(2,1)S(1)}, bf16[64,2048]{1,0:T(8,128)(2,1)S(1)}, u32[]{:S(2)}, u32[]{:S(2)}) %collective-permute-start.27) | collective-permute-done | bytes 262176 | tf_op jit(solution)/shard_map/ppermute | solution.py:67
  147.6 8.6 %middle.1 = (f32[1024,1024]{1,0:T(8,128)}, bf16[1024,1024]{1,0:T(8,128)(2,1)}) custom-call(s32[1]{0:T(128)} %bitcast.1.side_ref, bf16[1024,1024]{1,0:T(8,128)(2,1)} %get-tuple-element.383.attended_ref.refs_3_, bf16[1024,1024]{1,0:T(8,128)(2,1)} %bitcast.211, bf16[1024,1024]{1,0:T(8,128)(2,1)} %copy-done.6, bf16[1024,1024]{1,0:T(8,128)(2,1)} %get-tuple-element.384.rows_ref, ...), custom_call_target="tpu_custom_call" | custom-call | flops 2147483648 | bytes 12582912 | tf_op jit(solution)/shard_map/middle/pallas_call | solution.py:994
  156.6 1.8 maximum_select_fusion.11
  158.4 2.4 maximum_select_fusion.10
  164.7 2.3 copy.99
  169.5 34.8 %feed_forward.2 = (bf16[1024,1024]{1,0:T(8,128)(2,1)}, bf16[1024,1024]{1,0:T(8,128)(2,1)}, bf16[1024,1024]{1,0:T(8,128)(2,1)}, bf16[1024,1024]{1,0:T(8,128)(2,1)...) custom-call(s32[2]{0:T(128)} %pad_add_fusion.place_ref, bf16[1024,1024]{1,0:T(8,128)(2,1)} %get-tuple-element.397.own_ref, ...), custom_call_target="tpu_custom_call" | custom-call | flops 30064771072 | bytes 50331648 | tf_op jit(solution)/shard_map/feed_forward/pallas_call | solution.py:938
  210.7 37.1 %feed_forward.3 = (bf16[1024,1024]{1,0:T(8,128)(2,1)}, bf16[1024,1024]{1,0:T(8,128)(2,1)}, bf16[1024,1024]{1,0:T(8,128)(2,1)}, bf16[1024,1024]{1,0:T(8,128)(2,1)...) custom-call(s32[2]{0:T(128)} %pad_add_fusion.place_ref, bf16[1024,1024]{1,0:T(8,128)(2,1)} %get-tuple-element.397.own_ref, ...), custom_call_target="tpu_custom_call" | custom-call | flops 30064771072 | bytes 50331648 | tf_op jit(solution)/shard_map/feed_forward/pallas_call | solution.py:938
  248.3 1.8 fusion.5
  252.6 1.8 collective-permute-done.38.theirs_ref
  255.8 12.0 %norm_two_back.1 = (f32[1024,1024]{1,0:T(8,128)}, bf16[1024,1024]{1,0:T(8,128)(2,1)}, bf16[1024,1024]{1,0:T(8,128)(2,1)}, f32[2,1024]{1,0:T(2,128)}) custom-call(s32[1]{0:T(128)} %bitcast.1.side_ref, bf16[1024,1024]{1,0:T(8,128)(2,1)} %get-tuple-element.441.mine_ref, bf16[1024,1024]{1,0:T(8,128)(2,1)} %copy-done.23, ...), custom_call_target="tpu_custom_call" | custom-call | flops 2147483648 | bytes 25165824 | tf_op jit(solution)/shard_map/norm_two_back/pallas_call | solution.py:1040
  274.0 5.2 %collective-permute-start.39 = (bf16[64,2048]{1,0:T(8,128)(2,1)S(1)}, bf16[64,2048]{1,0:T(8,128)(2,1)S(1)}, u32[]{:S(2)}, u32[]{:S(2)}) collective-permute-start(bf16[64,2048]{1,0:T(8,128)(2,1)S(1)} %get-tuple-element.655), channel_id=1, source_target_pairs={{0,8},{2,10},{4,12},{6,14},{8,0},{10,2},{12,4},{14,6},{16,24},{18,... | collective-permute-start | bytes 786440 | tf_op jit(solution)/shard_map/ppermute | solution.py:67
  282.2 17.2 %attention_backward.1 = (bf16[1024,1024]{1,0:T(8,128)(2,1)}, bf16[1024,1024]{1,0:T(8,128)(2,1)}, bf16[1024,1024]{1,0:T(8,128)(2,1)}) custom-call(s32[1024,1]{1,0:T(8,128)} %copy.95.seg_col_ref, s32[1,1024]{1,0:T(1,128)} %fusion.36.seg_row_ref, bf16[1024,1024]{1,0:T(8,128)(2,1)} %get-tuple-element.367.query_ref, ...), custom_call_target="tpu_custom_call" | custom-call | flops 4697620480 | bytes 14680064 | tf_op jit(solution)/shard_map/attention_backward/pallas_call | solution.py:794
  300.6 1.7 fusion.2
  302.3 1.6 fusion.3
  307.5 8.1 %weight_grads.3 = (bf16[1024,1024]{1,0:T(8,128)(2,1)}, bf16[1024,1024]{1,0:T(8,128)(2,1)}) custom-call(s32[1]{0:T(128)} %bitcast.1.side_ref, bf16[1024,1024]{1,0:T(8,128)(2,1)} %get-tuple-element.352.normed_ref.refs_0_, bf16[1024,1024]{1,0:T(8,128)(2,1)} %get-tuple-element.476.refs_1_, bf16[1024,1024]{1,0:T(8,128)(2,1)} %get-tuple-element.477.refs_2_.gquery_ref, ...), custom_call_target="tpu_custom_call" | custom-call | flops 4294967296 | bytes 12582912 | tf_op jit(solution)/shard_map/weight_grads/pallas_call | solution.py:1204
  315.7 8.1 %weight_grads.4 = (bf16[1024,1024]{1,0:T(8,128)(2,1)}, bf16[1024,1024]{1,0:T(8,128)(2,1)}) custom-call(s32[1]{0:T(128)} %bitcast.1.side_ref, bf16[1024,1024]{1,0:T(8,128)(2,1)} %get-tuple-element.486.ssm_ref.refs_0_, bf16[1024,1024]{1,0:T(8,128)(2,1)} %get-tuple-element.473.gkey_ref.refs_1_, bf16[1024,1024]{1,0:T(8,128)(2,1)} %get-tuple-element.474.gvalue_ref.refs_2_), custom_call_target="tpu_custom_call" | custom-call | flops 4294967296 | bytes 12582912 | tf_op jit(solution)/shard_map/weight_grads/pallas_call | solution.py:1204
  327.1 2.6 collective-permute-done.47
  331.6 4.5 collective-permute-start.50
  341.0 28.7 %ssm_backward.1 = (f32[1024,8,128]{2,1,0:T(8,128)}, f32[1024,8,128]{2,1,0:T(8,128)}, f32[8,8,128]{2,1,0:T(8,128)}, f32[8,8,128]{2,1,0:T(8,128)}) custom-call(s32[16]{0:T(128)} %convert_reduce_fusion.starts_ref, s32[1]{0:T(128)} %bitcast.1.side_ref, bf16[1024,1024]{1,0:T(8,128)(2,1)} %get-tuple-element.473.gkey_ref.refs_1_, ...), custom_call_target="tpu_custom_call" | custom-call | flops 21474836480 | bytes 20971520 | tf_op jit(solution)/shard_map/ssm_backward/pallas_call | solution.py:598
  369.7 1.7 fusion
  371.4 1.7 fusion.1
  375.9 22.8 %ssm_backward_rest.1 = (bf16[1024,1024]{1,0:T(8,128)(2,1)}, f32[8,8,128]{2,1,0:T(8,128)}, f32[8,8,128]{2,1,0:T(8,128)}) custom-call(s32[16]{0:T(128)} %convert_reduce_fusion.starts_ref, f32[1024,8,128]{2,1,0:T(8,128)} %get-tuple-element.514.g_ref, f32[1024,8,128]{2,1,0:T(8,128)} %get-tuple-element.515.given_ref, ...), custom_call_target="tpu_custom_call" | custom-call | flops 21474836480 | bytes 20971520 | tf_op jit(solution)/shard_map/ssm_backward_rest/pallas_call | solution.py:624
  399.2 5.6 %weight_grads.5 = (bf16[1024,512]{1,0:T(8,128)(2,1)}, bf16[1024,512]{1,0:T(8,128)(2,1)}) custom-call(s32[1]{0:T(128)} %bitcast.1.side_ref, bf16[1024,1024]{1,0:T(8,128)(2,1)} %get-tuple-element.352.normed_ref.refs_0_, bf16[1024,1024]{1,0:T(8,128)(2,1)} %get-tuple-element.555.refs_1_.gmixed_ref), custom_call_target="tpu_custom_call" | custom-call | flops 2147483648 | bytes 6291456 | tf_op jit(solution)/shard_map/weight_grads/pallas_call | solution.py:1204
  405.9 2.3 collective-permute-start.60
  413.8 5.4 %collective-permute-done.59 = bf16[64,2048]{1,0:T(8,128)(2,1)S(1)} collective-permute-done((bf16[64,2048]{1,0:T(8,128)(2,1)S(1)}, bf16[64,2048]{1,0:T(8,128)(2,1)S(1)}, u32[]{:S(2)}, u32[]{:S(2)}) %collective-permute-start.59) | collective-permute-done | bytes 262176 | tf_op jit(solution)/shard_map/ppermute | solution.py:67
  420.2 8.7 %norm_one_back.2 = (f32[512,1024]{1,0:T(8,128)}, f32[2,1024]{1,0:T(2,128)}) custom-call(s32[1]{0:T(128)} %bitcast.1.side_ref, bf16[1024,1024]{1,0:T(8,128)(2,1)} %get-tuple-element.477.refs_2_.gquery_ref, bf16[1024,1024]{1,0:T(8,128)(2,1)} %get-tuple-element.555.refs_1_.gmixed_ref, bf16[1024,1024]{1,0:T(8,128)(2,1)} %get-tuple-element.384.rows_ref, ...), custom_call_target="tpu_custom_call" | custom-call | flops 2147483648 | bytes 10485760 | tf_op jit(solution)/shard_map/norm_one_back/pallas_call | solution.py:1095
  431.6 3.8 collective-permute-start.62
  435.3 1.6 collective-permute-start.63
  438.4 9.1 %norm_one_back.3 = (f32[2,512,1024]{2,1,0:T(8,128)}, f32[2,1024]{1,0:T(2,128)}) custom-call(s32[1]{0:T(128)} %bitcast.1.side_ref, bf16[1024,1024]{1,0:T(8,128)(2,1)} %get-tuple-element.477.refs_2_.gquery_ref, bf16[1024,1024]{1,0:T(8,128)(2,1)} %get-tuple-element.555.refs_1_.gmixed_ref, bf16[1024,1024]{1,0:T(8,128)(2,1)} %get-tuple-element.384.rows_ref, ...), custom_call_target="tpu_custom_call" | custom-call | flops 2147483648 | bytes 10485760 | tf_op jit(solution)/shard_map/norm_one_back/pallas_call | solution.py:1095
  448.3 1.8 convert_add_fusion.6
  456.6 2.0 collective-permute-start.68
  459.4 2.6 put.1
  464.9 1.9 collective-permute-start.72
  468.7 4.6 layer_out.1
  (342 shorter events, 115.0 us)
Async XLA Ops:
  15.4 23.9 %collective-permute-start.3 = (bf16[2,2,72,512]{3,2,1,0:T(8,128)(2,1)S(1)}, bf16[2,2,72,512]{3,2,1,0:T(8,128)(2,1)S(1)}, u32[]{:S(2)}, u32[]{:S(2)}) collective-permute-start(bf16[2,2,72,512]{3,2,1,0:T(8,128)(2,1)S(1)} %maximum_select_fusion.19), channel_id=1, source_target_pairs={{0,2},{2,0},{4,6},{6,4},{8,10},{10,8},{12,14},{14,12},{16,18},{18,... | collective-permute-start | bytes 884744 | tf_op jit(solution)/shard_map/ppermute | solution.py:67
  16.9 22.4 %collective-permute-start.4 = (bf16[2,2,72,512]{3,2,1,0:T(8,128)(2,1)S(1)}, bf16[2,2,72,512]{3,2,1,0:T(8,128)(2,1)S(1)}, u32[]{:S(2)}, u32[]{:S(2)}) collective-permute-start(bf16[2,2,72,512]{3,2,1,0:T(8,128)(2,1)S(1)} %maximum_select_fusion.19), channel_id=1, source_target_pairs={{0,4},{2,6},{4,0},{6,2},{8,12},{10,14},{12,8},{14,10},{16,20},{18,... | collective-permute-start | bytes 884744 | tf_op jit(solution)/shard_map/ppermute | solution.py:67
  18.4 20.9 %collective-permute-start.5 = (bf16[2,2,72,512]{3,2,1,0:T(8,128)(2,1)S(1)}, bf16[2,2,72,512]{3,2,1,0:T(8,128)(2,1)S(1)}, u32[]{:S(2)}, u32[]{:S(2)}) collective-permute-start(bf16[2,2,72,512]{3,2,1,0:T(8,128)(2,1)S(1)} %maximum_select_fusion.19), channel_id=1, source_target_pairs={{0,6},{2,4},{4,2},{6,0},{8,14},{10,12},{12,10},{14,8},{16,22},{18,... | collective-permute-start | bytes 884744 | tf_op jit(solution)/shard_map/ppermute | solution.py:67
  18.9 19.9 %collective-permute-start.7 = (bf16[64,2048]{1,0:T(8,128)(2,1)S(1)}, bf16[64,2048]{1,0:T(8,128)(2,1)S(1)}, u32[]{:S(2)}, u32[]{:S(2)}) collective-permute-start(bf16[64,2048]{1,0:T(8,128)(2,1)S(1)} %pad_maximum_fusion.6), channel_id=1, source_target_pairs={{0,16},{2,18},{4,20},{6,22},{8,24},{10,26},{12,28},{14,30},{16,0},... | collective-permute-start | bytes 786440 | tf_op jit(solution)/shard_map/ppermute | solution.py:67
  22.9 15.9 %collective-permute-start.8 = (bf16[64,2048]{1,0:T(8,128)(2,1)S(1)}, bf16[64,2048]{1,0:T(8,128)(2,1)S(1)}, u32[]{:S(2)}, u32[]{:S(2)}) collective-permute-start(bf16[64,2048]{1,0:T(8,128)(2,1)S(1)} %pad_maximum_fusion.6), channel_id=1, source_target_pairs={{0,24},{2,26},{4,28},{6,30},{8,16},{10,18},{12,20},{14,22},{16,8},... | collective-permute-start | bytes 786440 | tf_op jit(solution)/shard_map/ppermute | solution.py:67
  43.9 19.2 %collective-permute-start.10 = (bf16[2,2,64,1024]{3,2,1,0:T(8,128)(2,1)S(1)}, bf16[2,2,64,1024]{3,2,1,0:T(8,128)(2,1)S(1)}, u32[]{:S(2)}, u32[]{:S(2)}) collective-permute-start(bf16[2,2,64,1024]{3,2,1,0:T(8,128)(2,1)S(1)} %get-tuple-element.328), channel_id=1, source_target_pairs={{0,4},{2,6},{4,0},{6,2},{8,12},{10,14},{12,8},{14,10},{16,20},{18,... | collective-permute-start | bytes 1572872 | tf_op jit(solution)/shard_map/ppermute | solution.py:67
  45.5 17.7 %collective-permute-start.9 = (bf16[2,2,64,1024]{3,2,1,0:T(8,128)(2,1)S(1)}, bf16[2,2,64,1024]{3,2,1,0:T(8,128)(2,1)S(1)}, u32[]{:S(2)}, u32[]{:S(2)}) collective-permute-start(bf16[2,2,64,1024]{3,2,1,0:T(8,128)(2,1)S(1)} %get-tuple-element.326), channel_id=1, source_target_pairs={{0,2},{2,0},{4,6},{6,4},{8,10},{10,8},{12,14},{14,12},{16,18},{18,... | collective-permute-start | bytes 1572872 | tf_op jit(solution)/shard_map/ppermute | solution.py:67
  64.9 26.1 %collective-permute-start.14 = (bf16[2,2,2,64,1024]{4,3,1,0,2:T(8,128)(2,1)S(1)}, bf16[2,2,2,64,1024]{4,3,1,0,2:T(8,128)(2,1)S(1)}, u32[]{:S(2)}, u32[]{:S(2)}) collective-permute-start(bf16[2,2,2,64,1024]{4,3,1,0,2:T(8,128)(2,1)S(1)} %maximum_select_fusion.4), channel_id=1, source_target_pairs={{0,4},{2,6},{4,0},{6,2},{8,12},{10,14},{12,8},{14,10},{16,20},{18,... | collective-permute-start | bytes 3145736 | tf_op jit(solution)/shard_map/ppermute | solution.py:67
  65.6 25.5 %collective-permute-start.15 = (bf16[2,2,2,64,1024]{4,3,1,0,2:T(8,128)(2,1)S(1)}, bf16[2,2,2,64,1024]{4,3,1,0,2:T(8,128)(2,1)S(1)}, u32[]{:S(2)}, u32[]{:S(2)}) collective-permute-start(bf16[2,2,2,64,1024]{4,3,1,0,2:T(8,128)(2,1)S(1)} %maximum_select_fusion.5), channel_id=1, source_target_pairs={{0,2},{2,0},{4,6},{6,4},{8,10},{10,8},{12,14},{14,12},{16,18},{18,... | collective-permute-start | bytes 3145736 | tf_op jit(solution)/shard_map/ppermute | solution.py:67
  66.1 24.1 %collective-permute-start.16 = (bf16[64,2048]{1,0:T(8,128)(2,1)S(1)}, bf16[64,2048]{1,0:T(8,128)(2,1)S(1)}, u32[]{:S(2)}, u32[]{:S(2)}) collective-permute-start(bf16[64,2048]{1,0:T(8,128)(2,1)S(1)} %get-tuple-element.347), channel_id=1, source_target_pairs={{0,8},{2,10},{4,12},{6,14},{8,0},{10,2},{12,4},{14,6},{16,24},{18,... | collective-permute-start | bytes 786440 | tf_op jit(solution)/shard_map/ppermute | solution.py:67
  69.7 21.4 %collective-permute-start.17 = (bf16[64,2048]{1,0:T(8,128)(2,1)S(1)}, bf16[64,2048]{1,0:T(8,128)(2,1)S(1)}, u32[]{:S(2)}, u32[]{:S(2)}) collective-permute-start(bf16[64,2048]{1,0:T(8,128)(2,1)S(1)} %get-tuple-element.347), channel_id=1, source_target_pairs={{0,16},{2,18},{4,20},{6,22},{8,24},{10,26},{12,28},{14,30},{16,0},... | collective-permute-start | bytes 786440 | tf_op jit(solution)/shard_map/ppermute | solution.py:67
  72.4 18.7 %collective-permute-start.18 = (bf16[64,2048]{1,0:T(8,128)(2,1)S(1)}, bf16[64,2048]{1,0:T(8,128)(2,1)S(1)}, u32[]{:S(2)}, u32[]{:S(2)}) collective-permute-start(bf16[64,2048]{1,0:T(8,128)(2,1)S(1)} %get-tuple-element.347), channel_id=1, source_target_pairs={{0,24},{2,26},{4,28},{6,30},{8,16},{10,18},{12,20},{14,22},{16,8},... | collective-permute-start | bytes 786440 | tf_op jit(solution)/shard_map/ppermute | solution.py:67
  93.7 19.4 %collective-permute-start.20 = (bf16[2,2,64,1024]{3,2,1,0:T(8,128)(2,1)S(1)}, bf16[2,2,64,1024]{3,2,1,0:T(8,128)(2,1)S(1)}, u32[]{:S(2)}, u32[]{:S(2)}) collective-permute-start(bf16[2,2,64,1024]{3,2,1,0:T(8,128)(2,1)S(1)} %get-tuple-element.358), channel_id=1, source_target_pairs={{0,2},{2,0},{4,6},{6,4},{8,10},{10,8},{12,14},{14,12},{16,18},{18,... | collective-permute-start | bytes 1572872 | tf_op jit(solution)/shard_map/ppermute | solution.py:67
  95.1 18.0 %collective-permute-start.21 = (bf16[2,2,64,1024]{3,2,1,0:T(8,128)(2,1)S(1)}, bf16[2,2,64,1024]{3,2,1,0:T(8,128)(2,1)S(1)}, u32[]{:S(2)}, u32[]{:S(2)}) collective-permute-start(bf16[2,2,64,1024]{3,2,1,0:T(8,128)(2,1)S(1)} %get-tuple-element.360), channel_id=1, source_target_pairs={{0,4},{2,6},{4,0},{6,2},{8,12},{10,14},{12,8},{14,10},{16,20},{18,... | collective-permute-start | bytes 1572872 | tf_op jit(solution)/shard_map/ppermute | solution.py:67
  113.5 30.2 %collective-permute-start.24 = (bf16[2,2,2,64,1024]{4,3,1,0,2:T(8,128)(2,1)S(1)}, bf16[2,2,2,64,1024]{4,3,1,0,2:T(8,128)(2,1)S(1)}, u32[]{:S(2)}, u32[]{:S(2)}) collective-permute-start(bf16[2,2,2,64,1024]{4,3,1,0,2:T(8,128)(2,1)S(1)} %maximum_select_fusion.7), channel_id=1, source_target_pairs={{0,4},{2,6},{4,0},{6,2},{8,12},{10,14},{12,8},{14,10},{16,20},{18,... | collective-permute-start | bytes 3145736 | tf_op jit(solution)/shard_map/ppermute | solution.py:67
  115.0 28.7 %collective-permute-start.25 = (bf16[2,2,2,64,1024]{4,3,1,0,2:T(8,128)(2,1)S(1)}, bf16[2,2,2,64,1024]{4,3,1,0,2:T(8,128)(2,1)}, u32[]{:S(2)}, u32[]{:S(2)}) collective-permute-start(bf16[2,2,2,64,1024]{4,3,1,0,2:T(8,128)(2,1)S(1)} %maximum_select_fusion.8), channel_id=1, source_target_pairs={{0,2},{2,0},{4,6},{6,4},{8,10},{10,8},{12,14},{14,12},{16,18},{18,... | collective-permute-start | bytes 3145736 | tf_op jit(solution)/shard_map/ppermute | solution.py:67
  117.5 19.1 %collective-permute-start.26 = (bf16[64,2048]{1,0:T(8,128)(2,1)S(1)}, bf16[64,2048]{1,0:T(8,128)(2,1)S(1)}, u32[]{:S(2)}, u32[]{:S(2)}) collective-permute-start(bf16[64,2048]{1,0:T(8,128)(2,1)S(1)} %get-tuple-element.378), channel_id=1, source_target_pairs={{0,8},{2,10},{4,12},{6,14},{8,0},{10,2},{12,4},{14,6},{16,24},{18,... | collective-permute-start | bytes 786440 | tf_op jit(solution)/shard_map/ppermute | solution.py:67
  122.3 21.4 %collective-permute-start.27 = (bf16[64,2048]{1,0:T(8,128)(2,1)S(1)}, bf16[64,2048]{1,0:T(8,128)(2,1)S(1)}, u32[]{:S(2)}, u32[]{:S(2)}) collective-permute-start(bf16[64,2048]{1,0:T(8,128)(2,1)S(1)} %get-tuple-element.378), channel_id=1, source_target_pairs={{0,16},{2,18},{4,20},{6,22},{8,24},{10,26},{12,28},{14,30},{16,0},... | collective-permute-start | bytes 786440 | tf_op jit(solution)/shard_map/ppermute | solution.py:67
  123.8 19.9 %collective-permute-start.28 = (bf16[64,2048]{1,0:T(8,128)(2,1)S(1)}, bf16[64,2048]{1,0:T(8,128)(2,1)S(1)}, u32[]{:S(2)}, u32[]{:S(2)}) collective-permute-start(bf16[64,2048]{1,0:T(8,128)(2,1)S(1)} %get-tuple-element.378), channel_id=1, source_target_pairs={{0,24},{2,26},{4,28},{6,30},{8,16},{10,18},{12,20},{14,22},{16,8},... | collective-permute-start | bytes 786440 | tf_op jit(solution)/shard_map/ppermute | solution.py:67
  167.0 37.3 %collective-permute-start.31 = (bf16[2,2,2,64,1024]{4,3,1,0,2:T(8,128)(2,1)S(1)}, bf16[2,2,2,64,1024]{4,3,1,0,2:T(8,128)(2,1)S(1)}, u32[]{:S(2)}, u32[]{:S(2)}) collective-permute-start(bf16[2,2,2,64,1024]{4,3,1,0,2:T(8,128)(2,1)S(1)} %copy-done.11), channel_id=1, source_target_pairs={{0,4},{2,6},{4,0},{6,2},{8,12},{10,14},{12,8},{14,10},{16,20},{18,... | collective-permute-start | bytes 3145736 | tf_op jit(solution)/shard_map/ppermute | solution.py:67
  168.1 36.2 %collective-permute-start.32 = (bf16[2,2,2,64,1024]{4,3,1,0,2:T(8,128)(2,1)S(1)}, bf16[2,2,2,64,1024]{4,3,1,0,2:T(8,128)(2,1)S(1)}, u32[]{:S(2)}, u32[]{:S(2)}) collective-permute-start(bf16[2,2,2,64,1024]{4,3,1,0,2:T(8,128)(2,1)S(1)} %maximum_select_fusion.11), channel_id=1, source_target_pairs={{0,2},{2,0},{4,6},{6,4},{8,10},{10,8},{12,14},{14,12},{16,18},{18,... | collective-permute-start | bytes 3145736 | tf_op jit(solution)/shard_map/ppermute | solution.py:67
  208.6 39.2 %collective-permute-start.35 = (bf16[2,2,2,64,1024]{4,3,1,0,2:T(8,128)(2,1)S(1)}, bf16[2,2,2,64,1024]{4,3,1,0,2:T(8,128)(2,1)S(1)}, u32[]{:S(2)}, u32[]{:S(2)}) collective-permute-start(bf16[2,2,2,64,1024]{4,3,1,0,2:T(8,128)(2,1)S(1)} %copy_bitcast_fusion.4), channel_id=1, source_target_pairs={{0,2},{2,0},{4,6},{6,4},{8,10},{10,8},{12,14},{14,12},{16,18},{18,... | collective-permute-start | bytes 3145736 | tf_op jit(solution)/shard_map/ppermute | solution.py:67
  209.7 38.2 %collective-permute-start.34 = (bf16[2,2,2,64,1024]{4,3,1,0,2:T(8,128)(2,1)S(1)}, bf16[2,2,2,64,1024]{4,3,1,0,2:T(8,128)(2,1)}, u32[]{:S(2)}, u32[]{:S(2)}) collective-permute-start(bf16[2,2,2,64,1024]{4,3,1,0,2:T(8,128)(2,1)S(1)} %copy_bitcast_fusion.5), channel_id=1, source_target_pairs={{0,4},{2,6},{4,0},{6,2},{8,12},{10,14},{12,8},{14,10},{16,20},{18,... | collective-permute-start | bytes 3145736 | tf_op jit(solution)/shard_map/ppermute | solution.py:67
  250.3 17.5 %collective-permute-start.37 = (bf16[2,2,64,1024]{3,2,1,0:T(8,128)(2,1)S(1)}, bf16[2,2,64,1024]{3,2,1,0:T(8,128)(2,1)S(1)}, u32[]{:S(2)}, u32[]{:S(2)}) collective-permute-start(bf16[2,2,64,1024]{3,2,1,0:T(8,128)(2,1)S(1)} %dynamic-slice_bitcast_fusion.4), channel_id=1, source_target_pairs={{0,4},{2,6},{4,0},{6,2},{8,12},{10,14},{12,8},{14,10},{16,20},{18,... | collective-permute-start | bytes 1572872 | tf_op jit(solution)/shard_map/ppermute | solution.py:67
  251.5 16.4 %collective-permute-start.36 = (bf16[2,2,64,1024]{3,2,1,0:T(8,128)(2,1)S(1)}, bf16[2,2,64,1024]{3,2,1,0:T(8,128)(2,1)S(1)}, u32[]{:S(2)}, u32[]{:S(2)}) collective-permute-start(bf16[2,2,64,1024]{3,2,1,0:T(8,128)(2,1)S(1)} %dynamic-slice_bitcast_fusion.5), channel_id=1, source_target_pairs={{0,2},{2,0},{4,6},{6,4},{8,10},{10,8},{12,14},{14,12},{16,18},{18,... | collective-permute-start | bytes 1572872 | tf_op jit(solution)/shard_map/ppermute | solution.py:67
  270.8 29.8 %collective-permute-start.42 = (bf16[2,2,2,64,1024]{4,3,1,0,2:T(8,128)(2,1)}, bf16[2,2,2,64,1024]{4,3,1,0,2:T(8,128)(2,1)}, u32[]{:S(2)}, u32[]{:S(2)}) collective-permute-start(bf16[2,2,2,64,1024]{4,3,1,0,2:T(8,128)(2,1)} %copy_bitcast_fusion.3), channel_id=1, source_target_pairs={{0,4},{2,6},{4,0},{6,2},{8,12},{10,14},{12,8},{14,10},{16,20},{18,... | collective-permute-start | bytes 3145736 | tf_op jit(solution)/shard_map/ppermute | solution.py:67
  272.9 27.7 %collective-permute-start.43 = (bf16[2,2,2,64,1024]{4,3,1,0,2:T(8,128)(2,1)}, bf16[2,2,2,64,1024]{4,3,1,0,2:T(8,128)(2,1)}, u32[]{:S(2)}, u32[]{:S(2)}) collective-permute-start(bf16[2,2,2,64,1024]{4,3,1,0,2:T(8,128)(2,1)} %copy_bitcast_fusion.2), channel_id=1, source_target_pairs={{0,2},{2,0},{4,6},{6,4},{8,10},{10,8},{12,14},{14,12},{16,18},{18,... | collective-permute-start | bytes 3145736 | tf_op jit(solution)/shard_map/ppermute | solution.py:67
  274.0 25.4 %collective-permute-start.39 = (bf16[64,2048]{1,0:T(8,128)(2,1)S(1)}, bf16[64,2048]{1,0:T(8,128)(2,1)S(1)}, u32[]{:S(2)}, u32[]{:S(2)}) collective-permute-start(bf16[64,2048]{1,0:T(8,128)(2,1)S(1)} %get-tuple-element.655), channel_id=1, source_target_pairs={{0,8},{2,10},{4,12},{6,14},{8,0},{10,2},{12,4},{14,6},{16,24},{18,... | collective-permute-start | bytes 786440 | tf_op jit(solution)/shard_map/ppermute | solution.py:67
  279.2 21.4 %collective-permute-start.40 = (bf16[64,2048]{1,0:T(8,128)(2,1)S(1)}, bf16[64,2048]{1,0:T(8,128)(2,1)S(1)}, u32[]{:S(2)}, u32[]{:S(2)}) collective-permute-start(bf16[64,2048]{1,0:T(8,128)(2,1)S(1)} %get-tuple-element.654), channel_id=1, source_target_pairs={{0,16},{2,18},{4,20},{6,22},{8,24},{10,26},{12,28},{14,30},{16,0},... | collective-permute-start | bytes 786440 | tf_op jit(solution)/shard_map/ppermute | solution.py:67
  280.8 19.8 %collective-permute-start.41 = (bf16[64,2048]{1,0:T(8,128)(2,1)S(1)}, bf16[64,2048]{1,0:T(8,128)(2,1)S(1)}, u32[]{:S(2)}, u32[]{:S(2)}) collective-permute-start(bf16[64,2048]{1,0:T(8,128)(2,1)S(1)} %get-tuple-element.653), channel_id=1, source_target_pairs={{0,24},{2,26},{4,28},{6,30},{8,16},{10,18},{12,20},{14,22},{16,8},... | collective-permute-start | bytes 786440 | tf_op jit(solution)/shard_map/ppermute | solution.py:67
  304.9 18.9 %collective-permute-start.46 = (bf16[2,2,64,1024]{3,2,1,0:T(8,128)(2,1)S(1)}, bf16[2,2,64,1024]{3,2,1,0:T(8,128)(2,1)S(1)}, u32[]{:S(2)}, u32[]{:S(2)}) collective-permute-start(bf16[2,2,64,1024]{3,2,1,0:T(8,128)(2,1)S(1)} %dynamic-slice_bitcast_fusion.2), channel_id=1, source_target_pairs={{0,4},{2,6},{4,0},{6,2},{8,12},{10,14},{12,8},{14,10},{16,20},{18,... | collective-permute-start | bytes 1572872 | tf_op jit(solution)/shard_map/ppermute | solution.py:67
  306.5 17.3 %collective-permute-start.45 = (bf16[2,2,64,1024]{3,2,1,0:T(8,128)(2,1)S(1)}, bf16[2,2,64,1024]{3,2,1,0:T(8,128)(2,1)S(1)}, u32[]{:S(2)}, u32[]{:S(2)}) collective-permute-start(bf16[2,2,64,1024]{3,2,1,0:T(8,128)(2,1)S(1)} %dynamic-slice_bitcast_fusion.3), channel_id=1, source_target_pairs={{0,2},{2,0},{4,6},{6,4},{8,10},{10,8},{12,14},{14,12},{16,18},{18,... | collective-permute-start | bytes 1572872 | tf_op jit(solution)/shard_map/ppermute | solution.py:67
  331.6 38.1 %collective-permute-start.50 = (bf16[64,2048]{1,0:T(8,128)(2,1)}, bf16[64,2048]{1,0:T(8,128)(2,1)S(1)}, u32[]{:S(2)}, u32[]{:S(2)}) collective-permute-start(bf16[64,2048]{1,0:T(8,128)(2,1)} %get-tuple-element.652), channel_id=1, source_target_pairs={{0,8},{2,10},{4,12},{6,14},{8,0},{10,2},{12,4},{14,6},{16,24},{18,... | collective-permute-start | bytes 786440 | tf_op jit(solution)/shard_map/ppermute | solution.py:67
  336.1 33.6 %collective-permute-start.51 = (bf16[64,2048]{1,0:T(8,128)(2,1)}, bf16[64,2048]{1,0:T(8,128)(2,1)S(1)}, u32[]{:S(2)}, u32[]{:S(2)}) collective-permute-start(bf16[64,2048]{1,0:T(8,128)(2,1)} %get-tuple-element.651), channel_id=1, source_target_pairs={{0,16},{2,18},{4,20},{6,22},{8,24},{10,26},{12,28},{14,30},{16,0},... | collective-permute-start | bytes 786440 | tf_op jit(solution)/shard_map/ppermute | solution.py:67
  337.6 32.1 %collective-permute-start.52 = (bf16[64,2048]{1,0:T(8,128)(2,1)}, bf16[64,2048]{1,0:T(8,128)(2,1)S(1)}, u32[]{:S(2)}, u32[]{:S(2)}) collective-permute-start(bf16[64,2048]{1,0:T(8,128)(2,1)} %get-tuple-element.650), channel_id=1, source_target_pairs={{0,24},{2,26},{4,28},{6,30},{8,16},{10,18},{12,20},{14,22},{16,8},... | collective-permute-start | bytes 786440 | tf_op jit(solution)/shard_map/ppermute | solution.py:67
  339.1 30.6 %collective-permute-start.49 = (bf16[2,2,2,64,1024]{4,3,1,0,2:T(8,128)(2,1)S(1)}, bf16[2,2,2,64,1024]{4,3,1,0,2:T(8,128)(2,1)}, u32[]{:S(2)}, u32[]{:S(2)}) collective-permute-start(bf16[2,2,2,64,1024]{4,3,1,0,2:T(8,128)(2,1)S(1)} %copy_bitcast_fusion), channel_id=1, source_target_pairs={{0,2},{2,0},{4,6},{6,4},{8,10},{10,8},{12,14},{14,12},{16,18},{18,... | collective-permute-start | bytes 3145736 | tf_op jit(solution)/shard_map/ppermute | solution.py:67
  340.3 29.3 %collective-permute-start.48 = (bf16[2,2,2,64,1024]{4,3,1,0,2:T(8,128)(2,1)S(1)}, bf16[2,2,2,64,1024]{4,3,1,0,2:T(8,128)(2,1)}, u32[]{:S(2)}, u32[]{:S(2)}) collective-permute-start(bf16[2,2,2,64,1024]{4,3,1,0,2:T(8,128)(2,1)S(1)} %copy_bitcast_fusion.1), channel_id=1, source_target_pairs={{0,4},{2,6},{4,0},{6,2},{8,12},{10,14},{12,8},{14,10},{16,20},{18,... | collective-permute-start | bytes 3145736 | tf_op jit(solution)/shard_map/ppermute | solution.py:67
  373.2 25.5 %collective-permute-start.54 = (bf16[2,2,64,1024]{3,2,1,0:T(8,128)(2,1)S(1)}, bf16[2,2,64,1024]{3,2,1,0:T(8,128)(2,1)S(1)}, u32[]{:S(2)}, u32[]{:S(2)}) collective-permute-start(bf16[2,2,64,1024]{3,2,1,0:T(8,128)(2,1)S(1)} %dynamic-slice_bitcast_fusion), channel_id=1, source_target_pairs={{0,4},{2,6},{4,0},{6,2},{8,12},{10,14},{12,8},{14,10},{16,20},{18,... | collective-permute-start | bytes 1572872 | tf_op jit(solution)/shard_map/ppermute | solution.py:67
  374.9 23.9 %collective-permute-start.53 = (bf16[2,2,64,1024]{3,2,1,0:T(8,128)(2,1)S(1)}, bf16[2,2,64,1024]{3,2,1,0:T(8,128)(2,1)S(1)}, u32[]{:S(2)}, u32[]{:S(2)}) collective-permute-start(bf16[2,2,64,1024]{3,2,1,0:T(8,128)(2,1)S(1)} %dynamic-slice_bitcast_fusion.1), channel_id=1, source_target_pairs={{0,2},{2,0},{4,6},{6,4},{8,10},{10,8},{12,14},{14,12},{16,18},{18,... | collective-permute-start | bytes 1572872 | tf_op jit(solution)/shard_map/ppermute | solution.py:67
  405.2 14.0 %collective-permute-start.59 = (bf16[64,2048]{1,0:T(8,128)(2,1)S(1)}, bf16[64,2048]{1,0:T(8,128)(2,1)S(1)}, u32[]{:S(2)}, u32[]{:S(2)}) collective-permute-start(bf16[64,2048]{1,0:T(8,128)(2,1)S(1)} %get-tuple-element.646), channel_id=1, source_target_pairs={{0,8},{2,10},{4,12},{6,14},{8,0},{10,2},{12,4},{14,6},{16,24},{18,... | collective-permute-start | bytes 786440 | tf_op jit(solution)/shard_map/ppermute | solution.py:67
  405.9 23.0 %collective-permute-start.60 = (bf16[64,2048]{1,0:T(8,128)(2,1)S(1)}, bf16[64,2048]{1,0:T(8,128)(2,1)}, u32[]{:S(2)}, u32[]{:S(2)}) collective-permute-start(bf16[64,2048]{1,0:T(8,128)(2,1)S(1)} %get-tuple-element.645), channel_id=1, source_target_pairs={{0,16},{2,18},{4,20},{6,22},{8,24},{10,26},{12,28},{14,30},{16,0},... | collective-permute-start | bytes 786440 | tf_op jit(solution)/shard_map/ppermute | solution.py:67
  408.3 20.7 %collective-permute-start.61 = (bf16[64,2048]{1,0:T(8,128)(2,1)S(1)}, bf16[64,2048]{1,0:T(8,128)(2,1)}, u32[]{:S(2)}, u32[]{:S(2)}) collective-permute-start(bf16[64,2048]{1,0:T(8,128)(2,1)S(1)} %get-tuple-element.644), channel_id=1, source_target_pairs={{0,24},{2,26},{4,28},{6,30},{8,16},{10,18},{12,20},{14,22},{16,8},... | collective-permute-start | bytes 786440 | tf_op jit(solution)/shard_map/ppermute | solution.py:67
  412.1 16.9 %collective-permute-start.56 = (bf16[2,2,64,512]{3,2,1,0:T(8,128)(2,1)}, bf16[2,2,64,512]{3,2,1,0:T(8,128)(2,1)}, u32[]{:S(2)}, u32[]{:S(2)}) collective-permute-start(bf16[2,2,64,512]{3,2,1,0:T(8,128)(2,1)} %get-tuple-element.649), channel_id=1, source_target_pairs={{0,2},{2,0},{4,6},{6,4},{8,10},{10,8},{12,14},{14,12},{16,18},{18,... | collective-permute-start | bytes 786440 | tf_op jit(solution)/shard_map/ppermute | solution.py:67
  413.2 15.8 %collective-permute-start.57 = (bf16[2,2,64,512]{3,2,1,0:T(8,128)(2,1)}, bf16[2,2,64,512]{3,2,1,0:T(8,128)(2,1)}, u32[]{:S(2)}, u32[]{:S(2)}) collective-permute-start(bf16[2,2,64,512]{3,2,1,0:T(8,128)(2,1)} %get-tuple-element.648), channel_id=1, source_target_pairs={{0,4},{2,6},{4,0},{6,2},{8,12},{10,14},{12,8},{14,10},{16,20},{18,... | collective-permute-start | bytes 786440 | tf_op jit(solution)/shard_map/ppermute | solution.py:67
  431.4 25.1 %collective-permute-start.69 = (f32[512,1024]{1,0:T(8,128)}, f32[512,1024]{1,0:T(8,128)}, u32[]{:S(2)}, u32[]{:S(2)}) collective-permute-start(f32[512,1024]{1,0:T(8,128)} %get-tuple-element.571), channel_id=1, source_target_pairs={{0,1},{1,0},{2,3},{3,2},{4,5},{5,4},{6,7},{7,6},{8,9},{9,8},{10,11... | collective-permute-start | bytes 6291464 | tf_op jit(solution)/shard_map/ppermute | solution.py:236
  431.6 15.9 %collective-permute-start.62 = (bf16[64,512]{1,0:T(8,128)(2,1)S(1)}, bf16[64,512]{1,0:T(8,128)(2,1)S(1)}, u32[]{:S(2)}, u32[]{:S(2)}) collective-permute-start(bf16[64,512]{1,0:T(8,128)(2,1)S(1)} %get-tuple-element.674), channel_id=1, source_target_pairs={{0,8},{2,10},{4,12},{6,14},{8,0},{10,2},{12,4},{14,6},{16,24},{18,... | collective-permute-start | bytes 196616 | tf_op jit(solution)/shard_map/ppermute | solution.py:67
  450.1 17.5 %collective-permute-start.73 = (f32[512,1024]{1,0:T(8,128)}, f32[512,1024]{1,0:T(8,128)}, u32[]{:S(2)}, u32[]{:S(2)}) collective-permute-start(f32[512,1024]{1,0:T(8,128)} %convert_add_fusion.6), channel_id=1, source_target_pairs={{0,1},{1,0},{2,3},{3,2},{4,5},{5,4},{6,7},{7,6},{8,9},{9,8},{10,11... | collective-permute-start | bytes 6291464 | tf_op jit(solution)/shard_map/ppermute | solution.py:236
  453.8 13.8 %collective-permute-start.74 = (bf16[512,1024]{1,0:T(8,128)(2,1)S(1)}, bf16[512,1024]{1,0:T(8,128)(2,1)S(1)}, u32[]{:S(2)}, u32[]{:S(2)}) collective-permute-start(bf16[512,1024]{1,0:T(8,128)(2,1)S(1)} %constant_dynamic-slice_fusion.1), channel_id=1, source_target_pairs={{0,1},{1,0},{2,3},{3,2},{4,5},{5,4},{6,7},{7,6},{8,9},{9,8},{10,11... | collective-permute-start | bytes 3145736 | tf_op jit(solution)/shard_map/ppermute | solution.py:236
  (76 other events, 409.6 us)

commit v5 on v4

--- a/solution.py
+++ b/solution.py
@@ -96,19 +96,14 @@
             self.values = pieces
             return
         for bit in self.left.pop(0):
-            place = sum(1 for p in self.present if p > bit)
-            self.present.append(bit)
+            place = 0 if self.loose else sum(1 for p in self.present if p > bit)
+            self.present.insert(place, bit)
             upper = (self.index // bit) % 2 == 1
             pieces = [
                 in_order(upper, pieces[k], pieces[k + 1], place)
                 for k in range(0, len(pieces), 2)
             ]
         self.values = pieces[0]
-
-    def blocks(self, low):
-        after = low[-1][0]
-        rows = after * self.shape[0] // self.count
-        return self.shape[0] // (2 * rows), rows
 
     def split(self, lows, loose=False):
         cols = self.values.shape[-1] // 2
@@ -120,7 +115,7 @@
             part.shape = self.shape[:-1] + (cols,)
             part.left = self.left[: -len(lows)] + list(low)
             part.last = None
-            part.loose = loose and self.blocks(low)[1] % 16 == 0
+            part.loose = loose and self.shape[0] // self.count % 16 == 0
             out.append(part)
         return out
 
@@ -129,11 +124,14 @@
 
     def parts(self):
         if self.last is None:
-            return [self.result()], (1, self.shape[0]), jnp.int32(0)
+            return [self.result()], ((0,), 0), jnp.int32(0)
         half = (self.shape[0] // 2,) + self.shape[1:]
+        blocks = [0]
+        for bit in self.present[::-1]:
+            blocks = blocks + [b + bit for b in blocks]
         return (
             [v.reshape(half) for v in self.values],
-            self.blocks(((self.last,),)),
+            (tuple(blocks), self.last),
             (self.index // self.last) % 2,
         )
 
@@ -143,12 +141,14 @@
 
 
 class Scatter:
-    def __init__(self, full, count, index, low):
+    def __init__(self, full, count, index, low, singly=False):
         bits = bits_of(count)
         self.values = full.reshape((2,) * len(bits) + (full.shape[0] // count,) + full.shape[1:])
         self.count, self.index = count, index
         self.present = sorted(bits, reverse=True)
         self.left = groups_of(count, low)[::-1]
+        if singly:
+            self.left = [(b,) for group in self.left for b in group[::-1]]
 
     def block(self, group, mask):
         values, present = self.values, list(self.present)
@@ -546,7 +546,7 @@
 
 def ssm_backward_kernel(
     starts_ref, side_ref, gkey_ref, gvalue_ref, left_own_ref, left_other_ref, right_own_ref, right_other_ref,
-    drive_ref, decay_ref, coef_ref, g_ref, gm_ref, sum_ref, dsum_ref, wkey_ref, wvalue_ref, sems,
+    drive_ref, decay_ref, coef_ref, gmixed_ref, sum_ref, dsum_ref, g_ref, gm_ref, wkey_ref, wvalue_ref, sems,
 ):
     length, width = gkey_ref.shape
     cols = width // 2
@@ -574,71 +574,39 @@
         return 0
 
     lax.fori_loop(0, length // chunk, project, 0)
-    adjoint_states(
-        starts_ref, 0, drive_ref, g_ref, decay_ref, coef_ref, gm_ref, sum_ref, dsum_ref, None
-    )
-
-
-def ssm_backward_rest_kernel(
-    starts_ref, g_ref, given_ref, drive_ref, decay_ref, coef_ref,
-    gmixed_ref, sum_ref, dsum_ref, gm_ref,
-):
-    adjoint_states(
-        starts_ref, decay_ref.shape[0] // 2, drive_ref, g_ref, decay_ref, coef_ref, gm_ref,
-        sum_ref, dsum_ref, given_ref,
-    )
+    part = decay_ref.shape[0] // 2
+    for k in range(2):
+        mine = pl.ds(k * part, part)
+        adjoint_states(
+            starts_ref, k * part, drive_ref, g_ref, decay_ref, coef_ref, gm_ref,
+            sum_ref.at[mine], dsum_ref.at[mine], gm_ref if k else None,
+        )
     from_steps(gm_ref, gmixed_ref)
 
 
 def ssm_backward(starts, side, gkey, gvalue, left, right, drive, decay, coef):
     length, width = gkey.shape
     tiles = width // LANES
-    vm = pl.BlockSpec(memory_space=pltpu.VMEM)
-    half = (decay.shape[0] // 2,) + decay.shape[1:]
     return pl.pallas_call(
         ssm_backward_kernel,
         out_shape=(
-            jax.ShapeDtypeStruct((length, tiles, LANES), F32),
-            jax.ShapeDtypeStruct((length, tiles, LANES), F32),
-            jax.ShapeDtypeStruct(half, F32),
-            jax.ShapeDtypeStruct(half, F32),
-        ),
-        in_specs=[SMALL] * 2 + [vm] * 2 + [ANYWHERE] * 4 + [vm] * 3,
-        out_specs=(vm,) * 4,
-        scratch_shapes=[pltpu.VMEM((width, width), BF)] * 2 + [COPIES],
+            jax.ShapeDtypeStruct((length, width), BF),
+            jax.ShapeDtypeStruct(decay.shape, F32),
+            jax.ShapeDtypeStruct(decay.shape, F32),
+        ),
+        in_specs=[SMALL] * 2 + [WHOLE] * 2 + [ANYWHERE] * 4 + [WHOLE] * 3,
+        out_specs=(WHOLE,) * 3,
+        scratch_shapes=[pltpu.VMEM((length, tiles, LANES), F32)] * 2
+        + [pltpu.VMEM((width, width), BF)] * 2
+        + [COPIES],
         compiler_params=pltpu.CompilerParams(vmem_limit_bytes=VMEM),
         cost_estimate=pl.CostEstimate(
-            flops=20 * length * width * width,
+            flops=40 * length * width * width,
             bytes_accessed=20 * length * width,
             transcendentals=0,
         ),
         name="ssm_backward",
     )(starts, side, gkey, gvalue, *left, *right, drive, decay, coef)
-
-
-def ssm_backward_rest(starts, g, given, drive, decay, coef):
-    length, tiles, _ = drive.shape
-    width = tiles * LANES
-    vm = pl.BlockSpec(memory_space=pltpu.VMEM)
-    half = (decay.shape[0] // 2,) + decay.shape[1:]
-    return pl.pallas_call(
-        ssm_backward_rest_kernel,
-        out_shape=(
-            jax.ShapeDtypeStruct((length, width), BF),
-            jax.ShapeDtypeStruct(half, F32),
-            jax.ShapeDtypeStruct(half, F32),
-        ),
-        in_specs=[pl.BlockSpec(memory_space=pltpu.SMEM)] + [vm] * 5,
-        out_specs=(vm,) * 3,
-        scratch_shapes=[pltpu.VMEM((length, tiles, LANES), F32)],
-        compiler_params=pltpu.CompilerParams(vmem_limit_bytes=VMEM),
-        cost_estimate=pl.CostEstimate(
-            flops=20 * length * width * width,
-            bytes_accessed=20 * length * width,
-            transcendentals=0,
-        ),
-        name="ssm_backward_rest",
-    )(starts, g, given, drive, decay, coef)
 
 
 def attention_tiles(length):
@@ -851,15 +819,15 @@
         return pl.ds(pl.multiple_of(i * tile, tile), tile)
 
     weights = []
-    for k, (ref, (number, (many, rows))) in enumerate(zip((up_ref, down_ref), blocks)):
+    for k, (ref, (number, (places, last))) in enumerate(zip((up_ref, down_ref), blocks)):
+        rows = ref.shape[0] // (number * len(places))
         for p in range(number):
             source = pieces[k * blocks[0][0] + p]
             place = place_ref[k] if p == 0 else 1 - place_ref[k]
-            for h in range(many):
-                at = (2 * h + place) * rows if number == 2 else 0
+            for h, at in enumerate(places):
                 pltpu.make_async_copy(
                     source.at[pl.ds(h * rows, rows)],
-                    ref.at[pl.ds(pl.multiple_of(at, 16), rows)],
+                    ref.at[pl.ds(pl.multiple_of((at + place * last) * rows, rows), rows)],
                     weight_sems.at[k],
                 ).start()
         weights.append(pltpu.make_async_copy(ref, ref, weight_sems.at[k]))
@@ -1342,8 +1310,11 @@
     middle, normed_two = fence(ffn[1], middle, normed_two)
     send(ffn[1])
 
-    def scatters(left, right):
-        return [Scatter(left, count, index, X_FIRST), Scatter(right, count, index, Y_FIRST)]
+    def scatters(left, right, singly=False):
+        return [
+            Scatter(left, count, index, X_FIRST, singly),
+            Scatter(right, count, index, Y_FIRST, singly),
+        ]
 
     normed_other = pair(normed_two)
     *both, grad_up, grad_down = feed_forward(
@@ -1359,7 +1330,7 @@
         sums_one, own, other, gown, gother, grad_up, grad_down
     )
     send(sums_one)
-    sums_two = scatters(grad_up, grad_down)
+    sums_two = scatters(grad_up, grad_down, True)
 
     grad_middle, grad_branch, grad_attended, norm_two_sums = norm_two_back(
         at_side, gown, pair(gother), middle, cot, gain_two, right
@@ -1383,19 +1354,17 @@
     grads_right = weight_grads(at_side, (ssm_out,), (grad_key, grad_value))
     sums_left = pair_sum(*grads_left)
     grads_right = fence(sums_two, grads_right)
-    sums_attn = scatters(sums_left, pair_sum(*grads_right))
+    sums_attn = [
+        Scatter(
+            jnp.concatenate([sums_left, pair_sum(*grads_right)], axis=1), count, index, DIRECT
+        )
+    ]
     join_chains(sums_two)
     send(sums_attn + sums_two)
-    g_steps, gm_steps, sum_one, dsum_one = ssm_backward(
+    grad_mixed, state_sum, state_dsum = ssm_backward(
         starts, at_side, grad_key, grad_value, left, right, drive, decay, coef
     )
-    g_steps, gm_steps = fence(sums_attn + sums_two, g_steps, gm_steps)
-    send(sums_attn)
-    grad_mixed, sum_two, dsum_two = ssm_backward_rest(
-        starts, g_steps, gm_steps, drive, decay, coef
-    )
-    grad_mixed = fence(sums_attn, grad_mixed)
-    join_chains(sums_attn)
+    grad_mixed = fence(sums_attn + sums_two, grad_mixed)
     send(sums_attn)
     grads_mix = weight_grads(at_side, (normed,), (grad_mixed,))
     grads_mix, grad_mixed = tie(grads_mix, grad_mixed)
@@ -1408,16 +1377,16 @@
     for_partner, norm_one_first, grad_mixed = fence(
         sums_mix + sums_attn, for_partner, norm_one_first, grad_mixed
     )
-    send(sums_mix)
+    send(sums_mix + sums_two)
     got_grad = pair(for_partner)
     in_grad, norm_one_second = norm_one_back(
         at_side, grad_query, grad_mixed, rows, grad_middle, gain_one, left, mix_both, False
     )
     in_grad, norm_one_second, middle, own, other = fence(
-        sums_mix, in_grad, norm_one_second, middle, own, other
-    )
-
-    state_sums = jnp.concatenate([sum_one, sum_two, dsum_one, dsum_two]).reshape(
+        sums_mix + sums_two, in_grad, norm_one_second, middle, own, other
+    )
+
+    state_sums = jnp.concatenate([state_sum, state_dsum]).reshape(
         2 * states, width
     )
     sums = jnp.concatenate(

time: 482 us -> 471 us (0.977)
  local copies, waits for them, and re-layouts: 37.3 us -> 26.8 us
  Pallas kernels: 263 us -> 254 us
    pallas_call x1 -> x0, Pallas kernels: 22.8 us -> none  [ssm_backward_rest(): pl.pallas_call(ssm_backward_rest_kernel, out_shape=(jax.ShapeDtypeStruct(...]
    pallas_call x1, Pallas kernels: 28.7 us -> 43.3 us  [ssm_backward(): pl.pallas_call(ssm_backward_kernel, out_shape=(jax.ShapeDtypeStruct((leng...]
    optimization_barrier x10 -> x2, local copies, waits for them, and re-layouts: 10.3 us -> 0.43 us  [tie(): return lax.optimization_barrier(trees)]
    unnamed x101 -> x89, local copies, waits for them, and re-layouts: 13.7 us -> 11.3 us
    ppermute x60 -> x58, waiting for transfers between devices: 36.1 us -> 38.1 us  [swap(): return lax.ppermute(values, 'dp', [(i, i ^ mask) for i in range(count)])]
    ppermute x60 -> x58, starting transfers between devices: 92.5 us -> 92.9 us  [swap(): return lax.ppermute(values, 'dp', [(i, i ^ mask) for i in range(count)])]
    convert_element_type x13 -> x11, other arithmetic: 11.4 us -> 11.1 us  [merge(): self.values = total.astype(BF) if self.present else total]
  transfers between devices with their start and end apart: 75 -> 73, of which waited for: 14 -> 17; matrix products, arithmetic and copies ran while one was open for 6% -> 5% of each run, Pallas kernels for 54% -> 54%
where the time goes in v5:
time: 471 us; the launch traced here: 464 us
  Pallas kernels  254 us (54%)
  starting transfers between devices  95.6 us (20%)
  waiting for transfers between devices  46.8 us (10%)
  other arithmetic  38 us (8%)
  local copies, waits for them, and re-layouts  26.8 us (6%)
    ppermute x58, starting transfers between devices, swap(): return lax.ppermute(values, 'dp', [(i, i ^ mask) for i in range(count)])  92.9 us
    pallas_call x2, Pallas kernels, feed_forward(): pl.pallas_call(functools.partial(feed_forward_kernel, part, blocks), out_...  71.5 us
    pallas_call x1, Pallas kernels, ssm_backward(): pl.pallas_call(ssm_backward_kernel, out_shape=(jax.ShapeDtypeStruct((leng...  43.3 us
    ppermute x58, waiting for transfers between devices, swap(): return lax.ppermute(values, 'dp', [(i, i ^ mask) for i in range(count)])  38.1 us
    pallas_call x3, Pallas kernels, weight_grads(): pl.pallas_call(functools.partial(weight_grads_kernel, count), out_shape=(...  21.8 us
    pallas_call x2, Pallas kernels, norm_one_back(): pl.pallas_call(norm_one_kernel, grid_spec=pltpu.PrefetchScalarGridSpec(nu...  18.3 us
    pallas_call x1, Pallas kernels, attention_backward(): pl.pallas_call(attention_backward_kernel, grid=(heads // HEADS_EACH,), ou...  17.2 us
    pallas_call x1, Pallas kernels, ssm_rest(): pl.pallas_call(ssm_rest_kernel, out_shape=(jax.ShapeDtypeStruct((length,...  16.3 us
  transfers between devices with their start and end apart: 73, of which 17 were waited for; matrix products, arithmetic and copies ran while one was open for 5% of the time, Pallas kernels for 54%

profile of v5, /device:TPU:0, one launch (start us, length us, event | category | flops | bytes accessed | tf_op | source)
XLA Modules:
  0.0 463.8 jit_solution(10246607912891247294)
XLA Ops:
  2.3 3.0 collective-permute-start
  5.3 2.6 collective-permute-start.1
  8.9 4.2 collective-permute-done.1
  18.9 1.7 collective-permute-start.7
  20.6 2.3 collective-permute-done.6
  22.9 1.7 collective-permute-start.8
  25.4 13.3 %collective-permute-done.7 = bf16[64,2048]{1,0:T(8,128)(2,1)S(1)} collective-permute-done((bf16[64,2048]{1,0:T(8,128)(2,1)S(1)}, bf16[64,2048]{1,0:T(8,128)(2,1)S(1)}, u32[]{:S(2)}, u32[]{:S(2)}) %collective-permute-start.7) | collective-permute-done | bytes 262176 | tf_op jit(solution)/shard_map/ppermute | solution.py:67
  48.0 15.2 %ssm_forward.1 = (bf16[1024,1024]{1,0:T(8,128)(2,1)}, bf16[1024,1024]{1,0:T(8,128)(2,1)}, f32[1024,8,128]{2,1,0:T(8,128)}, bf16[256,1024]{1,0:T(8,128)(2,1)}, f32[16,8,128]{2,1,0:T(8,128)}) custom-call(s32[16]{0:T(128)} %convert_reduce_fusion.starts_ref, s32[1]{0:T(128)} %bitcast.1.side_ref, bf16[2,512,1024]{2,1,0:T(8,128)(2,1)} %bitcast.284, ...), custom_call_target="tpu_custom_call" | custom-call | flops 12884901888 | bytes 16777216 | tf_op jit(solution)/shard_map/ssm_forward/pallas_call | solution.py:416
  66.1 3.5 collective-permute-start.16
  73.8 16.3 %ssm_rest.1 = (bf16[1024,1024]{1,0:T(8,128)(2,1)}, bf16[2,1024,1024]{2,1,0:T(8,128)(2,1)}) custom-call(s32[16]{0:T(128)} %convert_reduce_fusion.starts_ref, s32[1]{0:T(128)} %bitcast.1.side_ref, bf16[2,512,1024]{2,1,0:T(8,128)(2,1)} %bitcast.285, bf16[2,512,1024]{2,1,0:T(8,128)(2,1)} %copy-done.40, f32[1024,8,128]{2,1,0:T(8,128)} %get-tuple-element.322.drive_ref, ...), custom_call_target="tpu_custom_call" | custom-call | flops 10737418240 | bytes 16777216 | tf_op jit(solution)/shard_map/ssm_rest/pallas_call | solution.py:445
  96.7 2.7 collective-permute-done.23.right_other_ref.other_ref
  100.9 12.2 %project.1 = (bf16[1024,1024]{1,0:T(8,128)(2,1)}, bf16[1024,1024]{1,0:T(8,128)(2,1)}, bf16[1024,1024]{1,0:T(8,128)(2,1)}) custom-call(s32[1]{0:T(128)} %bitcast.1.side_ref, bf16[1024,1024]{1,0:T(8,128)(2,1)} %get-tuple-element.337.normed_ref.refs_0_, bf16[1024,1024]{1,0:T(8,128)(2,1)} %get-tuple-element.472.ssm_ref.refs_0_, bf16[1024,1024]{1,0:T(8,128)(2,1)} %bitcast.204, ...), custom_call_target="tpu_custom_call" | custom-call | flops 6442450944 | bytes 16777216 | tf_op jit(solution)/shard_map/project/pallas_call | solution.py:494
  114.4 1.7 maximum_select_fusion.7
  120.3 4.8 %collective-permute-start.26 = (bf16[64,2048]{1,0:T(8,128)(2,1)S(1)}, bf16[64,2048]{1,0:T(8,128)(2,1)S(1)}, u32[]{:S(2)}, u32[]{:S(2)}) collective-permute-start(bf16[64,2048]{1,0:T(8,128)(2,1)S(1)} %get-tuple-element.363), channel_id=1, source_target_pairs={{0,8},{2,10},{4,12},{6,14},{8,0},{10,2},{12,4},{14,6},{16,24},{18,... | collective-permute-start | bytes 786440 | tf_op jit(solution)/shard_map/ppermute | solution.py:67
  128.7 10.7 %attention_forward.1 = (bf16[1024,1024]{1,0:T(8,128)(2,1)}, f32[8,1024,1]{2,1,0:T(8,128)}) custom-call(s32[1024,1]{1,0:T(8,128)} %copy.76.seg_col_ref, s32[1,1024]{1,0:T(1,128)} %fusion.34.seg_row_ref, bf16[1024,1024]{1,0:T(8,128)(2,1)} %get-tuple-element.352.query_ref, bf16[1024,1024]{1,0:T(8,128)(2,1)} %get-tuple-element.353.key_ref, ...), custom_call_target="tpu_custom_call" | custom-call | flops 1879048192 | bytes 8388608 | tf_op jit(solution)/shard_map/attention_forward/pallas_call | solution.py:694
  139.4 7.1 %collective-permute-done.27 = bf16[64,2048]{1,0:T(8,128)(2,1)S(1)} collective-permute-done((bf16[64,2048]{1,0:T(8,128)(2,1)S(1)}, bf16[64,2048]{1,0:T(8,128)(2,1)S(1)}, u32[]{:S(2)}, u32[]{:S(2)}) %collective-permute-start.27) | collective-permute-done | bytes 262176 | tf_op jit(solution)/shard_map/ppermute | solution.py:67
  149.5 8.6 %middle.1 = (f32[1024,1024]{1,0:T(8,128)}, bf16[1024,1024]{1,0:T(8,128)(2,1)}) custom-call(s32[1]{0:T(128)} %bitcast.1.side_ref, bf16[1024,1024]{1,0:T(8,128)(2,1)} %get-tuple-element.368.attended_ref.refs_3_, bf16[1024,1024]{1,0:T(8,128)(2,1)} %bitcast.200, bf16[1024,1024]{1,0:T(8,128)(2,1)} %copy-done.6, bf16[1024,1024]{1,0:T(8,128)(2,1)} %get-tuple-element.369.rows_ref, ...), custom_call_target="tpu_custom_call" | custom-call | flops 2147483648 | bytes 12582912 | tf_op jit(solution)/shard_map/middle/pallas_call | solution.py:962
  165.6 34.5 %feed_forward.2 = (bf16[1024,1024]{1,0:T(8,128)(2,1)}, bf16[1024,1024]{1,0:T(8,128)(2,1)}, bf16[1024,1024]{1,0:T(8,128)(2,1)}, bf16[1024,1024]{1,0:T(8,128)(2,1)...) custom-call(s32[2]{0:T(128)} %pad_add_fusion.place_ref, bf16[1024,1024]{1,0:T(8,128)(2,1)} %get-tuple-element.382.own_ref, ...), custom_call_target="tpu_custom_call" | custom-call | flops 30064771072 | bytes 50331648 | tf_op jit(solution)/shard_map/feed_forward/pallas_call | solution.py:906
  200.2 2.1 copy_bitcast_fusion.2
  205.2 37.0 %feed_forward.3 = (bf16[1024,1024]{1,0:T(8,128)(2,1)}, bf16[1024,1024]{1,0:T(8,128)(2,1)}, bf16[1024,1024]{1,0:T(8,128)(2,1)}, bf16[1024,1024]{1,0:T(8,128)(2,1)...) custom-call(s32[2]{0:T(128)} %pad_add_fusion.place_ref, bf16[1024,1024]{1,0:T(8,128)(2,1)} %get-tuple-element.382.own_ref, ...), custom_call_target="tpu_custom_call" | custom-call | flops 30064771072 | bytes 50331648 | tf_op jit(solution)/shard_map/feed_forward/pallas_call | solution.py:906
  242.7 1.8 fusion.6
  246.2 2.6 collective-permute-done.38.theirs_ref
  250.2 12.0 %norm_two_back.1 = (f32[1024,1024]{1,0:T(8,128)}, bf16[1024,1024]{1,0:T(8,128)(2,1)}, bf16[1024,1024]{1,0:T(8,128)(2,1)}, f32[2,1024]{1,0:T(2,128)}) custom-call(s32[1]{0:T(128)} %bitcast.1.side_ref, bf16[1024,1024]{1,0:T(8,128)(2,1)} %get-tuple-element.426.mine_ref, bf16[1024,1024]{1,0:T(8,128)(2,1)} %copy-done.20, ...), custom_call_target="tpu_custom_call" | custom-call | flops 2147483648 | bytes 25165824 | tf_op jit(solution)/shard_map/norm_two_back/pallas_call | solution.py:1008
  267.5 5.8 %collective-permute-start.39 = (bf16[64,2048]{1,0:T(8,128)(2,1)S(1)}, bf16[64,2048]{1,0:T(8,128)(2,1)S(1)}, u32[]{:S(2)}, u32[]{:S(2)}) collective-permute-start(bf16[64,2048]{1,0:T(8,128)(2,1)S(1)} %get-tuple-element.625), channel_id=1, source_target_pairs={{0,8},{2,10},{4,12},{6,14},{8,0},{10,2},{12,4},{14,6},{16,24},{18,... | collective-permute-start | bytes 786440 | tf_op jit(solution)/shard_map/ppermute | solution.py:67
  276.2 17.2 %attention_backward.1 = (bf16[1024,1024]{1,0:T(8,128)(2,1)}, bf16[1024,1024]{1,0:T(8,128)(2,1)}, bf16[1024,1024]{1,0:T(8,128)(2,1)}) custom-call(s32[1024,1]{1,0:T(8,128)} %copy.76.seg_col_ref, s32[1,1024]{1,0:T(1,128)} %fusion.34.seg_row_ref, bf16[1024,1024]{1,0:T(8,128)(2,1)} %get-tuple-element.352.query_ref, ...), custom_call_target="tpu_custom_call" | custom-call | flops 4697620480 | bytes 14680064 | tf_op jit(solution)/shard_map/attention_backward/pallas_call | solution.py:762
  301.2 8.1 %weight_grads.3 = (bf16[1024,1024]{1,0:T(8,128)(2,1)}, bf16[1024,1024]{1,0:T(8,128)(2,1)}) custom-call(s32[1]{0:T(128)} %bitcast.1.side_ref, bf16[1024,1024]{1,0:T(8,128)(2,1)} %get-tuple-element.337.normed_ref.refs_0_, bf16[1024,1024]{1,0:T(8,128)(2,1)} %get-tuple-element.462.refs_1_, bf16[1024,1024]{1,0:T(8,128)(2,1)} %get-tuple-element.463.refs_2_.gquery_ref, ...), custom_call_target="tpu_custom_call" | custom-call | flops 4294967296 | bytes 12582912 | tf_op jit(solution)/shard_map/weight_grads/pallas_call | solution.py:1172
  309.4 8.1 %weight_grads.4 = (bf16[1024,1024]{1,0:T(8,128)(2,1)}, bf16[1024,1024]{1,0:T(8,128)(2,1)}) custom-call(s32[1]{0:T(128)} %bitcast.1.side_ref, bf16[1024,1024]{1,0:T(8,128)(2,1)} %get-tuple-element.472.ssm_ref.refs_0_, bf16[1024,1024]{1,0:T(8,128)(2,1)} %get-tuple-element.458.gkey_ref.refs_1_, bf16[1024,1024]{1,0:T(8,128)(2,1)} %get-tuple-element.459.gvalue_ref.refs_2_), custom_call_target="tpu_custom_call" | custom-call | flops 4294967296 | bytes 12582912 | tf_op jit(solution)/shard_map/weight_grads/pallas_call | solution.py:1172
  320.4 2.7 add_convert_fusion.1
  323.4 2.5 add_convert_fusion
  327.2 5.9 %collective-permute-start.51 = (bf16[2,64,2048]{2,1,0:T(8,128)(2,1)}, bf16[2,64,2048]{2,1,0:T(8,128)(2,1)S(1)}, u32[]{:S(2)}, u32[]{:S(2)}) collective-permute-start(bf16[2,64,2048]{2,1,0:T(8,128)(2,1)} %dynamic-slice_bitcast_fusion.3), channel_id=1, source_target_pairs={{0,16},{2,18},{4,20},{6,22},{8,24},{10,26},{12,28},{14,30},{16,0},... | collective-permute-start | bytes 1572872 | tf_op jit(solution)/shard_map/ppermute | solution.py:67
  338.3 43.3 %ssm_backward.1 = (bf16[1024,1024]{1,0:T(8,128)(2,1)}, f32[16,8,128]{2,1,0:T(8,128)}, f32[16,8,128]{2,1,0:T(8,128)}) custom-call(s32[16]{0:T(128)} %convert_reduce_fusion.starts_ref, s32[1]{0:T(128)} %bitcast.1.side_ref, bf16[1024,1024]{1,0:T(8,128)(2,1)} %get-tuple-element.458.gkey_ref.refs_1_, bf16[1024,1024]{1,0:T(8,128)(2,1)} %get-tuple-element.459.gvalue_ref.refs_2_, ...), custom_call_target="tpu_custom_call" | custom-call | flops 42949672960 | bytes 20971520 | tf_op jit(solution)/shard_map/ssm_backward/pallas_call | solution.py:590
  381.6 1.8 collective-permute-done.50
  383.6 2.6 fusion.2
  386.1 5.7 %weight_grads.5 = (bf16[1024,512]{1,0:T(8,128)(2,1)}, bf16[1024,512]{1,0:T(8,128)(2,1)}) custom-call(s32[1]{0:T(128)} %bitcast.1.side_ref, bf16[1024,1024]{1,0:T(8,128)(2,1)} %get-tuple-element.337.normed_ref.refs_0_, bf16[1024,1024]{1,0:T(8,128)(2,1)} %get-tuple-element.523.refs_1_.gmixed_ref), custom_call_target="tpu_custom_call" | custom-call | flops 2147483648 | bytes 6291456 | tf_op jit(solution)/shard_map/weight_grads/pallas_call | solution.py:1172
  394.2 3.0 collective-permute-start.58
  400.7 5.0 %collective-permute-done.56 = bf16[64,2048]{1,0:T(8,128)(2,1)S(1)} collective-permute-done((bf16[64,2048]{1,0:T(8,128)(2,1)S(1)}, bf16[64,2048]{1,0:T(8,128)(2,1)S(1)}, u32[]{:S(2)}, u32[]{:S(2)}) %collective-permute-start.56) | collective-permute-done | bytes 262176 | tf_op jit(solution)/shard_map/ppermute | solution.py:67
  405.7 1.7 collective-permute-start.55
  407.5 8.7 %norm_one_back.2 = (f32[512,1024]{1,0:T(8,128)}, f32[2,1024]{1,0:T(2,128)}) custom-call(s32[1]{0:T(128)} %bitcast.1.side_ref, bf16[1024,1024]{1,0:T(8,128)(2,1)} %get-tuple-element.463.refs_2_.gquery_ref, bf16[1024,1024]{1,0:T(8,128)(2,1)} %get-tuple-element.523.refs_1_.gmixed_ref, bf16[1024,1024]{1,0:T(8,128)(2,1)} %get-tuple-element.369.rows_ref, ...), custom_call_target="tpu_custom_call" | custom-call | flops 2147483648 | bytes 10485760 | tf_op jit(solution)/shard_map/norm_one_back/pallas_call | solution.py:1063
  418.4 3.9 collective-permute-start.62
  422.4 2.0 collective-permute-start.60
  424.4 2.4 collective-permute-start.61
  426.8 9.6 %norm_one_back.3 = (f32[2,512,1024]{2,1,0:T(8,128)}, f32[2,1024]{1,0:T(2,128)}) custom-call(s32[1]{0:T(128)} %bitcast.1.side_ref, bf16[1024,1024]{1,0:T(8,128)(2,1)} %get-tuple-element.463.refs_2_.gquery_ref, bf16[1024,1024]{1,0:T(8,128)(2,1)} %get-tuple-element.523.refs_1_.gmixed_ref, bf16[1024,1024]{1,0:T(8,128)(2,1)} %get-tuple-element.369.rows_ref, ...), custom_call_target="tpu_custom_call" | custom-call | flops 2147483648 | bytes 10485760 | tf_op jit(solution)/shard_map/norm_one_back/pallas_call | solution.py:1063
  437.3 1.8 convert_add_fusion.5
  441.6 1.9 collective-permute-done.63
  447.9 2.6 put.1
  451.3 2.0 collective-permute-start.69
  453.4 2.4 collective-permute-start.70
  457.6 4.6 layer_out.1
  (313 shorter events, 104.7 us)
Async XLA Ops:
  15.4 23.9 %collective-permute-start.3 = (bf16[2,2,72,512]{3,2,1,0:T(8,128)(2,1)S(1)}, bf16[2,2,72,512]{3,2,1,0:T(8,128)(2,1)S(1)}, u32[]{:S(2)}, u32[]{:S(2)}) collective-permute-start(bf16[2,2,72,512]{3,2,1,0:T(8,128)(2,1)S(1)} %maximum_select_fusion.19), channel_id=1, source_target_pairs={{0,2},{2,0},{4,6},{6,4},{8,10},{10,8},{12,14},{14,12},{16,18},{18,... | collective-permute-start | bytes 884744 | tf_op jit(solution)/shard_map/ppermute | solution.py:67
  16.9 22.4 %collective-permute-start.4 = (bf16[2,2,72,512]{3,2,1,0:T(8,128)(2,1)S(1)}, bf16[2,2,72,512]{3,2,1,0:T(8,128)(2,1)S(1)}, u32[]{:S(2)}, u32[]{:S(2)}) collective-permute-start(bf16[2,2,72,512]{3,2,1,0:T(8,128)(2,1)S(1)} %maximum_select_fusion.19), channel_id=1, source_target_pairs={{0,4},{2,6},{4,0},{6,2},{8,12},{10,14},{12,8},{14,10},{16,20},{18,... | collective-permute-start | bytes 884744 | tf_op jit(solution)/shard_map/ppermute | solution.py:67
  18.4 20.9 %collective-permute-start.5 = (bf16[2,2,72,512]{3,2,1,0:T(8,128)(2,1)S(1)}, bf16[2,2,72,512]{3,2,1,0:T(8,128)(2,1)S(1)}, u32[]{:S(2)}, u32[]{:S(2)}) collective-permute-start(bf16[2,2,72,512]{3,2,1,0:T(8,128)(2,1)S(1)} %maximum_select_fusion.19), channel_id=1, source_target_pairs={{0,6},{2,4},{4,2},{6,0},{8,14},{10,12},{12,10},{14,8},{16,22},{18,... | collective-permute-start | bytes 884744 | tf_op jit(solution)/shard_map/ppermute | solution.py:67
  18.9 19.9 %collective-permute-start.7 = (bf16[64,2048]{1,0:T(8,128)(2,1)S(1)}, bf16[64,2048]{1,0:T(8,128)(2,1)S(1)}, u32[]{:S(2)}, u32[]{:S(2)}) collective-permute-start(bf16[64,2048]{1,0:T(8,128)(2,1)S(1)} %pad_maximum_fusion.6), channel_id=1, source_target_pairs={{0,16},{2,18},{4,20},{6,22},{8,24},{10,26},{12,28},{14,30},{16,0},... | collective-permute-start | bytes 786440 | tf_op jit(solution)/shard_map/ppermute | solution.py:67
  22.9 15.9 %collective-permute-start.8 = (bf16[64,2048]{1,0:T(8,128)(2,1)S(1)}, bf16[64,2048]{1,0:T(8,128)(2,1)S(1)}, u32[]{:S(2)}, u32[]{:S(2)}) collective-permute-start(bf16[64,2048]{1,0:T(8,128)(2,1)S(1)} %pad_maximum_fusion.6), channel_id=1, source_target_pairs={{0,24},{2,26},{4,28},{6,30},{8,16},{10,18},{12,20},{14,22},{16,8},... | collective-permute-start | bytes 786440 | tf_op jit(solution)/shard_map/ppermute | solution.py:67
  43.9 19.3 %collective-permute-start.10 = (bf16[2,2,64,1024]{3,2,1,0:T(8,128)(2,1)S(1)}, bf16[2,2,64,1024]{3,2,1,0:T(8,128)(2,1)S(1)}, u32[]{:S(2)}, u32[]{:S(2)}) collective-permute-start(bf16[2,2,64,1024]{3,2,1,0:T(8,128)(2,1)S(1)} %get-tuple-element.313), channel_id=1, source_target_pairs={{0,4},{2,6},{4,0},{6,2},{8,12},{10,14},{12,8},{14,10},{16,20},{18,... | collective-permute-start | bytes 1572872 | tf_op jit(solution)/shard_map/ppermute | solution.py:67
  45.5 17.7 %collective-permute-start.9 = (bf16[2,2,64,1024]{3,2,1,0:T(8,128)(2,1)S(1)}, bf16[2,2,64,1024]{3,2,1,0:T(8,128)(2,1)S(1)}, u32[]{:S(2)}, u32[]{:S(2)}) collective-permute-start(bf16[2,2,64,1024]{3,2,1,0:T(8,128)(2,1)S(1)} %get-tuple-element.311), channel_id=1, source_target_pairs={{0,2},{2,0},{4,6},{6,4},{8,10},{10,8},{12,14},{14,12},{16,18},{18,... | collective-permute-start | bytes 1572872 | tf_op jit(solution)/shard_map/ppermute | solution.py:67
  64.9 26.0 %collective-permute-start.14 = (bf16[2,2,2,64,1024]{4,3,2,1,0:T(8,128)(2,1)S(1)}, bf16[2,2,2,64,1024]{4,3,2,1,0:T(8,128)(2,1)S(1)}, u32[]{:S(2)}, u32[]{:S(2)}) collective-permute-start(bf16[2,2,2,64,1024]{4,3,2,1,0:T(8,128)(2,1)S(1)} %maximum_select_fusion.4), channel_id=1, source_target_pairs={{0,4},{2,6},{4,0},{6,2},{8,12},{10,14},{12,8},{14,10},{16,20},{18,... | collective-permute-start | bytes 3145736 | tf_op jit(solution)/shard_map/ppermute | solution.py:67
  65.5 25.4 %collective-permute-start.15 = (bf16[2,2,2,64,1024]{4,3,1,0,2:T(8,128)(2,1)S(1)}, bf16[2,2,2,64,1024]{4,3,1,0,2:T(8,128)(2,1)S(1)}, u32[]{:S(2)}, u32[]{:S(2)}) collective-permute-start(bf16[2,2,2,64,1024]{4,3,1,0,2:T(8,128)(2,1)S(1)} %maximum_select_fusion.5), channel_id=1, source_target_pairs={{0,2},{2,0},{4,6},{6,4},{8,10},{10,8},{12,14},{14,12},{16,18},{18,... | collective-permute-start | bytes 3145736 | tf_op jit(solution)/shard_map/ppermute | solution.py:67
  66.1 24.1 %collective-permute-start.16 = (bf16[64,2048]{1,0:T(8,128)(2,1)S(1)}, bf16[64,2048]{1,0:T(8,128)(2,1)S(1)}, u32[]{:S(2)}, u32[]{:S(2)}) collective-permute-start(bf16[64,2048]{1,0:T(8,128)(2,1)S(1)} %get-tuple-element.332), channel_id=1, source_target_pairs={{0,8},{2,10},{4,12},{6,14},{8,0},{10,2},{12,4},{14,6},{16,24},{18,... | collective-permute-start | bytes 786440 | tf_op jit(solution)/shard_map/ppermute | solution.py:67
  69.5 21.4 %collective-permute-start.17 = (bf16[64,2048]{1,0:T(8,128)(2,1)S(1)}, bf16[64,2048]{1,0:T(8,128)(2,1)S(1)}, u32[]{:S(2)}, u32[]{:S(2)}) collective-permute-start(bf16[64,2048]{1,0:T(8,128)(2,1)S(1)} %get-tuple-element.332), channel_id=1, source_target_pairs={{0,16},{2,18},{4,20},{6,22},{8,24},{10,26},{12,28},{14,30},{16,0},... | collective-permute-start | bytes 786440 | tf_op jit(solution)/shard_map/ppermute | solution.py:67
  72.4 18.5 %collective-permute-start.18 = (bf16[64,2048]{1,0:T(8,128)(2,1)S(1)}, bf16[64,2048]{1,0:T(8,128)(2,1)S(1)}, u32[]{:S(2)}, u32[]{:S(2)}) collective-permute-start(bf16[64,2048]{1,0:T(8,128)(2,1)S(1)} %get-tuple-element.332), channel_id=1, source_target_pairs={{0,24},{2,26},{4,28},{6,30},{8,16},{10,18},{12,20},{14,22},{16,8},... | collective-permute-start | bytes 786440 | tf_op jit(solution)/shard_map/ppermute | solution.py:67
  93.6 19.4 %collective-permute-start.20 = (bf16[2,2,64,1024]{3,2,1,0:T(8,128)(2,1)S(1)}, bf16[2,2,64,1024]{3,2,1,0:T(8,128)(2,1)}, u32[]{:S(2)}, u32[]{:S(2)}) collective-permute-start(bf16[2,2,64,1024]{3,2,1,0:T(8,128)(2,1)S(1)} %get-tuple-element.343), channel_id=1, source_target_pairs={{0,2},{2,0},{4,6},{6,4},{8,10},{10,8},{12,14},{14,12},{16,18},{18,... | collective-permute-start | bytes 1572872 | tf_op jit(solution)/shard_map/ppermute | solution.py:67
  95.3 17.8 %collective-permute-start.21 = (bf16[2,2,64,1024]{3,2,1,0:T(8,128)(2,1)S(1)}, bf16[2,2,64,1024]{3,2,1,0:T(8,128)(2,1)}, u32[]{:S(2)}, u32[]{:S(2)}) collective-permute-start(bf16[2,2,64,1024]{3,2,1,0:T(8,128)(2,1)S(1)} %get-tuple-element.345), channel_id=1, source_target_pairs={{0,4},{2,6},{4,0},{6,2},{8,12},{10,14},{12,8},{14,10},{16,20},{18,... | collective-permute-start | bytes 1572872 | tf_op jit(solution)/shard_map/ppermute | solution.py:67
  116.2 30.4 %collective-permute-start.24 = (bf16[2,2,2,64,1024]{4,3,2,1,0:T(8,128)(2,1)S(1)}, bf16[2,2,2,64,1024]{4,3,2,1,0:T(8,128)(2,1)}, u32[]{:S(2)}, u32[]{:S(2)}) collective-permute-start(bf16[2,2,2,64,1024]{4,3,2,1,0:T(8,128)(2,1)S(1)} %maximum_select_fusion.7), channel_id=1, source_target_pairs={{0,4},{2,6},{4,0},{6,2},{8,12},{10,14},{12,8},{14,10},{16,20},{18,... | collective-permute-start | bytes 3145736 | tf_op jit(solution)/shard_map/ppermute | solution.py:67
  117.8 28.7 %collective-permute-start.25 = (bf16[2,2,2,64,1024]{4,3,2,1,0:T(8,128)(2,1)S(1)}, bf16[2,2,2,64,1024]{4,3,2,1,0:T(8,128)(2,1)}, u32[]{:S(2)}, u32[]{:S(2)}) collective-permute-start(bf16[2,2,2,64,1024]{4,3,2,1,0:T(8,128)(2,1)S(1)} %maximum_select_fusion.8), channel_id=1, source_target_pairs={{0,2},{2,0},{4,6},{6,4},{8,10},{10,8},{12,14},{14,12},{16,18},{18,... | collective-permute-start | bytes 3145736 | tf_op jit(solution)/shard_map/ppermute | solution.py:67
  120.3 19.1 %collective-permute-start.26 = (bf16[64,2048]{1,0:T(8,128)(2,1)S(1)}, bf16[64,2048]{1,0:T(8,128)(2,1)S(1)}, u32[]{:S(2)}, u32[]{:S(2)}) collective-permute-start(bf16[64,2048]{1,0:T(8,128)(2,1)S(1)} %get-tuple-element.363), channel_id=1, source_target_pairs={{0,8},{2,10},{4,12},{6,14},{8,0},{10,2},{12,4},{14,6},{16,24},{18,... | collective-permute-start | bytes 786440 | tf_op jit(solution)/shard_map/ppermute | solution.py:67
  125.2 21.4 %collective-permute-start.27 = (bf16[64,2048]{1,0:T(8,128)(2,1)S(1)}, bf16[64,2048]{1,0:T(8,128)(2,1)S(1)}, u32[]{:S(2)}, u32[]{:S(2)}) collective-permute-start(bf16[64,2048]{1,0:T(8,128)(2,1)S(1)} %get-tuple-element.363), channel_id=1, source_target_pairs={{0,16},{2,18},{4,20},{6,22},{8,24},{10,26},{12,28},{14,30},{16,0},... | collective-permute-start | bytes 786440 | tf_op jit(solution)/shard_map/ppermute | solution.py:67
  126.6 19.9 %collective-permute-start.28 = (bf16[64,2048]{1,0:T(8,128)(2,1)S(1)}, bf16[64,2048]{1,0:T(8,128)(2,1)S(1)}, u32[]{:S(2)}, u32[]{:S(2)}) collective-permute-start(bf16[64,2048]{1,0:T(8,128)(2,1)S(1)} %get-tuple-element.363), channel_id=1, source_target_pairs={{0,24},{2,26},{4,28},{6,30},{8,16},{10,18},{12,20},{14,22},{16,8},... | collective-permute-start | bytes 786440 | tf_op jit(solution)/shard_map/ppermute | solution.py:67
  161.7 38.5 %collective-permute-start.31 = (bf16[2,2,2,64,1024]{4,3,2,1,0:T(8,128)(2,1)}, bf16[2,2,2,64,1024]{4,3,2,1,0:T(8,128)(2,1)S(1)}, u32[]{:S(2)}, u32[]{:S(2)}) collective-permute-start(bf16[2,2,2,64,1024]{4,3,2,1,0:T(8,128)(2,1)} %maximum_select_fusion.10), channel_id=1, source_target_pairs={{0,4},{2,6},{4,0},{6,2},{8,12},{10,14},{12,8},{14,10},{16,20},{18,... | collective-permute-start | bytes 3145736 | tf_op jit(solution)/shard_map/ppermute | solution.py:67
  162.9 37.3 %collective-permute-start.32 = (bf16[2,2,2,64,1024]{4,3,2,1,0:T(8,128)(2,1)S(1)}, bf16[2,2,2,64,1024]{4,3,2,1,0:T(8,128)(2,1)S(1)}, u32[]{:S(2)}, u32[]{:S(2)}) collective-permute-start(bf16[2,2,2,64,1024]{4,3,2,1,0:T(8,128)(2,1)S(1)} %maximum_select_fusion.11), channel_id=1, source_target_pairs={{0,2},{2,0},{4,6},{6,4},{8,10},{10,8},{12,14},{14,12},{16,18},{18,... | collective-permute-start | bytes 3145736 | tf_op jit(solution)/shard_map/ppermute | solution.py:67
  202.3 39.9 %collective-permute-start.35 = (bf16[2,2,2,64,1024]{4,3,1,0,2:T(8,128)(2,1)S(1)}, bf16[2,2,2,64,1024]{4,3,1,0,2:T(8,128)(2,1)S(1)}, u32[]{:S(2)}, u32[]{:S(2)}) collective-permute-start(bf16[2,2,2,64,1024]{4,3,1,0,2:T(8,128)(2,1)S(1)} %copy_bitcast_fusion.2), channel_id=1, source_target_pairs={{0,2},{2,0},{4,6},{6,4},{8,10},{10,8},{12,14},{14,12},{16,18},{18,... | collective-permute-start | bytes 3145736 | tf_op jit(solution)/shard_map/ppermute | solution.py:67
  204.0 38.2 %collective-permute-start.34 = (bf16[2,2,2,64,1024]{4,3,1,0,2:T(8,128)(2,1)S(1)}, bf16[2,2,2,64,1024]{4,3,1,0,2:T(8,128)(2,1)}, u32[]{:S(2)}, u32[]{:S(2)}) collective-permute-start(bf16[2,2,2,64,1024]{4,3,1,0,2:T(8,128)(2,1)S(1)} %copy_bitcast_fusion.3), channel_id=1, source_target_pairs={{0,4},{2,6},{4,0},{6,2},{8,12},{10,14},{12,8},{14,10},{16,20},{18,... | collective-permute-start | bytes 3145736 | tf_op jit(solution)/shard_map/ppermute | solution.py:67
  244.7 17.5 %collective-permute-start.37 = (bf16[2,2,64,1024]{3,2,1,0:T(8,128)(2,1)S(1)}, bf16[2,2,64,1024]{3,2,1,0:T(8,128)(2,1)S(1)}, u32[]{:S(2)}, u32[]{:S(2)}) collective-permute-start(bf16[2,2,64,1024]{3,2,1,0:T(8,128)(2,1)S(1)} %dynamic-slice_bitcast_fusion.6), channel_id=1, source_target_pairs={{0,4},{2,6},{4,0},{6,2},{8,12},{10,14},{12,8},{14,10},{16,20},{18,... | collective-permute-start | bytes 1572872 | tf_op jit(solution)/shard_map/ppermute | solution.py:67
  245.7 16.5 %collective-permute-start.36 = (bf16[2,2,64,1024]{3,2,1,0:T(8,128)(2,1)S(1)}, bf16[2,2,64,1024]{3,2,1,0:T(8,128)(2,1)S(1)}, u32[]{:S(2)}, u32[]{:S(2)}) collective-permute-start(bf16[2,2,64,1024]{3,2,1,0:T(8,128)(2,1)S(1)} %dynamic-slice_bitcast_fusion.7), channel_id=1, source_target_pairs={{0,2},{2,0},{4,6},{6,4},{8,10},{10,8},{12,14},{14,12},{16,18},{18,... | collective-permute-start | bytes 1572872 | tf_op jit(solution)/shard_map/ppermute | solution.py:67
  265.1 29.6 %collective-permute-start.42 = (bf16[2,2,2,64,1024]{4,3,1,0,2:T(8,128)(2,1)}, bf16[2,2,2,64,1024]{4,3,1,0,2:T(8,128)(2,1)}, u32[]{:S(2)}, u32[]{:S(2)}) collective-permute-start(bf16[2,2,2,64,1024]{4,3,1,0,2:T(8,128)(2,1)} %copy_bitcast_fusion.1), channel_id=1, source_target_pairs={{0,4},{2,6},{4,0},{6,2},{8,12},{10,14},{12,8},{14,10},{16,20},{18,... | collective-permute-start | bytes 3145736 | tf_op jit(solution)/shard_map/ppermute | solution.py:67
  267.0 27.7 %collective-permute-start.43 = (bf16[2,2,2,64,1024]{4,3,1,0,2:T(8,128)(2,1)}, bf16[2,2,2,64,1024]{4,3,1,0,2:T(8,128)(2,1)}, u32[]{:S(2)}, u32[]{:S(2)}) collective-permute-start(bf16[2,2,2,64,1024]{4,3,1,0,2:T(8,128)(2,1)} %copy_bitcast_fusion), channel_id=1, source_target_pairs={{0,2},{2,0},{4,6},{6,4},{8,10},{10,8},{12,14},{14,12},{16,18},{18,... | collective-permute-start | bytes 3145736 | tf_op jit(solution)/shard_map/ppermute | solution.py:67
  267.5 25.9 %collective-permute-start.39 = (bf16[64,2048]{1,0:T(8,128)(2,1)S(1)}, bf16[64,2048]{1,0:T(8,128)(2,1)S(1)}, u32[]{:S(2)}, u32[]{:S(2)}) collective-permute-start(bf16[64,2048]{1,0:T(8,128)(2,1)S(1)} %get-tuple-element.625), channel_id=1, source_target_pairs={{0,8},{2,10},{4,12},{6,14},{8,0},{10,2},{12,4},{14,6},{16,24},{18,... | collective-permute-start | bytes 786440 | tf_op jit(solution)/shard_map/ppermute | solution.py:67
  273.3 21.4 %collective-permute-start.40 = (bf16[64,2048]{1,0:T(8,128)(2,1)S(1)}, bf16[64,2048]{1,0:T(8,128)(2,1)S(1)}, u32[]{:S(2)}, u32[]{:S(2)}) collective-permute-start(bf16[64,2048]{1,0:T(8,128)(2,1)S(1)} %get-tuple-element.624), channel_id=1, source_target_pairs={{0,16},{2,18},{4,20},{6,22},{8,24},{10,26},{12,28},{14,30},{16,0},... | collective-permute-start | bytes 786440 | tf_op jit(solution)/shard_map/ppermute | solution.py:67
  274.8 19.9 %collective-permute-start.41 = (bf16[64,2048]{1,0:T(8,128)(2,1)S(1)}, bf16[64,2048]{1,0:T(8,128)(2,1)S(1)}, u32[]{:S(2)}, u32[]{:S(2)}) collective-permute-start(bf16[64,2048]{1,0:T(8,128)(2,1)S(1)} %get-tuple-element.623), channel_id=1, source_target_pairs={{0,24},{2,26},{4,28},{6,30},{8,16},{10,18},{12,20},{14,22},{16,8},... | collective-permute-start | bytes 786440 | tf_op jit(solution)/shard_map/ppermute | solution.py:67
  299.0 18.5 %collective-permute-start.46 = (bf16[2,2,64,1024]{3,2,1,0:T(8,128)(2,1)S(1)}, bf16[2,2,64,1024]{3,2,1,0:T(8,128)(2,1)S(1)}, u32[]{:S(2)}, u32[]{:S(2)}) collective-permute-start(bf16[2,2,64,1024]{3,2,1,0:T(8,128)(2,1)S(1)} %dynamic-slice_bitcast_fusion.4), channel_id=1, source_target_pairs={{0,4},{2,6},{4,0},{6,2},{8,12},{10,14},{12,8},{14,10},{16,20},{18,... | collective-permute-start | bytes 1572872 | tf_op jit(solution)/shard_map/ppermute | solution.py:67
  299.6 17.9 %collective-permute-start.45 = (bf16[2,2,64,1024]{3,2,1,0:T(8,128)(2,1)S(1)}, bf16[2,2,64,1024]{3,2,1,0:T(8,128)(2,1)S(1)}, u32[]{:S(2)}, u32[]{:S(2)}) collective-permute-start(bf16[2,2,64,1024]{3,2,1,0:T(8,128)(2,1)S(1)} %dynamic-slice_bitcast_fusion.5), channel_id=1, source_target_pairs={{0,2},{2,0},{4,6},{6,4},{8,10},{10,8},{12,14},{14,12},{16,18},{18,... | collective-permute-start | bytes 1572872 | tf_op jit(solution)/shard_map/ppermute | solution.py:67
  327.2 54.4 %collective-permute-start.51 = (bf16[2,64,2048]{2,1,0:T(8,128)(2,1)}, bf16[2,64,2048]{2,1,0:T(8,128)(2,1)S(1)}, u32[]{:S(2)}, u32[]{:S(2)}) collective-permute-start(bf16[2,64,2048]{2,1,0:T(8,128)(2,1)} %dynamic-slice_bitcast_fusion.3), channel_id=1, source_target_pairs={{0,16},{2,18},{4,20},{6,22},{8,24},{10,26},{12,28},{14,30},{16,0},... | collective-permute-start | bytes 1572872 | tf_op jit(solution)/shard_map/ppermute | solution.py:67
  334.6 47.0 %collective-permute-start.48 = (bf16[2,2,64,2048]{3,2,1,0:T(8,128)(2,1)}, bf16[2,2,64,2048]{3,2,1,0:T(8,128)(2,1)}, u32[]{:S(2)}, u32[]{:S(2)}) collective-permute-start(bf16[2,2,64,2048]{3,2,1,0:T(8,128)(2,1)} %get-tuple-element.616), channel_id=1, source_target_pairs={{0,2},{2,0},{4,6},{6,4},{8,10},{10,8},{12,14},{14,12},{16,18},{18,... | collective-permute-start | bytes 3145736 | tf_op jit(solution)/shard_map/ppermute | solution.py:67
  335.1 46.6 %collective-permute-start.49 = (bf16[2,2,64,2048]{3,2,1,0:T(8,128)(2,1)S(1)}, bf16[2,2,64,2048]{3,2,1,0:T(8,128)(2,1)}, u32[]{:S(2)}, u32[]{:S(2)}) collective-permute-start(bf16[2,2,64,2048]{3,2,1,0:T(8,128)(2,1)S(1)} %get-tuple-element.615), channel_id=1, source_target_pairs={{0,4},{2,6},{4,0},{6,2},{8,12},{10,14},{12,8},{14,10},{16,20},{18,... | collective-permute-start | bytes 3145736 | tf_op jit(solution)/shard_map/ppermute | solution.py:67
  336.7 46.7 %collective-permute-start.50 = (bf16[2,2,64,2048]{3,2,1,0:T(8,128)(2,1)S(1)}, bf16[2,2,64,2048]{3,2,1,0:T(8,128)(2,1)}, u32[]{:S(2)}, u32[]{:S(2)}) collective-permute-start(bf16[2,2,64,2048]{3,2,1,0:T(8,128)(2,1)S(1)} %get-tuple-element.614), channel_id=1, source_target_pairs={{0,6},{2,4},{4,2},{6,0},{8,14},{10,12},{12,10},{14,8},{16,22},{18,... | collective-permute-start | bytes 3145736 | tf_op jit(solution)/shard_map/ppermute | solution.py:67
  392.8 13.0 %collective-permute-start.56 = (bf16[64,2048]{1,0:T(8,128)(2,1)S(1)}, bf16[64,2048]{1,0:T(8,128)(2,1)S(1)}, u32[]{:S(2)}, u32[]{:S(2)}) collective-permute-start(bf16[64,2048]{1,0:T(8,128)(2,1)S(1)} %get-tuple-element.619), channel_id=1, source_target_pairs={{0,8},{2,10},{4,12},{6,14},{8,0},{10,2},{12,4},{14,6},{16,24},{18,... | collective-permute-start | bytes 786440 | tf_op jit(solution)/shard_map/ppermute | solution.py:67
  392.8 23.4 %collective-permute-start.57 = (bf16[64,2048]{1,0:T(8,128)(2,1)}, bf16[64,2048]{1,0:T(8,128)(2,1)S(1)}, u32[]{:S(2)}, u32[]{:S(2)}) collective-permute-start(bf16[64,2048]{1,0:T(8,128)(2,1)} %get-tuple-element.618), channel_id=1, source_target_pairs={{0,16},{2,18},{4,20},{6,22},{8,24},{10,26},{12,28},{14,30},{16,0},... | collective-permute-start | bytes 786440 | tf_op jit(solution)/shard_map/ppermute | solution.py:67
  394.2 22.0 %collective-permute-start.58 = (bf16[64,2048]{1,0:T(8,128)(2,1)}, bf16[64,2048]{1,0:T(8,128)(2,1)S(1)}, u32[]{:S(2)}, u32[]{:S(2)}) collective-permute-start(bf16[64,2048]{1,0:T(8,128)(2,1)} %get-tuple-element.617), channel_id=1, source_target_pairs={{0,24},{2,26},{4,28},{6,30},{8,16},{10,18},{12,20},{14,22},{16,8},... | collective-permute-start | bytes 786440 | tf_op jit(solution)/shard_map/ppermute | solution.py:67
  398.4 17.8 %collective-permute-start.53 = (bf16[2,2,64,512]{3,2,1,0:T(8,128)(2,1)}, bf16[2,2,64,512]{3,2,1,0:T(8,128)(2,1)}, u32[]{:S(2)}, u32[]{:S(2)}) collective-permute-start(bf16[2,2,64,512]{3,2,1,0:T(8,128)(2,1)} %get-tuple-element.622), channel_id=1, source_target_pairs={{0,2},{2,0},{4,6},{6,4},{8,10},{10,8},{12,14},{14,12},{16,18},{18,... | collective-permute-start | bytes 786440 | tf_op jit(solution)/shard_map/ppermute | solution.py:67
  399.2 17.0 %collective-permute-start.54 = (bf16[2,2,64,512]{3,2,1,0:T(8,128)(2,1)}, bf16[2,2,64,512]{3,2,1,0:T(8,128)(2,1)}, u32[]{:S(2)}, u32[]{:S(2)}) collective-permute-start(bf16[2,2,64,512]{3,2,1,0:T(8,128)(2,1)} %get-tuple-element.621), channel_id=1, source_target_pairs={{0,4},{2,6},{4,0},{6,2},{8,12},{10,14},{12,8},{14,10},{16,20},{18,... | collective-permute-start | bytes 786440 | tf_op jit(solution)/shard_map/ppermute | solution.py:67
  418.4 18.0 %collective-permute-start.62 = (bf16[64,2048]{1,0:T(8,128)(2,1)S(1)}, bf16[64,2048]{1,0:T(8,128)(2,1)S(1)}, u32[]{:S(2)}, u32[]{:S(2)}) collective-permute-start(bf16[64,2048]{1,0:T(8,128)(2,1)S(1)} %dynamic-slice_bitcast_fusion.8), channel_id=1, source_target_pairs={{0,8},{2,10},{4,12},{6,14},{8,0},{10,2},{12,4},{14,6},{16,24},{18,... | collective-permute-start | bytes 786440 | tf_op jit(solution)/shard_map/ppermute | solution.py:67
  422.3 14.1 %collective-permute-start.59 = (bf16[64,512]{1,0:T(8,128)(2,1)S(1)}, bf16[64,512]{1,0:T(8,128)(2,1)S(1)}, u32[]{:S(2)}, u32[]{:S(2)}) collective-permute-start(bf16[64,512]{1,0:T(8,128)(2,1)S(1)} %get-tuple-element.644), channel_id=1, source_target_pairs={{0,8},{2,10},{4,12},{6,14},{8,0},{10,2},{12,4},{14,6},{16,24},{18,... | collective-permute-start | bytes 196616 | tf_op jit(solution)/shard_map/ppermute | solution.py:67
  422.4 14.0 %collective-permute-start.60 = (bf16[64,512]{1,0:T(8,128)(2,1)S(1)}, bf16[64,512]{1,0:T(8,128)(2,1)S(1)}, u32[]{:S(2)}, u32[]{:S(2)}) collective-permute-start(bf16[64,512]{1,0:T(8,128)(2,1)S(1)} %get-tuple-element.643), channel_id=1, source_target_pairs={{0,16},{2,18},{4,20},{6,22},{8,24},{10,26},{12,28},{14,30},{16,0},... | collective-permute-start | bytes 196616 | tf_op jit(solution)/shard_map/ppermute | solution.py:67
  424.4 12.0 %collective-permute-start.61 = (bf16[64,512]{1,0:T(8,128)(2,1)S(1)}, bf16[64,512]{1,0:T(8,128)(2,1)S(1)}, u32[]{:S(2)}, u32[]{:S(2)}) collective-permute-start(bf16[64,512]{1,0:T(8,128)(2,1)S(1)} %get-tuple-element.642), channel_id=1, source_target_pairs={{0,24},{2,26},{4,28},{6,30},{8,16},{10,18},{12,20},{14,22},{16,8},... | collective-permute-start | bytes 196616 | tf_op jit(solution)/shard_map/ppermute | solution.py:67
  426.8 19.1 %collective-permute-start.67 = (f32[512,1024]{1,0:T(8,128)}, f32[512,1024]{1,0:T(8,128)}, u32[]{:S(2)}, u32[]{:S(2)}) collective-permute-start(f32[512,1024]{1,0:T(8,128)} %get-tuple-element.541), channel_id=1, source_target_pairs={{0,1},{1,0},{2,3},{3,2},{4,5},{5,4},{6,7},{7,6},{8,9},{9,8},{10,11... | collective-permute-start | bytes 6291464 | tf_op jit(solution)/shard_map/ppermute | solution.py:236
  439.1 17.5 %collective-permute-start.71 = (f32[512,1024]{1,0:T(8,128)}, f32[512,1024]{1,0:T(8,128)}, u32[]{:S(2)}, u32[]{:S(2)}) collective-permute-start(f32[512,1024]{1,0:T(8,128)} %convert_add_fusion.5), channel_id=1, source_target_pairs={{0,1},{1,0},{2,3},{3,2},{4,5},{5,4},{6,7},{7,6},{8,9},{9,8},{10,11... | collective-permute-start | bytes 6291464 | tf_op jit(solution)/shard_map/ppermute | solution.py:236
  440.8 15.8 %collective-permute-start.72 = (bf16[512,1024]{1,0:T(8,128)(2,1)S(1)}, bf16[512,1024]{1,0:T(8,128)(2,1)S(1)}, u32[]{:S(2)}, u32[]{:S(2)}) collective-permute-start(bf16[512,1024]{1,0:T(8,128)(2,1)S(1)} %constant_dynamic-slice_fusion.1), channel_id=1, source_target_pairs={{0,1},{1,0},{2,3},{3,2},{4,5},{5,4},{6,7},{7,6},{8,9},{9,8},{10,11... | collective-permute-start | bytes 3145736 | tf_op jit(solution)/shard_map/ppermute | solution.py:236
  (68 other events, 472.2 us)

commit v6 on v5

--- a/solution.py
+++ b/solution.py
@@ -354,7 +354,8 @@
 
 def ssm_forward_kernel(
     starts_ref, side_ref, mine_ref, got_ref, mix_own_ref, mix_other_ref, gain_ref, bias_ref, decay_ref, coef_ref,
-    rows_ref, normed_ref, drive_ref, out_ref, end_ref, y_ref, mix_ref, sems,
+    rows_out_ref, normed_out_ref, drive_out_ref, out_ref, end_ref,
+    y_ref, mix_ref, rows_ref, normed_ref, drive_ref, sems, out_sems,
 ):
     length, width = rows_ref.shape
     side = side_ref[0]
@@ -377,10 +378,19 @@
         return 0
 
     lax.fori_loop(0, length // chunk, project, 0)
+    stores = [
+        pltpu.make_async_copy(held, out, out_sems.at[k])
+        for k, (held, out) in enumerate(
+            ((drive_ref, drive_out_ref), (normed_ref, normed_out_ref), (rows_ref, rows_out_ref))
+        )
+    ]
+    for store in stores:
+        store.start()
     scan_states(
         starts_ref, 0, length // CUT, drive_ref, decay_ref, coef_ref, y_ref, None, end_ref
     )
     from_steps(y_ref, out_ref)
+    wait_all(stores)
 
 
 def ssm_rest_kernel(
@@ -423,11 +433,15 @@
             jax.ShapeDtypeStruct(decay.shape, F32),
         ),
         in_specs=[SMALL] * 2 + [ANYWHERE] * 4 + [WHOLE] * 4,
-        out_specs=(WHOLE,) * 5,
+        out_specs=(ANYWHERE,) * 3 + (WHOLE,) * 2,
         scratch_shapes=[
             pltpu.VMEM((length // CUT, tiles, LANES), F32),
             pltpu.VMEM((width, width), BF),
+            pltpu.VMEM((length, width), BF),
+            pltpu.VMEM((length, width), BF),
+            pltpu.VMEM((length, tiles, LANES), F32),
             COPIES,
+            pltpu.SemaphoreType.DMA((3,)),
         ],
         compiler_params=pltpu.CompilerParams(vmem_limit_bytes=VMEM),
         cost_estimate=pl.CostEstimate(
@@ -463,7 +477,7 @@
 
 def project_kernel(
     side_ref, normed_ref, ssm_ref, left_own_ref, left_other_ref, right_own_ref, right_other_ref,
-    query_ref, key_ref, value_ref, weights_ref, sems,
+    query_ref, key_ref, value_ref, rows_ref, weights_ref, held_ref, row_sems, sems, out_sems,
 ):
     width = normed_ref.shape[1]
     cols = width // 2
@@ -473,20 +487,34 @@
         (left_own_ref, left_other_ref, cols),
         (right_own_ref, right_other_ref, 0),
     )
-    copies = [
-        both_parts(
-            own.at[:, c : c + cols], other.at[:, c : c + cols], weights_ref.at[k], at, sems.at[k]
+    loads = [
+        pltpu.make_async_copy(ref, rows_ref.at[k], row_sems.at[k])
+        for k, ref in enumerate((normed_ref, ssm_ref))
+    ]
+    copies = []
+    for k, (own, other, c) in enumerate(sources):
+        if k < 2:
+            loads[k].start()
+        copies.append(
+            both_parts(
+                own.at[:, c : c + cols], other.at[:, c : c + cols], weights_ref.at[k], at, sems.at[k]
+            )
         )
-        for k, (own, other, c) in enumerate(sources)
-    ]
-    for k, (rows_ref, out_ref) in enumerate(
-        ((normed_ref, query_ref), (ssm_ref, key_ref), (ssm_ref, value_ref))
-    ):
+    stores = []
+    for k, (row, out_ref) in enumerate(((0, query_ref), (1, key_ref), (1, value_ref))):
+        if k < 2:
+            loads[k].wait()
         wait_all(copies[k])
-        for c in range(0, width, cols):
-            out_ref[:, c : c + cols] = dot_plain(
-                rows_ref[...], weights_ref[k, :, c : c + cols]
+        for h, c in enumerate(range(0, width, cols)):
+            held_ref[k, :, c : c + cols] = dot_plain(
+                rows_ref[row], weights_ref[k, :, c : c + cols]
             ).astype(BF)
+            store = pltpu.make_async_copy(
+                held_ref.at[k, :, c : c + cols], out_ref.at[:, c : c + cols], out_sems.at[k, h]
+            )
+            store.start()
+            stores.append(store)
+    wait_all(stores)
 
 
 def project(side, normed, ssm_out, left, right):
@@ -494,9 +522,16 @@
     return pl.pallas_call(
         project_kernel,
         out_shape=(jax.ShapeDtypeStruct((length, width), BF),) * 3,
-        in_specs=[SMALL] + [WHOLE] * 2 + [ANYWHERE] * 4,
-        out_specs=(WHOLE,) * 3,
-        scratch_shapes=[pltpu.VMEM((3, width, width), BF), pltpu.SemaphoreType.DMA((3, 2))],
+        in_specs=[SMALL] + [ANYWHERE] * 6,
+        out_specs=(ANYWHERE,) * 3,
+        scratch_shapes=[
+            pltpu.VMEM((2, length, width), BF),
+            pltpu.VMEM((3, width, width), BF),
+            pltpu.VMEM((3, length, width), BF),
+            pltpu.SemaphoreType.DMA((2,)),
+            pltpu.SemaphoreType.DMA((3, 2)),
+            pltpu.SemaphoreType.DMA((3, 2)),
+        ],
         compiler_params=pltpu.CompilerParams(vmem_limit_bytes=VMEM),
         cost_estimate=pl.CostEstimate(
             flops=6 * length * width * width, bytes_accessed=16 * length * width, transcendentals=0
@@ -545,18 +580,28 @@
 
 
 def ssm_backward_kernel(
-    starts_ref, side_ref, gkey_ref, gvalue_ref, left_own_ref, left_other_ref, right_own_ref, right_other_ref,
-    drive_ref, decay_ref, coef_ref, gmixed_ref, sum_ref, dsum_ref, g_ref, gm_ref, wkey_ref, wvalue_ref, sems,
+    starts_ref, side_ref, gkey_in_ref, gvalue_in_ref, left_own_ref, left_other_ref, right_own_ref, right_other_ref,
+    drive_in_ref, decay_ref, coef_ref, gmixed_ref, sum_ref, dsum_ref,
+    g_ref, gm_ref, wkey_ref, wvalue_ref, gkey_ref, gvalue_ref, drive_ref, sems, in_sems,
 ):
     length, width = gkey_ref.shape
     cols = width // 2
+    loads = [
+        pltpu.make_async_copy(source, held, in_sems.at[k])
+        for k, (source, held) in enumerate(
+            ((gkey_in_ref, gkey_ref), (gvalue_in_ref, gvalue_ref), (drive_in_ref, drive_ref))
+        )
+    ]
+    for load in loads[:2]:
+        load.start()
     at = cols_at(side_ref[0], cols)
     copies = both_parts(
         left_own_ref.at[:, cols:], left_other_ref.at[:, cols:], wkey_ref, at, sems.at[0]
     ) + both_parts(
         right_own_ref.at[:, :cols], right_other_ref.at[:, :cols], wvalue_ref, at, sems.at[1]
     )
-    wait_all(copies)
+    loads[2].start()
+    wait_all(copies + loads[:2])
     chunk = 256
 
     def project(i, _):
@@ -574,6 +619,7 @@
         return 0
 
     lax.fori_loop(0, length // chunk, project, 0)
+    loads[2].wait()
     part = decay_ref.shape[0] // 2
     for k in range(2):
         mine = pl.ds(k * part, part)
@@ -594,11 +640,12 @@
             jax.ShapeDtypeStruct(decay.shape, F32),
             jax.ShapeDtypeStruct(decay.shape, F32),
         ),
-        in_specs=[SMALL] * 2 + [WHOLE] * 2 + [ANYWHERE] * 4 + [WHOLE] * 3,
+        in_specs=[SMALL] * 2 + [ANYWHERE] * 7 + [WHOLE] * 2,
         out_specs=(WHOLE,) * 3,
         scratch_shapes=[pltpu.VMEM((length, tiles, LANES), F32)] * 2
         + [pltpu.VMEM((width, width), BF)] * 2
-        + [COPIES],
+        + [pltpu.VMEM((length, width), BF)] * 2
+        + [pltpu.VMEM((length, tiles, LANES), F32), COPIES, pltpu.SemaphoreType.DMA((3,))],
         compiler_params=pltpu.CompilerParams(vmem_limit_bytes=VMEM),
         cost_estimate=pl.CostEstimate(
             flops=40 * length * width * width,

time: 471 us -> 468 us (level)
  transfers between devices with their start and end apart: 73 -> 73, of which waited for: 17 -> 17; matrix products, arithmetic and copies ran while one was open for 5% -> 5% of each run, Pallas kernels for 54% -> 53%
where the time goes in v6:
time: 468 us; the launch traced here: 461 us
  Pallas kernels  250 us (53%)
  starting transfers between devices  95.7 us (20%)
  waiting for transfers between devices  48 us (10%)
  other arithmetic  38 us (8%)
  local copies, waits for them, and re-layouts  26.8 us (6%)
    ppermute x58, starting transfers between devices, swap(): return lax.ppermute(values, 'dp', [(i, i ^ mask) for i in range(count)])  93 us
    pallas_call x2, Pallas kernels, feed_forward(): pl.pallas_call(functools.partial(feed_forward_kernel, part, blocks), out_...  71.5 us
    pallas_call x1, Pallas kernels, ssm_backward(): pl.pallas_call(ssm_backward_kernel, out_shape=(jax.ShapeDtypeStruct((leng...  41.9 us
    ppermute x58, waiting for transfers between devices, swap(): return lax.ppermute(values, 'dp', [(i, i ^ mask) for i in range(count)])  39.3 us
    pallas_call x3, Pallas kernels, weight_grads(): pl.pallas_call(functools.partial(weight_grads_kernel, count), out_shape=(...  21.9 us
    pallas_call x2, Pallas kernels, norm_one_back(): pl.pallas_call(norm_one_kernel, grid_spec=pltpu.PrefetchScalarGridSpec(nu...  18.3 us
    pallas_call x1, Pallas kernels, attention_backward(): pl.pallas_call(attention_backward_kernel, grid=(heads // HEADS_EACH,), ou...  17.2 us
    pallas_call x1, Pallas kernels, ssm_rest(): pl.pallas_call(ssm_rest_kernel, out_shape=(jax.ShapeDtypeStruct((length,...  16.3 us
  transfers between devices with their start and end apart: 73, of which 17 were waited for; matrix products, arithmetic and copies ran while one was open for 5% of the time, Pallas kernels for 53%

profile of v6, /device:TPU:0, one launch (start us, length us, event | category | flops | bytes accessed | tf_op | source)
XLA Modules:
  0.0 461.0 jit_solution(8303000101063030192)
XLA Ops:
  2.3 3.0 collective-permute-start
  5.3 2.6 collective-permute-start.1
  8.9 4.2 collective-permute-done.1
  18.9 1.7 collective-permute-start.7
  20.6 2.3 collective-permute-done.6
  22.9 1.7 collective-permute-start.8
  25.4 13.3 %collective-permute-done.7 = bf16[64,2048]{1,0:T(8,128)(2,1)S(1)} collective-permute-done((bf16[64,2048]{1,0:T(8,128)(2,1)S(1)}, bf16[64,2048]{1,0:T(8,128)(2,1)S(1)}, u32[]{:S(2)}, u32[]{:S(2)}) %collective-permute-start.7) | collective-permute-done | bytes 262176 | tf_op jit(solution)/shard_map/ppermute | solution.py:67
  48.0 13.6 %ssm_forward.1 = (bf16[1024,1024]{1,0:T(8,128)(2,1)}, bf16[1024,1024]{1,0:T(8,128)(2,1)}, f32[1024,8,128]{2,1,0:T(8,128)}, bf16[256,1024]{1,0:T(8,128)(2,1)}, f32[16,8,128]{2,1,0:T(8,128)}) custom-call(s32[16]{0:T(128)} %convert_reduce_fusion.starts_ref, s32[1]{0:T(128)} %bitcast.1.side_ref, bf16[2,512,1024]{2,1,0:T(8,128)(2,1)} %bitcast.284, ...), custom_call_target="tpu_custom_call" | custom-call | flops 12884901888 | bytes 16777216 | tf_op jit(solution)/shard_map/ssm_forward/pallas_call | solution.py:426
  64.5 3.4 collective-permute-start.16
  72.2 16.3 %ssm_rest.1 = (bf16[1024,1024]{1,0:T(8,128)(2,1)}, bf16[2,1024,1024]{2,1,0:T(8,128)(2,1)}) custom-call(s32[16]{0:T(128)} %convert_reduce_fusion.starts_ref, s32[1]{0:T(128)} %bitcast.1.side_ref, bf16[2,512,1024]{2,1,0:T(8,128)(2,1)} %bitcast.285, bf16[2,512,1024]{2,1,0:T(8,128)(2,1)} %copy-done.40, ...), custom_call_target="tpu_custom_call" | custom-call | flops 10737418240 | bytes 16777216 | tf_op jit(solution)/shard_map/ssm_rest/pallas_call | solution.py:459
  95.1 2.7 collective-permute-done.23.right_other_ref.other_ref
  99.2 11.0 %project.1 = (bf16[1024,1024]{1,0:T(8,128)(2,1)}, bf16[1024,1024]{1,0:T(8,128)(2,1)}, bf16[1024,1024]{1,0:T(8,128)(2,1)}) custom-call(s32[1]{0:T(128)} %bitcast.1.side_ref, bf16[1024,1024]{1,0:T(8,128)(2,1)} %get-tuple-element.337.normed_ref.refs_0_, bf16[1024,1024]{1,0:T(8,128)(2,1)} %get-tuple-element.472.ssm_ref.refs_0_, bf16[1024,1024]{1,0:T(8,128)(2,1)} %bitcast.204, ...), custom_call_target="tpu_custom_call" | custom-call | flops 6442450944 | bytes 16777216 | tf_op jit(solution)/shard_map/project/pallas_call | solution.py:522
  111.7 1.7 maximum_select_fusion.7
  117.6 4.8 %collective-permute-start.26 = (bf16[64,2048]{1,0:T(8,128)(2,1)S(1)}, bf16[64,2048]{1,0:T(8,128)(2,1)S(1)}, u32[]{:S(2)}, u32[]{:S(2)}) collective-permute-start(bf16[64,2048]{1,0:T(8,128)(2,1)S(1)} %get-tuple-element.363), channel_id=1, source_target_pairs={{0,8},{2,10},{4,12},{6,14},{8,0},{10,2},{12,4},{14,6},{16,24},{18,... | collective-permute-start | bytes 786440 | tf_op jit(solution)/shard_map/ppermute | solution.py:67
  126.0 10.7 %attention_forward.1 = (bf16[1024,1024]{1,0:T(8,128)(2,1)}, f32[8,1024,1]{2,1,0:T(8,128)}) custom-call(s32[1024,1]{1,0:T(8,128)} %copy.76.seg_col_ref, s32[1,1024]{1,0:T(1,128)} %fusion.34.seg_row_ref, bf16[1024,1024]{1,0:T(8,128)(2,1)} %get-tuple-element.352.query_ref, bf16[1024,1024]{1,0:T(8,128)(2,1)} %get-tuple-element.353.key_ref, ...), custom_call_target="tpu_custom_call" | custom-call | flops 1879048192 | bytes 8388608 | tf_op jit(solution)/shard_map/attention_forward/pallas_call | solution.py:741
  136.7 7.1 %collective-permute-done.27 = bf16[64,2048]{1,0:T(8,128)(2,1)S(1)} collective-permute-done((bf16[64,2048]{1,0:T(8,128)(2,1)S(1)}, bf16[64,2048]{1,0:T(8,128)(2,1)S(1)}, u32[]{:S(2)}, u32[]{:S(2)}) %collective-permute-start.27) | collective-permute-done | bytes 262176 | tf_op jit(solution)/shard_map/ppermute | solution.py:67
  146.7 8.6 %middle.1 = (f32[1024,1024]{1,0:T(8,128)}, bf16[1024,1024]{1,0:T(8,128)(2,1)}) custom-call(s32[1]{0:T(128)} %bitcast.1.side_ref, bf16[1024,1024]{1,0:T(8,128)(2,1)} %get-tuple-element.368.attended_ref.refs_3_, bf16[1024,1024]{1,0:T(8,128)(2,1)} %bitcast.200, bf16[1024,1024]{1,0:T(8,128)(2,1)} %copy-done.6, bf16[1024,1024]{1,0:T(8,128)(2,1)} %get-tuple-element.369.rows_ref, ...), custom_call_target="tpu_custom_call" | custom-call | flops 2147483648 | bytes 12582912 | tf_op jit(solution)/shard_map/middle/pallas_call | solution.py:1009
  162.9 34.5 %feed_forward.2 = (bf16[1024,1024]{1,0:T(8,128)(2,1)}, bf16[1024,1024]{1,0:T(8,128)(2,1)}, bf16[1024,1024]{1,0:T(8,128)(2,1)}, bf16[1024,1024]{1,0:T(8,128)(2,1)...) custom-call(s32[2]{0:T(128)} %pad_add_fusion.place_ref, bf16[1024,1024]{1,0:T(8,128)(2,1)} %get-tuple-element.382.own_ref, ...), custom_call_target="tpu_custom_call" | custom-call | flops 30064771072 | bytes 50331648 | tf_op jit(solution)/shard_map/feed_forward/pallas_call | solution.py:953
  197.4 2.1 copy_bitcast_fusion.2
  202.5 37.0 %feed_forward.3 = (bf16[1024,1024]{1,0:T(8,128)(2,1)}, bf16[1024,1024]{1,0:T(8,128)(2,1)}, bf16[1024,1024]{1,0:T(8,128)(2,1)}, bf16[1024,1024]{1,0:T(8,128)(2,1)...) custom-call(s32[2]{0:T(128)} %pad_add_fusion.place_ref, bf16[1024,1024]{1,0:T(8,128)(2,1)} %get-tuple-element.382.own_ref, ...), custom_call_target="tpu_custom_call" | custom-call | flops 30064771072 | bytes 50331648 | tf_op jit(solution)/shard_map/feed_forward/pallas_call | solution.py:953
  240.0 1.8 fusion.6
  243.5 2.6 collective-permute-done.38.theirs_ref
  247.4 12.0 %norm_two_back.1 = (f32[1024,1024]{1,0:T(8,128)}, bf16[1024,1024]{1,0:T(8,128)(2,1)}, bf16[1024,1024]{1,0:T(8,128)(2,1)}, f32[2,1024]{1,0:T(2,128)}) custom-call(s32[1]{0:T(128)} %bitcast.1.side_ref, bf16[1024,1024]{1,0:T(8,128)(2,1)} %get-tuple-element.426.mine_ref, bf16[1024,1024]{1,0:T(8,128)(2,1)} %copy-done.20, ...), custom_call_target="tpu_custom_call" | custom-call | flops 2147483648 | bytes 25165824 | tf_op jit(solution)/shard_map/norm_two_back/pallas_call | solution.py:1055
  264.8 5.8 %collective-permute-start.39 = (bf16[64,2048]{1,0:T(8,128)(2,1)S(1)}, bf16[64,2048]{1,0:T(8,128)(2,1)S(1)}, u32[]{:S(2)}, u32[]{:S(2)}) collective-permute-start(bf16[64,2048]{1,0:T(8,128)(2,1)S(1)} %get-tuple-element.625), channel_id=1, source_target_pairs={{0,8},{2,10},{4,12},{6,14},{8,0},{10,2},{12,4},{14,6},{16,24},{18,... | collective-permute-start | bytes 786440 | tf_op jit(solution)/shard_map/ppermute | solution.py:67
  273.4 17.2 %attention_backward.1 = (bf16[1024,1024]{1,0:T(8,128)(2,1)}, bf16[1024,1024]{1,0:T(8,128)(2,1)}, bf16[1024,1024]{1,0:T(8,128)(2,1)}) custom-call(s32[1024,1]{1,0:T(8,128)} %copy.76.seg_col_ref, s32[1,1024]{1,0:T(1,128)} %fusion.34.seg_row_ref, bf16[1024,1024]{1,0:T(8,128)(2,1)} %get-tuple-element.352.query_ref, ...), custom_call_target="tpu_custom_call" | custom-call | flops 4697620480 | bytes 14680064 | tf_op jit(solution)/shard_map/attention_backward/pallas_call | solution.py:809
  298.4 8.0 %weight_grads.3 = (bf16[1024,1024]{1,0:T(8,128)(2,1)}, bf16[1024,1024]{1,0:T(8,128)(2,1)}) custom-call(s32[1]{0:T(128)} %bitcast.1.side_ref, bf16[1024,1024]{1,0:T(8,128)(2,1)} %get-tuple-element.337.normed_ref.refs_0_, bf16[1024,1024]{1,0:T(8,128)(2,1)} %get-tuple-element.462.refs_1_, bf16[1024,1024]{1,0:T(8,128)(2,1)} %get-tuple-element.463.refs_2_.gquery_ref, ...), custom_call_target="tpu_custom_call" | custom-call | flops 4294967296 | bytes 12582912 | tf_op jit(solution)/shard_map/weight_grads/pallas_call | solution.py:1219
  306.6 8.1 %weight_grads.4 = (bf16[1024,1024]{1,0:T(8,128)(2,1)}, bf16[1024,1024]{1,0:T(8,128)(2,1)}) custom-call(s32[1]{0:T(128)} %bitcast.1.side_ref, bf16[1024,1024]{1,0:T(8,128)(2,1)} %get-tuple-element.472.ssm_ref.refs_0_, bf16[1024,1024]{1,0:T(8,128)(2,1)} %get-tuple-element.458.gkey_in_ref.refs_1_, bf16[1024,1024]{1,0:T(8,128)(2,1)} %get-tuple-element.459.gvalue_in_ref.refs_2_), custom_call_target="tpu_custom_call" | custom-call | flops 4294967296 | bytes 12582912 | tf_op jit(solution)/shard_map/weight_grads/pallas_call | solution.py:1219
  317.6 2.7 add_convert_fusion.1
  320.6 2.5 add_convert_fusion
  324.4 6.0 %collective-permute-start.51 = (bf16[2,64,2048]{2,1,0:T(8,128)(2,1)}, bf16[2,64,2048]{2,1,0:T(8,128)(2,1)S(1)}, u32[]{:S(2)}, u32[]{:S(2)}) collective-permute-start(bf16[2,64,2048]{2,1,0:T(8,128)(2,1)} %dynamic-slice_bitcast_fusion.3), channel_id=1, source_target_pairs={{0,16},{2,18},{4,20},{6,22},{8,24},{10,26},{12,28},{14,30},{16,0},... | collective-permute-start | bytes 1572872 | tf_op jit(solution)/shard_map/ppermute | solution.py:67
  335.6 41.9 %ssm_backward.1 = (bf16[1024,1024]{1,0:T(8,128)(2,1)}, f32[16,8,128]{2,1,0:T(8,128)}, f32[16,8,128]{2,1,0:T(8,128)}) custom-call(s32[16]{0:T(128)} %convert_reduce_fusion.starts_ref, s32[1]{0:T(128)} %bitcast.1.side_ref, bf16[1024,1024]{1,0:T(8,128)(2,1)} %get-tuple-element.458.gkey_in_ref.refs_1_, ...), custom_call_target="tpu_custom_call" | custom-call | flops 42949672960 | bytes 20971520 | tf_op jit(solution)/shard_map/ssm_backward/pallas_call | solution.py:636
  377.6 3.1 collective-permute-done.50
  380.8 2.6 fusion.2
  383.4 5.7 %weight_grads.5 = (bf16[1024,512]{1,0:T(8,128)(2,1)}, bf16[1024,512]{1,0:T(8,128)(2,1)}) custom-call(s32[1]{0:T(128)} %bitcast.1.side_ref, bf16[1024,1024]{1,0:T(8,128)(2,1)} %get-tuple-element.337.normed_ref.refs_0_, bf16[1024,1024]{1,0:T(8,128)(2,1)} %get-tuple-element.523.refs_1_.gmixed_ref), custom_call_target="tpu_custom_call" | custom-call | flops 2147483648 | bytes 6291456 | tf_op jit(solution)/shard_map/weight_grads/pallas_call | solution.py:1219
  391.5 2.9 collective-permute-start.58
  397.9 5.0 %collective-permute-done.56 = bf16[64,2048]{1,0:T(8,128)(2,1)S(1)} collective-permute-done((bf16[64,2048]{1,0:T(8,128)(2,1)S(1)}, bf16[64,2048]{1,0:T(8,128)(2,1)S(1)}, u32[]{:S(2)}, u32[]{:S(2)}) %collective-permute-start.56) | collective-permute-done | bytes 262176 | tf_op jit(solution)/shard_map/ppermute | solution.py:67
  403.0 1.7 collective-permute-start.55
  404.7 8.7 %norm_one_back.2 = (f32[512,1024]{1,0:T(8,128)}, f32[2,1024]{1,0:T(2,128)}) custom-call(s32[1]{0:T(128)} %bitcast.1.side_ref, bf16[1024,1024]{1,0:T(8,128)(2,1)} %get-tuple-element.463.refs_2_.gquery_ref, bf16[1024,1024]{1,0:T(8,128)(2,1)} %get-tuple-element.523.refs_1_.gmixed_ref, bf16[1024,1024]{1,0:T(8,128)(2,1)} %get-tuple-element.369.rows_ref, ...), custom_call_target="tpu_custom_call" | custom-call | flops 2147483648 | bytes 10485760 | tf_op jit(solution)/shard_map/norm_one_back/pallas_call | solution.py:1110
  415.7 3.9 collective-permute-start.62
  419.7 2.0 collective-permute-start.60
  421.7 2.4 collective-permute-start.61
  424.0 9.6 %norm_one_back.3 = (f32[2,512,1024]{2,1,0:T(8,128)}, f32[2,1024]{1,0:T(2,128)}) custom-call(s32[1]{0:T(128)} %bitcast.1.side_ref, bf16[1024,1024]{1,0:T(8,128)(2,1)} %get-tuple-element.463.refs_2_.gquery_ref, bf16[1024,1024]{1,0:T(8,128)(2,1)} %get-tuple-element.523.refs_1_.gmixed_ref, bf16[1024,1024]{1,0:T(8,128)(2,1)} %get-tuple-element.369.rows_ref, ...), custom_call_target="tpu_custom_call" | custom-call | flops 2147483648 | bytes 10485760 | tf_op jit(solution)/shard_map/norm_one_back/pallas_call | solution.py:1110
  434.5 1.8 convert_add_fusion.5
  438.8 1.9 collective-permute-done.63
  445.1 2.6 put.1
  448.6 2.0 collective-permute-start.69
  450.6 2.4 collective-permute-start.70
  454.8 4.6 %layer_out.1 = f32[2,512,1024]{2,1,0:T(8,128)} custom-call(s32[1]{0:T(128)} %bitcast.1.side_ref, f32[1024,1024]{1,0:T(8,128)} %get-tuple-element.551.middle_ref, bf16[1024,1024]{1,0:T(8,128)(2,1)} %get-tuple-element.552.own_ref, bf16[1024,1024]{1,0:T(8,128)(2,1)} %get-tuple-element.553.other_ref, f32[512,1024]{1,0:T(8,128)} %collective-permute-done.71.sum_ref, ...), custom_call_target="tpu_custom_call" | custom-call | flops 2097152 | bytes 12582912 | tf_op jit(solution)/shard_map/layer_out/pallas_call | solution.py:1163
  (313 shorter events, 104.8 us)
Async XLA Ops:
  15.4 23.9 %collective-permute-start.3 = (bf16[2,2,72,512]{3,2,1,0:T(8,128)(2,1)S(1)}, bf16[2,2,72,512]{3,2,1,0:T(8,128)(2,1)S(1)}, u32[]{:S(2)}, u32[]{:S(2)}) collective-permute-start(bf16[2,2,72,512]{3,2,1,0:T(8,128)(2,1)S(1)} %maximum_select_fusion.19), channel_id=1, source_target_pairs={{0,2},{2,0},{4,6},{6,4},{8,10},{10,8},{12,14},{14,12},{16,18},{18,... | collective-permute-start | bytes 884744 | tf_op jit(solution)/shard_map/ppermute | solution.py:67
  16.9 22.4 %collective-permute-start.4 = (bf16[2,2,72,512]{3,2,1,0:T(8,128)(2,1)S(1)}, bf16[2,2,72,512]{3,2,1,0:T(8,128)(2,1)S(1)}, u32[]{:S(2)}, u32[]{:S(2)}) collective-permute-start(bf16[2,2,72,512]{3,2,1,0:T(8,128)(2,1)S(1)} %maximum_select_fusion.19), channel_id=1, source_target_pairs={{0,4},{2,6},{4,0},{6,2},{8,12},{10,14},{12,8},{14,10},{16,20},{18,... | collective-permute-start | bytes 884744 | tf_op jit(solution)/shard_map/ppermute | solution.py:67
  18.4 20.9 %collective-permute-start.5 = (bf16[2,2,72,512]{3,2,1,0:T(8,128)(2,1)S(1)}, bf16[2,2,72,512]{3,2,1,0:T(8,128)(2,1)S(1)}, u32[]{:S(2)}, u32[]{:S(2)}) collective-permute-start(bf16[2,2,72,512]{3,2,1,0:T(8,128)(2,1)S(1)} %maximum_select_fusion.19), channel_id=1, source_target_pairs={{0,6},{2,4},{4,2},{6,0},{8,14},{10,12},{12,10},{14,8},{16,22},{18,... | collective-permute-start | bytes 884744 | tf_op jit(solution)/shard_map/ppermute | solution.py:67
  18.9 19.9 %collective-permute-start.7 = (bf16[64,2048]{1,0:T(8,128)(2,1)S(1)}, bf16[64,2048]{1,0:T(8,128)(2,1)S(1)}, u32[]{:S(2)}, u32[]{:S(2)}) collective-permute-start(bf16[64,2048]{1,0:T(8,128)(2,1)S(1)} %pad_maximum_fusion.6), channel_id=1, source_target_pairs={{0,16},{2,18},{4,20},{6,22},{8,24},{10,26},{12,28},{14,30},{16,0},... | collective-permute-start | bytes 786440 | tf_op jit(solution)/shard_map/ppermute | solution.py:67
  22.9 15.9 %collective-permute-start.8 = (bf16[64,2048]{1,0:T(8,128)(2,1)S(1)}, bf16[64,2048]{1,0:T(8,128)(2,1)S(1)}, u32[]{:S(2)}, u32[]{:S(2)}) collective-permute-start(bf16[64,2048]{1,0:T(8,128)(2,1)S(1)} %pad_maximum_fusion.6), channel_id=1, source_target_pairs={{0,24},{2,26},{4,28},{6,30},{8,16},{10,18},{12,20},{14,22},{16,8},... | collective-permute-start | bytes 786440 | tf_op jit(solution)/shard_map/ppermute | solution.py:67
  43.9 17.7 %collective-permute-start.10 = (bf16[2,2,64,1024]{3,2,1,0:T(8,128)(2,1)S(1)}, bf16[2,2,64,1024]{3,2,1,0:T(8,128)(2,1)S(1)}, u32[]{:S(2)}, u32[]{:S(2)}) collective-permute-start(bf16[2,2,64,1024]{3,2,1,0:T(8,128)(2,1)S(1)} %get-tuple-element.313), channel_id=1, source_target_pairs={{0,4},{2,6},{4,0},{6,2},{8,12},{10,14},{12,8},{14,10},{16,20},{18,... | collective-permute-start | bytes 1572872 | tf_op jit(solution)/shard_map/ppermute | solution.py:67
  45.5 16.1 %collective-permute-start.9 = (bf16[2,2,64,1024]{3,2,1,0:T(8,128)(2,1)S(1)}, bf16[2,2,64,1024]{3,2,1,0:T(8,128)(2,1)S(1)}, u32[]{:S(2)}, u32[]{:S(2)}) collective-permute-start(bf16[2,2,64,1024]{3,2,1,0:T(8,128)(2,1)S(1)} %get-tuple-element.311), channel_id=1, source_target_pairs={{0,2},{2,0},{4,6},{6,4},{8,10},{10,8},{12,14},{14,12},{16,18},{18,... | collective-permute-start | bytes 1572872 | tf_op jit(solution)/shard_map/ppermute | solution.py:67
  63.3 25.9 %collective-permute-start.14 = (bf16[2,2,2,64,1024]{4,3,2,1,0:T(8,128)(2,1)S(1)}, bf16[2,2,2,64,1024]{4,3,2,1,0:T(8,128)(2,1)S(1)}, u32[]{:S(2)}, u32[]{:S(2)}) collective-permute-start(bf16[2,2,2,64,1024]{4,3,2,1,0:T(8,128)(2,1)S(1)} %maximum_select_fusion.4), channel_id=1, source_target_pairs={{0,4},{2,6},{4,0},{6,2},{8,12},{10,14},{12,8},{14,10},{16,20},{18,... | collective-permute-start | bytes 3145736 | tf_op jit(solution)/shard_map/ppermute | solution.py:67
  63.9 25.3 %collective-permute-start.15 = (bf16[2,2,2,64,1024]{4,3,1,0,2:T(8,128)(2,1)S(1)}, bf16[2,2,2,64,1024]{4,3,1,0,2:T(8,128)(2,1)S(1)}, u32[]{:S(2)}, u32[]{:S(2)}) collective-permute-start(bf16[2,2,2,64,1024]{4,3,1,0,2:T(8,128)(2,1)S(1)} %maximum_select_fusion.5), channel_id=1, source_target_pairs={{0,2},{2,0},{4,6},{6,4},{8,10},{10,8},{12,14},{14,12},{16,18},{18,... | collective-permute-start | bytes 3145736 | tf_op jit(solution)/shard_map/ppermute | solution.py:67
  64.5 24.0 %collective-permute-start.16 = (bf16[64,2048]{1,0:T(8,128)(2,1)S(1)}, bf16[64,2048]{1,0:T(8,128)(2,1)S(1)}, u32[]{:S(2)}, u32[]{:S(2)}) collective-permute-start(bf16[64,2048]{1,0:T(8,128)(2,1)S(1)} %get-tuple-element.332), channel_id=1, source_target_pairs={{0,8},{2,10},{4,12},{6,14},{8,0},{10,2},{12,4},{14,6},{16,24},{18,... | collective-permute-start | bytes 786440 | tf_op jit(solution)/shard_map/ppermute | solution.py:67
  67.9 21.4 %collective-permute-start.17 = (bf16[64,2048]{1,0:T(8,128)(2,1)S(1)}, bf16[64,2048]{1,0:T(8,128)(2,1)S(1)}, u32[]{:S(2)}, u32[]{:S(2)}) collective-permute-start(bf16[64,2048]{1,0:T(8,128)(2,1)S(1)} %get-tuple-element.332), channel_id=1, source_target_pairs={{0,16},{2,18},{4,20},{6,22},{8,24},{10,26},{12,28},{14,30},{16,0},... | collective-permute-start | bytes 786440 | tf_op jit(solution)/shard_map/ppermute | solution.py:67
  70.7 18.5 %collective-permute-start.18 = (bf16[64,2048]{1,0:T(8,128)(2,1)S(1)}, bf16[64,2048]{1,0:T(8,128)(2,1)S(1)}, u32[]{:S(2)}, u32[]{:S(2)}) collective-permute-start(bf16[64,2048]{1,0:T(8,128)(2,1)S(1)} %get-tuple-element.332), channel_id=1, source_target_pairs={{0,24},{2,26},{4,28},{6,30},{8,16},{10,18},{12,20},{14,22},{16,8},... | collective-permute-start | bytes 786440 | tf_op jit(solution)/shard_map/ppermute | solution.py:67
  92.0 18.2 %collective-permute-start.20 = (bf16[2,2,64,1024]{3,2,1,0:T(8,128)(2,1)S(1)}, bf16[2,2,64,1024]{3,2,1,0:T(8,128)(2,1)}, u32[]{:S(2)}, u32[]{:S(2)}) collective-permute-start(bf16[2,2,64,1024]{3,2,1,0:T(8,128)(2,1)S(1)} %get-tuple-element.343), channel_id=1, source_target_pairs={{0,2},{2,0},{4,6},{6,4},{8,10},{10,8},{12,14},{14,12},{16,18},{18,... | collective-permute-start | bytes 1572872 | tf_op jit(solution)/shard_map/ppermute | solution.py:67
  93.6 16.7 %collective-permute-start.21 = (bf16[2,2,64,1024]{3,2,1,0:T(8,128)(2,1)S(1)}, bf16[2,2,64,1024]{3,2,1,0:T(8,128)(2,1)}, u32[]{:S(2)}, u32[]{:S(2)}) collective-permute-start(bf16[2,2,64,1024]{3,2,1,0:T(8,128)(2,1)S(1)} %get-tuple-element.345), channel_id=1, source_target_pairs={{0,4},{2,6},{4,0},{6,2},{8,12},{10,14},{12,8},{14,10},{16,20},{18,... | collective-permute-start | bytes 1572872 | tf_op jit(solution)/shard_map/ppermute | solution.py:67
  113.4 30.4 %collective-permute-start.24 = (bf16[2,2,2,64,1024]{4,3,2,1,0:T(8,128)(2,1)S(1)}, bf16[2,2,2,64,1024]{4,3,2,1,0:T(8,128)(2,1)}, u32[]{:S(2)}, u32[]{:S(2)}) collective-permute-start(bf16[2,2,2,64,1024]{4,3,2,1,0:T(8,128)(2,1)S(1)} %maximum_select_fusion.7), channel_id=1, source_target_pairs={{0,4},{2,6},{4,0},{6,2},{8,12},{10,14},{12,8},{14,10},{16,20},{18,... | collective-permute-start | bytes 3145736 | tf_op jit(solution)/shard_map/ppermute | solution.py:67
  115.1 28.8 %collective-permute-start.25 = (bf16[2,2,2,64,1024]{4,3,2,1,0:T(8,128)(2,1)S(1)}, bf16[2,2,2,64,1024]{4,3,2,1,0:T(8,128)(2,1)}, u32[]{:S(2)}, u32[]{:S(2)}) collective-permute-start(bf16[2,2,2,64,1024]{4,3,2,1,0:T(8,128)(2,1)S(1)} %maximum_select_fusion.8), channel_id=1, source_target_pairs={{0,2},{2,0},{4,6},{6,4},{8,10},{10,8},{12,14},{14,12},{16,18},{18,... | collective-permute-start | bytes 3145736 | tf_op jit(solution)/shard_map/ppermute | solution.py:67
  117.6 19.1 %collective-permute-start.26 = (bf16[64,2048]{1,0:T(8,128)(2,1)S(1)}, bf16[64,2048]{1,0:T(8,128)(2,1)S(1)}, u32[]{:S(2)}, u32[]{:S(2)}) collective-permute-start(bf16[64,2048]{1,0:T(8,128)(2,1)S(1)} %get-tuple-element.363), channel_id=1, source_target_pairs={{0,8},{2,10},{4,12},{6,14},{8,0},{10,2},{12,4},{14,6},{16,24},{18,... | collective-permute-start | bytes 786440 | tf_op jit(solution)/shard_map/ppermute | solution.py:67
  122.4 21.4 %collective-permute-start.27 = (bf16[64,2048]{1,0:T(8,128)(2,1)S(1)}, bf16[64,2048]{1,0:T(8,128)(2,1)S(1)}, u32[]{:S(2)}, u32[]{:S(2)}) collective-permute-start(bf16[64,2048]{1,0:T(8,128)(2,1)S(1)} %get-tuple-element.363), channel_id=1, source_target_pairs={{0,16},{2,18},{4,20},{6,22},{8,24},{10,26},{12,28},{14,30},{16,0},... | collective-permute-start | bytes 786440 | tf_op jit(solution)/shard_map/ppermute | solution.py:67
  123.9 19.9 %collective-permute-start.28 = (bf16[64,2048]{1,0:T(8,128)(2,1)S(1)}, bf16[64,2048]{1,0:T(8,128)(2,1)S(1)}, u32[]{:S(2)}, u32[]{:S(2)}) collective-permute-start(bf16[64,2048]{1,0:T(8,128)(2,1)S(1)} %get-tuple-element.363), channel_id=1, source_target_pairs={{0,24},{2,26},{4,28},{6,30},{8,16},{10,18},{12,20},{14,22},{16,8},... | collective-permute-start | bytes 786440 | tf_op jit(solution)/shard_map/ppermute | solution.py:67
  159.0 38.5 %collective-permute-start.31 = (bf16[2,2,2,64,1024]{4,3,2,1,0:T(8,128)(2,1)}, bf16[2,2,2,64,1024]{4,3,2,1,0:T(8,128)(2,1)S(1)}, u32[]{:S(2)}, u32[]{:S(2)}) collective-permute-start(bf16[2,2,2,64,1024]{4,3,2,1,0:T(8,128)(2,1)} %maximum_select_fusion.10), channel_id=1, source_target_pairs={{0,4},{2,6},{4,0},{6,2},{8,12},{10,14},{12,8},{14,10},{16,20},{18,... | collective-permute-start | bytes 3145736 | tf_op jit(solution)/shard_map/ppermute | solution.py:67
  160.2 37.3 %collective-permute-start.32 = (bf16[2,2,2,64,1024]{4,3,2,1,0:T(8,128)(2,1)S(1)}, bf16[2,2,2,64,1024]{4,3,2,1,0:T(8,128)(2,1)S(1)}, u32[]{:S(2)}, u32[]{:S(2)}) collective-permute-start(bf16[2,2,2,64,1024]{4,3,2,1,0:T(8,128)(2,1)S(1)} %maximum_select_fusion.11), channel_id=1, source_target_pairs={{0,2},{2,0},{4,6},{6,4},{8,10},{10,8},{12,14},{14,12},{16,18},{18,... | collective-permute-start | bytes 3145736 | tf_op jit(solution)/shard_map/ppermute | solution.py:67
  199.6 39.9 %collective-permute-start.35 = (bf16[2,2,2,64,1024]{4,3,1,0,2:T(8,128)(2,1)S(1)}, bf16[2,2,2,64,1024]{4,3,1,0,2:T(8,128)(2,1)S(1)}, u32[]{:S(2)}, u32[]{:S(2)}) collective-permute-start(bf16[2,2,2,64,1024]{4,3,1,0,2:T(8,128)(2,1)S(1)} %copy_bitcast_fusion.2), channel_id=1, source_target_pairs={{0,2},{2,0},{4,6},{6,4},{8,10},{10,8},{12,14},{14,12},{16,18},{18,... | collective-permute-start | bytes 3145736 | tf_op jit(solution)/shard_map/ppermute | solution.py:67
  201.3 38.2 %collective-permute-start.34 = (bf16[2,2,2,64,1024]{4,3,1,0,2:T(8,128)(2,1)S(1)}, bf16[2,2,2,64,1024]{4,3,1,0,2:T(8,128)(2,1)}, u32[]{:S(2)}, u32[]{:S(2)}) collective-permute-start(bf16[2,2,2,64,1024]{4,3,1,0,2:T(8,128)(2,1)S(1)} %copy_bitcast_fusion.3), channel_id=1, source_target_pairs={{0,4},{2,6},{4,0},{6,2},{8,12},{10,14},{12,8},{14,10},{16,20},{18,... | collective-permute-start | bytes 3145736 | tf_op jit(solution)/shard_map/ppermute | solution.py:67
  241.9 17.5 %collective-permute-start.37 = (bf16[2,2,64,1024]{3,2,1,0:T(8,128)(2,1)S(1)}, bf16[2,2,64,1024]{3,2,1,0:T(8,128)(2,1)S(1)}, u32[]{:S(2)}, u32[]{:S(2)}) collective-permute-start(bf16[2,2,64,1024]{3,2,1,0:T(8,128)(2,1)S(1)} %dynamic-slice_bitcast_fusion.6), channel_id=1, source_target_pairs={{0,4},{2,6},{4,0},{6,2},{8,12},{10,14},{12,8},{14,10},{16,20},{18,... | collective-permute-start | bytes 1572872 | tf_op jit(solution)/shard_map/ppermute | solution.py:67
  242.9 16.5 %collective-permute-start.36 = (bf16[2,2,64,1024]{3,2,1,0:T(8,128)(2,1)S(1)}, bf16[2,2,64,1024]{3,2,1,0:T(8,128)(2,1)S(1)}, u32[]{:S(2)}, u32[]{:S(2)}) collective-permute-start(bf16[2,2,64,1024]{3,2,1,0:T(8,128)(2,1)S(1)} %dynamic-slice_bitcast_fusion.7), channel_id=1, source_target_pairs={{0,2},{2,0},{4,6},{6,4},{8,10},{10,8},{12,14},{14,12},{16,18},{18,... | collective-permute-start | bytes 1572872 | tf_op jit(solution)/shard_map/ppermute | solution.py:67
  262.3 29.6 %collective-permute-start.42 = (bf16[2,2,2,64,1024]{4,3,1,0,2:T(8,128)(2,1)}, bf16[2,2,2,64,1024]{4,3,1,0,2:T(8,128)(2,1)}, u32[]{:S(2)}, u32[]{:S(2)}) collective-permute-start(bf16[2,2,2,64,1024]{4,3,1,0,2:T(8,128)(2,1)} %copy_bitcast_fusion.1), channel_id=1, source_target_pairs={{0,4},{2,6},{4,0},{6,2},{8,12},{10,14},{12,8},{14,10},{16,20},{18,... | collective-permute-start | bytes 3145736 | tf_op jit(solution)/shard_map/ppermute | solution.py:67
  264.2 27.7 %collective-permute-start.43 = (bf16[2,2,2,64,1024]{4,3,1,0,2:T(8,128)(2,1)}, bf16[2,2,2,64,1024]{4,3,1,0,2:T(8,128)(2,1)}, u32[]{:S(2)}, u32[]{:S(2)}) collective-permute-start(bf16[2,2,2,64,1024]{4,3,1,0,2:T(8,128)(2,1)} %copy_bitcast_fusion), channel_id=1, source_target_pairs={{0,2},{2,0},{4,6},{6,4},{8,10},{10,8},{12,14},{14,12},{16,18},{18,... | collective-permute-start | bytes 3145736 | tf_op jit(solution)/shard_map/ppermute | solution.py:67
  264.8 25.9 %collective-permute-start.39 = (bf16[64,2048]{1,0:T(8,128)(2,1)S(1)}, bf16[64,2048]{1,0:T(8,128)(2,1)S(1)}, u32[]{:S(2)}, u32[]{:S(2)}) collective-permute-start(bf16[64,2048]{1,0:T(8,128)(2,1)S(1)} %get-tuple-element.625), channel_id=1, source_target_pairs={{0,8},{2,10},{4,12},{6,14},{8,0},{10,2},{12,4},{14,6},{16,24},{18,... | collective-permute-start | bytes 786440 | tf_op jit(solution)/shard_map/ppermute | solution.py:67
  270.5 21.4 %collective-permute-start.40 = (bf16[64,2048]{1,0:T(8,128)(2,1)S(1)}, bf16[64,2048]{1,0:T(8,128)(2,1)S(1)}, u32[]{:S(2)}, u32[]{:S(2)}) collective-permute-start(bf16[64,2048]{1,0:T(8,128)(2,1)S(1)} %get-tuple-element.624), channel_id=1, source_target_pairs={{0,16},{2,18},{4,20},{6,22},{8,24},{10,26},{12,28},{14,30},{16,0},... | collective-permute-start | bytes 786440 | tf_op jit(solution)/shard_map/ppermute | solution.py:67
  272.0 19.9 %collective-permute-start.41 = (bf16[64,2048]{1,0:T(8,128)(2,1)S(1)}, bf16[64,2048]{1,0:T(8,128)(2,1)S(1)}, u32[]{:S(2)}, u32[]{:S(2)}) collective-permute-start(bf16[64,2048]{1,0:T(8,128)(2,1)S(1)} %get-tuple-element.623), channel_id=1, source_target_pairs={{0,24},{2,26},{4,28},{6,30},{8,16},{10,18},{12,20},{14,22},{16,8},... | collective-permute-start | bytes 786440 | tf_op jit(solution)/shard_map/ppermute | solution.py:67
  296.2 18.5 %collective-permute-start.46 = (bf16[2,2,64,1024]{3,2,1,0:T(8,128)(2,1)S(1)}, bf16[2,2,64,1024]{3,2,1,0:T(8,128)(2,1)S(1)}, u32[]{:S(2)}, u32[]{:S(2)}) collective-permute-start(bf16[2,2,64,1024]{3,2,1,0:T(8,128)(2,1)S(1)} %dynamic-slice_bitcast_fusion.4), channel_id=1, source_target_pairs={{0,4},{2,6},{4,0},{6,2},{8,12},{10,14},{12,8},{14,10},{16,20},{18,... | collective-permute-start | bytes 1572872 | tf_op jit(solution)/shard_map/ppermute | solution.py:67
  296.9 17.9 %collective-permute-start.45 = (bf16[2,2,64,1024]{3,2,1,0:T(8,128)(2,1)S(1)}, bf16[2,2,64,1024]{3,2,1,0:T(8,128)(2,1)S(1)}, u32[]{:S(2)}, u32[]{:S(2)}) collective-permute-start(bf16[2,2,64,1024]{3,2,1,0:T(8,128)(2,1)S(1)} %dynamic-slice_bitcast_fusion.5), channel_id=1, source_target_pairs={{0,2},{2,0},{4,6},{6,4},{8,10},{10,8},{12,14},{14,12},{16,18},{18,... | collective-permute-start | bytes 1572872 | tf_op jit(solution)/shard_map/ppermute | solution.py:67
  324.4 53.1 %collective-permute-start.51 = (bf16[2,64,2048]{2,1,0:T(8,128)(2,1)}, bf16[2,64,2048]{2,1,0:T(8,128)(2,1)S(1)}, u32[]{:S(2)}, u32[]{:S(2)}) collective-permute-start(bf16[2,64,2048]{2,1,0:T(8,128)(2,1)} %dynamic-slice_bitcast_fusion.3), channel_id=1, source_target_pairs={{0,16},{2,18},{4,20},{6,22},{8,24},{10,26},{12,28},{14,30},{16,0},... | collective-permute-start | bytes 1572872 | tf_op jit(solution)/shard_map/ppermute | solution.py:67
  331.9 45.6 %collective-permute-start.48 = (bf16[2,2,64,2048]{3,2,1,0:T(8,128)(2,1)}, bf16[2,2,64,2048]{3,2,1,0:T(8,128)(2,1)}, u32[]{:S(2)}, u32[]{:S(2)}) collective-permute-start(bf16[2,2,64,2048]{3,2,1,0:T(8,128)(2,1)} %get-tuple-element.616), channel_id=1, source_target_pairs={{0,2},{2,0},{4,6},{6,4},{8,10},{10,8},{12,14},{14,12},{16,18},{18,... | collective-permute-start | bytes 3145736 | tf_op jit(solution)/shard_map/ppermute | solution.py:67
  332.4 45.2 %collective-permute-start.49 = (bf16[2,2,64,2048]{3,2,1,0:T(8,128)(2,1)S(1)}, bf16[2,2,64,2048]{3,2,1,0:T(8,128)(2,1)}, u32[]{:S(2)}, u32[]{:S(2)}) collective-permute-start(bf16[2,2,64,2048]{3,2,1,0:T(8,128)(2,1)S(1)} %get-tuple-element.615), channel_id=1, source_target_pairs={{0,4},{2,6},{4,0},{6,2},{8,12},{10,14},{12,8},{14,10},{16,20},{18,... | collective-permute-start | bytes 3145736 | tf_op jit(solution)/shard_map/ppermute | solution.py:67
  334.0 46.7 %collective-permute-start.50 = (bf16[2,2,64,2048]{3,2,1,0:T(8,128)(2,1)S(1)}, bf16[2,2,64,2048]{3,2,1,0:T(8,128)(2,1)}, u32[]{:S(2)}, u32[]{:S(2)}) collective-permute-start(bf16[2,2,64,2048]{3,2,1,0:T(8,128)(2,1)S(1)} %get-tuple-element.614), channel_id=1, source_target_pairs={{0,6},{2,4},{4,2},{6,0},{8,14},{10,12},{12,10},{14,8},{16,22},{18,... | collective-permute-start | bytes 3145736 | tf_op jit(solution)/shard_map/ppermute | solution.py:67
  390.0 13.0 %collective-permute-start.56 = (bf16[64,2048]{1,0:T(8,128)(2,1)S(1)}, bf16[64,2048]{1,0:T(8,128)(2,1)S(1)}, u32[]{:S(2)}, u32[]{:S(2)}) collective-permute-start(bf16[64,2048]{1,0:T(8,128)(2,1)S(1)} %get-tuple-element.619), channel_id=1, source_target_pairs={{0,8},{2,10},{4,12},{6,14},{8,0},{10,2},{12,4},{14,6},{16,24},{18,... | collective-permute-start | bytes 786440 | tf_op jit(solution)/shard_map/ppermute | solution.py:67
  390.0 23.4 %collective-permute-start.57 = (bf16[64,2048]{1,0:T(8,128)(2,1)}, bf16[64,2048]{1,0:T(8,128)(2,1)S(1)}, u32[]{:S(2)}, u32[]{:S(2)}) collective-permute-start(bf16[64,2048]{1,0:T(8,128)(2,1)} %get-tuple-element.618), channel_id=1, source_target_pairs={{0,16},{2,18},{4,20},{6,22},{8,24},{10,26},{12,28},{14,30},{16,0},... | collective-permute-start | bytes 786440 | tf_op jit(solution)/shard_map/ppermute | solution.py:67
  391.5 21.9 %collective-permute-start.58 = (bf16[64,2048]{1,0:T(8,128)(2,1)}, bf16[64,2048]{1,0:T(8,128)(2,1)S(1)}, u32[]{:S(2)}, u32[]{:S(2)}) collective-permute-start(bf16[64,2048]{1,0:T(8,128)(2,1)} %get-tuple-element.617), channel_id=1, source_target_pairs={{0,24},{2,26},{4,28},{6,30},{8,16},{10,18},{12,20},{14,22},{16,8},... | collective-permute-start | bytes 786440 | tf_op jit(solution)/shard_map/ppermute | solution.py:67
  395.6 17.8 %collective-permute-start.53 = (bf16[2,2,64,512]{3,2,1,0:T(8,128)(2,1)}, bf16[2,2,64,512]{3,2,1,0:T(8,128)(2,1)}, u32[]{:S(2)}, u32[]{:S(2)}) collective-permute-start(bf16[2,2,64,512]{3,2,1,0:T(8,128)(2,1)} %get-tuple-element.622), channel_id=1, source_target_pairs={{0,2},{2,0},{4,6},{6,4},{8,10},{10,8},{12,14},{14,12},{16,18},{18,... | collective-permute-start | bytes 786440 | tf_op jit(solution)/shard_map/ppermute | solution.py:67
  396.5 16.9 %collective-permute-start.54 = (bf16[2,2,64,512]{3,2,1,0:T(8,128)(2,1)}, bf16[2,2,64,512]{3,2,1,0:T(8,128)(2,1)}, u32[]{:S(2)}, u32[]{:S(2)}) collective-permute-start(bf16[2,2,64,512]{3,2,1,0:T(8,128)(2,1)} %get-tuple-element.621), channel_id=1, source_target_pairs={{0,4},{2,6},{4,0},{6,2},{8,12},{10,14},{12,8},{14,10},{16,20},{18,... | collective-permute-start | bytes 786440 | tf_op jit(solution)/shard_map/ppermute | solution.py:67
  415.7 18.0 %collective-permute-start.62 = (bf16[64,2048]{1,0:T(8,128)(2,1)S(1)}, bf16[64,2048]{1,0:T(8,128)(2,1)S(1)}, u32[]{:S(2)}, u32[]{:S(2)}) collective-permute-start(bf16[64,2048]{1,0:T(8,128)(2,1)S(1)} %dynamic-slice_bitcast_fusion.8), channel_id=1, source_target_pairs={{0,8},{2,10},{4,12},{6,14},{8,0},{10,2},{12,4},{14,6},{16,24},{18,... | collective-permute-start | bytes 786440 | tf_op jit(solution)/shard_map/ppermute | solution.py:67
  419.6 14.1 %collective-permute-start.59 = (bf16[64,512]{1,0:T(8,128)(2,1)S(1)}, bf16[64,512]{1,0:T(8,128)(2,1)S(1)}, u32[]{:S(2)}, u32[]{:S(2)}) collective-permute-start(bf16[64,512]{1,0:T(8,128)(2,1)S(1)} %get-tuple-element.644), channel_id=1, source_target_pairs={{0,8},{2,10},{4,12},{6,14},{8,0},{10,2},{12,4},{14,6},{16,24},{18,... | collective-permute-start | bytes 196616 | tf_op jit(solution)/shard_map/ppermute | solution.py:67
  419.7 14.0 %collective-permute-start.60 = (bf16[64,512]{1,0:T(8,128)(2,1)S(1)}, bf16[64,512]{1,0:T(8,128)(2,1)S(1)}, u32[]{:S(2)}, u32[]{:S(2)}) collective-permute-start(bf16[64,512]{1,0:T(8,128)(2,1)S(1)} %get-tuple-element.643), channel_id=1, source_target_pairs={{0,16},{2,18},{4,20},{6,22},{8,24},{10,26},{12,28},{14,30},{16,0},... | collective-permute-start | bytes 196616 | tf_op jit(solution)/shard_map/ppermute | solution.py:67
  421.7 12.0 %collective-permute-start.61 = (bf16[64,512]{1,0:T(8,128)(2,1)S(1)}, bf16[64,512]{1,0:T(8,128)(2,1)S(1)}, u32[]{:S(2)}, u32[]{:S(2)}) collective-permute-start(bf16[64,512]{1,0:T(8,128)(2,1)S(1)} %get-tuple-element.642), channel_id=1, source_target_pairs={{0,24},{2,26},{4,28},{6,30},{8,16},{10,18},{12,20},{14,22},{16,8},... | collective-permute-start | bytes 196616 | tf_op jit(solution)/shard_map/ppermute | solution.py:67
  424.0 19.1 %collective-permute-start.67 = (f32[512,1024]{1,0:T(8,128)}, f32[512,1024]{1,0:T(8,128)}, u32[]{:S(2)}, u32[]{:S(2)}) collective-permute-start(f32[512,1024]{1,0:T(8,128)} %get-tuple-element.541), channel_id=1, source_target_pairs={{0,1},{1,0},{2,3},{3,2},{4,5},{5,4},{6,7},{7,6},{8,9},{9,8},{10,11... | collective-permute-start | bytes 6291464 | tf_op jit(solution)/shard_map/ppermute | solution.py:236
  436.3 17.5 %collective-permute-start.71 = (f32[512,1024]{1,0:T(8,128)}, f32[512,1024]{1,0:T(8,128)}, u32[]{:S(2)}, u32[]{:S(2)}) collective-permute-start(f32[512,1024]{1,0:T(8,128)} %convert_add_fusion.5), channel_id=1, source_target_pairs={{0,1},{1,0},{2,3},{3,2},{4,5},{5,4},{6,7},{7,6},{8,9},{9,8},{10,11... | collective-permute-start | bytes 6291464 | tf_op jit(solution)/shard_map/ppermute | solution.py:236
  438.0 15.8 %collective-permute-start.72 = (bf16[512,1024]{1,0:T(8,128)(2,1)S(1)}, bf16[512,1024]{1,0:T(8,128)(2,1)S(1)}, u32[]{:S(2)}, u32[]{:S(2)}) collective-permute-start(bf16[512,1024]{1,0:T(8,128)(2,1)S(1)} %constant_dynamic-slice_fusion.1), channel_id=1, source_target_pairs={{0,1},{1,0},{2,3},{3,2},{4,5},{5,4},{6,7},{7,6},{8,9},{9,8},{10,11... | collective-permute-start | bytes 3145736 | tf_op jit(solution)/shard_map/ppermute | solution.py:236
  (68 other events, 472.0 us)
